TPU v7x, 32 devices: a whole 2x2x4 slice. The times are simulated.
32 devices in a mesh: dp: 4 (over y, core), expert: 8 (over z, x).
Axes of the slice: x: 2, y: 2, z: 4, core: 2. Of those that a mesh axis runs over, the one named last changes fastest.
Arguments:
- frames_in: bfloat16 [32, 256, 1024], P(('dp', 'expert')), may hold values from -6 to 6
- pit_order: int32 [16, 2], replicated, may hold values from 0 to 1, each once within a row
- expert_ids: int32 [32, 256, 2], P(('dp', 'expert')), may hold values from 0 to 7, all different within a row; in each aligned block of 256 rows (0 to 255, 256 to 511, ..., all dimensions but the last counted through in order) at most 80 rows name the same one
- norm_gains: float32 [2, 1024], replicated, may hold values from 0.25 to 1.75
- attn_qkv: bfloat16 [3, 1024, 1024], P(None, 'expert'), may hold values from -6 to 6
- attn_out: bfloat16 [1024, 1024], P('expert'), may hold values from -0.1875 to 0.1875
- router: float32 [1024, 8], replicated, may hold values from -0.046875 to 0.046875
- expert_in: bfloat16 [8, 1024, 4096], P('expert', None, 'dp'), may hold values from -0.1875 to 0.1875
- expert_out: bfloat16 [8, 4096, 1024], P('expert', 'dp'), may hold values from -0.09375 to 0.09375
Outputs:
- layer_out: bfloat16 [32, 256, 1024], P(('dp', 'expert'))
Inputs may be any that keep to these rules, and one draw needn't show every extreme that they name: `expert_ids`: at most 80 frames of one stream name the same expert, and in every draw some stream names some expert exactly 80 times; each frame names 2 different experts.
All inputs are finite; a program needn't handle non-finite values.
Results may differ from a plain program's by a relative error of at most 0.011.
Values may be sent and summed in bfloat16 or wider, within the bound.
No kernel may reach another device: no remote copies, remote signals or barrier semaphores. Data moves between devices by JAX's collectives and lax.ppermute only.
A program may use at most 128 MiB of HBM per device.

v0:
```python
import jax
import jax.numpy as jnp
from jax import lax
from jax.sharding import PartitionSpec as P

HEAD_DIM = 64


epsilon = 1e-05


def from_partner(block, axis, bit):
    count = lax.axis_size(axis)
    route = []
    for low in range(count):
        high = low | 1 << bit
        if high != low and high < count:
            route += [(low, high), (high, low)]
    return lax.ppermute(block, axis, route)


def layer_norm(values, gain):
    mean = jnp.mean(values, axis=-1, keepdims=True)
    centred = values - mean
    spread = jnp.mean(centred * centred, axis=-1, keepdims=True)
    return centred * lax.rsqrt(spread + epsilon) * gain


def body(
    frames_in, pit_order, expert_ids, norm_gains, attn_qkv, attn_out, router, expert_in, expert_out
):
    dp_count = lax.axis_size("dp")
    exp_count = lax.axis_size("expert")
    dp_index = lax.axis_index("dp")
    exp_index = lax.axis_index("expert")
    frames = frames_in.shape[1]
    width = frames_in.shape[2]
    heads = width // HEAD_DIM
    top = expert_ids.shape[2]
    capacity = frames * top * 5 // (4 * exp_count)
    partner = from_partner(frames_in, "dp", dp_count.bit_length() - 2)
    half = dp_count // 2
    speaker = dp_index // half
    meeting = dp_index % half * exp_count + exp_index
    source = pit_order[meeting, speaker]
    stream = jnp.where(source == speaker, frames_in[0], partner[0])
    resid = stream.astype(jnp.float32)
    normed = layer_norm(resid, norm_gains[0]).astype(jnp.bfloat16)
    columns = normed
    projected = jnp.einsum(
        "fc,jcd->jfd",
        columns,
        lax.all_gather(attn_qkv, "expert", axis=1, tiled=True),
        preferred_element_type=jnp.float32,
    )
    projected = projected.astype(jnp.bfloat16).reshape(3, frames, heads, HEAD_DIM)
    scores = (
        jnp.einsum("qhd,khd->hqk", projected[0], projected[1], preferred_element_type=jnp.float32)
        / HEAD_DIM**0.5
    )
    highest = jnp.max(scores, axis=-1, keepdims=True)
    weights = jnp.exp(scores - highest)
    probs = (weights / jnp.sum(weights, axis=-1, keepdims=True)).astype(jnp.bfloat16)
    context = jnp.einsum("hqk,khd->qhd", probs, projected[2], preferred_element_type=jnp.float32)
    context = context.reshape(frames, width).astype(jnp.bfloat16)
    columns = context
    attended = jnp.dot(
        columns,
        lax.all_gather(attn_out, "expert", axis=0, tiled=True),
        preferred_element_type=jnp.float32,
    )
    mixed = (resid + attended).astype(jnp.bfloat16)
    mixed_wide = mixed.astype(jnp.float32)
    normed2 = layer_norm(mixed_wide, norm_gains[1]).astype(jnp.bfloat16)
    logits = jnp.dot(normed2.astype(jnp.float32), router, precision=lax.Precision.HIGHEST)
    chosen = expert_ids[0]
    picked = jnp.take_along_axis(logits, chosen, axis=1)
    gate_first = jax.nn.sigmoid(picked[:, 0] - picked[:, 1])
    gate_second = 1.0 - gate_first
    flat = chosen.reshape(-1)
    onehot = (flat[:, None] == jnp.arange(exp_count, dtype=jnp.int32)[None, :]).astype(jnp.int32)
    ranks = jnp.sum(onehot * (jnp.cumsum(onehot, axis=0) - 1), axis=1)
    positions = flat * capacity + ranks
    rows = jnp.repeat(normed2, top, axis=0)
    outgoing = jnp.zeros((exp_count * capacity, width), jnp.bfloat16).at[positions].set(rows)
    outgoing = outgoing.reshape(exp_count, capacity, width)
    piece = lax.all_gather(
        lax.all_to_all(outgoing, "expert", split_axis=0, concat_axis=0, tiled=True),
        "dp",
        axis=0,
        tiled=True,
    )
    flat_rows = piece.reshape(-1, piece.shape[-1])
    hidden = jax.nn.silu(
        jnp.dot(flat_rows, expert_in[0], preferred_element_type=jnp.float32)
    ).astype(jnp.bfloat16)
    partials = (
        jnp.dot(hidden, expert_out[0], preferred_element_type=jnp.float32)
        .astype(jnp.bfloat16)
        .reshape(piece.shape)
    )
    summed = lax.psum_scatter(partials, "dp", scatter_dimension=0, tiled=True).astype(jnp.float32)
    answer = summed.astype(jnp.bfloat16)
    returned = lax.all_to_all(answer, "expert", split_axis=0, concat_axis=0, tiled=True)
    back = returned.reshape(exp_count * capacity, width)[positions]
    back = back.reshape(frames, top, width).astype(jnp.float32)
    result = mixed_wide + gate_first[:, None] * back[:, 0] + gate_second[:, None] * back[:, 1]
    return result.astype(jnp.bfloat16)[None]


def solution(mesh):
    return jax.shard_map(
        body,
        mesh=mesh,
        in_specs=(
            P(("dp", "expert"), None, None),
            P(),
            P(("dp", "expert"), None, None),
            P(),
            P(None, "expert", None),
            P("expert", None),
            P(),
            P("expert", None, "dp"),
            P("expert", "dp", None),
        ),
        out_specs=P(("dp", "expert"), None, None),
        check_vma=False,
    )
```

profile of v0, /device:TPU:16, one launch (start us, length us, event | category | flops | bytes accessed | tf_op | source)
XLA Modules:
  0.0 362.3 jit_solution(8958401638173468485)
XLA Ops:
  7.3 1.6 collective-permute-start
  10.8 1.3 dynamic_slice.3
  13.0 1.1 reduce-window.6
  15.3 6.0 %collective-permute-done = bf16[1,256,1024]{2,1,0:T(8,128)(2,1)S(1)} collective-permute-done((bf16[1,256,1024]{2,1,0:T(8,128)(2,1)}, bf16[1,256,1024]{2,1,0:T(8,128)(2,1)S(1)}, u32[]{:S(2)}, u32[]{:S(2)}) %collective-permute-start) | collective-permute-done | bytes 524320 | tf_op jit(solution)/shard_map/ppermute | solution.py:19
  21.2 1.3 convert_reduce_fusion.1
  22.8 86.0 %all-gather.4.cloned.1.call-done = bf16[3,1024,1024]{2,1,0:T(8,128)(2,1)} async-done(((bf16[3,128,1024]{2,1,0:T(8,128)(2,1)}), bf16[3,1024,1024]{2,1,0:T(8,128)(2,1)}) %all-gather.4.cloned.1.call-update) | async-done | bytes 6291472 | tf_op jit(solution)/shard_map/all_gather | solution.py:53
  108.8 4.7 %fusion.9 = bf16[3,256,1024]{2,1,0:T(8,128)(2,1)S(1)} fusion(bf16[3,1024,1024]{2,1,0:T(8,128)(2,1)} %all-gather.4.cloned.1.call-done, bf16[1,256,1024]{2,1,0:T(8,128)(2,1)S(1)} %get-tuple-element.8, f32[1024]{0:T(1024)S(1)} %bitcast.102, f32[256]{0:T(256)S(1)} %add_rsqrt_fusion.1, f32[256]{0:T(256)S(1)} %broadcast_multiply_fusion.2), kind=kOutput, calls=%fused_computation.19 | convolution fusion | flops 1612709888 | bytes 8394752 | tf_op jit(solution)/shard_map/fc,jcd->jfd/dot_general | solution.py:50
  113.5 1.1 fusion.50
  114.6 2.1 copy.38
  116.6 2.1 copy.37
  118.7 1.0 copy.36
  119.7 4.7 %fusion.52 = (f32[16,256]{1,0:T(8,128)S(1)}, f32[16,256,256]{1,2,0:T(8,128)}) fusion(bf16[256,16,64]{0,2,1:T(8,128)(2,1)} %bitcast.95, bf16[256,16,64]{0,2,1:T(8,128)(2,1)} %bitcast.94), kind=kOutput, calls=%fused_computation.82 | convolution fusion | flops 137363712 | bytes 5259264 | tf_op jit(solution)/shard_map/sub | solution.py:62
  124.4 3.5 fusion.12
  127.9 30.8 %all-gather.6.cloned.1.call-done = bf16[1024,1024]{1,0:T(8,128)(2,1)} async-done(((bf16[128,1024]{1,0:T(8,128)(2,1)}), bf16[1024,1024]{1,0:T(8,128)(2,1)}) %all-gather.6.cloned.1.call-update) | async-done | bytes 2097168 | tf_op jit(solution)/shard_map/all_gather | solution.py:69
  158.7 2.6 convert_reduce_fusion
  163.7 1.2 reshape.164
  165.0 3.6 scatter_custom_fusion
  168.6 33.6 %all_to_all.10 = bf16[8,80,1024]{2,1,0:T(8,128)(2,1)} all-to-all(bf16[8,80,1024]{2,1,0:T(8,128)(2,1)S(1)} %bitcast.93), channel_id=1, replica_groups=mesh['dp'=4,'expert'=8] {'expert'}, dimensions={0} | all-to-all | bytes 2621440 | tf_op jit(solution)/shard_map/all_to_all | solution.py:88
  202.4 40.7 %all-gather.8.cloned.1.call-done = bf16[32,80,1024]{2,1,0:T(8,128)(2,1)} async-done(((bf16[8,80,1024]{2,1,0:T(8,128)(2,1)}), bf16[32,80,1024]{2,1,0:T(8,128)(2,1)}) %all-gather.8.cloned.1.call-update) | async-done | bytes 5242896 | tf_op jit(solution)/shard_map/all_gather | solution.py:87
  243.1 7.8 %fusion.5 = f32[2560,1024]{1,0:T(8,128)S(1)} fusion(bf16[2560,1024]{1,0:T(8,128)(2,1)} %bitcast.103, bf16[1,1024,1024]{2,1,0:T(8,128)(2,1)S(1)} %copy-done), kind=kOutput, calls=%fused_computation.11 | convolution fusion | flops 5368709120 | bytes 17825792 | tf_op jit(solution)/shard_map/dot_general | solution.py:95
  250.9 7.5 %convolution_convert_fusion = bf16[2560,1024]{1,0:T(8,128)(2,1)} fusion(f32[2560,1024]{1,0:T(8,128)S(1)} %fusion.5, bf16[1,1024,1024]{2,1,0:T(8,128)(2,1)S(1)} %copy-done.6), kind=kOutput, calls=%fused_computation.5 | convolution fusion | flops 5384437760 | bytes 17825792 | tf_op jit(solution)/shard_map/dot_general | solution.py:98
  258.4 51.6 %reduce-scatter.2.cloned.1.call-done = bf16[8,80,1024]{2,1,0:T(8,128)(2,1)} async-done(((bf16[32,80,1024]{2,1,0:T(8,128)(2,1)}), bf16[8,80,1024]{2,1,0:T(8,128)(2,1)}) %reduce-scatter.2.cloned.1.call-update) | async-done | bytes 1310736 | tf_op jit(solution)/shard_map/reduce_scatter | solution.py:102
  310.0 6.0 %all-to-all-start.1 = ((bf16[8,80,1024]{2,1,0:T(8,128)(2,1)}), bf16[8,80,1024]{2,1,0:T(8,128)(2,1)S(1)}, u32[]{:S(2)}, u32[]{:S(2)}) async-start(bf16[8,80,1024]{2,1,0:T(8,128)(2,1)} %reduce-scatter.2.cloned.1.call-done), calls=%async_computation.2 | async-start | bytes 2621440 | tf_op jit(solution)/shard_map/all_to_all | solution.py:104
  316.8 1.0 reshape.154
  318.5 1.5 fusion.53
  320.0 3.5 gather_fusion.1
  324.3 0.9 and_select_fusion
  325.5 18.7 %all-to-all-done.1 = bf16[8,80,1024]{2,1,0:T(8,128)(2,1)S(1)} async-done(((bf16[8,80,1024]{2,1,0:T(8,128)(2,1)}), bf16[8,80,1024]{2,1,0:T(8,128)(2,1)S(1)}, u32[]{:S(2)}, u32[]{:S(2)}) %all-to-all-start.1) | async-done | bytes 1310752 | tf_op jit(solution)/shard_map/all_to_all | solution.py:104
  344.1 2.9 gather_fusion
  347.1 3.5 reshape.145
  350.5 4.0 %fusion.49 = (f32[256,1,1024]{2,1,0:T(1,128)S(1)}, f32[256,1,1024]{2,1,0:T(1,128)S(1)}) fusion(f32[256,2,1024]{2,1,0:T(2,128)} %reshape.145), kind=kLoop, calls=%fused_computation.79 | loop fusion | bytes 4194304 | tf_op jit(solution)/shard_map/slice | solution.py:107
  354.5 1.2 fusion.29
  (48 shorter events, 9.4 us)
Async XLA Ops:
  6.5 236.6 %copy-start = (bf16[1,1024,1024]{2,1,0:T(8,128)(2,1)S(1)}, bf16[1,1024,1024]{2,1,0:T(8,128)(2,1)}, u32[]{:S(2)}) copy-start(bf16[1,1024,1024]{2,1,0:T(8,128)(2,1)} %param.16) | copy-start | bytes 6291460
  6.5 102.2 %all-gather.4.cloned.1.call-start = ((), (), s32[]{:S(2)}) async-start(), calls=%async_computation.3 | async-start | bytes 7077888 | tf_op jit(solution)/shard_map/all_gather | solution.py:53
  7.3 151.4 %all-gather.6.cloned.1.call-start = ((), (), s32[]{:S(2)}) async-start(), calls=%async_computation.4 | async-start | bytes 2359296 | tf_op jit(solution)/shard_map/all_gather | solution.py:69
  7.3 13.9 %collective-permute-start = (bf16[1,256,1024]{2,1,0:T(8,128)(2,1)}, bf16[1,256,1024]{2,1,0:T(8,128)(2,1)S(1)}, u32[]{:S(2)}, u32[]{:S(2)}) collective-permute-start(bf16[1,256,1024]{2,1,0:T(8,128)(2,1)} %param.9), channel_id=1, source_target_pairs={{0,16},{16,0},{8,24},{24,8},{1,17},{17,1},{9,25},{25,9},{2,18},{18... | collective-permute-start | bytes 1572872 | tf_op jit(solution)/shard_map/ppermute | solution.py:19
  8.9 234.2 %all-gather.8.cloned.1.call-start = ((), (), s32[]{:S(2)}) async-start(), calls=%async_computation.5 | async-start | bytes 6553600 | tf_op jit(solution)/shard_map/all_gather | solution.py:87
  119.7 4.7 %copy-start.4 = (bf16[1,256,1024]{1,2,0:T(8,128)(2,1)S(1)}, bf16[1,256,1024]{1,2,0:T(8,128)(2,1)}, u32[]{:S(2)}) copy-start(bf16[1,256,1024]{1,2,0:T(8,128)(2,1)} %copy.36) | copy-start | bytes 1572868
  161.3 0.8 copy-start.1
  162.4 0.8 copy-start.3
  202.2 107.8 %reduce-scatter.2.cloned.1.call-start = ((), (), s32[]{:S(2)}) async-start(), calls=%async_computation.6 | async-start | bytes 6553600 | tf_op jit(solution)/shard_map/reduce_scatter | solution.py:102
  243.1 7.8 %copy-start.6 = (bf16[1,1024,1024]{2,1,0:T(8,128)(2,1)S(1)}, bf16[1,1024,1024]{2,1,0:T(8,128)(2,1)}, u32[]{:S(2)}) copy-start(bf16[1,1024,1024]{2,1,0:T(8,128)(2,1)} %param.17) | copy-start | bytes 6291460
  258.4 57.6 %copy-start.5 = (s32[1,256,2]{1,2,0:T(2,128)S(1)}, s32[1,256,2]{1,2,0:T(2,128)}, u32[]{:S(2)}) copy-start(s32[1,256,2]{1,2,0:T(2,128)} %param.11) | copy-start | bytes 6148
  310.0 34.1 %all-to-all-start.1 = ((bf16[8,80,1024]{2,1,0:T(8,128)(2,1)}), bf16[8,80,1024]{2,1,0:T(8,128)(2,1)S(1)}, u32[]{:S(2)}, u32[]{:S(2)}) async-start(bf16[8,80,1024]{2,1,0:T(8,128)(2,1)} %reduce-scatter.2.cloned.1.call-done), calls=%async_computation.2 | async-start | bytes 2621440 | tf_op jit(solution)/shard_map/all_to_all | solution.py:104
  347.0 7.5 %copy-start.2 = (bf16[256,1024]{1,0:T(8,128)(2,1)S(1)}, bf16[256,1024]{1,0:T(8,128)(2,1)}, u32[]{:S(2)}) copy-start(bf16[256,1024]{1,0:T(8,128)(2,1)} %copy-done.1) | copy-start | bytes 1572868
Sparse Core Ops, SparseCore 0:
  9.5 99.1 all-gather.3
  110.9 47.7 all-gather.5
  202.3 40.7 all-gather.7
  258.5 51.3 reduce-scatter.1
where the time goes:
time: 367 us; the launch traced here: 362 us
  waiting for transfers between devices  234 us (64%)
  blocking collectives  33.6 us (9%)
  local copies, waits for them, and re-layouts  33 us (9%)
  matrix products  32.3 us (9%)
  between operations  14 us (4%)
  starting transfers between devices  7.91 us (2%)
  other arithmetic  7.15 us (2%)
    all_gather x1, waiting for transfers between devices, body(): lax.all_gather(attn_qkv, 'expert', axis=1, tiled=True)  86 us
    reduce_scatter x1, waiting for transfers between devices, body(): lax.psum_scatter(partials, 'dp', scatter_dimension=0, tiled=True)  51.6 us
    all_gather x1, waiting for transfers between devices, body(): lax.all_gather(lax.all_to_all(outgoing, 'expert', split_axis=0, concat_ax...  40.7 us
    all_to_all x1, blocking collectives, body(): lax.all_to_all(outgoing, 'expert', split_axis=0, concat_axis=0, tiled=True)  33.6 us
    all_gather x1, waiting for transfers between devices, body(): lax.all_gather(attn_out, 'expert', axis=0, tiled=True)  30.8 us
    all_to_all x1, waiting for transfers between devices, body(): lax.all_to_all(answer, 'expert', split_axis=0, concat_axis=0, tiled=True)  18.7 us
    dot_general x1, matrix products, body(): jnp.dot(flat_rows, expert_in[0], preferred_element_type=jnp.float32)  7.77 us
    dot_general x1, matrix products, body(): jnp.dot(hidden, expert_out[0], preferred_element_type=jnp.float32)  7.52 us
  transfers between devices with their start and end apart: 6, of which 6 were waited for; matrix products, arithmetic and copies ran while one was open for 10% of the time, Pallas kernels for 0%

commit v1 on v0

v1 whole, which is shorter than its diff:
```python
import functools

import jax
import jax.numpy as jnp
from jax import lax
from jax.experimental import pallas as pl
from jax.experimental.pallas import tpu as pltpu
from jax.sharding import PartitionSpec as P

HEAD_DIM = 64
epsilon = 1e-05
BF16 = jnp.bfloat16
F32 = jnp.float32
VMEM = pl.BlockSpec(memory_space=pltpu.VMEM)
SMEM = pl.BlockSpec(memory_space=pltpu.SMEM)
ANY = pl.BlockSpec(memory_space=pl.ANY)


def params(mib):
    return pltpu.CompilerParams(vmem_limit_bytes=mib << 20)


def cost(flops, moved, special=0):
    return pl.CostEstimate(flops=flops, bytes_accessed=moved, transcendentals=special)


def swap(block, axis, mask):
    count = lax.axis_size(axis)
    return lax.ppermute(block, axis, [(i, i ^ mask) for i in range(count)])


def layer_norm(values, gain):
    mean = jnp.mean(values, axis=-1, keepdims=True)
    centred = values - mean
    spread = jnp.mean(centred * centred, axis=-1, keepdims=True)
    return centred * lax.rsqrt(spread + epsilon) * gain


def norm_kernel(count, place_ref, gain_ref, *refs):
    raw, (normed_ref, own_ref) = refs[:count], refs[count:]
    gain = gain_ref[0:1, :]
    for k in range(count):
        where = place_ref[k]
        block = raw[k][0]
        normed_ref[where] = layer_norm(block.astype(F32), gain).astype(BF16)

        @pl.when(where == 0)
        def _():
            own_ref[...] = block


def attention_kernel(count, shards, me_ref, normed_ref, *refs):
    pieces, outs = refs[:shards], refs[shards : shards + count]
    weights, sems = refs[shards + count :]
    depth, cols = pieces[0].shape[1:]
    me = me_ref[0]
    copies = []
    for k in range(shards):
        rows = pl.ds(pl.multiple_of((me ^ k) * depth, depth), depth)
        copy = pltpu.make_async_copy(pieces[k], weights.at[:, rows, :], sems.at[k])
        copy.start()
        copies.append(copy)
    for copy in copies:
        copy.wait()
    frames = normed_ref.shape[1]
    head = lax.broadcasted_iota(jnp.int32, (frames, cols), 1) // HEAD_DIM
    scale = HEAD_DIM**-0.5
    for k in range(count):
        x = normed_ref[k]
        q, key, val = [
            jnp.dot(x, weights[i], preferred_element_type=F32).astype(BF16) for i in range(3)
        ]
        q = q * jnp.asarray(scale, BF16)
        total = jnp.zeros((frames, cols), F32)
        for h in range(cols // HEAD_DIM):
            mine = head == h
            scores = lax.dot_general(
                jnp.where(mine, q, jnp.zeros_like(q)),
                key,
                (((1,), (1,)), ((), ())),
                preferred_element_type=F32,
            )
            exps = jnp.exp(scores - jnp.max(scores, axis=-1, keepdims=True))
            norm = 1.0 / jnp.sum(exps, axis=-1, keepdims=True)
            probs = (exps * norm).astype(BF16)
            total = jnp.where(mine, jnp.dot(probs, val, preferred_element_type=F32), total)
        outs[k][...] = total.astype(BF16)


def mix_kernel(count, experts, capacity, me_ref, own_ref, proj_ref, gain_ref, router_ref, rows_ref, cols_ref, *refs):
    blocks, (slots_ref, mixed_ref, gate_ref) = refs[:count], refs[count:]
    frames, depth = blocks[0].shape
    me = me_ref[0]
    total = own_ref[...].astype(F32)
    for k in range(count):
        rows = pl.ds(pl.multiple_of((me ^ k) * depth, depth), depth)
        total += jnp.dot(blocks[k][...], proj_ref[rows, :], preferred_element_type=F32)
    mixed = total.astype(BF16)
    mixed_ref[...] = mixed
    normed = layer_norm(mixed.astype(F32), gain_ref[1:2, :]).astype(BF16)
    first, second = rows_ref[0:1, :], rows_ref[1:2, :]
    which = lax.broadcasted_iota(jnp.int32, (experts, frames), 0)
    named = ((which == first) | (which == second)).astype(F32)
    before = (
        lax.broadcasted_iota(jnp.int32, (frames, frames), 0)
        < lax.broadcasted_iota(jnp.int32, (frames, frames), 1)
    ).astype(F32)
    rank = jnp.dot(named, before, preferred_element_type=F32) + (which * capacity).astype(F32)
    slot = lax.broadcasted_iota(jnp.int32, (experts * capacity, frames), 0).astype(F32)
    place0 = jnp.sum(jnp.where(which == first, rank, 0.0), axis=0, keepdims=True)
    place1 = jnp.sum(jnp.where(which == second, rank, 0.0), axis=0, keepdims=True)
    spread = ((slot == place0) | (slot == place1)).astype(F32).astype(BF16)
    slots_ref[...] = jnp.dot(spread, normed, preferred_element_type=F32).astype(BF16)
    high = router_ref[...].astype(BF16)
    rest = router_ref[...] - high.astype(F32)
    middle = rest.astype(BF16)
    low = (rest - middle.astype(F32)).astype(BF16)
    logits = (
        jnp.dot(normed, low, preferred_element_type=F32)
        + jnp.dot(normed, middle, preferred_element_type=F32)
    ) + jnp.dot(normed, high, preferred_element_type=F32)
    lane = lax.broadcasted_iota(jnp.int32, (frames, experts), 1)
    ahead = jnp.sum(jnp.where(lane == cols_ref[:, 0:1], logits, 0.0), axis=1, keepdims=True)
    behind = jnp.sum(jnp.where(lane == cols_ref[:, 1:2], logits, 0.0), axis=1, keepdims=True)
    gate_ref[...] = jnp.broadcast_to(jax.nn.sigmoid(ahead - behind), gate_ref.shape)


def expert_kernel(count, order, slots_ref, *refs):
    firsts, seconds, answer_ref = refs[:count], refs[count : 2 * count], refs[2 * count]
    first_buf, second_buf, total, sems = refs[2 * count + 1 :]
    copies = []
    for at, k in enumerate(order):
        pair = (
            pltpu.make_async_copy(firsts[k].at[0], first_buf.at[at], sems.at[0, at]),
            pltpu.make_async_copy(seconds[k].at[0], second_buf.at[at], sems.at[1, at]),
        )
        pair[0].start()
        pair[1].start()
        copies.append(pair)
    width = first_buf.shape[2]
    step = min(512, width)
    for at in range(count):
        copies[at][0].wait()
        copies[at][1].wait()
        for part in range(0, width, step):
            up = jnp.dot(
                slots_ref[...], first_buf[at, :, part : part + step], preferred_element_type=F32
            )
            half = 0.5 * up
            hidden = (half + half * jnp.tanh(half)).astype(BF16)
            down = jnp.dot(
                hidden, second_buf[at, part : part + step, :], preferred_element_type=F32
            )
            if at == 0 and part == 0:
                total[...] = down
            elif at == count - 1 and part + step == width:
                answer_ref[...] = (total[...] + down).astype(BF16)
            else:
                total[...] += down


def combine_kernel(experts, capacity, answer_ref, mixed_ref, gate_ref, cols_ref, out_ref):
    frames = mixed_ref.shape[0]
    first, second = cols_ref[:, 0:1], cols_ref[:, 1:2]
    lane = lax.broadcasted_iota(jnp.int32, (frames, experts), 1)
    named = ((lane == first) | (lane == second)).astype(F32)
    before = (
        lax.broadcasted_iota(jnp.int32, (frames, frames), 1)
        < lax.broadcasted_iota(jnp.int32, (frames, frames), 0)
    ).astype(F32)
    rank = jnp.dot(before, named, preferred_element_type=F32) + (lane * capacity).astype(F32)
    slot = lax.broadcasted_iota(jnp.int32, (frames, experts * capacity), 1).astype(F32)
    back = []
    for chosen in (first, second):
        place = jnp.sum(jnp.where(lane == chosen, rank, 0.0), axis=1, keepdims=True)
        pick = (slot == place).astype(F32).astype(BF16)
        back.append(jnp.dot(pick, answer_ref[...], preferred_element_type=F32))
    gate = gate_ref[:, 0:1]
    result = mixed_ref[...].astype(F32) + gate * back[0] + (1.0 - gate) * back[1]
    out_ref[0] = result.astype(BF16)


def body(
    frames_in, pit_order, expert_ids, norm_gains, attn_qkv, attn_out, router, expert_in, expert_out
):
    dp_count = lax.axis_size("dp")
    exp_count = lax.axis_size("expert")
    me = lax.axis_index("dp").astype(jnp.int32)
    exp_index = lax.axis_index("expert").astype(jnp.int32)
    frames, width = frames_in.shape[1:]
    top = expert_ids.shape[2]
    capacity = frames * top * 5 // (4 * exp_count)
    slots_count = exp_count * capacity
    half = dp_count // 2
    share = width // dp_count
    me_arr = me[None]

    own_cols = lax.dynamic_slice_in_dim(attn_qkv, me * share, share, axis=2)
    qkv = {0: own_cols}
    for far in range(2, exp_count, 2):
        qkv[far] = swap(own_cols, "expert", far)
    for far in range(0, exp_count, 2):
        qkv[far | 1] = swap(qkv[far], "expert", 1)

    raw = {0: frames_in}
    bit = half
    while bit:
        for k in list(raw):
            raw[k | bit] = swap(raw[k], "dp", bit)
        bit //= 2

    proj_rows = attn_out.shape[0] // dp_count
    proj = lax.all_gather(
        lax.dynamic_slice_in_dim(attn_out, me * proj_rows, proj_rows, axis=0),
        ("expert", "dp"),
        axis=0,
        tiled=True,
    )

    expert_in, expert_out, raw[half] = lax.optimization_barrier((expert_in, expert_out, raw[half]))
    firsts, seconds = {0: expert_in}, {0: expert_out}
    bit = half
    while bit:
        for held in (firsts, seconds):
            for k in list(held):
                held[k | bit] = swap(held[k], "dp", bit)
        bit //= 2

    member = jnp.arange(dp_count, dtype=jnp.int32)
    meeting = ((me ^ member) % half) * exp_count + exp_index
    place = jnp.where(pit_order[meeting, 0] == 0, member, member ^ half)

    normed, stream = pl.pallas_call(
        functools.partial(norm_kernel, dp_count),
        out_shape=(
            jax.ShapeDtypeStruct((dp_count, frames, width), BF16),
            jax.ShapeDtypeStruct((frames, width), BF16),
        ),
        in_specs=[SMEM, VMEM] + [VMEM] * dp_count,
        out_specs=(VMEM, VMEM),
        compiler_params=params(32),
        cost_estimate=cost(dp_count * frames * width * 8, dp_count * frames * width * 4),
        name="norm",
    )(place, norm_gains, *[raw[k] for k in range(dp_count)])

    contexts = pl.pallas_call(
        functools.partial(attention_kernel, dp_count, exp_count),
        out_shape=[jax.ShapeDtypeStruct((frames, share), BF16)] * dp_count,
        in_specs=[SMEM, VMEM] + [ANY] * exp_count,
        out_specs=[VMEM] * dp_count,
        scratch_shapes=[
            pltpu.VMEM((3, width, share), BF16),
            pltpu.SemaphoreType.DMA((exp_count,)),
        ],
        compiler_params=params(32),
        cost_estimate=cost(
            2 * frames * width * width * 3 + 16 * frames * frames * width, 5 << 20, frames * frames * 16
        ),
        name="attention",
    )(exp_index[None], normed, *[qkv[k] for k in range(exp_count)])

    blocks = [contexts[0]] + [swap(contexts[k], "dp", k) for k in range(1, dp_count)]

    cols = expert_ids[0]
    rows = cols.T
    slots, mixed, gate = pl.pallas_call(
        functools.partial(mix_kernel, dp_count, exp_count, capacity),
        out_shape=(
            jax.ShapeDtypeStruct((slots_count, width), BF16),
            jax.ShapeDtypeStruct((frames, width), BF16),
            jax.ShapeDtypeStruct((frames, 128), F32),
        ),
        in_specs=[SMEM] + [VMEM] * (6 + dp_count),
        out_specs=(VMEM, VMEM, VMEM),
        compiler_params=params(32),
        cost_estimate=cost(2 * frames * width * (width + slots_count), 5 << 20),
        name="mix",
    )(me_arr, stream, proj, norm_gains, router, rows, cols, *blocks)

    arrived = lax.all_to_all(
        slots.reshape(exp_count, capacity, width), "expert", split_axis=0, concat_axis=0, tiled=True
    ).reshape(slots_count, width)

    order = sorted(range(dp_count), key=lambda k: (k & half, k))
    inner = expert_in.shape[2]
    answer = pl.pallas_call(
        functools.partial(expert_kernel, dp_count, order),
        out_shape=jax.ShapeDtypeStruct((slots_count, width), BF16),
        in_specs=[VMEM] + [ANY] * (2 * dp_count),
        out_specs=VMEM,
        scratch_shapes=[
            pltpu.VMEM((dp_count, width, inner), BF16),
            pltpu.VMEM((dp_count, inner, width), BF16),
            pltpu.VMEM((slots_count, width), F32),
            pltpu.SemaphoreType.DMA((2, dp_count)),
        ],
        compiler_params=params(48),
        cost_estimate=cost(4 * slots_count * width * inner * dp_count, 18 << 20),
        name="experts",
    )(arrived, *[firsts[k] for k in range(dp_count)], *[seconds[k] for k in range(dp_count)])

    returned = lax.all_to_all(
        answer.reshape(exp_count, capacity, width), "expert", split_axis=0, concat_axis=0, tiled=True
    ).reshape(slots_count, width)

    return pl.pallas_call(
        functools.partial(combine_kernel, exp_count, capacity),
        out_shape=jax.ShapeDtypeStruct((1, frames, width), BF16),
        in_specs=[VMEM] * 4,
        out_specs=VMEM,
        compiler_params=params(32),
        cost_estimate=cost(4 * frames * slots_count * width, 3 << 20),
        name="combine",
    )(returned, mixed, gate, cols)


def solution(mesh):
    return jax.shard_map(
        body,
        mesh=mesh,
        in_specs=(
            P(("dp", "expert"), None, None),
            P(),
            P(("dp", "expert"), None, None),
            P(),
            P(None, "expert", None),
            P("expert", None),
            P(),
            P("expert", None, "dp"),
            P("expert", "dp", None),
        ),
        out_specs=P(("dp", "expert"), None, None),
        check_vma=False,
    )
```

time: 367 us -> 227 us (0.62)
  waiting for transfers between devices: 234 us -> 110 us
  matrix products: 32.3 us -> 0 us
  Pallas kernels: 0 us -> 28.1 us
  local copies, waits for them, and re-layouts: 33 us -> 10.3 us
  starting transfers between devices: 7.91 us -> 25.1 us
  other arithmetic: 7.15 us -> 0.02 us
    all_gather x3 -> x1, waiting for transfers between devices: 157 us -> 0.01 us  [body(): lax.all_gather(lax.dynamic_slice_in_dim(attn_out, me * proj_rows, proj_ro...]
    ppermute x1 -> x19, waiting for transfers between devices: 5.95 us -> 96 us  [swap(): return lax.ppermute(block, axis, [(i, i ^ mask) for i in range(count)])]
    reduce_scatter x1 -> x0, waiting for transfers between devices: 51.6 us -> none  [body(): lax.psum_scatter(partials, 'dp', scatter_dimension=0, tiled=True)]
    pallas_call x0 -> x5, Pallas kernels: none -> 28.1 us  [the longest x1 14.1 us: body(): pl.pallas_call(functools.partial(expert_kernel, dp_count, order), out_sha...]
    dot_general x6 -> x0, matrix products: 27.6 us -> none  [the longest x1 7.77 us: body(): jnp.dot(flat_rows, expert_in[0], preferred_element_type=jnp.float32)]
    ppermute x1 -> x19, starting transfers between devices: 1.58 us -> 19 us  [swap(): return lax.ppermute(block, axis, [(i, i ^ mask) for i in range(count)])]
    slice x7 -> x0, local copies, waits for them, and re-layouts: 11.2 us -> none  [the longest x1 4.02 us: body(): back[:, 0]]
    gather x5 -> x1, local copies, waits for them, and re-layouts: 9.03 us -> 1.32 us  [body(): place = jnp.where(pit_order[meeting, 0] == 0, member, member ^ half)]
  transfers between devices with their start and end apart: 6 -> 21, of which waited for: 6 -> 13; matrix products, arithmetic and copies ran while one was open for 10% -> 1% of each run, Pallas kernels for 0% -> 5%
where the time goes in v1:
time: 227 us; the launch traced here: 224 us
  waiting for transfers between devices  110 us (48%)
  blocking collectives  36.5 us (16%)
  Pallas kernels  28.1 us (12%)
  starting transfers between devices  25.1 us (11%)
  between operations  13.5 us (6%)
  local copies, waits for them, and re-layouts  10.3 us (5%)
    ppermute x19, waiting for transfers between devices, swap(): return lax.ppermute(block, axis, [(i, i ^ mask) for i in range(count)])  96 us
    all_to_all x1, blocking collectives, body(): lax.all_to_all(answer.reshape(exp_count, capacity, width), 'expert', spli...  36.5 us
    ppermute x19, starting transfers between devices, swap(): return lax.ppermute(block, axis, [(i, i ^ mask) for i in range(count)])  19 us
    all_to_all x1, waiting for transfers between devices, body(): lax.all_to_all(slots.reshape(exp_count, capacity, width), 'expert', split...  14.3 us
    pallas_call x1, Pallas kernels, body(): pl.pallas_call(functools.partial(expert_kernel, dp_count, order), out_sha...  14.1 us
    unnamed x28, local copies, waits for them, and re-layouts  7.37 us
    pallas_call x1, Pallas kernels, body(): pl.pallas_call(functools.partial(attention_kernel, dp_count, exp_count),...  6.99 us
    all_to_all x1, starting transfers between devices, body(): lax.all_to_all(slots.reshape(exp_count, capacity, width), 'expert', split...  6.14 us
  transfers between devices with their start and end apart: 21, of which 13 were waited for; matrix products, arithmetic and copies ran while one was open for 1% of the time, Pallas kernels for 5%

profile of v1, /device:TPU:16, one launch (start us, length us, event | category | flops | bytes accessed | tf_op | source)
XLA Modules:
  0.0 223.8 jit_solution(17842210781384647757)
XLA Ops:
  6.5 1.5 constant_dynamic-slice_fusion
  8.1 1.6 collective-permute-start.1
  9.7 12.4 %collective-permute-done.1.refs_2_ = bf16[1,256,1024]{2,1,0:T(8,128)(2,1)S(1)} collective-permute-done((bf16[1,256,1024]{2,1,0:T(8,128)(2,1)}, bf16[1,256,1024]{2,1,0:T(8,128)(2,1)S(1)}, u32[]{:S(2)}, u32[]{:S(2)}) %collective-permute-start.1) | collective-permute-done | bytes 524320 | tf_op jit(solution)/shard_map/ppermute | solution.py:29
  22.0 1.9 collective-permute-start.14
  24.6 3.5 %collective-permute-start.6 = (bf16[3,128,256]{2,1,0:T(8,128)(2,1)S(1)}, bf16[3,128,256]{2,1,0:T(8,128)(2,1)S(1)}, u32[]{:S(2)}, u32[]{:S(2)}) collective-permute-start(bf16[3,128,256]{2,1,0:T(8,128)(2,1)S(1)} %constant_dynamic-slice_fusion.1.refs_0_), channel_id=1, source_target_pairs={{0,4},{1,5},{2,6},{3,7},{4,0},{5,1},{6,2},{7,3},{8,12},{9,13},{10,... | collective-permute-start | bytes 589832 | tf_op jit(solution)/shard_map/ppermute | solution.py:29
  28.1 12.2 %collective-permute-done.8.refs_6_ = bf16[3,128,256]{2,1,0:T(8,128)(2,1)S(1)} collective-permute-done((bf16[3,128,256]{2,1,0:T(8,128)(2,1)S(1)}, bf16[3,128,256]{2,1,0:T(8,128)(2,1)S(1)}, u32[]{:S(2)}, u32[]{:S(2)}) %collective-permute-start.8) | collective-permute-done | bytes 196640 | tf_op jit(solution)/shard_map/ppermute | solution.py:29
  40.9 3.4 %collective-permute-start.4 = (bf16[3,128,256]{2,1,0:T(8,128)(2,1)S(1)}, bf16[3,128,256]{2,1,0:T(8,128)(2,1)}, u32[]{:S(2)}, u32[]{:S(2)}) collective-permute-start(bf16[3,128,256]{2,1,0:T(8,128)(2,1)S(1)} %constant_dynamic-slice_fusion.1.refs_0_), channel_id=1, source_target_pairs={{0,2},{1,3},{2,0},{3,1},{4,6},{5,7},{6,4},{7,5},{8,10},{9,11},{10,... | collective-permute-start | bytes 589832 | tf_op jit(solution)/shard_map/ppermute | solution.py:29
  44.3 4.7 %collective-permute-done.4.refs_2_ = bf16[3,128,256]{2,1,0:T(8,128)(2,1)} collective-permute-done((bf16[3,128,256]{2,1,0:T(8,128)(2,1)S(1)}, bf16[3,128,256]{2,1,0:T(8,128)(2,1)}, u32[]{:S(2)}, u32[]{:S(2)}) %collective-permute-start.4) | collective-permute-done | bytes 196640 | tf_op jit(solution)/shard_map/ppermute | solution.py:29
  49.0 1.5 collective-permute-start.3
  50.5 1.3 gather_fusion
  51.8 3.3 %collective-permute-done.3.refs_1_ = bf16[3,128,256]{2,1,0:T(8,128)(2,1)S(1)} collective-permute-done((bf16[3,128,256]{2,1,0:T(8,128)(2,1)S(1)}, bf16[3,128,256]{2,1,0:T(8,128)(2,1)S(1)}, u32[]{:S(2)}, u32[]{:S(2)}) %collective-permute-start.3) | collective-permute-done | bytes 196640 | tf_op jit(solution)/shard_map/ppermute | solution.py:29
  55.8 1.5 collective-permute-start.9
  57.8 1.5 collective-permute-start.5
  59.3 1.0 copy-done.2
  61.1 2.0 norm.1
  63.1 5.4 %collective-permute-done.7.refs_5_ = bf16[3,128,256]{2,1,0:T(8,128)(2,1)S(1)} collective-permute-done((bf16[3,128,256]{2,1,0:T(8,128)(2,1)S(1)}, bf16[3,128,256]{2,1,0:T(8,128)(2,1)S(1)}, u32[]{:S(2)}, u32[]{:S(2)}) %collective-permute-start.7) | collective-permute-done | bytes 196640 | tf_op jit(solution)/shard_map/ppermute | solution.py:29
  68.5 2.5 %collective-permute-done.5.refs_3_ = bf16[3,128,256]{2,1,0:T(8,128)(2,1)S(1)} collective-permute-done((bf16[3,128,256]{2,1,0:T(8,128)(2,1)}, bf16[3,128,256]{2,1,0:T(8,128)(2,1)S(1)}, u32[]{:S(2)}, u32[]{:S(2)}) %collective-permute-start.5) | collective-permute-done | bytes 196640 | tf_op jit(solution)/shard_map/ppermute | solution.py:29
  71.0 7.0 %attention.1 = (bf16[256,256]{1,0:T(8,128)(2,1)S(1)}, bf16[256,256]{1,0:T(8,128)(2,1)S(1)}, bf16[256,256]{1,0:T(8,128)(2,1)S(1)}, bf16[256,256]{1,0:T(8,128)(2,1)S(1)}) custom-call(s32[1]{0:T(128)} %bitcast.4.me_ref, bf16[4,256,1024]{2,1,0:T(8,128)(2,1)S(1)} %get-tuple-element.19.normed_ref, bf16[3,128,256]{2,1,0:T(8,128)(2,1)S(1)} %constant_dynamic-slice_fusion.1.refs_0_, ...), custom_call_target="tpu_custom_call" | custom-call | flops 2684354560 | bytes 5242880 | tf_op jit(solution)/shard_map/attention/pallas_call | solution.py:246
  78.1 1.6 collective-permute-start.11
  80.4 42.2 %collective-permute-done.11.refs_2_ = bf16[256,256]{1,0:T(8,128)(2,1)S(1)} collective-permute-done((bf16[256,256]{1,0:T(8,128)(2,1)S(1)}, bf16[256,256]{1,0:T(8,128)(2,1)S(1)}, u32[]{:S(2)}, u32[]{:S(2)}) %collective-permute-start.11) | collective-permute-done | bytes 131104 | tf_op jit(solution)/shard_map/ppermute | solution.py:29
  123.0 1.6 copy-done.1
  124.6 2.8 %mix.1 = (bf16[640,1024]{1,0:T(8,128)(2,1)}, bf16[256,1024]{1,0:T(8,128)(2,1)S(1)}, f32[256,128]{1,0:T(8,128)S(1)}) custom-call(s32[1]{0:T(128)} %bitcast.me_ref, bf16[256,1024]{1,0:T(8,128)(2,1)S(1)} %get-tuple-element.18.own_ref, bf16[1024,1024]{1,0:T(8,128)(2,1)S(1)} %copy-done.1, f32[2,1024]{1,0:T(2,128)S(1)} %copy-done.4, ...), custom_call_target="tpu_custom_call" | custom-call | flops 872415232 | bytes 5242880 | tf_op jit(solution)/shard_map/mix/pallas_call | solution.py:266
  127.4 6.1 %all-to-all-start = ((bf16[8,80,1024]{2,1,0:T(8,128)(2,1)}), bf16[8,80,1024]{2,1,0:T(8,128)(2,1)S(1)}, u32[]{:S(2)}, u32[]{:S(2)}) async-start(bf16[8,80,1024]{2,1,0:T(8,128)(2,1)} %bitcast.5), calls=%async_computation | async-start | bytes 2621440 | tf_op jit(solution)/shard_map/all_to_all | solution.py:280
  134.5 3.3 %collective-permute-done.13.refs_1_ = bf16[1,1024,1024]{2,1,0:T(8,128)(2,1)S(1)} collective-permute-done((bf16[1,1024,1024]{2,1,0:T(8,128)(2,1)}, bf16[1,1024,1024]{2,1,0:T(8,128)(2,1)S(1)}, u32[]{:S(2)}, u32[]{:S(2)}) %collective-permute-start.13) | collective-permute-done | bytes 2097184 | tf_op jit(solution)/shard_map/ppermute | solution.py:29
  137.9 6.0 %collective-permute-done.16.refs_5_ = bf16[1,1024,1024]{2,1,0:T(8,128)(2,1)S(1)} collective-permute-done((bf16[1,1024,1024]{2,1,0:T(8,128)(2,1)}, bf16[1,1024,1024]{2,1,0:T(8,128)(2,1)S(1)}, u32[]{:S(2)}, u32[]{:S(2)}) %collective-permute-start.16) | collective-permute-done | bytes 2097184 | tf_op jit(solution)/shard_map/ppermute | solution.py:29
  143.9 3.0 %collective-permute-done.15.refs_3_ = bf16[1,1024,1024]{2,1,0:T(8,128)(2,1)S(1)} collective-permute-done((bf16[1,1024,1024]{2,1,0:T(8,128)(2,1)}, bf16[1,1024,1024]{2,1,0:T(8,128)(2,1)S(1)}, u32[]{:S(2)}, u32[]{:S(2)}) %collective-permute-start.15) | collective-permute-done | bytes 2097184 | tf_op jit(solution)/shard_map/ppermute | solution.py:29
  146.9 1.4 copy-done.12
  148.3 14.3 %all-to-all-done = bf16[8,80,1024]{2,1,0:T(8,128)(2,1)S(1)} async-done(((bf16[8,80,1024]{2,1,0:T(8,128)(2,1)}), bf16[8,80,1024]{2,1,0:T(8,128)(2,1)S(1)}, u32[]{:S(2)}, u32[]{:S(2)}) %all-to-all-start) | async-done | bytes 1310752 | tf_op jit(solution)/shard_map/all_to_all | solution.py:280
  162.6 1.6 copy-done.5
  164.2 14.1 %experts.1 = bf16[640,1024]{1,0:T(8,128)(2,1)S(1)} custom-call(bf16[640,1024]{1,0:T(8,128)(2,1)S(1)} %bitcast.15, bf16[1,1024,1024]{2,1,0:T(8,128)(2,1)S(1)} %copy-done.5, bf16[1,1024,1024]{2,1,0:T(8,128)(2,1)} %copy-done.10, bf16[1,1024,1024]{2,1,0:T(8,128)(2,1)} %collective-permute-done.14.refs_2_, bf16[1,1024,1024]{2,1,0:T(8,128)(2,1)} %copy-done.12, ...), custom_call_target="tpu_custom_call" | custom-call | flops 10737418240 | bytes 18874368 | tf_op jit(solution)/shard_map/experts/pallas_call | solution.py:286
  178.3 36.5 %all_to_all.10 = bf16[8,80,1024]{2,1,0:T(8,128)(2,1)S(1)} all-to-all(bf16[8,80,1024]{2,1,0:T(8,128)(2,1)S(1)} %bitcast.16), channel_id=1, replica_groups=mesh['dp'=4,'expert'=8] {'expert'}, dimensions={0} | all-to-all | bytes 2621440 | tf_op jit(solution)/shard_map/all_to_all | solution.py:302
  214.8 2.2 combine.1
  (51 shorter events, 5.6 us)
Async XLA Ops:
  6.5 17.5 %copy-start = (bf16[3,128,1024]{2,1,0:T(8,128)(2,1)S(1)}, bf16[3,128,1024]{2,1,0:T(8,128)(2,1)}, u32[]{:S(2)}) copy-start(bf16[3,128,1024]{2,1,0:T(8,128)(2,1)} %param.13) | copy-start | bytes 2359300
  6.5 116.5 %all-gather.2.cloned.1.call-start = ((), (), s32[]{:S(2)}) async-start(), calls=%async_computation.2 | async-start | bytes 2162688 | tf_op jit(solution)/shard_map/all_gather | solution.py:213
  8.1 13.9 %collective-permute-start.1 = (bf16[1,256,1024]{2,1,0:T(8,128)(2,1)}, bf16[1,256,1024]{2,1,0:T(8,128)(2,1)S(1)}, u32[]{:S(2)}, u32[]{:S(2)}) collective-permute-start(bf16[1,256,1024]{2,1,0:T(8,128)(2,1)} %refs_0_.1), channel_id=1, source_target_pairs={{0,16},{8,24},{16,0},{24,8},{1,17},{9,25},{17,1},{25,9},{2,18},{10... | collective-permute-start | bytes 1572872 | tf_op jit(solution)/shard_map/ppermute | solution.py:29
  22.0 112.0 %collective-permute-start.14 = (bf16[1,1024,1024]{2,1,0:T(8,128)(2,1)}, bf16[1,1024,1024]{2,1,0:T(8,128)(2,1)}, u32[]{:S(2)}, u32[]{:S(2)}) collective-permute-start(bf16[1,1024,1024]{2,1,0:T(8,128)(2,1)} %refs_0_.2), channel_id=1, source_target_pairs={{0,16},{8,24},{16,0},{24,8},{1,17},{9,25},{17,1},{25,9},{2,18},{10... | collective-permute-start | bytes 6291464 | tf_op jit(solution)/shard_map/ppermute | solution.py:29
  23.9 110.3 %collective-permute-start.17 = (bf16[1,1024,1024]{2,1,0:T(8,128)(2,1)}, bf16[1,1024,1024]{2,1,0:T(8,128)(2,1)}, u32[]{:S(2)}, u32[]{:S(2)}) collective-permute-start(bf16[1,1024,1024]{2,1,0:T(8,128)(2,1)} %refs_4_), channel_id=1, source_target_pairs={{0,16},{8,24},{16,0},{24,8},{1,17},{9,25},{17,1},{25,9},{2,18},{10... | collective-permute-start | bytes 6291464 | tf_op jit(solution)/shard_map/ppermute | solution.py:29
  24.1 16.2 %collective-permute-start.8 = (bf16[3,128,256]{2,1,0:T(8,128)(2,1)S(1)}, bf16[3,128,256]{2,1,0:T(8,128)(2,1)S(1)}, u32[]{:S(2)}, u32[]{:S(2)}) collective-permute-start(bf16[3,128,256]{2,1,0:T(8,128)(2,1)S(1)} %constant_dynamic-slice_fusion.1.refs_0_), channel_id=1, source_target_pairs={{0,6},{1,7},{2,4},{3,5},{4,2},{5,3},{6,0},{7,1},{8,14},{9,15},{10,... | collective-permute-start | bytes 589832 | tf_op jit(solution)/shard_map/ppermute | solution.py:29
  24.6 16.3 %collective-permute-start.6 = (bf16[3,128,256]{2,1,0:T(8,128)(2,1)S(1)}, bf16[3,128,256]{2,1,0:T(8,128)(2,1)S(1)}, u32[]{:S(2)}, u32[]{:S(2)}) collective-permute-start(bf16[3,128,256]{2,1,0:T(8,128)(2,1)S(1)} %constant_dynamic-slice_fusion.1.refs_0_), channel_id=1, source_target_pairs={{0,4},{1,5},{2,6},{3,7},{4,0},{5,1},{6,2},{7,3},{8,12},{9,13},{10,... | collective-permute-start | bytes 589832 | tf_op jit(solution)/shard_map/ppermute | solution.py:29
  28.1 29.2 %collective-permute-start = (bf16[1,256,1024]{2,1,0:T(8,128)(2,1)}, bf16[1,256,1024]{2,1,0:T(8,128)(2,1)S(1)}, u32[]{:S(2)}, u32[]{:S(2)}) collective-permute-start(bf16[1,256,1024]{2,1,0:T(8,128)(2,1)} %refs_0_.1), channel_id=1, source_target_pairs={{0,8},{8,0},{16,24},{24,16},{1,9},{9,1},{17,25},{25,17},{2,10},{10... | collective-permute-start | bytes 1572872 | tf_op jit(solution)/shard_map/ppermute | solution.py:29
  40.3 17.5 %collective-permute-start.2 = (bf16[1,256,1024]{2,1,0:T(8,128)(2,1)S(1)}, bf16[1,256,1024]{2,1,0:T(8,128)(2,1)S(1)}, u32[]{:S(2)}, u32[]{:S(2)}) collective-permute-start(bf16[1,256,1024]{2,1,0:T(8,128)(2,1)S(1)} %collective-permute-done.1.refs_2_), channel_id=1, source_target_pairs={{0,8},{8,0},{16,24},{24,16},{1,9},{9,1},{17,25},{25,17},{2,10},{10... | collective-permute-start | bytes 1572872 | tf_op jit(solution)/shard_map/ppermute | solution.py:29
  40.9 8.1 %collective-permute-start.4 = (bf16[3,128,256]{2,1,0:T(8,128)(2,1)S(1)}, bf16[3,128,256]{2,1,0:T(8,128)(2,1)}, u32[]{:S(2)}, u32[]{:S(2)}) collective-permute-start(bf16[3,128,256]{2,1,0:T(8,128)(2,1)S(1)} %constant_dynamic-slice_fusion.1.refs_0_), channel_id=1, source_target_pairs={{0,2},{1,3},{2,0},{3,1},{4,6},{5,7},{6,4},{7,5},{8,10},{9,11},{10,... | collective-permute-start | bytes 589832 | tf_op jit(solution)/shard_map/ppermute | solution.py:29
  49.0 6.1 %collective-permute-start.3 = (bf16[3,128,256]{2,1,0:T(8,128)(2,1)S(1)}, bf16[3,128,256]{2,1,0:T(8,128)(2,1)S(1)}, u32[]{:S(2)}, u32[]{:S(2)}) collective-permute-start(bf16[3,128,256]{2,1,0:T(8,128)(2,1)S(1)} %constant_dynamic-slice_fusion.1.refs_0_), channel_id=1, source_target_pairs={{0,1},{1,0},{2,3},{3,2},{4,5},{5,4},{6,7},{7,6},{8,9},{9,8},{10,11... | collective-permute-start | bytes 589832 | tf_op jit(solution)/shard_map/ppermute | solution.py:29
  55.8 7.3 %collective-permute-start.9 = (bf16[3,128,256]{2,1,0:T(8,128)(2,1)S(1)}, bf16[3,128,256]{2,1,0:T(8,128)(2,1)S(1)}, u32[]{:S(2)}, u32[]{:S(2)}) collective-permute-start(bf16[3,128,256]{2,1,0:T(8,128)(2,1)S(1)} %collective-permute-done.8.refs_6_), channel_id=1, source_target_pairs={{0,1},{1,0},{2,3},{3,2},{4,5},{5,4},{6,7},{7,6},{8,9},{9,8},{10,11... | collective-permute-start | bytes 589832 | tf_op jit(solution)/shard_map/ppermute | solution.py:29
  57.3 11.2 %collective-permute-start.7 = (bf16[3,128,256]{2,1,0:T(8,128)(2,1)S(1)}, bf16[3,128,256]{2,1,0:T(8,128)(2,1)S(1)}, u32[]{:S(2)}, u32[]{:S(2)}) collective-permute-start(bf16[3,128,256]{2,1,0:T(8,128)(2,1)S(1)} %collective-permute-done.6.refs_4_), channel_id=1, source_target_pairs={{0,1},{1,0},{2,3},{3,2},{4,5},{5,4},{6,7},{7,6},{8,9},{9,8},{10,11... | collective-permute-start | bytes 589832 | tf_op jit(solution)/shard_map/ppermute | solution.py:29
  57.8 13.2 %collective-permute-start.5 = (bf16[3,128,256]{2,1,0:T(8,128)(2,1)}, bf16[3,128,256]{2,1,0:T(8,128)(2,1)S(1)}, u32[]{:S(2)}, u32[]{:S(2)}) collective-permute-start(bf16[3,128,256]{2,1,0:T(8,128)(2,1)} %collective-permute-done.4.refs_2_), channel_id=1, source_target_pairs={{0,1},{1,0},{2,3},{3,2},{4,5},{5,4},{6,7},{7,6},{8,9},{9,8},{10,11... | collective-permute-start | bytes 589832 | tf_op jit(solution)/shard_map/ppermute | solution.py:29
  59.3 1.0 copy-start.2
  61.1 10.0 %copy-start.7 = (bf16[3,128,256]{2,1,0:T(8,128)(2,1)S(1)}, bf16[3,128,256]{2,1,0:T(8,128)(2,1)}, u32[]{:S(2)}) copy-start(bf16[3,128,256]{2,1,0:T(8,128)(2,1)} %copy-done.6) | copy-start | bytes 589828
  71.0 8.9 %copy-start.9 = (s32[1,256,2]{1,2,0:T(2,128)S(1)}, s32[1,256,2]{1,2,0:T(2,128)}, u32[]{:S(2)}) copy-start(s32[1,256,2]{1,2,0:T(2,128)} %param.11) | copy-start | bytes 6148
  71.0 9.2 %copy-start.8 = (f32[1024,8]{0,1:T(8,128)S(1)}, f32[1024,8]{0,1:T(8,128)}, u32[]{:S(2)}) copy-start(f32[1024,8]{0,1:T(8,128)} %param.15) | copy-start | bytes 98308
  71.0 52.0 %copy-start.4 = (f32[2,1024]{1,0:T(2,128)S(1)}, f32[2,1024]{1,0:T(2,128)}, u32[]{:S(2)}) copy-start(f32[2,1024]{1,0:T(2,128)} %gain_ref.3) | copy-start | bytes 24580
  78.0 2.4 %collective-permute-start.10 = (bf16[256,256]{1,0:T(8,128)(2,1)S(1)}, bf16[256,256]{1,0:T(8,128)(2,1)S(1)}, u32[]{:S(2)}, u32[]{:S(2)}) collective-permute-start(bf16[256,256]{1,0:T(8,128)(2,1)S(1)} %get-tuple-element.21), channel_id=1, source_target_pairs={{0,8},{8,0},{16,24},{24,16},{1,9},{9,1},{17,25},{25,17},{2,10},{10... | collective-permute-start | bytes 393224 | tf_op jit(solution)/shard_map/ppermute | solution.py:29
  78.1 44.5 %collective-permute-start.11 = (bf16[256,256]{1,0:T(8,128)(2,1)S(1)}, bf16[256,256]{1,0:T(8,128)(2,1)S(1)}, u32[]{:S(2)}, u32[]{:S(2)}) collective-permute-start(bf16[256,256]{1,0:T(8,128)(2,1)S(1)} %get-tuple-element.22), channel_id=1, source_target_pairs={{0,16},{8,24},{16,0},{24,8},{1,17},{9,25},{17,1},{25,9},{2,18},{10... | collective-permute-start | bytes 393224 | tf_op jit(solution)/shard_map/ppermute | solution.py:29
  79.7 43.3 %collective-permute-start.12 = (bf16[256,256]{1,0:T(8,128)(2,1)S(1)}, bf16[256,256]{1,0:T(8,128)(2,1)S(1)}, u32[]{:S(2)}, u32[]{:S(2)}) collective-permute-start(bf16[256,256]{1,0:T(8,128)(2,1)S(1)} %get-tuple-element.23), channel_id=1, source_target_pairs={{0,24},{8,16},{16,8},{24,0},{1,25},{9,17},{17,9},{25,1},{2,26},{10... | collective-permute-start | bytes 393224 | tf_op jit(solution)/shard_map/ppermute | solution.py:29
  123.0 1.6 copy-start.1
  127.4 35.2 %all-to-all-start = ((bf16[8,80,1024]{2,1,0:T(8,128)(2,1)}), bf16[8,80,1024]{2,1,0:T(8,128)(2,1)S(1)}, u32[]{:S(2)}, u32[]{:S(2)}) async-start(bf16[8,80,1024]{2,1,0:T(8,128)(2,1)} %bitcast.5), calls=%async_computation | async-start | bytes 2621440 | tf_op jit(solution)/shard_map/all_to_all | solution.py:280
  133.5 4.4 %collective-permute-start.13 = (bf16[1,1024,1024]{2,1,0:T(8,128)(2,1)}, bf16[1,1024,1024]{2,1,0:T(8,128)(2,1)S(1)}, u32[]{:S(2)}, u32[]{:S(2)}) collective-permute-start(bf16[1,1024,1024]{2,1,0:T(8,128)(2,1)} %refs_0_.2), channel_id=1, source_target_pairs={{0,8},{8,0},{16,24},{24,16},{1,9},{9,1},{17,25},{25,17},{2,10},{10... | collective-permute-start | bytes 6291464 | tf_op jit(solution)/shard_map/ppermute | solution.py:29
  133.7 10.1 %collective-permute-start.16 = (bf16[1,1024,1024]{2,1,0:T(8,128)(2,1)}, bf16[1,1024,1024]{2,1,0:T(8,128)(2,1)S(1)}, u32[]{:S(2)}, u32[]{:S(2)}) collective-permute-start(bf16[1,1024,1024]{2,1,0:T(8,128)(2,1)} %refs_4_), channel_id=1, source_target_pairs={{0,8},{8,0},{16,24},{24,16},{1,9},{9,1},{17,25},{25,17},{2,10},{10... | collective-permute-start | bytes 6291464 | tf_op jit(solution)/shard_map/ppermute | solution.py:29
  134.0 12.9 %collective-permute-start.15 = (bf16[1,1024,1024]{2,1,0:T(8,128)(2,1)}, bf16[1,1024,1024]{2,1,0:T(8,128)(2,1)S(1)}, u32[]{:S(2)}, u32[]{:S(2)}) collective-permute-start(bf16[1,1024,1024]{2,1,0:T(8,128)(2,1)} %collective-permute-done.14.refs_2_), channel_id=1, source_target_pairs={{0,8},{8,0},{16,24},{24,16},{1,9},{9,1},{17,25},{25,17},{2,10},{10... | collective-permute-start | bytes 6291464 | tf_op jit(solution)/shard_map/ppermute | solution.py:29
  134.2 14.0 %collective-permute-start.18 = (bf16[1,1024,1024]{2,1,0:T(8,128)(2,1)}, bf16[1,1024,1024]{2,1,0:T(8,128)(2,1)}, u32[]{:S(2)}, u32[]{:S(2)}) collective-permute-start(bf16[1,1024,1024]{2,1,0:T(8,128)(2,1)} %collective-permute-done.17.refs_6_), channel_id=1, source_target_pairs={{0,8},{8,0},{16,24},{24,16},{1,9},{9,1},{17,25},{25,17},{2,10},{10... | collective-permute-start | bytes 6291464 | tf_op jit(solution)/shard_map/ppermute | solution.py:29
  137.9 9.0 %copy-start.10 = (bf16[1,1024,1024]{2,1,0:T(8,128)(2,1)}, bf16[1,1024,1024]{2,1,0:T(8,128)(2,1)S(1)}, u32[]{:S(2)}) copy-start(bf16[1,1024,1024]{2,1,0:T(8,128)(2,1)S(1)} %collective-permute-done.13.refs_1_) | copy-start | bytes 6291460
  143.9 3.0 %copy-start.11 = (bf16[1,1024,1024]{2,1,0:T(8,128)(2,1)}, bf16[1,1024,1024]{2,1,0:T(8,128)(2,1)S(1)}, u32[]{:S(2)}) copy-start(bf16[1,1024,1024]{2,1,0:T(8,128)(2,1)S(1)} %collective-permute-done.16.refs_5_) | copy-start | bytes 6291460
  146.9 1.4 copy-start.12
  162.6 1.6 copy-start.5
  (2 other events, 1.4 us)
Sparse Core Ops, SparseCore 0:
  10.2 67.3 all-gather.1

commit v2 on v1

v2 whole, which is shorter than its diff:
```python
import functools

import jax
import jax.numpy as jnp
from jax import lax
from jax.experimental import pallas as pl
from jax.experimental.pallas import tpu as pltpu
from jax.sharding import PartitionSpec as P

HEAD_DIM = 64
epsilon = 1e-05
BF16 = jnp.bfloat16
F32 = jnp.float32
VMEM = pl.BlockSpec(memory_space=pltpu.VMEM)
SMEM = pl.BlockSpec(memory_space=pltpu.SMEM)
ANY = pl.BlockSpec(memory_space=pl.ANY)


def params(mib):
    return pltpu.CompilerParams(vmem_limit_bytes=mib << 20)


def cost(flops, moved, special=0):
    return pl.CostEstimate(flops=flops >> 8, bytes_accessed=moved >> 8, transcendentals=special >> 8)


def swap(block, axis, mask):
    count = lax.axis_size(axis)
    return lax.ppermute(block, axis, [(i, i ^ mask) for i in range(count)])


def layer_norm(values, gain):
    mean = jnp.mean(values, axis=-1, keepdims=True)
    centred = values - mean
    spread = jnp.mean(centred * centred, axis=-1, keepdims=True)
    return centred * lax.rsqrt(spread + epsilon) * gain


def norm_kernel(count, place_ref, gain_ref, *refs):
    raw, (normed_ref, own_ref) = refs[:count], refs[count:]
    gain = gain_ref[0:1, :]
    for k in range(count):
        where = place_ref[k]
        block = raw[k][0]
        normed_ref[where] = layer_norm(block.astype(F32), gain).astype(BF16)

        @pl.when(where == 0)
        def _():
            own_ref[...] = block


def attention_kernel(count, shards, me_ref, near_ref, far_ref, *refs):
    pieces, outs = refs[:shards], refs[shards : shards + count]
    weights, sems = refs[shards + count :]
    depth, cols = pieces[0].shape[1:]
    me = me_ref[0]
    copies = []
    for k in range(shards):
        rows = pl.ds(pl.multiple_of((me ^ k) * depth, depth), depth)
        copy = pltpu.make_async_copy(pieces[k], weights.at[:, rows, :], sems.at[k])
        copy.start()
        copies.append(copy)
    for copy in copies:
        copy.wait()
    frames = near_ref.shape[1]
    head = lax.broadcasted_iota(jnp.int32, (frames, cols), 1) // HEAD_DIM
    scale = HEAD_DIM**-0.5
    for k in range(count):
        x = (far_ref if k & 1 else near_ref)[k >> 1]
        q, key, val = [
            jnp.dot(x, weights[i], preferred_element_type=F32).astype(BF16) for i in range(3)
        ]
        q = q * jnp.asarray(scale, BF16)
        total = jnp.zeros((frames, cols), F32)
        for h in range(cols // HEAD_DIM):
            mine = head == h
            scores = lax.dot_general(
                jnp.where(mine, q, jnp.zeros_like(q)),
                key,
                (((1,), (1,)), ((), ())),
                preferred_element_type=F32,
            )
            exps = jnp.exp(scores - jnp.max(scores, axis=-1, keepdims=True))
            norm = 1.0 / jnp.sum(exps, axis=-1, keepdims=True)
            probs = (exps * norm).astype(BF16)
            total = jnp.where(mine, jnp.dot(probs, val, preferred_element_type=F32), total)
        outs[k][...] = total.astype(BF16)


def mix_kernel(
    count, experts, capacity, me_ref, own_ref, near_ref, far_ref, gain_ref, router_ref, rows_ref, cols_ref, *refs
):
    blocks, (slots_ref, mixed_ref, gate_ref), (wide,) = refs[:count], refs[count : count + 3], refs[count + 3 :]
    frames, depth = blocks[0].shape
    me = me_ref[0]
    part = near_ref.shape[1]
    for held, side in ((near_ref, me & 1), (far_ref, 1 - (me & 1))):
        total = jnp.zeros((frames, part), F32)
        for k in range(count):
            rows = pl.ds(pl.multiple_of((me ^ k) * depth, depth), depth)
            total += jnp.dot(blocks[k][...], held[rows, :], preferred_element_type=F32)
        wide[:, pl.ds(pl.multiple_of(side * part, part), part)] = total
    mixed = (own_ref[...].astype(F32) + wide[...]).astype(BF16)
    mixed_ref[...] = mixed
    normed = layer_norm(mixed.astype(F32), gain_ref[1:2, :]).astype(BF16)
    first, second = rows_ref[0:1, :], rows_ref[1:2, :]
    which = lax.broadcasted_iota(jnp.int32, (experts, frames), 0)
    named = ((which == first) | (which == second)).astype(F32)
    before = (
        lax.broadcasted_iota(jnp.int32, (frames, frames), 0)
        < lax.broadcasted_iota(jnp.int32, (frames, frames), 1)
    ).astype(F32)
    rank = jnp.dot(named, before, preferred_element_type=F32) + (which * capacity).astype(F32)
    slot = lax.broadcasted_iota(jnp.int32, (experts * capacity, frames), 0).astype(F32)
    place0 = jnp.sum(jnp.where(which == first, rank, 0.0), axis=0, keepdims=True)
    place1 = jnp.sum(jnp.where(which == second, rank, 0.0), axis=0, keepdims=True)
    spread = ((slot == place0) | (slot == place1)).astype(F32).astype(BF16)
    slots_ref[...] = jnp.dot(spread, normed, preferred_element_type=F32).astype(BF16)
    high = router_ref[...].astype(BF16)
    rest = router_ref[...] - high.astype(F32)
    middle = rest.astype(BF16)
    low = (rest - middle.astype(F32)).astype(BF16)
    logits = (
        jnp.dot(normed, low, preferred_element_type=F32)
        + jnp.dot(normed, middle, preferred_element_type=F32)
    ) + jnp.dot(normed, high, preferred_element_type=F32)
    lane = lax.broadcasted_iota(jnp.int32, (frames, experts), 1)
    ahead = jnp.sum(jnp.where(lane == cols_ref[:, 0:1], logits, 0.0), axis=1, keepdims=True)
    behind = jnp.sum(jnp.where(lane == cols_ref[:, 1:2], logits, 0.0), axis=1, keepdims=True)
    gate_ref[...] = jnp.broadcast_to(jax.nn.sigmoid(ahead - behind), gate_ref.shape)


def fetch(plan, refs, buf, sems):
    copies = []
    for at, pieces in enumerate(plan):
        started = []
        for p, (source, view, place) in enumerate(pieces):
            copy = pltpu.make_async_copy(
                refs[source].at[(0, *view)], buf.at[(at, *place)], sems.at[at, p]
            )
            copy.start()
            started.append(copy)
        copies.append(started)
    return copies


def hidden_kernel(plan, sources, slots_ref, *refs):
    hidden_ref, buf, sems = refs[sources:]
    inner = buf.shape[2]
    copies = fetch(plan, refs[:sources], buf, sems)
    step = min(512, inner)
    for at in range(len(plan)):
        for copy in copies[at]:
            copy.wait()
        for part in range(0, inner, step):
            half = 0.5 * jnp.dot(
                slots_ref[...], buf[at, :, part : part + step], preferred_element_type=F32
            )
            hidden_ref[at, :, part : part + step] = (half + half * jnp.tanh(half)).astype(BF16)


def answer_kernel(plan, sources, near_ref, far_ref, *refs):
    answer_ref, buf, total, sems = refs[sources:]
    copies = fetch(plan, refs[:sources], buf, sems)
    near = near_ref.shape[0]
    for at in range(len(plan)):
        for copy in copies[at]:
            copy.wait()
        hidden = near_ref[at] if at < near else far_ref[at - near]
        down = jnp.dot(hidden, buf[at], preferred_element_type=F32)
        if at == 0:
            total[...] = down
        elif at < len(plan) - 1:
            total[...] += down
        else:
            answer_ref[...] = (total[...] + down).astype(BF16)


def combine_kernel(experts, capacity, count, mixed_ref, gate_ref, cols_ref, *refs):
    answers, out_ref = refs[:count], refs[count]
    frames = mixed_ref.shape[0]
    first, second = cols_ref[:, 0:1], cols_ref[:, 1:2]
    lane = lax.broadcasted_iota(jnp.int32, (frames, experts), 1)
    named = ((lane == first) | (lane == second)).astype(F32)
    before = (
        lax.broadcasted_iota(jnp.int32, (frames, frames), 1)
        < lax.broadcasted_iota(jnp.int32, (frames, frames), 0)
    ).astype(F32)
    rank = jnp.dot(before, named, preferred_element_type=F32) + (lane * capacity).astype(F32)
    slot = lax.broadcasted_iota(jnp.int32, (frames, experts * capacity), 1).astype(F32)
    picks = []
    for chosen in (first, second):
        place = jnp.sum(jnp.where(lane == chosen, rank, 0.0), axis=1, keepdims=True)
        picks.append((slot == place).astype(F32).astype(BF16))
    gate = gate_ref[:, 0:1]
    cols = mixed_ref.shape[1] // count
    for c in range(count):
        where = slice(c * cols, (c + 1) * cols)
        back = [jnp.dot(pick, answers[c][...], preferred_element_type=F32) for pick in picks]
        result = mixed_ref[:, where].astype(F32) + gate * back[0] + (1.0 - gate) * back[1]
        out_ref[0, :, where] = result.astype(BF16)


def spread_over(block, axis, low):
    held = {0: block}
    bit = lax.axis_size(axis) // 2
    while bit >= low:
        for k in list(held):
            held[k | bit] = swap(held[k], axis, bit)
        bit //= 2
    return held


def swap_all(held):
    return {k: swap(block, "dp", 1) for k, block in held.items() if k}


def after(values, earlier):
    return lax.optimization_barrier((values, earlier))[0]


def body(
    frames_in, pit_order, expert_ids, norm_gains, attn_qkv, attn_out, router, expert_in, expert_out
):
    dp_count = lax.axis_size("dp")
    exp_count = lax.axis_size("expert")
    me = lax.axis_index("dp").astype(jnp.int32)
    exp_index = lax.axis_index("expert").astype(jnp.int32)
    frames, width = frames_in.shape[1:]
    top = expert_ids.shape[2]
    capacity = frames * top * 5 // (4 * exp_count)
    slots_count = exp_count * capacity
    half = dp_count // 2
    share = width // dp_count
    inner = expert_in.shape[2]

    raw = spread_over(frames_in, "dp", 2)

    qkv = {0: lax.dynamic_slice_in_dim(attn_qkv, me * share, share, axis=2)}
    for far in range(2, exp_count, 2):
        qkv[far] = swap(qkv[0], "expert", far)
    for far in range(0, exp_count, 2):
        qkv[far | 1] = swap(qkv[far], "expert", 1)

    rows = width // 2
    proj_near = lax.all_gather(
        lax.dynamic_slice_in_dim(attn_out, (me % 2) * rows, rows, axis=1),
        "expert",
        axis=0,
        tiled=True,
    )

    in_cuts = [(0, rows // 2), (rows // 2, width - rows // 2)]
    in_chunks = [lax.slice_in_dim(expert_in, a, a + n, axis=1) for a, n in in_cuts]
    out_chunks = [expert_out[:, :, :rows], expert_out[:, :, rows:]]
    in_held = [spread_over(in_chunks[0], "dp", 2)]
    early = [*[qkv[k] for k in range(2, exp_count, 2)], in_held[0]]
    raw[half] = after(raw[half], early)

    groups = len(raw)
    member = jnp.arange(groups, dtype=jnp.int32) * 2
    meeting = ((me ^ member) % half) * exp_count + exp_index
    place = jnp.where(pit_order[meeting, 0] == 0, member, member ^ half) // 2

    near, stream = pl.pallas_call(
        functools.partial(norm_kernel, groups),
        out_shape=(
            jax.ShapeDtypeStruct((groups, frames, width), BF16),
            jax.ShapeDtypeStruct((frames, width), BF16),
        ),
        in_specs=[SMEM, VMEM] + [VMEM] * groups,
        out_specs=(VMEM, VMEM),
        compiler_params=params(32),
        cost_estimate=cost(groups * frames * width * 8, groups * frames * width * 4),
        name="norm",
    )(place, norm_gains, *[raw[2 * k] for k in range(groups)])
    far = swap(near, "dp", 1)
    in_core = swap(after(expert_in, far), "dp", 1)

    contexts = pl.pallas_call(
        functools.partial(attention_kernel, dp_count, exp_count),
        out_shape=[jax.ShapeDtypeStruct((frames, share), BF16)] * dp_count,
        in_specs=[SMEM, VMEM, VMEM] + [ANY] * exp_count,
        out_specs=[VMEM] * dp_count,
        scratch_shapes=[
            pltpu.VMEM((3, width, share), BF16),
            pltpu.SemaphoreType.DMA((exp_count,)),
        ],
        compiler_params=params(32),
        cost_estimate=cost(
            2 * frames * width * width * 3 + 16 * frames * frames * width, 5 << 20, frames * frames * 16
        ),
        name="attention",
    )(exp_index[None], near, far, *[qkv[k] for k in range(exp_count)])

    crossed = [swap(contexts[k], "dp", k) for k in range(1, dp_count)]

    proj_far = swap(after(proj_near, contexts), "dp", 1)

    in_held.append(spread_over(after(in_chunks[1], crossed), "dp", 2))
    in_hop = [swap_all(after(in_held[0], crossed))]
    out_core = swap(after(expert_out, crossed), "dp", 1)
    out_held = [spread_over(after(out_chunks[0], proj_far), "dp", 2)]

    cols = expert_ids[0]
    slots, mixed, gate = pl.pallas_call(
        functools.partial(mix_kernel, dp_count, exp_count, capacity),
        out_shape=(
            jax.ShapeDtypeStruct((slots_count, width), BF16),
            jax.ShapeDtypeStruct((frames, width), BF16),
            jax.ShapeDtypeStruct((frames, 128), F32),
        ),
        in_specs=[SMEM] + [VMEM] * (7 + dp_count),
        out_specs=(VMEM, VMEM, VMEM),
        scratch_shapes=[pltpu.VMEM((frames, width), F32)],
        compiler_params=params(32),
        cost_estimate=cost(2 * frames * width * (width + slots_count), 5 << 20),
        name="mix",
    )(me[None], stream, proj_near, proj_far, norm_gains, router, cols.T, cols, contexts[0], *crossed)

    arrived = lax.all_to_all(
        slots.reshape(exp_count, capacity, width), "expert", split_axis=0, concat_axis=0, tiled=True
    ).reshape(slots_count, width)

    out_held.append(spread_over(after(out_chunks[1], (mixed, in_core, out_core)), "dp", 2))
    in_hop.append(swap_all(after(in_held[1], arrived)))

    whole = (slice(None), slice(None))
    distant = range(2, dp_count)
    places = [(pl.ds(a, n), slice(None)) for a, n in in_cuts]

    def hidden_units(slots_in, plan, sources, name):
        return pl.pallas_call(
            functools.partial(hidden_kernel, plan, len(sources)),
            out_shape=jax.ShapeDtypeStruct((len(plan), slots_count, inner), BF16),
            in_specs=[VMEM] + [ANY] * len(sources),
            out_specs=VMEM,
            scratch_shapes=[
                pltpu.VMEM((len(plan), width, inner), BF16),
                pltpu.SemaphoreType.DMA((len(plan), max(len(pieces) for pieces in plan))),
            ],
            compiler_params=params(32),
            cost_estimate=cost(2 * slots_count * width * inner * len(plan), 8 << 20),
            name=name,
        )(slots_in, *sources)

    hidden_near = hidden_units(
        arrived, [[(k, whole, whole)] for k in range(2)], [expert_in, in_core], "hidden_near"
    )
    hidden_far = hidden_units(
        after(arrived, hidden_near),
        [[(2 * at + p, whole, places[p]) for p in range(2)] for at in range(len(distant))],
        [(in_hop if k & 1 else in_held)[p][k & ~1] for k in distant for p in range(2)],
        "hidden_far",
    )
    out_hop = [swap_all(after(out_held[0], (hidden_near, in_hop)))]

    returned = []
    for c in range(2):
        if c:
            out_hop.append(swap_all(after(out_held[c], answer)))
        piece = (slice(None), pl.ds(c * rows, rows))
        sources = [expert_out, out_core] + [(out_hop if k & 1 else out_held)[c][k & ~1] for k in distant]
        answer = pl.pallas_call(
            functools.partial(
                answer_kernel,
                [[(k, piece if k < 2 else whole, whole)] for k in range(dp_count)],
                len(sources),
            ),
            out_shape=jax.ShapeDtypeStruct((slots_count, rows), BF16),
            in_specs=[VMEM, VMEM] + [ANY] * len(sources),
            out_specs=VMEM,
            scratch_shapes=[
                pltpu.VMEM((dp_count, inner, rows), BF16),
                pltpu.VMEM((slots_count, rows), F32),
                pltpu.SemaphoreType.DMA((dp_count, 1)),
            ],
            compiler_params=params(32),
            cost_estimate=cost(2 * slots_count * rows * inner * dp_count, 10 << 20),
            name="answer",
        )(hidden_near, hidden_far, *sources)
        returned.append(
            lax.all_to_all(
                answer.reshape(exp_count, capacity, rows), "expert", split_axis=0, concat_axis=0, tiled=True
            ).reshape(slots_count, rows)
        )

    return pl.pallas_call(
        functools.partial(combine_kernel, exp_count, capacity, len(returned)),
        out_shape=jax.ShapeDtypeStruct((1, frames, width), BF16),
        in_specs=[VMEM] * (3 + len(returned)),
        out_specs=VMEM,
        compiler_params=params(32),
        cost_estimate=cost(4 * frames * slots_count * width, 3 << 20),
        name="combine",
    )(mixed, gate, cols, *returned)


def solution(mesh):
    return jax.shard_map(
        body,
        mesh=mesh,
        in_specs=(
            P(("dp", "expert"), None, None),
            P(),
            P(("dp", "expert"), None, None),
            P(),
            P(None, "expert", None),
            P("expert", None),
            P(),
            P("expert", None, "dp"),
            P("expert", "dp", None),
        ),
        out_specs=P(("dp", "expert"), None, None),
        check_vma=False,
    )
```

time: 227 us -> 229 us (level)
  blocking collectives: 36.5 us -> 22 us
  local copies, waits for them, and re-layouts: 10.3 us -> 18 us
  Pallas kernels: 28.1 us -> 34 us
  starting transfers between devices: 25.1 us -> 28.3 us
    all_to_all x1, blocking collectives: 36.5 us -> 22 us  [body(): lax.all_to_all(answer.reshape(exp_count, capacity, rows), 'expert', split...]
    all_to_all x1, waiting for transfers between devices: 14.3 us -> 0.01 us  [body(): lax.all_to_all(slots.reshape(exp_count, capacity, width), 'expert', split...]
    ppermute x19 -> x23, waiting for transfers between devices: 96 us -> 109 us  [swap(): return lax.ppermute(block, axis, [(i, i ^ mask) for i in range(count)])]
    all_to_all x0 -> x1, starting transfers between devices: none -> 5.99 us  [body(): lax.all_to_all(answer.reshape(exp_count, capacity, rows), 'expert', split...]
    slice x0 -> x3, local copies, waits for them, and re-layouts: none -> 5.81 us  [the longest x1 3.2 us: body(): out_chunks = [expert_out[:, :, :rows], expert_out[:, :, rows:]]]
    pallas_call x3 -> x6, Pallas kernels: 18.3 us -> 23.9 us  [the longest x2 9.96 us: hidden_units(): pl.pallas_call(functools.partial(hidden_kernel, plan, len(sources)), out_...]
    unnamed x28 -> x36, local copies, waits for them, and re-layouts: 7.37 us -> 9.73 us
    ppermute x19 -> x23, starting transfers between devices: 19 us -> 17.2 us  [swap(): return lax.ppermute(block, axis, [(i, i ^ mask) for i in range(count)])]
  transfers between devices with their start and end apart: 21 -> 26, of which waited for: 13 -> 14; matrix products, arithmetic and copies ran while one was open for 1% -> 3% of each run, Pallas kernels for 5% -> 12%
where the time goes in v2:
time: 229 us; the launch traced here: 225 us
  waiting for transfers between devices  109 us (48%)
  Pallas kernels  34 us (15%)
  starting transfers between devices  28.3 us (12%)
  blocking collectives  22 us (10%)
  local copies, waits for them, and re-layouts  18 us (8%)
  between operations  13.6 us (6%)
    ppermute x23, waiting for transfers between devices, swap(): return lax.ppermute(block, axis, [(i, i ^ mask) for i in range(count)])  109 us
    all_to_all x1, blocking collectives, body(): lax.all_to_all(answer.reshape(exp_count, capacity, rows), 'expert', split...  22 us
    ppermute x23, starting transfers between devices, swap(): return lax.ppermute(block, axis, [(i, i ^ mask) for i in range(count)])  17.2 us
    pallas_call x2, Pallas kernels, hidden_units(): pl.pallas_call(functools.partial(hidden_kernel, plan, len(sources)), out_...  9.96 us
    unnamed x36, local copies, waits for them, and re-layouts  9.73 us
    pallas_call x2, Pallas kernels, body(): pl.pallas_call(functools.partial(answer_kernel, [[(k, piece if k < 2 else...  9.37 us
    pallas_call x1, Pallas kernels, body(): pl.pallas_call(functools.partial(attention_kernel, dp_count, exp_count),...  7.24 us
    all_to_all x1, starting transfers between devices, body(): lax.all_to_all(answer.reshape(exp_count, capacity, rows), 'expert', split...  5.99 us
  transfers between devices with their start and end apart: 26, of which 14 were waited for; matrix products, arithmetic and copies ran while one was open for 3% of the time, Pallas kernels for 12%

profile of v2, /device:TPU:16, one launch (start us, length us, event | category | flops | bytes accessed | tf_op | source)
XLA Modules:
  0.0 225.1 jit_solution(18437792198119612028)
XLA Ops:
  6.6 1.7 constant_dynamic-slice_fusion.1
  8.3 1.6 collective-permute-start
  11.6 1.6 collective-permute-start.1
  13.5 1.6 collective-permute-start.3
  15.8 4.4 %collective-permute-done.1.refs_2_ = bf16[3,128,256]{2,1,0:T(8,128)(2,1)S(1)} collective-permute-done((bf16[3,128,256]{2,1,0:T(8,128)(2,1)S(1)}, bf16[3,128,256]{2,1,0:T(8,128)(2,1)S(1)}, u32[]{:S(2)}, u32[]{:S(2)}) %collective-permute-start.1) | collective-permute-done | bytes 196640 | tf_op jit(solution)/shard_map/ppermute | solution.py:29
  20.2 9.7 %collective-permute-done.2.refs_4_ = bf16[3,128,256]{2,1,0:T(8,128)(2,1)S(1)} collective-permute-done((bf16[3,128,256]{2,1,0:T(8,128)(2,1)S(1)}, bf16[3,128,256]{2,1,0:T(8,128)(2,1)S(1)}, u32[]{:S(2)}, u32[]{:S(2)}) %collective-permute-start.2) | collective-permute-done | bytes 196640 | tf_op jit(solution)/shard_map/ppermute | solution.py:29
  30.0 5.8 %collective-permute-done.3.refs_6_ = bf16[3,128,256]{2,1,0:T(8,128)(2,1)S(1)} collective-permute-done((bf16[3,128,256]{2,1,0:T(8,128)(2,1)S(1)}, bf16[3,128,256]{2,1,0:T(8,128)(2,1)S(1)}, u32[]{:S(2)}, u32[]{:S(2)}) %collective-permute-start.3) | collective-permute-done | bytes 196640 | tf_op jit(solution)/shard_map/ppermute | solution.py:29
  37.2 1.6 collective-permute-start.6
  41.3 4.0 %collective-permute-done.6.refs_1_ = bf16[3,128,256]{2,1,0:T(8,128)(2,1)S(1)} collective-permute-done((bf16[3,128,256]{2,1,0:T(8,128)(2,1)S(1)}, bf16[3,128,256]{2,1,0:T(8,128)(2,1)S(1)}, u32[]{:S(2)}, u32[]{:S(2)}) %collective-permute-start.6) | collective-permute-done | bytes 196640 | tf_op jit(solution)/shard_map/ppermute | solution.py:29
  45.3 8.4 %collective-permute-done.7.refs_3_ = bf16[3,128,256]{2,1,0:T(8,128)(2,1)S(1)} collective-permute-done((bf16[3,128,256]{2,1,0:T(8,128)(2,1)S(1)}, bf16[3,128,256]{2,1,0:T(8,128)(2,1)S(1)}, u32[]{:S(2)}, u32[]{:S(2)}) %collective-permute-start.7) | collective-permute-done | bytes 196640 | tf_op jit(solution)/shard_map/ppermute | solution.py:29
  53.7 5.3 %collective-permute-done.8.refs_5_ = bf16[3,128,256]{2,1,0:T(8,128)(2,1)S(1)} collective-permute-done((bf16[3,128,256]{2,1,0:T(8,128)(2,1)S(1)}, bf16[3,128,256]{2,1,0:T(8,128)(2,1)S(1)}, u32[]{:S(2)}, u32[]{:S(2)}) %collective-permute-start.8) | collective-permute-done | bytes 196640 | tf_op jit(solution)/shard_map/ppermute | solution.py:29
  59.0 3.8 %collective-permute-done.9.refs_7_ = bf16[3,128,256]{2,1,0:T(8,128)(2,1)S(1)} collective-permute-done((bf16[3,128,256]{2,1,0:T(8,128)(2,1)S(1)}, bf16[3,128,256]{2,1,0:T(8,128)(2,1)S(1)}, u32[]{:S(2)}, u32[]{:S(2)}) %collective-permute-start.9) | collective-permute-done | bytes 196640 | tf_op jit(solution)/shard_map/ppermute | solution.py:29
  62.8 7.2 %attention.1 = (bf16[256,256]{1,0:T(8,128)(2,1)S(1)}, bf16[256,256]{1,0:T(8,128)(2,1)}, bf16[256,256]{1,0:T(8,128)(2,1)}, bf16[256,256]{1,0:T(8,128)(2,1)}) custom-call(s32[1]{0:T(128)} %bitcast.2.me_ref, bf16[2,256,1024]{2,1,0:T(8,128)(2,1)S(1)} %get-tuple-element.28.near_ref, bf16[2,256,1024]{2,1,0:T(8,128)(2,1)S(1)} %collective-permute-done.5.far_ref, ...), custom_call_target="tpu_custom_call" | custom-call | flops 10485760 | bytes 20480 | tf_op jit(solution)/shard_map/attention/pallas_call | solution.py:280
  73.2 4.0 %collective-permute-done.12.refs_2_ = bf16[256,256]{1,0:T(8,128)(2,1)S(1)} collective-permute-done((bf16[256,256]{1,0:T(8,128)(2,1)}, bf16[256,256]{1,0:T(8,128)(2,1)S(1)}, u32[]{:S(2)}, u32[]{:S(2)}) %collective-permute-start.12) | collective-permute-done | bytes 131104 | tf_op jit(solution)/shard_map/ppermute | solution.py:29
  79.5 2.9 %mix.1 = (bf16[640,1024]{1,0:T(8,128)(2,1)}, bf16[256,1024]{1,0:T(8,128)(2,1)S(1)}, f32[256,128]{1,0:T(8,128)S(1)}) custom-call(s32[1]{0:T(128)} %bitcast.me_ref, bf16[256,1024]{1,0:T(8,128)(2,1)S(1)} %get-tuple-element.27.own_ref, bf16[1024,512]{1,0:T(8,128)(2,1)S(1)} %copy-done.7, bf16[1024,512]{1,0:T(8,128)(2,1)S(1)} %collective-permute-done.10.far_ref, ...), custom_call_target="tpu_custom_call" | custom-call | flops 3407872 | bytes 20480 | tf_op jit(solution)/shard_map/mix/pallas_call | solution.py:306
  83.8 5.1 %all-to-all-start = ((bf16[8,80,1024]{2,1,0:T(8,128)(2,1)}), bf16[8,80,1024]{2,1,0:T(8,128)(2,1)S(1)}, u32[]{:S(2)}, u32[]{:S(2)}) async-start(bf16[8,80,1024]{2,1,0:T(8,128)(2,1)} %bitcast.5), calls=%async_computation | async-start | bytes 2621440 | tf_op jit(solution)/shard_map/all_to_all | solution.py:321
  89.0 1.5 slice.13
  90.5 1.6 collective-permute-start.15
  92.6 34.5 %collective-permute-done.15.refs_1_ = bf16[1,768,1024]{2,1,0:T(8,128)(2,1)} collective-permute-done((bf16[1,768,1024]{2,1,0:T(8,128)(2,1)S(1)}, bf16[1,768,1024]{2,1,0:T(8,128)(2,1)}, u32[]{:S(2)}, u32[]{:S(2)}) %collective-permute-start.15) | collective-permute-done | bytes 1572896 | tf_op jit(solution)/shard_map/ppermute | solution.py:29
  127.1 3.2 %fusion.6 = (bf16[1,1024,512]{2,1,0:T(8,128)(2,1)}, bf16[1,1024,512]{2,1,0:T(8,128)(2,1)S(1)}) fusion(bf16[1,1024,1024]{2,1,0:T(8,128)(2,1)} %refs_0_.7), kind=kLoop, calls=%fused_computation.18 | loop fusion | bytes 4194304 | tf_op jit(solution)/shard_map/slice | solution.py:255
  133.2 5.0 %hidden_near.1.near_ref = bf16[2,640,1024]{2,1,0:T(8,128)(2,1)S(1)} custom-call(bf16[640,1024]{1,0:T(8,128)(2,1)S(1)} %bitcast.13, bf16[1,1024,1024]{2,1,0:T(8,128)(2,1)} %refs_0_.5, bf16[1,1024,1024]{2,1,0:T(8,128)(2,1)} %collective-permute-done.14.refs_1_), custom_call_target="tpu_custom_call" | custom-call | flops 10485760 | bytes 32768 | tf_op jit(solution)/shard_map/hidden_near/pallas_call | solution.py:333
  138.2 17.3 %collective-permute-done.19.refs_2_ = bf16[1,1024,512]{2,1,0:T(8,128)(2,1)S(1)} collective-permute-done((bf16[1,1024,512]{2,1,0:T(8,128)(2,1)S(1)}, bf16[1,1024,512]{2,1,0:T(8,128)(2,1)S(1)}, u32[]{:S(2)}, u32[]{:S(2)}) %collective-permute-start.19) | collective-permute-done | bytes 1048608 | tf_op jit(solution)/shard_map/ppermute | solution.py:29
  155.4 1.6 collective-permute-start.21
  157.0 5.0 %hidden_far.1.far_ref = bf16[2,640,1024]{2,1,0:T(8,128)(2,1)S(1)} custom-call(bf16[640,1024]{1,0:T(8,128)(2,1)S(1)} %bitcast.14, bf16[1,256,1024]{2,1,0:T(8,128)(2,1)} %collective-permute-done.4.refs_0_, bf16[1,768,1024]{2,1,0:T(8,128)(2,1)} %collective-permute-done.15.refs_1_, bf16[1,256,1024]{2,1,0:T(8,128)(2,1)S(1)} %collective-permute-done.16.refs_2_, ...), custom_call_target="tpu_custom_call" | custom-call | flops 10485760 | bytes 32768 | tf_op jit(solution)/shard_map/hidden_far/pallas_call | solution.py:333
  162.0 5.1 %answer.2 = bf16[640,512]{1,0:T(8,128)(2,1)S(1)} custom-call(bf16[2,640,1024]{2,1,0:T(8,128)(2,1)S(1)} %hidden_near.1.near_ref, bf16[2,640,1024]{2,1,0:T(8,128)(2,1)S(1)} %hidden_far.1.far_ref, bf16[1,1024,1024]{2,1,0:T(8,128)(2,1)} %refs_0_.7, bf16[1,1024,1024]{2,1,0:T(8,128)(2,1)} %collective-permute-done.18.refs_1_, ...), custom_call_target="tpu_custom_call" | custom-call | flops 10485760 | bytes 40960 | tf_op jit(solution)/shard_map/answer/pallas_call | solution.py:364
  168.0 6.0 %all-to-all-start.1 = ((bf16[8,80,512]{2,1,0:T(8,128)(2,1)}), bf16[8,80,512]{2,1,0:T(8,128)(2,1)}, u32[]{:S(2)}, u32[]{:S(2)}) async-start(bf16[8,80,512]{2,1,0:T(8,128)(2,1)} %bitcast.15), calls=%async_computation.1 | async-start | bytes 1310720 | tf_op jit(solution)/shard_map/all_to_all | solution.py:383
  174.0 7.4 %collective-permute-done.21.refs_2_ = bf16[1,1024,512]{2,1,0:T(8,128)(2,1)} collective-permute-done((bf16[1,1024,512]{2,1,0:T(8,128)(2,1)}, bf16[1,1024,512]{2,1,0:T(8,128)(2,1)}, u32[]{:S(2)}, u32[]{:S(2)}) %collective-permute-start.21) | collective-permute-done | bytes 1048608 | tf_op jit(solution)/shard_map/ppermute | solution.py:29
  181.3 2.9 %collective-permute-done.22.refs_3_ = bf16[1,1024,512]{2,1,0:T(8,128)(2,1)S(1)} collective-permute-done((bf16[1,1024,512]{2,1,0:T(8,128)(2,1)}, bf16[1,1024,512]{2,1,0:T(8,128)(2,1)S(1)}, u32[]{:S(2)}, u32[]{:S(2)}) %collective-permute-start.22) | collective-permute-done | bytes 1048608 | tf_op jit(solution)/shard_map/ppermute | solution.py:29
  184.2 1.7 copy-done.2
  185.9 4.3 %answer.3 = bf16[640,512]{1,0:T(8,128)(2,1)S(1)} custom-call(bf16[2,640,1024]{2,1,0:T(8,128)(2,1)S(1)} %hidden_near.1.near_ref, bf16[2,640,1024]{2,1,0:T(8,128)(2,1)S(1)} %copy-done.2, bf16[1,1024,1024]{2,1,0:T(8,128)(2,1)} %refs_0_.7, bf16[1,1024,1024]{2,1,0:T(8,128)(2,1)} %collective-permute-done.18.refs_1_, ...), custom_call_target="tpu_custom_call" | custom-call | flops 10485760 | bytes 40960 | tf_op jit(solution)/shard_map/answer/pallas_call | solution.py:364
  191.1 22.0 %all_to_all.15 = bf16[8,80,512]{2,1,0:T(8,128)(2,1)S(1)} all-to-all(bf16[8,80,512]{2,1,0:T(8,128)(2,1)} %bitcast.16), channel_id=1, replica_groups=mesh['dp'=4,'expert'=8] {'expert'}, dimensions={0} | all-to-all | bytes 1310720 | tf_op jit(solution)/shard_map/all_to_all | solution.py:383
  215.0 3.3 %combine.1 = bf16[1,256,1024]{2,1,0:T(8,128)(2,1)} custom-call(bf16[256,1024]{1,0:T(8,128)(2,1)S(1)} %copy-done.9, f32[256,128]{1,0:T(8,128)S(1)} %copy-done.12, s32[256,2]{1,0:T(8,128)S(1)} %bitcast.20, bf16[640,512]{1,0:T(8,128)(2,1)} %bitcast.8.refs_0_, bf16[640,512]{1,0:T(8,128)(2,1)S(1)} %bitcast.17), custom_call_target="tpu_custom_call" | custom-call | flops 2621440 | bytes 12288 | tf_op jit(solution)/shard_map/combine/pallas_call | solution.py:388
  (75 shorter events, 20.6 us)
Async XLA Ops:
  6.5 29.3 %copy-start.10 = (bf16[1,256,1024]{2,1,0:T(8,128)(2,1)S(1)}, bf16[1,256,1024]{2,1,0:T(8,128)(2,1)}, u32[]{:S(2)}) copy-start(bf16[1,256,1024]{2,1,0:T(8,128)(2,1)} %refs_0_.4) | copy-start | bytes 1572868
  6.5 8.6 %copy-start.14 = (s32[16,2]{0,1:T(2,128)S(1)}, s32[16,2]{0,1:T(2,128)}, u32[]{:S(2)}) copy-start(s32[16,2]{0,1:T(2,128)} %param.10) | copy-start | bytes 388
  6.5 29.3 %copy-start.13 = (f32[2,1024]{1,0:T(2,128)S(1)}, f32[2,1024]{1,0:T(2,128)}, u32[]{:S(2)}) copy-start(f32[2,1024]{1,0:T(2,128)} %gain_ref.3) | copy-start | bytes 24580
  6.5 63.5 %all-gather.2.cloned.1.call-start = ((), (), s32[]{:S(2)}) async-start(), calls=%async_computation.3 | async-start | bytes 1179648 | tf_op jit(solution)/shard_map/all_gather | solution.py:246
  8.3 27.5 %collective-permute-start = (bf16[1,256,1024]{2,1,0:T(8,128)(2,1)}, bf16[1,256,1024]{2,1,0:T(8,128)(2,1)S(1)}, u32[]{:S(2)}, u32[]{:S(2)}) collective-permute-start(bf16[1,256,1024]{2,1,0:T(8,128)(2,1)} %refs_0_.4), channel_id=1, source_target_pairs={{0,16},{8,24},{16,0},{24,8},{1,17},{9,25},{17,1},{25,9},{2,18},{10... | collective-permute-start | bytes 1572872 | tf_op jit(solution)/shard_map/ppermute | solution.py:29
  11.0 24.8 %collective-permute-start.4 = (bf16[1,256,1024]{2,1,0:T(8,128)(2,1)S(1)}, bf16[1,256,1024]{2,1,0:T(8,128)(2,1)}, u32[]{:S(2)}, u32[]{:S(2)}) collective-permute-start(bf16[1,256,1024]{2,1,0:T(8,128)(2,1)S(1)} %slice.12), channel_id=1, source_target_pairs={{0,16},{8,24},{16,0},{24,8},{1,17},{9,25},{17,1},{25,9},{2,18},{10... | collective-permute-start | bytes 1572872 | tf_op jit(solution)/shard_map/ppermute | solution.py:29
  11.6 8.6 %collective-permute-start.1 = (bf16[3,128,256]{2,1,0:T(8,128)(2,1)S(1)}, bf16[3,128,256]{2,1,0:T(8,128)(2,1)S(1)}, u32[]{:S(2)}, u32[]{:S(2)}) collective-permute-start(bf16[3,128,256]{2,1,0:T(8,128)(2,1)S(1)} %constant_dynamic-slice_fusion.refs_0_), channel_id=1, source_target_pairs={{0,2},{1,3},{2,0},{3,1},{4,6},{5,7},{6,4},{7,5},{8,10},{9,11},{10,... | collective-permute-start | bytes 589832 | tf_op jit(solution)/shard_map/ppermute | solution.py:29
  13.2 16.8 %collective-permute-start.2 = (bf16[3,128,256]{2,1,0:T(8,128)(2,1)S(1)}, bf16[3,128,256]{2,1,0:T(8,128)(2,1)S(1)}, u32[]{:S(2)}, u32[]{:S(2)}) collective-permute-start(bf16[3,128,256]{2,1,0:T(8,128)(2,1)S(1)} %constant_dynamic-slice_fusion.refs_0_), channel_id=1, source_target_pairs={{0,4},{1,5},{2,6},{3,7},{4,0},{5,1},{6,2},{7,3},{8,12},{9,13},{10,... | collective-permute-start | bytes 589832 | tf_op jit(solution)/shard_map/ppermute | solution.py:29
  13.5 22.2 %collective-permute-start.3 = (bf16[3,128,256]{2,1,0:T(8,128)(2,1)S(1)}, bf16[3,128,256]{2,1,0:T(8,128)(2,1)S(1)}, u32[]{:S(2)}, u32[]{:S(2)}) collective-permute-start(bf16[3,128,256]{2,1,0:T(8,128)(2,1)S(1)} %constant_dynamic-slice_fusion.refs_0_), channel_id=1, source_target_pairs={{0,6},{1,7},{2,4},{3,5},{4,2},{5,3},{6,0},{7,1},{8,14},{9,15},{10,... | collective-permute-start | bytes 589832 | tf_op jit(solution)/shard_map/ppermute | solution.py:29
  37.1 35.0 %copy-start.15 = (f32[1024,8]{0,1:T(8,128)S(1)}, f32[1024,8]{0,1:T(8,128)}, u32[]{:S(2)}) copy-start(f32[1024,8]{0,1:T(8,128)} %param.15) | copy-start | bytes 98308
  37.1 25.7 %collective-permute-start.5 = (bf16[2,256,1024]{2,1,0:T(8,128)(2,1)S(1)}, bf16[2,256,1024]{2,1,0:T(8,128)(2,1)S(1)}, u32[]{:S(2)}, u32[]{:S(2)}) collective-permute-start(bf16[2,256,1024]{2,1,0:T(8,128)(2,1)S(1)} %get-tuple-element.28.near_ref), channel_id=1, source_target_pairs={{0,8},{8,0},{16,24},{24,16},{1,9},{9,1},{17,25},{25,17},{2,10},{10... | collective-permute-start | bytes 3145736 | tf_op jit(solution)/shard_map/ppermute | solution.py:29
  37.2 8.1 %collective-permute-start.6 = (bf16[3,128,256]{2,1,0:T(8,128)(2,1)S(1)}, bf16[3,128,256]{2,1,0:T(8,128)(2,1)S(1)}, u32[]{:S(2)}, u32[]{:S(2)}) collective-permute-start(bf16[3,128,256]{2,1,0:T(8,128)(2,1)S(1)} %constant_dynamic-slice_fusion.refs_0_), channel_id=1, source_target_pairs={{0,1},{1,0},{2,3},{3,2},{4,5},{5,4},{6,7},{7,6},{8,9},{9,8},{10,11... | collective-permute-start | bytes 589832 | tf_op jit(solution)/shard_map/ppermute | solution.py:29
  38.7 15.0 %collective-permute-start.7 = (bf16[3,128,256]{2,1,0:T(8,128)(2,1)S(1)}, bf16[3,128,256]{2,1,0:T(8,128)(2,1)S(1)}, u32[]{:S(2)}, u32[]{:S(2)}) collective-permute-start(bf16[3,128,256]{2,1,0:T(8,128)(2,1)S(1)} %collective-permute-done.1.refs_2_), channel_id=1, source_target_pairs={{0,1},{1,0},{2,3},{3,2},{4,5},{5,4},{6,7},{7,6},{8,9},{9,8},{10,11... | collective-permute-start | bytes 589832 | tf_op jit(solution)/shard_map/ppermute | solution.py:29
  39.3 19.7 %collective-permute-start.8 = (bf16[3,128,256]{2,1,0:T(8,128)(2,1)S(1)}, bf16[3,128,256]{2,1,0:T(8,128)(2,1)S(1)}, u32[]{:S(2)}, u32[]{:S(2)}) collective-permute-start(bf16[3,128,256]{2,1,0:T(8,128)(2,1)S(1)} %collective-permute-done.2.refs_4_), channel_id=1, source_target_pairs={{0,1},{1,0},{2,3},{3,2},{4,5},{5,4},{6,7},{7,6},{8,9},{9,8},{10,11... | collective-permute-start | bytes 589832 | tf_op jit(solution)/shard_map/ppermute | solution.py:29
  40.8 22.0 %collective-permute-start.9 = (bf16[3,128,256]{2,1,0:T(8,128)(2,1)S(1)}, bf16[3,128,256]{2,1,0:T(8,128)(2,1)S(1)}, u32[]{:S(2)}, u32[]{:S(2)}) collective-permute-start(bf16[3,128,256]{2,1,0:T(8,128)(2,1)S(1)} %collective-permute-done.3.refs_6_), channel_id=1, source_target_pairs={{0,1},{1,0},{2,3},{3,2},{4,5},{5,4},{6,7},{7,6},{8,9},{9,8},{10,11... | collective-permute-start | bytes 589832 | tf_op jit(solution)/shard_map/ppermute | solution.py:29
  62.8 9.6 %copy-start.16 = (s32[1,256,2]{1,2,0:T(2,128)S(1)}, s32[1,256,2]{1,2,0:T(2,128)}, u32[]{:S(2)}) copy-start(s32[1,256,2]{1,2,0:T(2,128)} %param.11) | copy-start | bytes 6148
  70.0 8.2 %collective-permute-start.10 = (bf16[1024,512]{1,0:T(8,128)(2,1)}, bf16[1024,512]{1,0:T(8,128)(2,1)S(1)}, u32[]{:S(2)}, u32[]{:S(2)}) collective-permute-start(bf16[1024,512]{1,0:T(8,128)(2,1)} %all-gather.2.cloned.1.call-done.near_ref), channel_id=1, source_target_pairs={{0,8},{8,0},{16,24},{24,16},{1,9},{9,1},{17,25},{25,17},{2,10},{10... | collective-permute-start | bytes 3145736 | tf_op jit(solution)/shard_map/ppermute | solution.py:29
  70.1 3.0 %collective-permute-start.11 = (bf16[256,256]{1,0:T(8,128)(2,1)}, bf16[256,256]{1,0:T(8,128)(2,1)S(1)}, u32[]{:S(2)}, u32[]{:S(2)}) collective-permute-start(bf16[256,256]{1,0:T(8,128)(2,1)} %get-tuple-element.30), channel_id=1, source_target_pairs={{0,8},{8,0},{16,24},{24,16},{1,9},{9,1},{17,25},{25,17},{2,10},{10... | collective-permute-start | bytes 393224 | tf_op jit(solution)/shard_map/ppermute | solution.py:29
  70.6 6.6 %collective-permute-start.12 = (bf16[256,256]{1,0:T(8,128)(2,1)}, bf16[256,256]{1,0:T(8,128)(2,1)S(1)}, u32[]{:S(2)}, u32[]{:S(2)}) collective-permute-start(bf16[256,256]{1,0:T(8,128)(2,1)} %get-tuple-element.31), channel_id=1, source_target_pairs={{0,16},{8,24},{16,0},{24,8},{1,17},{9,25},{17,1},{25,9},{2,18},{10... | collective-permute-start | bytes 393224 | tf_op jit(solution)/shard_map/ppermute | solution.py:29
  72.1 6.1 %collective-permute-start.13 = (bf16[256,256]{1,0:T(8,128)(2,1)}, bf16[256,256]{1,0:T(8,128)(2,1)S(1)}, u32[]{:S(2)}, u32[]{:S(2)}) collective-permute-start(bf16[256,256]{1,0:T(8,128)(2,1)} %get-tuple-element.32), channel_id=1, source_target_pairs={{0,24},{8,16},{16,8},{24,0},{1,25},{9,17},{17,9},{25,1},{2,26},{10... | collective-permute-start | bytes 393224 | tf_op jit(solution)/shard_map/ppermute | solution.py:29
  83.8 43.3 %all-to-all-start = ((bf16[8,80,1024]{2,1,0:T(8,128)(2,1)}), bf16[8,80,1024]{2,1,0:T(8,128)(2,1)S(1)}, u32[]{:S(2)}, u32[]{:S(2)}) async-start(bf16[8,80,1024]{2,1,0:T(8,128)(2,1)} %bitcast.5), calls=%async_computation | async-start | bytes 2621440 | tf_op jit(solution)/shard_map/all_to_all | solution.py:321
  90.5 36.6 %collective-permute-start.15 = (bf16[1,768,1024]{2,1,0:T(8,128)(2,1)S(1)}, bf16[1,768,1024]{2,1,0:T(8,128)(2,1)}, u32[]{:S(2)}, u32[]{:S(2)}) collective-permute-start(bf16[1,768,1024]{2,1,0:T(8,128)(2,1)S(1)} %slice.13), channel_id=1, source_target_pairs={{0,16},{8,24},{16,0},{24,8},{1,17},{9,25},{17,1},{25,9},{2,18},{10... | collective-permute-start | bytes 4718600 | tf_op jit(solution)/shard_map/ppermute | solution.py:29
  92.1 39.8 %collective-permute-start.14 = (bf16[1,1024,1024]{2,1,0:T(8,128)(2,1)}, bf16[1,1024,1024]{2,1,0:T(8,128)(2,1)}, u32[]{:S(2)}, u32[]{:S(2)}) collective-permute-start(bf16[1,1024,1024]{2,1,0:T(8,128)(2,1)} %refs_0_.5), channel_id=1, source_target_pairs={{0,8},{8,0},{16,24},{24,16},{1,9},{9,1},{17,25},{25,17},{2,10},{10... | collective-permute-start | bytes 6291464 | tf_op jit(solution)/shard_map/ppermute | solution.py:29
  92.1 63.4 %collective-permute-start.18 = (bf16[1,1024,1024]{2,1,0:T(8,128)(2,1)}, bf16[1,1024,1024]{2,1,0:T(8,128)(2,1)}, u32[]{:S(2)}, u32[]{:S(2)}) collective-permute-start(bf16[1,1024,1024]{2,1,0:T(8,128)(2,1)} %refs_0_.7), channel_id=1, source_target_pairs={{0,8},{8,0},{16,24},{24,16},{1,9},{9,1},{17,25},{25,17},{2,10},{10... | collective-permute-start | bytes 6291464 | tf_op jit(solution)/shard_map/ppermute | solution.py:29
  127.1 28.3 %collective-permute-start.17 = (bf16[1,768,1024]{2,1,0:T(8,128)(2,1)}, bf16[1,768,1024]{2,1,0:T(8,128)(2,1)S(1)}, u32[]{:S(2)}, u32[]{:S(2)}) collective-permute-start(bf16[1,768,1024]{2,1,0:T(8,128)(2,1)} %collective-permute-done.15.refs_1_), channel_id=1, source_target_pairs={{0,8},{8,0},{16,24},{24,16},{1,9},{9,1},{17,25},{25,17},{2,10},{10... | collective-permute-start | bytes 4718600 | tf_op jit(solution)/shard_map/ppermute | solution.py:29
  130.3 25.1 %collective-permute-start.19 = (bf16[1,1024,512]{2,1,0:T(8,128)(2,1)S(1)}, bf16[1,1024,512]{2,1,0:T(8,128)(2,1)S(1)}, u32[]{:S(2)}, u32[]{:S(2)}) collective-permute-start(bf16[1,1024,512]{2,1,0:T(8,128)(2,1)S(1)} %get-tuple-element.43), channel_id=1, source_target_pairs={{0,16},{8,24},{16,0},{24,8},{1,17},{9,25},{17,1},{25,9},{2,18},{10... | collective-permute-start | bytes 3145736 | tf_op jit(solution)/shard_map/ppermute | solution.py:29
  131.9 6.3 %collective-permute-start.16 = (bf16[1,256,1024]{2,1,0:T(8,128)(2,1)}, bf16[1,256,1024]{2,1,0:T(8,128)(2,1)S(1)}, u32[]{:S(2)}, u32[]{:S(2)}) collective-permute-start(bf16[1,256,1024]{2,1,0:T(8,128)(2,1)} %collective-permute-done.4.refs_0_), channel_id=1, source_target_pairs={{0,8},{8,0},{16,24},{24,16},{1,9},{9,1},{17,25},{25,17},{2,10},{10... | collective-permute-start | bytes 1572872 | tf_op jit(solution)/shard_map/ppermute | solution.py:29
  155.4 6.6 %collective-permute-start.20 = (bf16[1,1024,512]{2,1,0:T(8,128)(2,1)S(1)}, bf16[1,1024,512]{2,1,0:T(8,128)(2,1)S(1)}, u32[]{:S(2)}, u32[]{:S(2)}) collective-permute-start(bf16[1,1024,512]{2,1,0:T(8,128)(2,1)S(1)} %collective-permute-done.19.refs_2_), channel_id=1, source_target_pairs={{0,8},{8,0},{16,24},{24,16},{1,9},{9,1},{17,25},{25,17},{2,10},{10... | collective-permute-start | bytes 3145736 | tf_op jit(solution)/shard_map/ppermute | solution.py:29
  155.4 25.9 %collective-permute-start.21 = (bf16[1,1024,512]{2,1,0:T(8,128)(2,1)}, bf16[1,1024,512]{2,1,0:T(8,128)(2,1)}, u32[]{:S(2)}, u32[]{:S(2)}) collective-permute-start(bf16[1,1024,512]{2,1,0:T(8,128)(2,1)} %get-tuple-element.45), channel_id=1, source_target_pairs={{0,16},{8,24},{16,0},{24,8},{1,17},{9,25},{17,1},{25,9},{2,18},{10... | collective-permute-start | bytes 3145736 | tf_op jit(solution)/shard_map/ppermute | solution.py:29
  162.0 5.1 %copy-start.1 = (bf16[2,640,1024]{2,1,0:T(8,128)(2,1)}, bf16[2,640,1024]{2,1,0:T(8,128)(2,1)S(1)}, u32[]{:S(2)}) copy-start(bf16[2,640,1024]{2,1,0:T(8,128)(2,1)S(1)} %hidden_far.1.far_ref) | copy-start | bytes 7864324
  168.0 23.1 %all-to-all-start.1 = ((bf16[8,80,512]{2,1,0:T(8,128)(2,1)}), bf16[8,80,512]{2,1,0:T(8,128)(2,1)}, u32[]{:S(2)}, u32[]{:S(2)}) async-start(bf16[8,80,512]{2,1,0:T(8,128)(2,1)} %bitcast.15), calls=%async_computation.1 | async-start | bytes 1310720 | tf_op jit(solution)/shard_map/all_to_all | solution.py:383
  181.3 2.9 %collective-permute-start.22 = (bf16[1,1024,512]{2,1,0:T(8,128)(2,1)}, bf16[1,1024,512]{2,1,0:T(8,128)(2,1)S(1)}, u32[]{:S(2)}, u32[]{:S(2)}) collective-permute-start(bf16[1,1024,512]{2,1,0:T(8,128)(2,1)} %collective-permute-done.21.refs_2_), channel_id=1, source_target_pairs={{0,8},{8,0},{16,24},{24,16},{1,9},{9,1},{17,25},{25,17},{2,10},{10... | collective-permute-start | bytes 3145736 | tf_op jit(solution)/shard_map/ppermute | solution.py:29
  (11 other events, 17.6 us)
Sparse Core Ops, SparseCore 0:
  9.5 52.4 all-gather.1

commit v3 on v2

--- a/solution.py
+++ b/solution.py
@@ -130,28 +130,16 @@
     gate_ref[...] = jnp.broadcast_to(jax.nn.sigmoid(ahead - behind), gate_ref.shape)
 
 
-def fetch(plan, refs, buf, sems):
-    copies = []
-    for at, pieces in enumerate(plan):
-        started = []
-        for p, (source, view, place) in enumerate(pieces):
-            copy = pltpu.make_async_copy(
-                refs[source].at[(0, *view)], buf.at[(at, *place)], sems.at[at, p]
-            )
-            copy.start()
-            started.append(copy)
-        copies.append(started)
-    return copies
-
-
-def hidden_kernel(plan, sources, slots_ref, *refs):
-    hidden_ref, buf, sems = refs[sources:]
-    inner = buf.shape[2]
-    copies = fetch(plan, refs[:sources], buf, sems)
+def hidden_kernel(slots_ref, weight_ref, hidden_ref, buf, sems):
+    count, _, inner = buf.shape
+    copies = [
+        pltpu.make_async_copy(weight_ref.at[at], buf.at[at], sems.at[at]) for at in range(count)
+    ]
+    for copy in copies:
+        copy.start()
     step = min(512, inner)
-    for at in range(len(plan)):
-        for copy in copies[at]:
-            copy.wait()
+    for at in range(count):
+        copies[at].wait()
         for part in range(0, inner, step):
             half = 0.5 * jnp.dot(
                 slots_ref[...], buf[at, :, part : part + step], preferred_element_type=F32
@@ -159,18 +147,22 @@
             hidden_ref[at, :, part : part + step] = (half + half * jnp.tanh(half)).astype(BF16)
 
 
-def answer_kernel(plan, sources, near_ref, far_ref, *refs):
-    answer_ref, buf, total, sems = refs[sources:]
-    copies = fetch(plan, refs[:sources], buf, sems)
-    near = near_ref.shape[0]
-    for at in range(len(plan)):
-        for copy in copies[at]:
-            copy.wait()
-        hidden = near_ref[at] if at < near else far_ref[at - near]
-        down = jnp.dot(hidden, buf[at], preferred_element_type=F32)
-        if at == 0:
+def answer_kernel(near_ref, far_ref, near_weight, far_weight, answer_ref, buf, total, sems):
+    count = near_ref.shape[0]
+    steps = [(near_ref, near_weight, at) for at in range(count)]
+    steps += [(far_ref, far_weight, at) for at in range(count)]
+    copies = [
+        pltpu.make_async_copy(weight.at[at], buf.at[k], sems.at[k])
+        for k, (_, weight, at) in enumerate(steps)
+    ]
+    for copy in copies:
+        copy.start()
+    for k, (hidden, _, at) in enumerate(steps):
+        copies[k].wait()
+        down = jnp.dot(hidden[at], buf[k], preferred_element_type=F32)
+        if k == 0:
             total[...] = down
-        elif at < len(plan) - 1:
+        elif k < len(steps) - 1:
             total[...] += down
         else:
             answer_ref[...] = (total[...] + down).astype(BF16)
@@ -211,8 +203,10 @@
     return held
 
 
-def swap_all(held):
-    return {k: swap(block, "dp", 1) for k, block in held.items() if k}
+def over_chips(block):
+    count = lax.axis_size("dp")
+    groups = [list(range(core, count, 2)) for core in range(2)]
+    return lax.all_gather(block, "dp", axis=0, tiled=True, axis_index_groups=groups)
 
 
 def after(values, earlier):
@@ -250,12 +244,9 @@
         tiled=True,
     )
 
-    in_cuts = [(0, rows // 2), (rows // 2, width - rows // 2)]
-    in_chunks = [lax.slice_in_dim(expert_in, a, a + n, axis=1) for a, n in in_cuts]
-    out_chunks = [expert_out[:, :, :rows], expert_out[:, :, rows:]]
-    in_held = [spread_over(in_chunks[0], "dp", 2)]
-    early = [*[qkv[k] for k in range(2, exp_count, 2)], in_held[0]]
-    raw[half] = after(raw[half], early)
+    early = [qkv[k] for k in range(2, exp_count, 2)]
+    raw_half = raw[half]
+    raw[half] = after(raw_half, early)
 
     groups = len(raw)
     member = jnp.arange(groups, dtype=jnp.int32) * 2
@@ -275,7 +266,12 @@
         name="norm",
     )(place, norm_gains, *[raw[2 * k] for k in range(groups)])
     far = swap(near, "dp", 1)
-    in_core = swap(after(expert_in, far), "dp", 1)
+
+    in_near = over_chips(after(expert_in, raw_half))
+    out_near = []
+    for c, earlier in enumerate((near, far)):
+        piece = lax.slice_in_dim(expert_out, c * rows, (c + 1) * rows, axis=2)
+        out_near.append(over_chips(after(piece, earlier)))
 
     contexts = pl.pallas_call(
         functools.partial(attention_kernel, dp_count, exp_count),
@@ -297,11 +293,6 @@
 
     proj_far = swap(after(proj_near, contexts), "dp", 1)
 
-    in_held.append(spread_over(after(in_chunks[1], crossed), "dp", 2))
-    in_hop = [swap_all(after(in_held[0], crossed))]
-    out_core = swap(after(expert_out, crossed), "dp", 1)
-    out_held = [spread_over(after(out_chunks[0], proj_far), "dp", 2)]
-
     cols = expert_ids[0]
     slots, mixed, gate = pl.pallas_call(
         functools.partial(mix_kernel, dp_count, exp_count, capacity),
@@ -322,63 +313,44 @@
         slots.reshape(exp_count, capacity, width), "expert", split_axis=0, concat_axis=0, tiled=True
     ).reshape(slots_count, width)
 
-    out_held.append(spread_over(after(out_chunks[1], (mixed, in_core, out_core)), "dp", 2))
-    in_hop.append(swap_all(after(in_held[1], arrived)))
-
-    whole = (slice(None), slice(None))
-    distant = range(2, dp_count)
-    places = [(pl.ds(a, n), slice(None)) for a, n in in_cuts]
-
-    def hidden_units(slots_in, plan, sources, name):
+
+    in_far = swap(after(in_near, arrived), "dp", 1)
+
+    def hidden_units(slots_in, weight, name):
         return pl.pallas_call(
-            functools.partial(hidden_kernel, plan, len(sources)),
-            out_shape=jax.ShapeDtypeStruct((len(plan), slots_count, inner), BF16),
-            in_specs=[VMEM] + [ANY] * len(sources),
+            hidden_kernel,
+            out_shape=jax.ShapeDtypeStruct((groups, slots_count, inner), BF16),
+            in_specs=[VMEM, ANY],
             out_specs=VMEM,
             scratch_shapes=[
-                pltpu.VMEM((len(plan), width, inner), BF16),
-                pltpu.SemaphoreType.DMA((len(plan), max(len(pieces) for pieces in plan))),
+                pltpu.VMEM((groups, width, inner), BF16),
+                pltpu.SemaphoreType.DMA((groups,)),
             ],
             compiler_params=params(32),
-            cost_estimate=cost(2 * slots_count * width * inner * len(plan), 8 << 20),
+            cost_estimate=cost(2 * slots_count * width * inner * groups, 8 << 20),
             name=name,
-        )(slots_in, *sources)
-
-    hidden_near = hidden_units(
-        arrived, [[(k, whole, whole)] for k in range(2)], [expert_in, in_core], "hidden_near"
-    )
-    hidden_far = hidden_units(
-        after(arrived, hidden_near),
-        [[(2 * at + p, whole, places[p]) for p in range(2)] for at in range(len(distant))],
-        [(in_hop if k & 1 else in_held)[p][k & ~1] for k in distant for p in range(2)],
-        "hidden_far",
-    )
-    out_hop = [swap_all(after(out_held[0], (hidden_near, in_hop)))]
+        )(slots_in, weight)
+
+    hidden_near = hidden_units(arrived, in_near, "hidden_near")
+    hidden_far = hidden_units(after(arrived, hidden_near), in_far, "hidden_far")
 
     returned = []
     for c in range(2):
-        if c:
-            out_hop.append(swap_all(after(out_held[c], answer)))
-        piece = (slice(None), pl.ds(c * rows, rows))
-        sources = [expert_out, out_core] + [(out_hop if k & 1 else out_held)[c][k & ~1] for k in distant]
+        out_far = swap(after(out_near[c], answer if c else hidden_near), "dp", 1)
         answer = pl.pallas_call(
-            functools.partial(
-                answer_kernel,
-                [[(k, piece if k < 2 else whole, whole)] for k in range(dp_count)],
-                len(sources),
-            ),
+            answer_kernel,
             out_shape=jax.ShapeDtypeStruct((slots_count, rows), BF16),
-            in_specs=[VMEM, VMEM] + [ANY] * len(sources),
+            in_specs=[VMEM, VMEM, ANY, ANY],
             out_specs=VMEM,
             scratch_shapes=[
                 pltpu.VMEM((dp_count, inner, rows), BF16),
                 pltpu.VMEM((slots_count, rows), F32),
-                pltpu.SemaphoreType.DMA((dp_count, 1)),
+                pltpu.SemaphoreType.DMA((dp_count,)),
             ],
             compiler_params=params(32),
             cost_estimate=cost(2 * slots_count * rows * inner * dp_count, 10 << 20),
             name="answer",
-        )(hidden_near, hidden_far, *sources)
+        )(hidden_near, hidden_far, out_near[c], out_far)
         returned.append(
             lax.all_to_all(
                 answer.reshape(exp_count, capacity, rows), "expert", split_axis=0, concat_axis=0, tiled=True

time: 229 us -> 265 us (1.16)
  waiting for transfers between devices: 109 us -> 139 us
  local copies, waits for them, and re-layouts: 18 us -> 35.3 us
  starting transfers between devices: 28.3 us -> 21.7 us
  Pallas kernels: 34 us -> 29.2 us
    all_gather x0 -> x3, waiting for transfers between devices: none -> 69.2 us  [over_chips(): lax.all_gather(block, 'dp', axis=0, tiled=True, axis_index_groups=groups)]
    ppermute x23 -> x16, waiting for transfers between devices: 109 us -> 51.7 us  [swap(): return lax.ppermute(block, axis, [(i, i ^ mask) for i in range(count)])]
    unnamed x36 -> x74, local copies, waits for them, and re-layouts: 9.73 us -> 28.8 us
    all_to_all x1, waiting for transfers between devices: 0.01 us -> 10.4 us  [body(): lax.all_to_all(slots.reshape(exp_count, capacity, width), 'expert', split...]
    all_to_all x1, waiting for transfers between devices: 0.01 us -> 7.54 us  [body(): lax.all_to_all(answer.reshape(exp_count, capacity, rows), 'expert', split...]
    ppermute x23 -> x16, starting transfers between devices: 17.2 us -> 11.2 us  [swap(): return lax.ppermute(block, axis, [(i, i ^ mask) for i in range(count)])]
    pallas_call x4, Pallas kernels: 19.3 us -> 15.2 us  [the longest x2 8.79 us: hidden_units(): pl.pallas_call(hidden_kernel, out_shape=jax.ShapeDtypeStruct((groups, slo...]
    slice x3 -> x1, local copies, waits for them, and re-layouts: 5.81 us -> 3.42 us  [body(): piece = lax.slice_in_dim(expert_out, c * rows, (c + 1) * rows, axis=2)]
  transfers between devices with their start and end apart: 26 -> 22, of which waited for: 14 -> 15; matrix products, arithmetic and copies ran while one was open for 3% -> 2% of each run, Pallas kernels for 12% -> 10%
where the time goes in v3:
time: 265 us; the launch traced here: 261 us
  waiting for transfers between devices  139 us (52%)
  local copies, waits for them, and re-layouts  35.3 us (13%)
  Pallas kernels  29.2 us (11%)
  blocking collectives  22.7 us (9%)
  starting transfers between devices  21.7 us (8%)
  between operations  13.3 us (5%)
    all_gather x3, waiting for transfers between devices, over_chips(): lax.all_gather(block, 'dp', axis=0, tiled=True, axis_index_groups=groups)  69.2 us
    ppermute x16, waiting for transfers between devices, swap(): return lax.ppermute(block, axis, [(i, i ^ mask) for i in range(count)])  51.7 us
    unnamed x74, local copies, waits for them, and re-layouts  28.8 us
    all_to_all x1, blocking collectives, body(): lax.all_to_all(answer.reshape(exp_count, capacity, rows), 'expert', split...  22.7 us
    ppermute x16, starting transfers between devices, swap(): return lax.ppermute(block, axis, [(i, i ^ mask) for i in range(count)])  11.2 us
    all_to_all x1, waiting for transfers between devices, body(): lax.all_to_all(slots.reshape(exp_count, capacity, width), 'expert', split...  10.4 us
    pallas_call x2, Pallas kernels, hidden_units(): pl.pallas_call(hidden_kernel, out_shape=jax.ShapeDtypeStruct((groups, slo...  8.79 us
    all_to_all x1, waiting for transfers between devices, body(): lax.all_to_all(answer.reshape(exp_count, capacity, rows), 'expert', split...  7.54 us
  transfers between devices with their start and end apart: 22, of which 15 were waited for; matrix products, arithmetic and copies ran while one was open for 2% of the time, Pallas kernels for 10%

profile of v3, /device:TPU:16, one launch (start us, length us, event | category | flops | bytes accessed | tf_op | source)
XLA Modules:
  0.0 261.1 jit_solution(224086131436860946)
XLA Ops:
  6.5 1.6 constant_dynamic-slice_fusion.1
  8.3 1.6 collective-permute-start
  9.9 1.6 collective-permute-start.1
  11.8 1.6 collective-permute-start.3
  14.8 3.4 %collective-permute-done.1.refs_2_ = bf16[3,128,256]{2,1,0:T(8,128)(2,1)S(1)} collective-permute-done((bf16[3,128,256]{2,1,0:T(8,128)(2,1)S(1)}, bf16[3,128,256]{2,1,0:T(8,128)(2,1)S(1)}, u32[]{:S(2)}, u32[]{:S(2)}) %collective-permute-start.1) | collective-permute-done | bytes 196640 | tf_op jit(solution)/shard_map/ppermute | solution.py:29
  18.2 10.0 %collective-permute-done.2.refs_4_ = bf16[3,128,256]{2,1,0:T(8,128)(2,1)S(1)} collective-permute-done((bf16[3,128,256]{2,1,0:T(8,128)(2,1)S(1)}, bf16[3,128,256]{2,1,0:T(8,128)(2,1)S(1)}, u32[]{:S(2)}, u32[]{:S(2)}) %collective-permute-start.2) | collective-permute-done | bytes 196640 | tf_op jit(solution)/shard_map/ppermute | solution.py:29
  28.3 6.1 %collective-permute-done.3.refs_6_ = bf16[3,128,256]{2,1,0:T(8,128)(2,1)S(1)} collective-permute-done((bf16[3,128,256]{2,1,0:T(8,128)(2,1)S(1)}, bf16[3,128,256]{2,1,0:T(8,128)(2,1)S(1)}, u32[]{:S(2)}, u32[]{:S(2)}) %collective-permute-start.3) | collective-permute-done | bytes 196640 | tf_op jit(solution)/shard_map/ppermute | solution.py:29
  43.0 7.6 %collective-permute-done.5.refs_1_ = bf16[3,128,256]{2,1,0:T(8,128)(2,1)S(1)} collective-permute-done((bf16[3,128,256]{2,1,0:T(8,128)(2,1)S(1)}, bf16[3,128,256]{2,1,0:T(8,128)(2,1)S(1)}, u32[]{:S(2)}, u32[]{:S(2)}) %collective-permute-start.5) | collective-permute-done | bytes 196640 | tf_op jit(solution)/shard_map/ppermute | solution.py:29
  50.6 5.6 %collective-permute-done.6.refs_3_ = bf16[3,128,256]{2,1,0:T(8,128)(2,1)S(1)} collective-permute-done((bf16[3,128,256]{2,1,0:T(8,128)(2,1)S(1)}, bf16[3,128,256]{2,1,0:T(8,128)(2,1)S(1)}, u32[]{:S(2)}, u32[]{:S(2)}) %collective-permute-start.6) | collective-permute-done | bytes 196640 | tf_op jit(solution)/shard_map/ppermute | solution.py:29
  56.2 4.2 %collective-permute-done.7.refs_5_ = bf16[3,128,256]{2,1,0:T(8,128)(2,1)S(1)} collective-permute-done((bf16[3,128,256]{2,1,0:T(8,128)(2,1)S(1)}, bf16[3,128,256]{2,1,0:T(8,128)(2,1)S(1)}, u32[]{:S(2)}, u32[]{:S(2)}) %collective-permute-start.7) | collective-permute-done | bytes 196640 | tf_op jit(solution)/shard_map/ppermute | solution.py:29
  60.4 4.1 %collective-permute-done.8.refs_7_ = bf16[3,128,256]{2,1,0:T(8,128)(2,1)S(1)} collective-permute-done((bf16[3,128,256]{2,1,0:T(8,128)(2,1)}, bf16[3,128,256]{2,1,0:T(8,128)(2,1)S(1)}, u32[]{:S(2)}, u32[]{:S(2)}) %collective-permute-start.8) | collective-permute-done | bytes 196640 | tf_op jit(solution)/shard_map/ppermute | solution.py:29
  65.5 6.6 %attention.1 = (bf16[256,256]{1,0:T(8,128)(2,1)S(1)}, bf16[256,256]{1,0:T(8,128)(2,1)S(1)}, bf16[256,256]{1,0:T(8,128)(2,1)S(1)}, bf16[256,256]{1,0:T(8,128)(2,1)S(1)}) custom-call(s32[1]{0:T(128)} %bitcast.2.me_ref, bf16[2,256,1024]{2,1,0:T(8,128)(2,1)S(1)} %get-tuple-element.25.near_ref, bf16[2,256,1024]{2,1,0:T(8,128)(2,1)S(1)} %collective-permute-done.4.far_ref, ...), custom_call_target="tpu_custom_call" | custom-call | flops 10485760 | bytes 20480 | tf_op jit(solution)/shard_map/attention/pallas_call | solution.py:276
  78.3 6.1 %collective-permute-done.11.refs_2_ = bf16[256,256]{1,0:T(8,128)(2,1)S(1)} collective-permute-done((bf16[256,256]{1,0:T(8,128)(2,1)}, bf16[256,256]{1,0:T(8,128)(2,1)S(1)}, u32[]{:S(2)}, u32[]{:S(2)}) %collective-permute-start.11) | collective-permute-done | bytes 131104 | tf_op jit(solution)/shard_map/ppermute | solution.py:29
  85.1 3.7 %collective-permute-done.12.refs_3_ = bf16[256,256]{1,0:T(8,128)(2,1)S(1)} collective-permute-done((bf16[256,256]{1,0:T(8,128)(2,1)}, bf16[256,256]{1,0:T(8,128)(2,1)S(1)}, u32[]{:S(2)}, u32[]{:S(2)}) %collective-permute-start.12) | collective-permute-done | bytes 131104 | tf_op jit(solution)/shard_map/ppermute | solution.py:29
  95.4 2.9 %mix.1 = (bf16[640,1024]{1,0:T(8,128)(2,1)}, bf16[256,1024]{1,0:T(8,128)(2,1)S(1)}, f32[256,128]{1,0:T(8,128)S(1)}) custom-call(s32[1]{0:T(128)} %bitcast.me_ref, bf16[256,1024]{1,0:T(8,128)(2,1)S(1)} %copy-done.13, bf16[1024,512]{1,0:T(8,128)(2,1)S(1)} %copy-done.11, bf16[1024,512]{1,0:T(8,128)(2,1)S(1)} %collective-permute-done.9.far_ref, ...), custom_call_target="tpu_custom_call" | custom-call | flops 3407872 | bytes 20480 | tf_op jit(solution)/shard_map/mix/pallas_call | solution.py:297
  99.0 4.2 %all-to-all-start = ((bf16[8,80,1024]{2,1,0:T(8,128)(2,1)}), bf16[8,80,1024]{2,1,0:T(8,128)(2,1)S(1)}, u32[]{:S(2)}, u32[]{:S(2)}) async-start(bf16[8,80,1024]{2,1,0:T(8,128)(2,1)} %bitcast.5), calls=%async_computation | async-start | bytes 2621440 | tf_op jit(solution)/shard_map/all_to_all | solution.py:312
  103.2 19.5 %all-gather.7.cloned.1.call-done.weight_ref = bf16[2,1024,1024]{2,1,0:T(8,128)(2,1)} async-done(((bf16[1,1024,1024]{2,1,0:T(8,128)(2,1)}), bf16[2,1024,1024]{2,1,0:T(8,128)(2,1)}) %all-gather.7.cloned.1.call-update) | async-done | bytes 4194320 | tf_op jit(solution)/shard_map/all_gather | solution.py:209
  122.7 10.4 %all-to-all-done = bf16[8,80,1024]{2,1,0:T(8,128)(2,1)S(1)} async-done(((bf16[8,80,1024]{2,1,0:T(8,128)(2,1)}), bf16[8,80,1024]{2,1,0:T(8,128)(2,1)S(1)}, u32[]{:S(2)}, u32[]{:S(2)}) %all-to-all-start) | async-done | bytes 1310752 | tf_op jit(solution)/shard_map/all_to_all | solution.py:312
  133.1 3.4 %fusion.6 = (bf16[1,1024,512]{2,1,0:T(8,128)(2,1)}, bf16[1,1024,512]{2,1,0:T(8,128)(2,1)}) fusion(bf16[1,1024,1024]{2,1,0:T(8,128)(2,1)} %param.17), kind=kLoop, calls=%fused_computation.18 | loop fusion | bytes 4194304 | tf_op jit(solution)/shard_map/slice | solution.py:273
  138.1 2.2 copy-done.6
  140.3 3.7 %hidden_near.1.near_ref = bf16[2,640,1024]{2,1,0:T(8,128)(2,1)S(1)} custom-call(bf16[640,1024]{1,0:T(8,128)(2,1)S(1)} %bitcast.13, bf16[2,1024,1024]{2,1,0:T(8,128)(2,1)S(1)} %copy-done.6), custom_call_target="tpu_custom_call" | custom-call | flops 10485760 | bytes 32768 | tf_op jit(solution)/shard_map/hidden_near/pallas_call | solution.py:320
  144.0 27.2 %all-gather.9.cloned.1.call-done.near_weight = bf16[2,1024,512]{2,1,0:T(8,128)(2,1)} async-done(((bf16[1,1024,512]{2,1,0:T(8,128)(2,1)}), bf16[2,1024,512]{2,1,0:T(8,128)(2,1)}) %all-gather.9.cloned.1.call-update) | async-done | bytes 2097168 | tf_op jit(solution)/shard_map/all_gather | solution.py:209
  172.5 5.1 %hidden_far.1.far_ref = bf16[2,640,1024]{2,1,0:T(8,128)(2,1)S(1)} custom-call(bf16[640,1024]{1,0:T(8,128)(2,1)S(1)} %bitcast.14, bf16[2,1024,1024]{2,1,0:T(8,128)(2,1)} %collective-permute-done.13.weight_ref), custom_call_target="tpu_custom_call" | custom-call | flops 10485760 | bytes 32768 | tf_op jit(solution)/shard_map/hidden_far/pallas_call | solution.py:320
  177.7 3.2 %answer.2 = bf16[640,512]{1,0:T(8,128)(2,1)S(1)} custom-call(bf16[2,640,1024]{2,1,0:T(8,128)(2,1)S(1)} %hidden_near.1.near_ref, bf16[2,640,1024]{2,1,0:T(8,128)(2,1)S(1)} %hidden_far.1.far_ref, bf16[2,1024,512]{2,1,0:T(8,128)(2,1)S(1)} %copy-done.9, bf16[2,1024,512]{2,1,0:T(8,128)(2,1)} %collective-permute-done.14.far_weight), custom_call_target="tpu_custom_call" | custom-call | flops 10485760 | bytes 40960 | tf_op jit(solution)/shard_map/answer/pallas_call | solution.py:340
  183.2 22.5 %all-gather.11.cloned.1.call-done.near_weight = bf16[2,1024,512]{2,1,0:T(8,128)(2,1)} async-done(((bf16[1,1024,512]{2,1,0:T(8,128)(2,1)}), bf16[2,1024,512]{2,1,0:T(8,128)(2,1)}) %all-gather.11.cloned.1.call-update) | async-done | bytes 2097168 | tf_op jit(solution)/shard_map/all_gather | solution.py:209
  205.7 6.0 %all-to-all-start.1 = ((bf16[8,80,512]{2,1,0:T(8,128)(2,1)}), bf16[8,80,512]{2,1,0:T(8,128)(2,1)}, u32[]{:S(2)}, u32[]{:S(2)}) async-start(bf16[8,80,512]{2,1,0:T(8,128)(2,1)} %bitcast.15), calls=%async_computation.1 | async-start | bytes 1310720 | tf_op jit(solution)/shard_map/all_to_all | solution.py:355
  211.7 1.7 copy-done.2
  213.5 1.6 copy-done.10
  215.1 3.2 %answer.3 = bf16[640,512]{1,0:T(8,128)(2,1)S(1)} custom-call(bf16[2,640,1024]{2,1,0:T(8,128)(2,1)S(1)} %hidden_near.1.near_ref, bf16[2,640,1024]{2,1,0:T(8,128)(2,1)S(1)} %copy-done.2, bf16[2,1024,512]{2,1,0:T(8,128)(2,1)S(1)} %copy-done.10, bf16[2,1024,512]{2,1,0:T(8,128)(2,1)} %collective-permute-done.15.far_weight), custom_call_target="tpu_custom_call" | custom-call | flops 10485760 | bytes 40960 | tf_op jit(solution)/shard_map/answer/pallas_call | solution.py:340
  219.2 7.5 %all-to-all-done.1 = bf16[8,80,512]{2,1,0:T(8,128)(2,1)} async-done(((bf16[8,80,512]{2,1,0:T(8,128)(2,1)}), bf16[8,80,512]{2,1,0:T(8,128)(2,1)}, u32[]{:S(2)}, u32[]{:S(2)}) %all-to-all-start.1) | async-done | bytes 655392 | tf_op jit(solution)/shard_map/all_to_all | solution.py:355
  226.7 22.7 %all_to_all.15 = bf16[8,80,512]{2,1,0:T(8,128)(2,1)S(1)} all-to-all(bf16[8,80,512]{2,1,0:T(8,128)(2,1)} %bitcast.16), channel_id=1, replica_groups=mesh['dp'=4,'expert'=8] {'expert'}, dimensions={0} | all-to-all | bytes 1310720 | tf_op jit(solution)/shard_map/all_to_all | solution.py:355
  251.3 3.3 %combine.1 = bf16[1,256,1024]{2,1,0:T(8,128)(2,1)} custom-call(bf16[256,1024]{1,0:T(8,128)(2,1)S(1)} %copy-done.15, f32[256,128]{1,0:T(8,128)S(1)} %copy-done.20, s32[256,2]{1,0:T(8,128)S(1)} %bitcast.20, bf16[640,512]{1,0:T(8,128)(2,1)} %bitcast.8.refs_0_, bf16[640,512]{1,0:T(8,128)(2,1)S(1)} %bitcast.17), custom_call_target="tpu_custom_call" | custom-call | flops 2621440 | bytes 12288 | tf_op jit(solution)/shard_map/combine/pallas_call | solution.py:360
  (106 shorter events, 33.5 us)
Async XLA Ops:
  6.5 3.3 %copy-start = (bf16[3,128,1024]{2,1,0:T(8,128)(2,1)S(1)}, bf16[3,128,1024]{2,1,0:T(8,128)(2,1)}, u32[]{:S(2)}) copy-start(bf16[3,128,1024]{2,1,0:T(8,128)(2,1)} %param.13) | copy-start | bytes 2359300
  6.5 68.1 %all-gather.5.cloned.1.call-start = ((), (), s32[]{:S(2)}) async-start(), calls=%async_computation.3 | async-start | bytes 1179648 | tf_op jit(solution)/shard_map/all_gather | solution.py:240
  8.2 114.5 %all-gather.7.cloned.1.call-start = ((), (), s32[]{:S(2)}) async-start(), calls=%async_computation.4 | async-start | bytes 6291456 | tf_op jit(solution)/shard_map/all_gather | solution.py:209
  8.3 26.8 %collective-permute-start = (bf16[1,256,1024]{2,1,0:T(8,128)(2,1)}, bf16[1,256,1024]{2,1,0:T(8,128)(2,1)S(1)}, u32[]{:S(2)}, u32[]{:S(2)}) collective-permute-start(bf16[1,256,1024]{2,1,0:T(8,128)(2,1)} %refs_0_.1), channel_id=1, source_target_pairs={{0,16},{8,24},{16,0},{24,8},{1,17},{9,25},{17,1},{25,9},{2,18},{10... | collective-permute-start | bytes 1572872 | tf_op jit(solution)/shard_map/ppermute | solution.py:29
  9.9 8.4 %collective-permute-start.1 = (bf16[3,128,256]{2,1,0:T(8,128)(2,1)S(1)}, bf16[3,128,256]{2,1,0:T(8,128)(2,1)S(1)}, u32[]{:S(2)}, u32[]{:S(2)}) collective-permute-start(bf16[3,128,256]{2,1,0:T(8,128)(2,1)S(1)} %constant_dynamic-slice_fusion.refs_0_), channel_id=1, source_target_pairs={{0,2},{1,3},{2,0},{3,1},{4,6},{5,7},{6,4},{7,5},{8,10},{9,11},{10,... | collective-permute-start | bytes 589832 | tf_op jit(solution)/shard_map/ppermute | solution.py:29
  11.5 16.8 %collective-permute-start.2 = (bf16[3,128,256]{2,1,0:T(8,128)(2,1)S(1)}, bf16[3,128,256]{2,1,0:T(8,128)(2,1)S(1)}, u32[]{:S(2)}, u32[]{:S(2)}) collective-permute-start(bf16[3,128,256]{2,1,0:T(8,128)(2,1)S(1)} %constant_dynamic-slice_fusion.refs_0_), channel_id=1, source_target_pairs={{0,4},{1,5},{2,6},{3,7},{4,0},{5,1},{6,2},{7,3},{8,12},{9,13},{10,... | collective-permute-start | bytes 589832 | tf_op jit(solution)/shard_map/ppermute | solution.py:29
  11.8 22.5 %collective-permute-start.3 = (bf16[3,128,256]{2,1,0:T(8,128)(2,1)S(1)}, bf16[3,128,256]{2,1,0:T(8,128)(2,1)S(1)}, u32[]{:S(2)}, u32[]{:S(2)}) collective-permute-start(bf16[3,128,256]{2,1,0:T(8,128)(2,1)S(1)} %constant_dynamic-slice_fusion.refs_0_), channel_id=1, source_target_pairs={{0,6},{1,7},{2,4},{3,5},{4,2},{5,3},{6,0},{7,1},{8,14},{9,15},{10,... | collective-permute-start | bytes 589832 | tf_op jit(solution)/shard_map/ppermute | solution.py:29
  38.9 25.7 %collective-permute-start.4 = (bf16[2,256,1024]{2,1,0:T(8,128)(2,1)S(1)}, bf16[2,256,1024]{2,1,0:T(8,128)(2,1)S(1)}, u32[]{:S(2)}, u32[]{:S(2)}) collective-permute-start(bf16[2,256,1024]{2,1,0:T(8,128)(2,1)S(1)} %get-tuple-element.25.near_ref), channel_id=1, source_target_pairs={{0,8},{8,0},{16,24},{24,16},{1,9},{9,1},{17,25},{25,17},{2,10},{10... | collective-permute-start | bytes 3145736 | tf_op jit(solution)/shard_map/ppermute | solution.py:29
  38.9 37.6 %copy-start.34 = (f32[1024,8]{0,1:T(8,128)S(1)}, f32[1024,8]{0,1:T(8,128)}, u32[]{:S(2)}) copy-start(f32[1024,8]{0,1:T(8,128)} %param.15) | copy-start | bytes 98308
  38.9 11.7 %collective-permute-start.5 = (bf16[3,128,256]{2,1,0:T(8,128)(2,1)S(1)}, bf16[3,128,256]{2,1,0:T(8,128)(2,1)S(1)}, u32[]{:S(2)}, u32[]{:S(2)}) collective-permute-start(bf16[3,128,256]{2,1,0:T(8,128)(2,1)S(1)} %constant_dynamic-slice_fusion.refs_0_), channel_id=1, source_target_pairs={{0,1},{1,0},{2,3},{3,2},{4,5},{5,4},{6,7},{7,6},{8,9},{9,8},{10,11... | collective-permute-start | bytes 589832 | tf_op jit(solution)/shard_map/ppermute | solution.py:29
  40.5 15.7 %collective-permute-start.6 = (bf16[3,128,256]{2,1,0:T(8,128)(2,1)S(1)}, bf16[3,128,256]{2,1,0:T(8,128)(2,1)S(1)}, u32[]{:S(2)}, u32[]{:S(2)}) collective-permute-start(bf16[3,128,256]{2,1,0:T(8,128)(2,1)S(1)} %collective-permute-done.1.refs_2_), channel_id=1, source_target_pairs={{0,1},{1,0},{2,3},{3,2},{4,5},{5,4},{6,7},{7,6},{8,9},{9,8},{10,11... | collective-permute-start | bytes 589832 | tf_op jit(solution)/shard_map/ppermute | solution.py:29
  41.0 19.4 %collective-permute-start.7 = (bf16[3,128,256]{2,1,0:T(8,128)(2,1)S(1)}, bf16[3,128,256]{2,1,0:T(8,128)(2,1)S(1)}, u32[]{:S(2)}, u32[]{:S(2)}) collective-permute-start(bf16[3,128,256]{2,1,0:T(8,128)(2,1)S(1)} %collective-permute-done.2.refs_4_), channel_id=1, source_target_pairs={{0,1},{1,0},{2,3},{3,2},{4,5},{5,4},{6,7},{7,6},{8,9},{9,8},{10,11... | collective-permute-start | bytes 589832 | tf_op jit(solution)/shard_map/ppermute | solution.py:29
  42.5 22.1 %collective-permute-start.8 = (bf16[3,128,256]{2,1,0:T(8,128)(2,1)}, bf16[3,128,256]{2,1,0:T(8,128)(2,1)S(1)}, u32[]{:S(2)}, u32[]{:S(2)}) collective-permute-start(bf16[3,128,256]{2,1,0:T(8,128)(2,1)} %copy-done.17), channel_id=1, source_target_pairs={{0,1},{1,0},{2,3},{3,2},{4,5},{5,4},{6,7},{7,6},{8,9},{9,8},{10,11... | collective-permute-start | bytes 589832 | tf_op jit(solution)/shard_map/ppermute | solution.py:29
  65.5 11.3 %copy-start.35 = (s32[1,256,2]{1,2,0:T(2,128)S(1)}, s32[1,256,2]{1,2,0:T(2,128)}, u32[]{:S(2)}) copy-start(s32[1,256,2]{1,2,0:T(2,128)} %param.11) | copy-start | bytes 6148
  65.5 24.0 %copy-start.30 = (f32[2,1024]{1,0:T(2,128)S(1)}, f32[2,1024]{1,0:T(2,128)}, u32[]{:S(2)}) copy-start(f32[2,1024]{1,0:T(2,128)} %gain_ref.3) | copy-start | bytes 24580
  74.6 14.9 %collective-permute-start.9 = (bf16[1024,512]{1,0:T(8,128)(2,1)}, bf16[1024,512]{1,0:T(8,128)(2,1)S(1)}, u32[]{:S(2)}, u32[]{:S(2)}) collective-permute-start(bf16[1024,512]{1,0:T(8,128)(2,1)} %all-gather.5.cloned.1.call-done.near_ref), channel_id=1, source_target_pairs={{0,8},{8,0},{16,24},{24,16},{1,9},{9,1},{17,25},{25,17},{2,10},{10... | collective-permute-start | bytes 3145736 | tf_op jit(solution)/shard_map/ppermute | solution.py:29
  74.7 3.0 %collective-permute-start.10 = (bf16[256,256]{1,0:T(8,128)(2,1)}, bf16[256,256]{1,0:T(8,128)(2,1)S(1)}, u32[]{:S(2)}, u32[]{:S(2)}) collective-permute-start(bf16[256,256]{1,0:T(8,128)(2,1)} %copy-done.33), channel_id=1, source_target_pairs={{0,8},{8,0},{16,24},{24,16},{1,9},{9,1},{17,25},{25,17},{2,10},{10... | collective-permute-start | bytes 393224 | tf_op jit(solution)/shard_map/ppermute | solution.py:29
  75.1 9.3 %collective-permute-start.11 = (bf16[256,256]{1,0:T(8,128)(2,1)}, bf16[256,256]{1,0:T(8,128)(2,1)S(1)}, u32[]{:S(2)}, u32[]{:S(2)}) collective-permute-start(bf16[256,256]{1,0:T(8,128)(2,1)} %copy-done.32), channel_id=1, source_target_pairs={{0,16},{8,24},{16,0},{24,8},{1,17},{9,25},{17,1},{25,9},{2,18},{10... | collective-permute-start | bytes 393224 | tf_op jit(solution)/shard_map/ppermute | solution.py:29
  75.6 13.2 %collective-permute-start.12 = (bf16[256,256]{1,0:T(8,128)(2,1)}, bf16[256,256]{1,0:T(8,128)(2,1)S(1)}, u32[]{:S(2)}, u32[]{:S(2)}) collective-permute-start(bf16[256,256]{1,0:T(8,128)(2,1)} %copy-done.31), channel_id=1, source_target_pairs={{0,24},{8,16},{16,8},{24,0},{1,25},{9,17},{17,9},{25,1},{2,26},{10... | collective-permute-start | bytes 393224 | tf_op jit(solution)/shard_map/ppermute | solution.py:29
  99.0 37.5 %copy-start.14 = (bf16[256,1024]{1,0:T(8,128)(2,1)}, bf16[256,1024]{1,0:T(8,128)(2,1)S(1)}, u32[]{:S(2)}) copy-start(bf16[256,1024]{1,0:T(8,128)(2,1)S(1)} %get-tuple-element.31.mixed_ref) | copy-start | bytes 1572868
  99.0 34.0 %all-to-all-start = ((bf16[8,80,1024]{2,1,0:T(8,128)(2,1)}), bf16[8,80,1024]{2,1,0:T(8,128)(2,1)S(1)}, u32[]{:S(2)}, u32[]{:S(2)}) async-start(bf16[8,80,1024]{2,1,0:T(8,128)(2,1)} %bitcast.5), calls=%async_computation | async-start | bytes 2621440 | tf_op jit(solution)/shard_map/all_to_all | solution.py:312
  103.2 67.9 %all-gather.9.cloned.1.call-start = ((), (), s32[]{:S(2)}) async-start(), calls=%async_computation.5 | async-start | bytes 3145728 | tf_op jit(solution)/shard_map/all_gather | solution.py:209
  133.0 3.5 %copy-start.3 = (bf16[8,80,1024]{2,1,0:T(8,128)(2,1)}, bf16[8,80,1024]{2,1,0:T(8,128)(2,1)S(1)}, u32[]{:S(2)}) copy-start(bf16[8,80,1024]{2,1,0:T(8,128)(2,1)S(1)} %all-to-all-done) | copy-start | bytes 3932164
  133.1 38.1 %collective-permute-start.13 = (bf16[2,1024,1024]{2,1,0:T(8,128)(2,1)}, bf16[2,1024,1024]{2,1,0:T(8,128)(2,1)}, u32[]{:S(2)}, u32[]{:S(2)}) collective-permute-start(bf16[2,1024,1024]{2,1,0:T(8,128)(2,1)} %all-gather.7.cloned.1.call-done.weight_ref), channel_id=1, source_target_pairs={{0,8},{8,0},{16,24},{24,16},{1,9},{9,1},{17,25},{25,17},{2,10},{10... | collective-permute-start | bytes 12582920 | tf_op jit(solution)/shard_map/ppermute | solution.py:29
  136.6 69.2 %all-gather.11.cloned.1.call-start = ((), (), s32[]{:S(2)}) async-start(), calls=%async_computation.6 | async-start | bytes 3145728 | tf_op jit(solution)/shard_map/all_gather | solution.py:209
  138.1 2.2 copy-start.6
  171.2 6.5 %collective-permute-start.14 = (bf16[2,1024,512]{2,1,0:T(8,128)(2,1)}, bf16[2,1024,512]{2,1,0:T(8,128)(2,1)}, u32[]{:S(2)}, u32[]{:S(2)}) collective-permute-start(bf16[2,1024,512]{2,1,0:T(8,128)(2,1)} %all-gather.9.cloned.1.call-done.near_weight), channel_id=1, source_target_pairs={{0,8},{8,0},{16,24},{24,16},{1,9},{9,1},{17,25},{25,17},{2,10},{10... | collective-permute-start | bytes 6291464 | tf_op jit(solution)/shard_map/ppermute | solution.py:29
  172.5 5.1 %copy-start.9 = (bf16[2,1024,512]{2,1,0:T(8,128)(2,1)S(1)}, bf16[2,1024,512]{2,1,0:T(8,128)(2,1)}, u32[]{:S(2)}) copy-start(bf16[2,1024,512]{2,1,0:T(8,128)(2,1)} %all-gather.9.cloned.1.call-done.near_weight) | copy-start | bytes 6291460
  205.7 6.0 %collective-permute-start.15 = (bf16[2,1024,512]{2,1,0:T(8,128)(2,1)}, bf16[2,1024,512]{2,1,0:T(8,128)(2,1)}, u32[]{:S(2)}, u32[]{:S(2)}) collective-permute-start(bf16[2,1024,512]{2,1,0:T(8,128)(2,1)} %all-gather.11.cloned.1.call-done.near_weight), channel_id=1, source_target_pairs={{0,8},{8,0},{16,24},{24,16},{1,9},{9,1},{17,25},{25,17},{2,10},{10... | collective-permute-start | bytes 6291464 | tf_op jit(solution)/shard_map/ppermute | solution.py:29
  205.7 21.0 %all-to-all-start.1 = ((bf16[8,80,512]{2,1,0:T(8,128)(2,1)}), bf16[8,80,512]{2,1,0:T(8,128)(2,1)}, u32[]{:S(2)}, u32[]{:S(2)}) async-start(bf16[8,80,512]{2,1,0:T(8,128)(2,1)} %bitcast.15), calls=%async_computation.1 | async-start | bytes 1310720 | tf_op jit(solution)/shard_map/all_to_all | solution.py:355
  211.7 1.7 copy-start.2
  213.5 1.6 copy-start.10
  (26 other events, 23.0 us)
Sparse Core Ops, SparseCore 0:
  9.5 50.1 all-gather.4
  61.2 61.4 all-gather.6
  136.7 34.4 all-gather.8
  172.6 33.1 all-gather.10

commit v4 on v3

--- a/solution.py
+++ b/solution.py
@@ -14,6 +14,7 @@
 VMEM = pl.BlockSpec(memory_space=pltpu.VMEM)
 SMEM = pl.BlockSpec(memory_space=pltpu.SMEM)
 ANY = pl.BlockSpec(memory_space=pl.ANY)
+HBM = pl.BlockSpec(memory_space=pltpu.HBM)
 
 
 def params(mib):
@@ -130,16 +131,20 @@
     gate_ref[...] = jnp.broadcast_to(jax.nn.sigmoid(ahead - behind), gate_ref.shape)
 
 
-def hidden_kernel(slots_ref, weight_ref, hidden_ref, buf, sems):
+def hidden_kernel(cuts, slots_ref, *refs):
+    hidden_ref, buf, sems = refs[len(cuts) :]
     count, _, inner = buf.shape
-    copies = [
-        pltpu.make_async_copy(weight_ref.at[at], buf.at[at], sems.at[at]) for at in range(count)
-    ]
-    for copy in copies:
+    copies = [[] for _ in range(count)]
+    for k, (at, start, size) in enumerate(cuts):
+        copy = pltpu.make_async_copy(
+            refs[k].at[0], buf.at[at, pl.ds(start, size), :], sems.at[k]
+        )
         copy.start()
+        copies[at].append(copy)
     step = min(512, inner)
     for at in range(count):
-        copies[at].wait()
+        for copy in copies[at]:
+            copy.wait()
         for part in range(0, inner, step):
             half = 0.5 * jnp.dot(
                 slots_ref[...], buf[at, :, part : part + step], preferred_element_type=F32
@@ -147,22 +152,23 @@
             hidden_ref[at, :, part : part + step] = (half + half * jnp.tanh(half)).astype(BF16)
 
 
-def answer_kernel(near_ref, far_ref, near_weight, far_weight, answer_ref, buf, total, sems):
-    count = near_ref.shape[0]
-    steps = [(near_ref, near_weight, at) for at in range(count)]
-    steps += [(far_ref, far_weight, at) for at in range(count)]
+def answer_kernel(count, start, near_ref, far_ref, *refs):
+    weights, (answer_ref, buf, total, sems) = refs[:count], refs[count:]
+    near = near_ref.shape[0]
+    cols = buf.shape[2]
     copies = [
-        pltpu.make_async_copy(weight.at[at], buf.at[k], sems.at[k])
-        for k, (_, weight, at) in enumerate(steps)
+        pltpu.make_async_copy(weights[at].at[0, :, pl.ds(start, cols)], buf.at[at], sems.at[at])
+        for at in range(count)
     ]
     for copy in copies:
         copy.start()
-    for k, (hidden, _, at) in enumerate(steps):
-        copies[k].wait()
-        down = jnp.dot(hidden[at], buf[k], preferred_element_type=F32)
-        if k == 0:
+    for at in range(count):
+        copies[at].wait()
+        hidden = near_ref[at] if at < near else far_ref[at - near]
+        down = jnp.dot(hidden, buf[at], preferred_element_type=F32)
+        if at == 0:
             total[...] = down
-        elif k < len(steps) - 1:
+        elif at < count - 1:
             total[...] += down
         else:
             answer_ref[...] = (total[...] + down).astype(BF16)
@@ -203,10 +209,8 @@
     return held
 
 
-def over_chips(block):
-    count = lax.axis_size("dp")
-    groups = [list(range(core, count, 2)) for core in range(2)]
-    return lax.all_gather(block, "dp", axis=0, tiled=True, axis_index_groups=groups)
+def other_core(held):
+    return {k: swap(block, "dp", 1) for k, block in held.items()}
 
 
 def after(values, earlier):
@@ -244,9 +248,12 @@
         tiled=True,
     )
 
-    early = [qkv[k] for k in range(2, exp_count, 2)]
-    raw_half = raw[half]
-    raw[half] = after(raw_half, early)
+    in_cuts = [(0, rows // 2), (rows // 2, width - rows // 2)]
+    in_chunks = [lax.slice_in_dim(expert_in, a, a + n, axis=1) for a, n in in_cuts]
+    in_held = [spread_over(in_chunks[0], "dp", 2)]
+
+    early = [qkv[1], *[qkv[k] for k in range(2, exp_count, 2)], qkv[3], in_held[0]]
+    raw[half] = after(raw[half], early)
 
     groups = len(raw)
     member = jnp.arange(groups, dtype=jnp.int32) * 2
@@ -266,12 +273,7 @@
         name="norm",
     )(place, norm_gains, *[raw[2 * k] for k in range(groups)])
     far = swap(near, "dp", 1)
-
-    in_near = over_chips(after(expert_in, raw_half))
-    out_near = []
-    for c, earlier in enumerate((near, far)):
-        piece = lax.slice_in_dim(expert_out, c * rows, (c + 1) * rows, axis=2)
-        out_near.append(over_chips(after(piece, earlier)))
+    in_held.append(spread_over(after(in_chunks[1], near), "dp", 2))
 
     contexts = pl.pallas_call(
         functools.partial(attention_kernel, dp_count, exp_count),
@@ -293,6 +295,17 @@
 
     proj_far = swap(after(proj_near, contexts), "dp", 1)
 
+    in_far = [swap(after(expert_in, crossed), "dp", 1)]
+    in_near = [expert_in]
+    places = [(0, 0, width)]
+    for k in range(2, dp_count, 2):
+        for held, cut in zip(in_held, in_cuts):
+            in_near.append(held[k])
+            in_far.append(swap(after(held[k], crossed), "dp", 1))
+            places.append((k // 2, *cut))
+    out_near = spread_over(after(expert_out, crossed), "dp", 2)
+    out_far = {0: swap(after(expert_out, in_far), "dp", 1)}
+
     cols = expert_ids[0]
     slots, mixed, gate = pl.pallas_call(
         functools.partial(mix_kernel, dp_count, exp_count, capacity),
@@ -314,33 +327,33 @@
     ).reshape(slots_count, width)
 
 
-    in_far = swap(after(in_near, arrived), "dp", 1)
-
-    def hidden_units(slots_in, weight, name):
+    def hidden_units(slots_in, held, name):
         return pl.pallas_call(
-            hidden_kernel,
+            functools.partial(hidden_kernel, places),
             out_shape=jax.ShapeDtypeStruct((groups, slots_count, inner), BF16),
-            in_specs=[VMEM, ANY],
+            in_specs=[VMEM] + [HBM] * len(places),
             out_specs=VMEM,
             scratch_shapes=[
                 pltpu.VMEM((groups, width, inner), BF16),
-                pltpu.SemaphoreType.DMA((groups,)),
+                pltpu.SemaphoreType.DMA((len(places),)),
             ],
             compiler_params=params(32),
             cost_estimate=cost(2 * slots_count * width * inner * groups, 8 << 20),
             name=name,
-        )(slots_in, weight)
+        )(slots_in, *held)
 
     hidden_near = hidden_units(arrived, in_near, "hidden_near")
     hidden_far = hidden_units(after(arrived, hidden_near), in_far, "hidden_far")
+    distant = {k: block for k, block in out_near.items() if k}
+    out_far.update(other_core(after(distant, hidden_near)))
+    weights = [held[k] for held in (out_near, out_far) for k in sorted(held)]
 
     returned = []
     for c in range(2):
-        out_far = swap(after(out_near[c], answer if c else hidden_near), "dp", 1)
         answer = pl.pallas_call(
-            answer_kernel,
+            functools.partial(answer_kernel, dp_count, c * rows),
             out_shape=jax.ShapeDtypeStruct((slots_count, rows), BF16),
-            in_specs=[VMEM, VMEM, ANY, ANY],
+            in_specs=[VMEM, VMEM] + [HBM] * dp_count,
             out_specs=VMEM,
             scratch_shapes=[
                 pltpu.VMEM((dp_count, inner, rows), BF16),
@@ -350,7 +363,7 @@
             compiler_params=params(32),
             cost_estimate=cost(2 * slots_count * rows * inner * dp_count, 10 << 20),
             name="answer",
-        )(hidden_near, hidden_far, out_near[c], out_far)
+        )(after(hidden_near, answer) if c else hidden_near, hidden_far, *weights)
         returned.append(
             lax.all_to_all(
                 answer.reshape(exp_count, capacity, rows), "expert", split_axis=0, concat_axis=0, tiled=True

time: 265 us -> 235 us (0.89)
  waiting for transfers between devices: 139 us -> 109 us
  blocking collectives: 22.7 us -> 42.4 us
  local copies, waits for them, and re-layouts: 35.3 us -> 15.9 us
    all_gather x3 -> x0, waiting for transfers between devices: 69.2 us -> none  [over_chips(): lax.all_gather(block, 'dp', axis=0, tiled=True, axis_index_groups=groups)]
    ppermute x16 -> x21, waiting for transfers between devices: 51.7 us -> 90.5 us  [swap(): return lax.ppermute(block, axis, [(i, i ^ mask) for i in range(count)])]
    all_to_all x1 -> x2, blocking collectives: 22.7 us -> 42.4 us  [body(): lax.all_to_all(answer.reshape(exp_count, capacity, rows), 'expert', split...]
    unnamed x74 -> x48, local copies, waits for them, and re-layouts: 28.8 us -> 11.2 us
    all_to_all x1, waiting for transfers between devices: 10.4 us -> 18.5 us  [body(): lax.all_to_all(slots.reshape(exp_count, capacity, width), 'expert', split...]
    all_to_all x1 -> x0, waiting for transfers between devices: 7.54 us -> none  [body(): lax.all_to_all(answer.reshape(exp_count, capacity, rows), 'expert', split...]
    all_to_all x1 -> x0, starting transfers between devices: 6.02 us -> none  [body(): lax.all_to_all(answer.reshape(exp_count, capacity, rows), 'expert', split...]
    ppermute x16 -> x21, starting transfers between devices: 11.2 us -> 15.7 us  [swap(): return lax.ppermute(block, axis, [(i, i ^ mask) for i in range(count)])]
  transfers between devices with their start and end apart: 22 -> 23, of which waited for: 15 -> 13; matrix products, arithmetic and copies ran while one was open for 2% -> 2% of each run, Pallas kernels for 10% -> 9%
where the time goes in v4:
time: 235 us; the launch traced here: 231 us
  waiting for transfers between devices  109 us (46%)
  blocking collectives  42.4 us (18%)
  Pallas kernels  29.4 us (13%)
  starting transfers between devices  21 us (9%)
  local copies, waits for them, and re-layouts  15.9 us (7%)
  between operations  13.6 us (6%)
    ppermute x21, waiting for transfers between devices, swap(): return lax.ppermute(block, axis, [(i, i ^ mask) for i in range(count)])  90.5 us
    all_to_all x2, blocking collectives, body(): lax.all_to_all(answer.reshape(exp_count, capacity, rows), 'expert', split...  42.4 us
    all_to_all x1, waiting for transfers between devices, body(): lax.all_to_all(slots.reshape(exp_count, capacity, width), 'expert', split...  18.5 us
    ppermute x21, starting transfers between devices, swap(): return lax.ppermute(block, axis, [(i, i ^ mask) for i in range(count)])  15.7 us
    unnamed x48, local copies, waits for them, and re-layouts  11.2 us
    pallas_call x2, Pallas kernels, body(): pl.pallas_call(functools.partial(answer_kernel, dp_count, c * rows), out_...  7.39 us
    pallas_call x2, Pallas kernels, hidden_units(): pl.pallas_call(functools.partial(hidden_kernel, places), out_shape=jax.Sh...  7.26 us
    pallas_call x1, Pallas kernels, body(): pl.pallas_call(functools.partial(attention_kernel, dp_count, exp_count),...  7.15 us
  transfers between devices with their start and end apart: 23, of which 13 were waited for; matrix products, arithmetic and copies ran while one was open for 2% of the time, Pallas kernels for 9%

profile of v4, /device:TPU:16, one launch (start us, length us, event | category | flops | bytes accessed | tf_op | source)
XLA Modules:
  0.0 231.4 jit_solution(11546375121309979426)
XLA Ops:
  6.6 1.7 constant_dynamic-slice_fusion.1
  9.4 1.6 collective-permute-start.6
  13.2 2.3 collective-permute-start.3
  16.2 12.0 %collective-permute-done.4.refs_6_ = bf16[3,128,256]{2,1,0:T(8,128)(2,1)S(1)} collective-permute-done((bf16[3,128,256]{2,1,0:T(8,128)(2,1)S(1)}, bf16[3,128,256]{2,1,0:T(8,128)(2,1)S(1)}, u32[]{:S(2)}, u32[]{:S(2)}) %collective-permute-start.4) | collective-permute-done | bytes 196640 | tf_op jit(solution)/shard_map/ppermute | solution.py:30
  28.2 1.7 collective-permute-start.1
  30.2 2.2 collective-permute-done.3.refs_4_
  32.5 1.4 collective-permute-done.1.refs_1_
  33.9 2.1 collective-permute-done.5.refs_3_
  36.8 1.3 norm.1
  38.9 1.7 collective-permute-start.9
  41.0 9.5 %collective-permute-done.9.refs_7_ = bf16[3,128,256]{2,1,0:T(8,128)(2,1)S(1)} collective-permute-done((bf16[3,128,256]{2,1,0:T(8,128)(2,1)S(1)}, bf16[3,128,256]{2,1,0:T(8,128)(2,1)S(1)}, u32[]{:S(2)}, u32[]{:S(2)}) %collective-permute-start.9) | collective-permute-done | bytes 196640 | tf_op jit(solution)/shard_map/ppermute | solution.py:30
  50.5 5.0 %collective-permute-done.8.refs_5_ = bf16[3,128,256]{2,1,0:T(8,128)(2,1)S(1)} collective-permute-done((bf16[3,128,256]{2,1,0:T(8,128)(2,1)}, bf16[3,128,256]{2,1,0:T(8,128)(2,1)S(1)}, u32[]{:S(2)}, u32[]{:S(2)}) %collective-permute-start.8) | collective-permute-done | bytes 196640 | tf_op jit(solution)/shard_map/ppermute | solution.py:30
  55.5 7.2 %attention.1 = (bf16[256,256]{1,0:T(8,128)(2,1)S(1)}, bf16[256,256]{1,0:T(8,128)(2,1)}, bf16[256,256]{1,0:T(8,128)(2,1)}, bf16[256,256]{1,0:T(8,128)(2,1)S(1)}) custom-call(s32[1]{0:T(128)} %bitcast.2.me_ref, bf16[2,256,1024]{2,1,0:T(8,128)(2,1)S(1)} %get-tuple-element.27.near_ref, bf16[2,256,1024]{2,1,0:T(8,128)(2,1)S(1)} %collective-permute-done.7.far_ref, ...), custom_call_target="tpu_custom_call" | custom-call | flops 10485760 | bytes 20480 | tf_op jit(solution)/shard_map/attention/pallas_call | solution.py:278
  65.3 1.5 collective-permute-start.14
  69.9 35.7 %collective-permute-done.12.refs_2_ = bf16[256,256]{1,0:T(8,128)(2,1)S(1)} collective-permute-done((bf16[256,256]{1,0:T(8,128)(2,1)}, bf16[256,256]{1,0:T(8,128)(2,1)S(1)}, u32[]{:S(2)}, u32[]{:S(2)}) %collective-permute-start.12) | collective-permute-done | bytes 131104 | tf_op jit(solution)/shard_map/ppermute | solution.py:30
  105.5 1.9 collective-permute-done.13.refs_3_
  109.6 4.1 %mix.1 = (bf16[640,1024]{1,0:T(8,128)(2,1)}, bf16[256,1024]{1,0:T(8,128)(2,1)S(1)}, f32[256,128]{1,0:T(8,128)S(1)}) custom-call(s32[1]{0:T(128)} %bitcast.me_ref, bf16[256,1024]{1,0:T(8,128)(2,1)S(1)} %copy-done.12, bf16[1024,512]{1,0:T(8,128)(2,1)S(1)} %copy-done.8, bf16[1024,512]{1,0:T(8,128)(2,1)} %collective-permute-done.10.far_ref, ...), custom_call_target="tpu_custom_call" | custom-call | flops 3407872 | bytes 20480 | tf_op jit(solution)/shard_map/mix/pallas_call | solution.py:310
  114.5 5.3 %all-to-all-start = ((bf16[8,80,1024]{2,1,0:T(8,128)(2,1)}), bf16[8,80,1024]{2,1,0:T(8,128)(2,1)S(1)}, u32[]{:S(2)}, u32[]{:S(2)}) async-start(bf16[8,80,1024]{2,1,0:T(8,128)(2,1)} %bitcast.5), calls=%async_computation | async-start | bytes 2621440 | tf_op jit(solution)/shard_map/all_to_all | solution.py:325
  119.8 1.5 collective-permute-start.18
  121.8 3.7 %collective-permute-done.16.refs_1_ = bf16[1,256,1024]{2,1,0:T(8,128)(2,1)S(1)} collective-permute-done((bf16[1,256,1024]{2,1,0:T(8,128)(2,1)S(1)}, bf16[1,256,1024]{2,1,0:T(8,128)(2,1)S(1)}, u32[]{:S(2)}, u32[]{:S(2)}) %collective-permute-start.16) | collective-permute-done | bytes 524320 | tf_op jit(solution)/shard_map/ppermute | solution.py:30
  125.4 1.7 collective-permute-done.17.refs_2_
  128.4 1.4 copy-done.4
  129.9 18.5 %all-to-all-done = bf16[8,80,1024]{2,1,0:T(8,128)(2,1)S(1)} async-done(((bf16[8,80,1024]{2,1,0:T(8,128)(2,1)}), bf16[8,80,1024]{2,1,0:T(8,128)(2,1)S(1)}, u32[]{:S(2)}, u32[]{:S(2)}) %all-to-all-start) | async-done | bytes 1310752 | tf_op jit(solution)/shard_map/all_to_all | solution.py:325
  148.3 1.6 copy-done.3
  149.9 3.6 %hidden_near.1.near_ref = bf16[2,640,1024]{2,1,0:T(8,128)(2,1)S(1)} custom-call(bf16[640,1024]{1,0:T(8,128)(2,1)S(1)} %bitcast.13, bf16[1,1024,1024]{2,1,0:T(8,128)(2,1)S(1)} %copy-done.3, bf16[1,256,1024]{2,1,0:T(8,128)(2,1)S(1)} %copy-done.10, bf16[1,768,1024]{2,1,0:T(8,128)(2,1)} %collective-permute-done.14.refs_2_), custom_call_target="tpu_custom_call" | custom-call | flops 10485760 | bytes 32768 | tf_op jit(solution)/shard_map/hidden_near/pallas_call | solution.py:331
  153.5 14.6 %collective-permute-done.18.refs_1_ = bf16[1,1024,1024]{2,1,0:T(8,128)(2,1)} collective-permute-done((bf16[1,1024,1024]{2,1,0:T(8,128)(2,1)}, bf16[1,1024,1024]{2,1,0:T(8,128)(2,1)}, u32[]{:S(2)}, u32[]{:S(2)}) %collective-permute-start.18) | collective-permute-done | bytes 2097184 | tf_op jit(solution)/shard_map/ppermute | solution.py:30
  168.1 3.7 %hidden_far.1.far_ref = bf16[2,640,1024]{2,1,0:T(8,128)(2,1)S(1)} custom-call(bf16[640,1024]{1,0:T(8,128)(2,1)S(1)} %bitcast.14, bf16[1,1024,1024]{2,1,0:T(8,128)(2,1)S(1)} %copy-done.5, bf16[1,256,1024]{2,1,0:T(8,128)(2,1)S(1)} %collective-permute-done.16.refs_1_, bf16[1,768,1024]{2,1,0:T(8,128)(2,1)S(1)} %copy-done.7), custom_call_target="tpu_custom_call" | custom-call | flops 10485760 | bytes 32768 | tf_op jit(solution)/shard_map/hidden_far/pallas_call | solution.py:331
  172.5 3.7 %answer.2 = bf16[640,512]{1,0:T(8,128)(2,1)S(1)} custom-call(bf16[2,640,1024]{2,1,0:T(8,128)(2,1)S(1)} %hidden_near.1.near_ref, bf16[2,640,1024]{2,1,0:T(8,128)(2,1)S(1)} %hidden_far.1.far_ref, bf16[1,1024,1024]{2,1,0:T(8,128)(2,1)S(1)} %copy-done.1, bf16[1,1024,1024]{2,1,0:T(8,128)(2,1)} %collective-permute-done.18.refs_1_, ...), custom_call_target="tpu_custom_call" | custom-call | flops 10485760 | bytes 40960 | tf_op jit(solution)/shard_map/answer/pallas_call | solution.py:353
  176.2 3.7 %answer.3 = bf16[640,512]{1,0:T(8,128)(2,1)S(1)} custom-call(bf16[2,640,1024]{2,1,0:T(8,128)(2,1)S(1)} %hidden_near.1.near_ref, bf16[2,640,1024]{2,1,0:T(8,128)(2,1)S(1)} %hidden_far.1.far_ref, bf16[1,1024,1024]{2,1,0:T(8,128)(2,1)S(1)} %copy-done.1, bf16[1,1024,1024]{2,1,0:T(8,128)(2,1)} %collective-permute-done.18.refs_1_, ...), custom_call_target="tpu_custom_call" | custom-call | flops 10485760 | bytes 40960 | tf_op jit(solution)/shard_map/answer/pallas_call | solution.py:353
  179.9 21.9 %all_to_all.15 = bf16[8,80,512]{2,1,0:T(8,128)(2,1)S(1)} all-to-all(bf16[8,80,512]{2,1,0:T(8,128)(2,1)S(1)} %bitcast.16), channel_id=1, replica_groups=mesh['dp'=4,'expert'=8] {'expert'}, dimensions={0} | all-to-all | bytes 1310720 | tf_op jit(solution)/shard_map/all_to_all | solution.py:368
  201.8 20.5 %all_to_all.16 = bf16[8,80,512]{2,1,0:T(8,128)(2,1)S(1)} all-to-all(bf16[8,80,512]{2,1,0:T(8,128)(2,1)S(1)} %bitcast.15), channel_id=1, replica_groups=mesh['dp'=4,'expert'=8] {'expert'}, dimensions={0} | all-to-all | bytes 1310720 | tf_op jit(solution)/shard_map/all_to_all | solution.py:368
  222.3 2.2 combine.1
  (81 shorter events, 17.7 us)
Async XLA Ops:
  6.5 30.3 %copy-start.15 = (bf16[1,256,1024]{2,1,0:T(8,128)(2,1)S(1)}, bf16[1,256,1024]{2,1,0:T(8,128)(2,1)}, u32[]{:S(2)}) copy-start(bf16[1,256,1024]{2,1,0:T(8,128)(2,1)} %refs_0_.2) | copy-start | bytes 1572868
  6.5 9.0 %copy-start.21 = (s32[16,2]{0,1:T(2,128)S(1)}, s32[16,2]{0,1:T(2,128)}, u32[]{:S(2)}) copy-start(s32[16,2]{0,1:T(2,128)} %param.10) | copy-start | bytes 388
  6.5 30.3 %copy-start.18 = (f32[2,1024]{1,0:T(2,128)S(1)}, f32[2,1024]{1,0:T(2,128)}, u32[]{:S(2)}) copy-start(f32[2,1024]{1,0:T(2,128)} %gain_ref.3) | copy-start | bytes 24580
  6.5 57.4 %all-gather.2.cloned.1.call-start = ((), (), s32[]{:S(2)}) async-start(), calls=%async_computation.3 | async-start | bytes 1179648 | tf_op jit(solution)/shard_map/all_gather | solution.py:244
  9.4 26.6 %collective-permute-start.6 = (bf16[1,256,1024]{2,1,0:T(8,128)(2,1)S(1)}, bf16[1,256,1024]{2,1,0:T(8,128)(2,1)S(1)}, u32[]{:S(2)}, u32[]{:S(2)}) collective-permute-start(bf16[1,256,1024]{2,1,0:T(8,128)(2,1)S(1)} %slice.6), channel_id=1, source_target_pairs={{0,16},{8,24},{16,0},{24,8},{1,17},{9,25},{17,1},{25,9},{2,18},{10... | collective-permute-start | bytes 1572872 | tf_op jit(solution)/shard_map/ppermute | solution.py:30
  11.0 25.0 %collective-permute-start = (bf16[1,256,1024]{2,1,0:T(8,128)(2,1)}, bf16[1,256,1024]{2,1,0:T(8,128)(2,1)S(1)}, u32[]{:S(2)}, u32[]{:S(2)}) collective-permute-start(bf16[1,256,1024]{2,1,0:T(8,128)(2,1)} %refs_0_.2), channel_id=1, source_target_pairs={{0,16},{8,24},{16,0},{24,8},{1,17},{9,25},{17,1},{25,9},{2,18},{10... | collective-permute-start | bytes 1572872 | tf_op jit(solution)/shard_map/ppermute | solution.py:30
  11.5 16.7 %collective-permute-start.4 = (bf16[3,128,256]{2,1,0:T(8,128)(2,1)S(1)}, bf16[3,128,256]{2,1,0:T(8,128)(2,1)S(1)}, u32[]{:S(2)}, u32[]{:S(2)}) collective-permute-start(bf16[3,128,256]{2,1,0:T(8,128)(2,1)S(1)} %constant_dynamic-slice_fusion.refs_0_), channel_id=1, source_target_pairs={{0,6},{1,7},{2,4},{3,5},{4,2},{5,3},{6,0},{7,1},{8,14},{9,15},{10,... | collective-permute-start | bytes 589832 | tf_op jit(solution)/shard_map/ppermute | solution.py:30
  12.0 17.9 %collective-permute-start.2 = (bf16[3,128,256]{2,1,0:T(8,128)(2,1)S(1)}, bf16[3,128,256]{2,1,0:T(8,128)(2,1)S(1)}, u32[]{:S(2)}, u32[]{:S(2)}) collective-permute-start(bf16[3,128,256]{2,1,0:T(8,128)(2,1)S(1)} %constant_dynamic-slice_fusion.refs_0_), channel_id=1, source_target_pairs={{0,2},{1,3},{2,0},{3,1},{4,6},{5,7},{6,4},{7,5},{8,10},{9,11},{10,... | collective-permute-start | bytes 589832 | tf_op jit(solution)/shard_map/ppermute | solution.py:30
  13.2 19.2 %collective-permute-start.3 = (bf16[3,128,256]{2,1,0:T(8,128)(2,1)S(1)}, bf16[3,128,256]{2,1,0:T(8,128)(2,1)}, u32[]{:S(2)}, u32[]{:S(2)}) collective-permute-start(bf16[3,128,256]{2,1,0:T(8,128)(2,1)S(1)} %constant_dynamic-slice_fusion.refs_0_), channel_id=1, source_target_pairs={{0,4},{1,5},{2,6},{3,7},{4,0},{5,1},{6,2},{7,3},{8,12},{9,13},{10,... | collective-permute-start | bytes 589832 | tf_op jit(solution)/shard_map/ppermute | solution.py:30
  28.2 5.7 %collective-permute-start.1 = (bf16[3,128,256]{2,1,0:T(8,128)(2,1)S(1)}, bf16[3,128,256]{2,1,0:T(8,128)(2,1)S(1)}, u32[]{:S(2)}, u32[]{:S(2)}) collective-permute-start(bf16[3,128,256]{2,1,0:T(8,128)(2,1)S(1)} %constant_dynamic-slice_fusion.refs_0_), channel_id=1, source_target_pairs={{0,1},{1,0},{2,3},{3,2},{4,5},{5,4},{6,7},{7,6},{8,9},{9,8},{10,11... | collective-permute-start | bytes 589832 | tf_op jit(solution)/shard_map/ppermute | solution.py:30
  29.9 6.1 %collective-permute-start.5 = (bf16[3,128,256]{2,1,0:T(8,128)(2,1)S(1)}, bf16[3,128,256]{2,1,0:T(8,128)(2,1)S(1)}, u32[]{:S(2)}, u32[]{:S(2)}) collective-permute-start(bf16[3,128,256]{2,1,0:T(8,128)(2,1)S(1)} %collective-permute-done.2.refs_2_), channel_id=1, source_target_pairs={{0,1},{1,0},{2,3},{3,2},{4,5},{5,4},{6,7},{7,6},{8,9},{9,8},{10,11... | collective-permute-start | bytes 589832 | tf_op jit(solution)/shard_map/ppermute | solution.py:30
  38.9 25.1 %copy-start.2 = (bf16[1,1024,1024]{2,1,0:T(8,128)(2,1)S(1)}, bf16[1,1024,1024]{2,1,0:T(8,128)(2,1)}, u32[]{:S(2)}) copy-start(bf16[1,1024,1024]{2,1,0:T(8,128)(2,1)} %refs_0_.3) | copy-start | bytes 6291460
  38.9 16.5 %collective-permute-start.7 = (bf16[2,256,1024]{2,1,0:T(8,128)(2,1)S(1)}, bf16[2,256,1024]{2,1,0:T(8,128)(2,1)S(1)}, u32[]{:S(2)}, u32[]{:S(2)}) collective-permute-start(bf16[2,256,1024]{2,1,0:T(8,128)(2,1)S(1)} %get-tuple-element.27.near_ref), channel_id=1, source_target_pairs={{0,8},{8,0},{16,24},{24,16},{1,9},{9,1},{17,25},{25,17},{2,10},{10... | collective-permute-start | bytes 3145736 | tf_op jit(solution)/shard_map/ppermute | solution.py:30
  38.9 11.6 %collective-permute-start.9 = (bf16[3,128,256]{2,1,0:T(8,128)(2,1)S(1)}, bf16[3,128,256]{2,1,0:T(8,128)(2,1)S(1)}, u32[]{:S(2)}, u32[]{:S(2)}) collective-permute-start(bf16[3,128,256]{2,1,0:T(8,128)(2,1)S(1)} %collective-permute-done.4.refs_6_), channel_id=1, source_target_pairs={{0,1},{1,0},{2,3},{3,2},{4,5},{5,4},{6,7},{7,6},{8,9},{9,8},{10,11... | collective-permute-start | bytes 589832 | tf_op jit(solution)/shard_map/ppermute | solution.py:30
  40.6 14.9 %collective-permute-start.8 = (bf16[3,128,256]{2,1,0:T(8,128)(2,1)}, bf16[3,128,256]{2,1,0:T(8,128)(2,1)S(1)}, u32[]{:S(2)}, u32[]{:S(2)}) collective-permute-start(bf16[3,128,256]{2,1,0:T(8,128)(2,1)} %collective-permute-done.3.refs_4_), channel_id=1, source_target_pairs={{0,1},{1,0},{2,3},{3,2},{4,5},{5,4},{6,7},{7,6},{8,9},{9,8},{10,11... | collective-permute-start | bytes 589832 | tf_op jit(solution)/shard_map/ppermute | solution.py:30
  63.9 43.5 %copy-start.12 = (bf16[256,1024]{1,0:T(8,128)(2,1)S(1)}, bf16[256,1024]{1,0:T(8,128)(2,1)}, u32[]{:S(2)}) copy-start(bf16[256,1024]{1,0:T(8,128)(2,1)} %copy-done.11) | copy-start | bytes 1572868
  63.9 43.5 %collective-permute-start.10 = (bf16[1024,512]{1,0:T(8,128)(2,1)}, bf16[1024,512]{1,0:T(8,128)(2,1)}, u32[]{:S(2)}, u32[]{:S(2)}) collective-permute-start(bf16[1024,512]{1,0:T(8,128)(2,1)} %all-gather.2.cloned.1.call-done.near_ref), channel_id=1, source_target_pairs={{0,8},{8,0},{16,24},{24,16},{1,9},{9,1},{17,25},{25,17},{2,10},{10... | collective-permute-start | bytes 3145736 | tf_op jit(solution)/shard_map/ppermute | solution.py:30
  65.3 55.9 %collective-permute-start.14 = (bf16[1,768,1024]{2,1,0:T(8,128)(2,1)}, bf16[1,768,1024]{2,1,0:T(8,128)(2,1)}, u32[]{:S(2)}, u32[]{:S(2)}) collective-permute-start(bf16[1,768,1024]{2,1,0:T(8,128)(2,1)} %slice.7), channel_id=1, source_target_pairs={{0,16},{8,24},{16,0},{24,8},{1,17},{9,25},{17,1},{25,9},{2,18},{10... | collective-permute-start | bytes 4718600 | tf_op jit(solution)/shard_map/ppermute | solution.py:30
  66.8 3.1 %collective-permute-start.11 = (bf16[256,256]{1,0:T(8,128)(2,1)}, bf16[256,256]{1,0:T(8,128)(2,1)S(1)}, u32[]{:S(2)}, u32[]{:S(2)}) collective-permute-start(bf16[256,256]{1,0:T(8,128)(2,1)} %get-tuple-element.29), channel_id=1, source_target_pairs={{0,8},{8,0},{16,24},{24,16},{1,9},{9,1},{17,25},{25,17},{2,10},{10... | collective-permute-start | bytes 393224 | tf_op jit(solution)/shard_map/ppermute | solution.py:30
  67.0 38.6 %collective-permute-start.12 = (bf16[256,256]{1,0:T(8,128)(2,1)}, bf16[256,256]{1,0:T(8,128)(2,1)S(1)}, u32[]{:S(2)}, u32[]{:S(2)}) collective-permute-start(bf16[256,256]{1,0:T(8,128)(2,1)} %get-tuple-element.30), channel_id=1, source_target_pairs={{0,16},{8,24},{16,0},{24,8},{1,17},{9,25},{17,1},{25,9},{2,18},{10... | collective-permute-start | bytes 393224 | tf_op jit(solution)/shard_map/ppermute | solution.py:30
  67.5 39.9 %collective-permute-start.13 = (bf16[256,256]{1,0:T(8,128)(2,1)S(1)}, bf16[256,256]{1,0:T(8,128)(2,1)S(1)}, u32[]{:S(2)}, u32[]{:S(2)}) collective-permute-start(bf16[256,256]{1,0:T(8,128)(2,1)S(1)} %copy-done.20), channel_id=1, source_target_pairs={{0,24},{8,16},{16,8},{24,0},{1,25},{9,17},{17,9},{25,1},{2,26},{10... | collective-permute-start | bytes 393224 | tf_op jit(solution)/shard_map/ppermute | solution.py:30
  114.5 33.8 %all-to-all-start = ((bf16[8,80,1024]{2,1,0:T(8,128)(2,1)}), bf16[8,80,1024]{2,1,0:T(8,128)(2,1)S(1)}, u32[]{:S(2)}, u32[]{:S(2)}) async-start(bf16[8,80,1024]{2,1,0:T(8,128)(2,1)} %bitcast.5), calls=%async_computation | async-start | bytes 2621440 | tf_op jit(solution)/shard_map/all_to_all | solution.py:325
  119.8 8.6 %collective-permute-start.15 = (bf16[1,1024,1024]{2,1,0:T(8,128)(2,1)}, bf16[1,1024,1024]{2,1,0:T(8,128)(2,1)S(1)}, u32[]{:S(2)}, u32[]{:S(2)}) collective-permute-start(bf16[1,1024,1024]{2,1,0:T(8,128)(2,1)} %refs_0_.3), channel_id=1, source_target_pairs={{0,8},{8,0},{16,24},{24,16},{1,9},{9,1},{17,25},{25,17},{2,10},{10... | collective-permute-start | bytes 6291464 | tf_op jit(solution)/shard_map/ppermute | solution.py:30
  119.8 48.4 %collective-permute-start.18 = (bf16[1,1024,1024]{2,1,0:T(8,128)(2,1)}, bf16[1,1024,1024]{2,1,0:T(8,128)(2,1)}, u32[]{:S(2)}, u32[]{:S(2)}) collective-permute-start(bf16[1,1024,1024]{2,1,0:T(8,128)(2,1)} %refs_0_.5), channel_id=1, source_target_pairs={{0,16},{8,24},{16,0},{24,8},{1,17},{9,25},{17,1},{25,9},{2,18},{10... | collective-permute-start | bytes 6291464 | tf_op jit(solution)/shard_map/ppermute | solution.py:30
  121.2 5.9 %collective-permute-start.17 = (bf16[1,768,1024]{2,1,0:T(8,128)(2,1)}, bf16[1,768,1024]{2,1,0:T(8,128)(2,1)S(1)}, u32[]{:S(2)}, u32[]{:S(2)}) collective-permute-start(bf16[1,768,1024]{2,1,0:T(8,128)(2,1)} %collective-permute-done.14.refs_2_), channel_id=1, source_target_pairs={{0,8},{8,0},{16,24},{24,16},{1,9},{9,1},{17,25},{25,17},{2,10},{10... | collective-permute-start | bytes 4718600 | tf_op jit(solution)/shard_map/ppermute | solution.py:30
  121.5 3.9 %collective-permute-start.16 = (bf16[1,256,1024]{2,1,0:T(8,128)(2,1)S(1)}, bf16[1,256,1024]{2,1,0:T(8,128)(2,1)S(1)}, u32[]{:S(2)}, u32[]{:S(2)}) collective-permute-start(bf16[1,256,1024]{2,1,0:T(8,128)(2,1)S(1)} %copy-done.10), channel_id=1, source_target_pairs={{0,8},{8,0},{16,24},{24,16},{1,9},{9,1},{17,25},{25,17},{2,10},{10... | collective-permute-start | bytes 1572872 | tf_op jit(solution)/shard_map/ppermute | solution.py:30
  129.7 42.1 %collective-permute-start.19 = (bf16[1,1024,1024]{2,1,0:T(8,128)(2,1)}, bf16[1,1024,1024]{2,1,0:T(8,128)(2,1)}, u32[]{:S(2)}, u32[]{:S(2)}) collective-permute-start(bf16[1,1024,1024]{2,1,0:T(8,128)(2,1)} %refs_0_.5), channel_id=1, source_target_pairs={{0,8},{8,0},{16,24},{24,16},{1,9},{9,1},{17,25},{25,17},{2,10},{10... | collective-permute-start | bytes 6291464 | tf_op jit(solution)/shard_map/ppermute | solution.py:30
  149.9 18.2 %copy-start.5 = (bf16[1,1024,1024]{2,1,0:T(8,128)(2,1)S(1)}, bf16[1,1024,1024]{2,1,0:T(8,128)(2,1)}, u32[]{:S(2)}) copy-start(bf16[1,1024,1024]{2,1,0:T(8,128)(2,1)} %copy-done.4) | copy-start | bytes 6291460
  149.9 18.2 %copy-start.7 = (bf16[1,768,1024]{2,1,0:T(8,128)(2,1)S(1)}, bf16[1,768,1024]{2,1,0:T(8,128)(2,1)}, u32[]{:S(2)}) copy-start(bf16[1,768,1024]{2,1,0:T(8,128)(2,1)} %copy-done.6) | copy-start | bytes 4718596
  153.5 19.0 %copy-start.1 = (bf16[1,1024,1024]{2,1,0:T(8,128)(2,1)S(1)}, bf16[1,1024,1024]{2,1,0:T(8,128)(2,1)}, u32[]{:S(2)}) copy-start(bf16[1,1024,1024]{2,1,0:T(8,128)(2,1)} %refs_0_.5) | copy-start | bytes 6291460
  168.1 4.4 %collective-permute-start.20 = (bf16[1,1024,1024]{2,1,0:T(8,128)(2,1)}, bf16[1,1024,1024]{2,1,0:T(8,128)(2,1)S(1)}, u32[]{:S(2)}, u32[]{:S(2)}) collective-permute-start(bf16[1,1024,1024]{2,1,0:T(8,128)(2,1)} %collective-permute-done.18.refs_1_), channel_id=1, source_target_pairs={{0,8},{8,0},{16,24},{24,16},{1,9},{9,1},{17,25},{25,17},{2,10},{10... | collective-permute-start | bytes 6291464 | tf_op jit(solution)/shard_map/ppermute | solution.py:30
  179.9 42.4 %copy-start.14 = (bf16[256,1024]{1,0:T(8,128)(2,1)S(1)}, bf16[256,1024]{1,0:T(8,128)(2,1)}, u32[]{:S(2)}) copy-start(bf16[256,1024]{1,0:T(8,128)(2,1)} %copy-done.13) | copy-start | bytes 1572868
  (14 other events, 30.3 us)
Sparse Core Ops, SparseCore 0:
  9.5 49.1 all-gather.1

commit v5 on v4

--- a/solution.py
+++ b/solution.py
@@ -131,16 +131,21 @@
     gate_ref[...] = jnp.broadcast_to(jax.nn.sigmoid(ahead - behind), gate_ref.shape)
 
 
-def hidden_kernel(cuts, slots_ref, *refs):
-    hidden_ref, buf, sems = refs[len(cuts) :]
-    count, _, inner = buf.shape
-    copies = [[] for _ in range(count)]
+def fetch(cuts, refs, buf, sems):
+    copies = [[] for _ in range(buf.shape[0])]
     for k, (at, start, size) in enumerate(cuts):
         copy = pltpu.make_async_copy(
             refs[k].at[0], buf.at[at, pl.ds(start, size), :], sems.at[k]
         )
         copy.start()
         copies[at].append(copy)
+    return copies
+
+
+def hidden_kernel(cuts, slots_ref, *refs):
+    hidden_ref, buf, sems = refs[len(cuts) :]
+    count, _, inner = buf.shape
+    copies = fetch(cuts, refs, buf, sems)
     step = min(512, inner)
     for at in range(count):
         for copy in copies[at]:
@@ -152,26 +157,25 @@
             hidden_ref[at, :, part : part + step] = (half + half * jnp.tanh(half)).astype(BF16)
 
 
-def answer_kernel(count, start, near_ref, far_ref, *refs):
-    weights, (answer_ref, buf, total, sems) = refs[:count], refs[count:]
+def answer_kernel(cuts, near_ref, far_ref, *refs):
+    answer_ref, buf, total, sems = refs[len(cuts) :]
     near = near_ref.shape[0]
-    cols = buf.shape[2]
-    copies = [
-        pltpu.make_async_copy(weights[at].at[0, :, pl.ds(start, cols)], buf.at[at], sems.at[at])
-        for at in range(count)
-    ]
-    for copy in copies:
-        copy.start()
+    count, _, width = buf.shape
+    copies = fetch(cuts, refs, buf, sems)
+    step = width // 2
     for at in range(count):
-        copies[at].wait()
+        for copy in copies[at]:
+            copy.wait()
         hidden = near_ref[at] if at < near else far_ref[at - near]
-        down = jnp.dot(hidden, buf[at], preferred_element_type=F32)
-        if at == 0:
-            total[...] = down
-        elif at < count - 1:
-            total[...] += down
-        else:
-            answer_ref[...] = (total[...] + down).astype(BF16)
+        for part in range(0, width, step):
+            where = slice(part, part + step)
+            down = jnp.dot(hidden, buf[at, :, where], preferred_element_type=F32)
+            if at == 0:
+                total[:, where] = down
+            elif at < count - 1:
+                total[:, where] += down
+            else:
+                answer_ref[:, where] = (total[:, where] + down).astype(BF16)
 
 
 def combine_kernel(experts, capacity, count, mixed_ref, gate_ref, cols_ref, *refs):
@@ -209,8 +213,9 @@
     return held
 
 
-def other_core(held):
-    return {k: swap(block, "dp", 1) for k, block in held.items()}
+def cut(size, sixteenths):
+    starts = [sum(sixteenths[:i]) * size // 16 for i in range(len(sixteenths) + 1)]
+    return [(a, b - a) for a, b in zip(starts, starts[1:])]
 
 
 def after(values, earlier):
@@ -248,8 +253,10 @@
         tiled=True,
     )
 
-    in_cuts = [(0, rows // 2), (rows // 2, width - rows // 2)]
+    in_cuts = cut(width, (5, 8, 3))
+    out_cuts = cut(inner, (3, 13))
     in_chunks = [lax.slice_in_dim(expert_in, a, a + n, axis=1) for a, n in in_cuts]
+    out_chunks = [lax.slice_in_dim(expert_out, a, a + n, axis=1) for a, n in out_cuts]
     in_held = [spread_over(in_chunks[0], "dp", 2)]
 
     early = [qkv[1], *[qkv[k] for k in range(2, exp_count, 2)], qkv[3], in_held[0]]
@@ -274,6 +281,8 @@
     )(place, norm_gains, *[raw[2 * k] for k in range(groups)])
     far = swap(near, "dp", 1)
     in_held.append(spread_over(after(in_chunks[1], near), "dp", 2))
+    far = after(far, in_held[1])
+    in_held.append(spread_over(after(in_chunks[2], (in_held[1], far, qkv)), "dp", 2))
 
     contexts = pl.pallas_call(
         functools.partial(attention_kernel, dp_count, exp_count),
@@ -291,20 +300,12 @@
         name="attention",
     )(exp_index[None], near, far, *[qkv[k] for k in range(exp_count)])
 
+    contexts = after(contexts, in_held[2])
     crossed = [swap(contexts[k], "dp", k) for k in range(1, dp_count)]
 
     proj_far = swap(after(proj_near, contexts), "dp", 1)
 
-    in_far = [swap(after(expert_in, crossed), "dp", 1)]
-    in_near = [expert_in]
-    places = [(0, 0, width)]
-    for k in range(2, dp_count, 2):
-        for held, cut in zip(in_held, in_cuts):
-            in_near.append(held[k])
-            in_far.append(swap(after(held[k], crossed), "dp", 1))
-            places.append((k // 2, *cut))
-    out_near = spread_over(after(expert_out, crossed), "dp", 2)
-    out_far = {0: swap(after(expert_out, in_far), "dp", 1)}
+    out_held = [spread_over(after(out_chunks[0], crossed), "dp", 2)]
 
     cols = expert_ids[0]
     slots, mixed, gate = pl.pallas_call(
@@ -322,6 +323,16 @@
         name="mix",
     )(me[None], stream, proj_near, proj_far, norm_gains, router, cols.T, cols, contexts[0], *crossed)
 
+    slots = after(slots, out_held[0])
+    out_held.append(spread_over(after(out_chunks[1], (out_held[0], mixed)), "dp", 2))
+    in_far, in_near, in_places = [swap(after(expert_in, mixed), "dp", 1)], [expert_in], [(0, 0, width)]
+    out_far, out_near, out_places = [swap(after(expert_out, mixed), "dp", 1)], [expert_out], [(0, 0, inner)]
+    for k in range(2, dp_count, 2):
+        for held, place in zip(in_held, in_cuts):
+            in_near.append(held[k])
+            in_far.append(swap(after(held[k], mixed), "dp", 1))
+            in_places.append((k // 2, *place))
+
     arrived = lax.all_to_all(
         slots.reshape(exp_count, capacity, width), "expert", split_axis=0, concat_axis=0, tiled=True
     ).reshape(slots_count, width)
@@ -329,56 +340,55 @@
 
     def hidden_units(slots_in, held, name):
         return pl.pallas_call(
-            functools.partial(hidden_kernel, places),
+            functools.partial(hidden_kernel, in_places),
             out_shape=jax.ShapeDtypeStruct((groups, slots_count, inner), BF16),
-            in_specs=[VMEM] + [HBM] * len(places),
+            in_specs=[VMEM] + [ANY] * len(in_places),
             out_specs=VMEM,
             scratch_shapes=[
                 pltpu.VMEM((groups, width, inner), BF16),
-                pltpu.SemaphoreType.DMA((len(places),)),
+                pltpu.SemaphoreType.DMA((len(in_places),)),
             ],
-            compiler_params=params(32),
+            compiler_params=params(48),
             cost_estimate=cost(2 * slots_count * width * inner * groups, 8 << 20),
             name=name,
         )(slots_in, *held)
 
     hidden_near = hidden_units(arrived, in_near, "hidden_near")
     hidden_far = hidden_units(after(arrived, hidden_near), in_far, "hidden_far")
-    distant = {k: block for k, block in out_near.items() if k}
-    out_far.update(other_core(after(distant, hidden_near)))
-    weights = [held[k] for held in (out_near, out_far) for k in sorted(held)]
-
-    returned = []
-    for c in range(2):
-        answer = pl.pallas_call(
-            functools.partial(answer_kernel, dp_count, c * rows),
-            out_shape=jax.ShapeDtypeStruct((slots_count, rows), BF16),
-            in_specs=[VMEM, VMEM] + [HBM] * dp_count,
-            out_specs=VMEM,
-            scratch_shapes=[
-                pltpu.VMEM((dp_count, inner, rows), BF16),
-                pltpu.VMEM((slots_count, rows), F32),
-                pltpu.SemaphoreType.DMA((dp_count,)),
-            ],
-            compiler_params=params(32),
-            cost_estimate=cost(2 * slots_count * rows * inner * dp_count, 10 << 20),
-            name="answer",
-        )(after(hidden_near, answer) if c else hidden_near, hidden_far, *weights)
-        returned.append(
-            lax.all_to_all(
-                answer.reshape(exp_count, capacity, rows), "expert", split_axis=0, concat_axis=0, tiled=True
-            ).reshape(slots_count, rows)
-        )
+    for k in range(2, dp_count, 2):
+        for held, place in zip(out_held, out_cuts):
+            out_near.append(held[k])
+            out_far.append(swap(after(held[k], hidden_near), "dp", 1))
+            out_places.append((k // 2, *place))
+    out_places += [(groups + at, *place) for at, *place in out_places]
+
+    answer = pl.pallas_call(
+        functools.partial(answer_kernel, out_places),
+        out_shape=jax.ShapeDtypeStruct((slots_count, width), BF16),
+        in_specs=[VMEM, VMEM] + [ANY] * len(out_places),
+        out_specs=VMEM,
+        scratch_shapes=[
+            pltpu.VMEM((dp_count, inner, width), BF16),
+            pltpu.VMEM((slots_count, width), F32),
+            pltpu.SemaphoreType.DMA((len(out_places),)),
+        ],
+        compiler_params=params(48),
+        cost_estimate=cost(2 * slots_count * width * inner * dp_count, 10 << 20),
+        name="answer",
+    )(hidden_near, hidden_far, *out_near, *out_far)
+    returned = lax.all_to_all(
+        answer.reshape(exp_count, capacity, width), "expert", split_axis=0, concat_axis=0, tiled=True
+    ).reshape(slots_count, width)
 
     return pl.pallas_call(
-        functools.partial(combine_kernel, exp_count, capacity, len(returned)),
+        functools.partial(combine_kernel, exp_count, capacity, 1),
         out_shape=jax.ShapeDtypeStruct((1, frames, width), BF16),
-        in_specs=[VMEM] * (3 + len(returned)),
+        in_specs=[VMEM] * 4,
         out_specs=VMEM,
         compiler_params=params(32),
         cost_estimate=cost(4 * frames * slots_count * width, 3 << 20),
         name="combine",
-    )(mixed, gate, cols, *returned)
+    )(mixed, gate, cols, returned)
 
 
 def solution(mesh):

time: 235 us -> 216 us (0.919)
  waiting for transfers between devices: 109 us -> 75.6 us
  local copies, waits for them, and re-layouts: 15.9 us -> 26.1 us
  Pallas kernels: 29.4 us -> 36.3 us
  blocking collectives: 42.4 us -> 35.8 us
  starting transfers between devices: 21 us -> 25 us
    ppermute x21 -> x25, waiting for transfers between devices: 90.5 us -> 52.1 us  [swap(): return lax.ppermute(block, axis, [(i, i ^ mask) for i in range(count)])]
    pallas_call x5 -> x4, Pallas kernels: 16.8 us -> 25.4 us  [the longest x2 13 us: hidden_units(): pl.pallas_call(functools.partial(hidden_kernel, in_places), out_shape=jax...]
    all_to_all x2 -> x1, blocking collectives: 42.4 us -> 35.8 us  [body(): lax.all_to_all(answer.reshape(exp_count, capacity, width), 'expert', spli...]
    all_to_all x1, waiting for transfers between devices: 18.5 us -> 23.5 us  [body(): lax.all_to_all(slots.reshape(exp_count, capacity, width), 'expert', split...]
    slice x0 -> x2, local copies, waits for them, and re-layouts: none -> 4.64 us  [body(): lax.slice_in_dim(expert_out, a, a + n, axis=1)]
    unnamed x48 -> x62, local copies, waits for them, and re-layouts: 11.2 us -> 14.7 us
    ppermute x21 -> x25, starting transfers between devices: 15.7 us -> 19.2 us  [swap(): return lax.ppermute(block, axis, [(i, i ^ mask) for i in range(count)])]
    slice x2 -> x3, local copies, waits for them, and re-layouts: 2.36 us -> 5.37 us  [body(): lax.slice_in_dim(expert_in, a, a + n, axis=1)]
  transfers between devices with their start and end apart: 23 -> 27, of which waited for: 13 -> 11; matrix products, arithmetic and copies ran while one was open for 2% -> 5% of each run, Pallas kernels for 9% -> 11%
where the time goes in v5:
time: 216 us; the launch traced here: 212 us
  waiting for transfers between devices  75.6 us (35%)
  Pallas kernels  36.3 us (17%)
  blocking collectives  35.8 us (17%)
  local copies, waits for them, and re-layouts  26.1 us (12%)
  starting transfers between devices  25 us (12%)
  between operations  13.7 us (6%)
    ppermute x25, waiting for transfers between devices, swap(): return lax.ppermute(block, axis, [(i, i ^ mask) for i in range(count)])  52.1 us
    all_to_all x1, blocking collectives, body(): lax.all_to_all(answer.reshape(exp_count, capacity, width), 'expert', spli...  35.8 us
    all_to_all x1, waiting for transfers between devices, body(): lax.all_to_all(slots.reshape(exp_count, capacity, width), 'expert', split...  23.5 us
    ppermute x25, starting transfers between devices, swap(): return lax.ppermute(block, axis, [(i, i ^ mask) for i in range(count)])  19.2 us
    unnamed x62, local copies, waits for them, and re-layouts  14.7 us
    pallas_call x2, Pallas kernels, hidden_units(): pl.pallas_call(functools.partial(hidden_kernel, in_places), out_shape=jax...  13 us
    pallas_call x1, Pallas kernels, body(): pl.pallas_call(functools.partial(answer_kernel, out_places), out_shape=ja...  10.3 us
    pallas_call x1, Pallas kernels, body(): pl.pallas_call(functools.partial(attention_kernel, dp_count, exp_count),...  6.6 us
  transfers between devices with their start and end apart: 27, of which 11 were waited for; matrix products, arithmetic and copies ran while one was open for 5% of the time, Pallas kernels for 11%

profile of v5, /device:TPU:16, one launch (start us, length us, event | category | flops | bytes accessed | tf_op | source)
XLA Modules:
  0.0 212.5 jit_solution(15284759791818574991)
XLA Ops:
  6.5 2.1 slice.15
  8.6 1.5 collective-permute-start.6
  10.7 1.6 collective-permute-start.1
  12.2 1.6 collective-permute-start.2
  14.9 2.3 %slice.16 = bf16[1,512,1024]{2,1,0:T(8,128)(2,1)} slice(bf16[1,1024,1024]{2,1,0:T(8,128)(2,1)} %refs_0_.4), slice={[0:1], [320:832], [0:1024]} | slice | bytes 2097152 | tf_op jit(solution)/shard_map/slice | solution.py:258
  17.8 1.6 collective-permute-start.4
  20.6 9.8 %collective-permute-done.3.refs_4_ = bf16[3,128,256]{2,1,0:T(8,128)(2,1)S(1)} collective-permute-done((bf16[3,128,256]{2,1,0:T(8,128)(2,1)S(1)}, bf16[3,128,256]{2,1,0:T(8,128)(2,1)S(1)}, u32[]{:S(2)}, u32[]{:S(2)}) %collective-permute-start.3) | collective-permute-done | bytes 196640 | tf_op jit(solution)/shard_map/ppermute | solution.py:30
  30.4 6.5 %collective-permute-done.4.refs_6_ = bf16[3,128,256]{2,1,0:T(8,128)(2,1)S(1)} collective-permute-done((bf16[3,128,256]{2,1,0:T(8,128)(2,1)S(1)}, bf16[3,128,256]{2,1,0:T(8,128)(2,1)S(1)}, u32[]{:S(2)}, u32[]{:S(2)}) %collective-permute-start.4) | collective-permute-done | bytes 196640 | tf_op jit(solution)/shard_map/ppermute | solution.py:30
  36.9 1.3 norm.1
  38.3 1.6 collective-permute-start.8
  39.9 1.1 collective-permute-start.9
  42.9 21.1 %collective-permute-done.8.refs_2_ = bf16[1,512,1024]{2,1,0:T(8,128)(2,1)S(1)} collective-permute-done((bf16[1,512,1024]{2,1,0:T(8,128)(2,1)}, bf16[1,512,1024]{2,1,0:T(8,128)(2,1)S(1)}, u32[]{:S(2)}, u32[]{:S(2)}) %collective-permute-start.8) | collective-permute-done | bytes 1048608 | tf_op jit(solution)/shard_map/ppermute | solution.py:30
  64.1 1.6 collective-permute-start.11
  65.7 6.6 %attention.1 = (bf16[256,256]{1,0:T(8,128)(2,1)S(1)}, bf16[256,256]{1,0:T(8,128)(2,1)S(1)}, bf16[256,256]{1,0:T(8,128)(2,1)S(1)}, bf16[256,256]{1,0:T(8,128)(2,1)S(1)}) custom-call(s32[1]{0:T(128)} %bitcast.2.me_ref, bf16[2,256,1024]{2,1,0:T(8,128)(2,1)S(1)} %get-tuple-element.36.near_ref, bf16[2,256,1024]{2,1,0:T(8,128)(2,1)S(1)} %collective-permute-done.7.far_ref, ...), custom_call_target="tpu_custom_call" | custom-call | flops 10485760 | bytes 20480 | tf_op jit(solution)/shard_map/attention/pallas_call | solution.py:287
  76.2 1.4 collective-permute-start.14
  77.6 1.8 slice.18
  80.1 2.7 %collective-permute-done.14.refs_2_ = bf16[256,256]{1,0:T(8,128)(2,1)S(1)} collective-permute-done((bf16[256,256]{1,0:T(8,128)(2,1)}, bf16[256,256]{1,0:T(8,128)(2,1)S(1)}, u32[]{:S(2)}, u32[]{:S(2)}) %collective-permute-start.14) | collective-permute-done | bytes 131104 | tf_op jit(solution)/shard_map/ppermute | solution.py:30
  84.3 1.4 collective-permute-start.16
  91.6 2.9 %mix.1 = (bf16[640,1024]{1,0:T(8,128)(2,1)}, bf16[256,1024]{1,0:T(8,128)(2,1)S(1)}, f32[256,128]{1,0:T(8,128)S(1)}) custom-call(s32[1]{0:T(128)} %bitcast.me_ref, bf16[256,1024]{1,0:T(8,128)(2,1)S(1)} %copy-done.7, bf16[1024,512]{1,0:T(8,128)(2,1)S(1)} %copy-done.1, bf16[1024,512]{1,0:T(8,128)(2,1)S(1)} %collective-permute-done.12.far_ref, ...), custom_call_target="tpu_custom_call" | custom-call | flops 3407872 | bytes 20480 | tf_op jit(solution)/shard_map/mix/pallas_call | solution.py:311
  96.5 5.8 %all-to-all-start = ((bf16[8,80,1024]{2,1,0:T(8,128)(2,1)}), bf16[8,80,1024]{2,1,0:T(8,128)(2,1)S(1)}, u32[]{:S(2)}, u32[]{:S(2)}) async-start(bf16[8,80,1024]{2,1,0:T(8,128)(2,1)} %bitcast.5), calls=%async_computation | async-start | bytes 2621440 | tf_op jit(solution)/shard_map/all_to_all | solution.py:336
  102.3 2.9 %slice.19 = bf16[1,832,1024]{2,1,0:T(8,128)(2,1)} slice(bf16[1,1024,1024]{2,1,0:T(8,128)(2,1)} %refs_0_.5), slice={[0:1], [192:1024], [0:1024]} | slice | bytes 3407872 | tf_op jit(solution)/shard_map/slice | solution.py:259
  105.1 1.4 collective-permute-start.21
  107.0 23.5 %all-to-all-done = bf16[8,80,1024]{2,1,0:T(8,128)(2,1)S(1)} async-done(((bf16[8,80,1024]{2,1,0:T(8,128)(2,1)}), bf16[8,80,1024]{2,1,0:T(8,128)(2,1)S(1)}, u32[]{:S(2)}, u32[]{:S(2)}) %all-to-all-start) | async-done | bytes 1310752 | tf_op jit(solution)/shard_map/all_to_all | solution.py:336
  130.6 1.1 copy-done.5
  132.7 6.5 %hidden_near.1.near_ref = bf16[2,640,1024]{2,1,0:T(8,128)(2,1)} custom-call(bf16[640,1024]{1,0:T(8,128)(2,1)S(1)} %bitcast.11, bf16[1,1024,1024]{2,1,0:T(8,128)(2,1)} %refs_0_.4, bf16[1,320,1024]{2,1,0:T(8,128)(2,1)S(1)} %copy-done.5, bf16[1,512,1024]{2,1,0:T(8,128)(2,1)S(1)} %copy-done.3, bf16[1,192,1024]{2,1,0:T(8,128)(2,1)S(1)} %copy-done.12), custom_call_target="tpu_custom_call" | custom-call | flops 10485760 | bytes 32768 | tf_op jit(solution)/shard_map/hidden_near/pallas_call | solution.py:342
  139.2 4.9 %collective-permute-done.21.refs_2_ = bf16[1,832,1024]{2,1,0:T(8,128)(2,1)} collective-permute-done((bf16[1,832,1024]{2,1,0:T(8,128)(2,1)}, bf16[1,832,1024]{2,1,0:T(8,128)(2,1)}, u32[]{:S(2)}, u32[]{:S(2)}) %collective-permute-start.21) | collective-permute-done | bytes 1703968 | tf_op jit(solution)/shard_map/ppermute | solution.py:30
  144.5 3.3 %collective-permute-done.20.refs_3_ = bf16[1,192,1024]{2,1,0:T(8,128)(2,1)S(1)} collective-permute-done((bf16[1,192,1024]{2,1,0:T(8,128)(2,1)S(1)}, bf16[1,192,1024]{2,1,0:T(8,128)(2,1)S(1)}, u32[]{:S(2)}, u32[]{:S(2)}) %collective-permute-start.20) | collective-permute-done | bytes 393248 | tf_op jit(solution)/shard_map/ppermute | solution.py:30
  148.2 2.4 %collective-permute-done.18.refs_1_ = bf16[1,320,1024]{2,1,0:T(8,128)(2,1)S(1)} collective-permute-done((bf16[1,320,1024]{2,1,0:T(8,128)(2,1)S(1)}, bf16[1,320,1024]{2,1,0:T(8,128)(2,1)S(1)}, u32[]{:S(2)}, u32[]{:S(2)}) %collective-permute-start.18) | collective-permute-done | bytes 655392 | tf_op jit(solution)/shard_map/ppermute | solution.py:30
  150.8 6.5 %hidden_far.1.far_ref = bf16[2,640,1024]{2,1,0:T(8,128)(2,1)} custom-call(bf16[640,1024]{1,0:T(8,128)(2,1)S(1)} %bitcast.12, bf16[1,1024,1024]{2,1,0:T(8,128)(2,1)} %collective-permute-done.17.refs_0_, bf16[1,320,1024]{2,1,0:T(8,128)(2,1)S(1)} %collective-permute-done.18.refs_1_, bf16[1,512,1024]{2,1,0:T(8,128)(2,1)S(1)} %collective-permute-done.19.refs_2_, ...), custom_call_target="tpu_custom_call" | custom-call | flops 10485760 | bytes 32768 | tf_op jit(solution)/shard_map/hidden_far/pallas_call | solution.py:342
  157.3 10.3 %answer.1 = bf16[640,1024]{1,0:T(8,128)(2,1)S(1)} custom-call(bf16[2,640,1024]{2,1,0:T(8,128)(2,1)} %hidden_near.1.near_ref, bf16[2,640,1024]{2,1,0:T(8,128)(2,1)} %hidden_far.1.far_ref, bf16[1,1024,1024]{2,1,0:T(8,128)(2,1)} %refs_0_.5, bf16[1,192,1024]{2,1,0:T(8,128)(2,1)} %collective-permute-done.16.refs_1_, ...), custom_call_target="tpu_custom_call" | custom-call | flops 20971520 | bytes 40960 | tf_op jit(solution)/shard_map/answer/pallas_call | solution.py:365
  167.6 35.8 %all_to_all.10 = bf16[8,80,1024]{2,1,0:T(8,128)(2,1)S(1)} all-to-all(bf16[8,80,1024]{2,1,0:T(8,128)(2,1)S(1)} %bitcast.13), channel_id=1, replica_groups=mesh['dp'=4,'expert'=8] {'expert'}, dimensions={0} | all-to-all | bytes 2621440 | tf_op jit(solution)/shard_map/all_to_all | solution.py:379
  203.5 2.2 %combine.1 = bf16[1,256,1024]{2,1,0:T(8,128)(2,1)} custom-call(bf16[256,1024]{1,0:T(8,128)(2,1)S(1)} %copy-done.9, f32[256,128]{1,0:T(8,128)S(1)} %copy-done.14, s32[256,2]{1,0:T(8,128)S(1)} %bitcast.17, bf16[640,1024]{1,0:T(8,128)(2,1)S(1)} %bitcast.14), custom_call_target="tpu_custom_call" | custom-call | flops 2621440 | bytes 12288 | tf_op jit(solution)/shard_map/combine/pallas_call | solution.py:383
  (104 shorter events, 21.9 us)
Async XLA Ops:
  6.5 69.2 %all-gather.2.cloned.1.call-start = ((), (), s32[]{:S(2)}) async-start(), calls=%async_computation.2 | async-start | bytes 1179648 | tf_op jit(solution)/shard_map/all_gather | solution.py:249
  8.6 28.3 %collective-permute-start.6 = (bf16[1,320,1024]{2,1,0:T(8,128)(2,1)}, bf16[1,320,1024]{2,1,0:T(8,128)(2,1)S(1)}, u32[]{:S(2)}, u32[]{:S(2)}) collective-permute-start(bf16[1,320,1024]{2,1,0:T(8,128)(2,1)} %slice.15), channel_id=1, source_target_pairs={{0,16},{8,24},{16,0},{24,8},{1,17},{9,25},{17,1},{25,9},{2,18},{10... | collective-permute-start | bytes 1966088 | tf_op jit(solution)/shard_map/ppermute | solution.py:30
  10.1 26.7 %collective-permute-start = (bf16[1,256,1024]{2,1,0:T(8,128)(2,1)}, bf16[1,256,1024]{2,1,0:T(8,128)(2,1)S(1)}, u32[]{:S(2)}, u32[]{:S(2)}) collective-permute-start(bf16[1,256,1024]{2,1,0:T(8,128)(2,1)} %refs_0_.3), channel_id=1, source_target_pairs={{0,16},{8,24},{16,0},{24,8},{1,17},{9,25},{17,1},{25,9},{2,18},{10... | collective-permute-start | bytes 1572872 | tf_op jit(solution)/shard_map/ppermute | solution.py:30
  10.6 26.2 %copy-start.23 = (f32[2,1024]{1,0:T(2,128)S(1)}, f32[2,1024]{1,0:T(2,128)}, u32[]{:S(2)}) copy-start(f32[2,1024]{1,0:T(2,128)} %gain_ref.3) | copy-start | bytes 24580
  10.7 7.2 %collective-permute-start.1 = (bf16[3,128,256]{2,1,0:T(8,128)(2,1)S(1)}, bf16[3,128,256]{2,1,0:T(8,128)(2,1)S(1)}, u32[]{:S(2)}, u32[]{:S(2)}) collective-permute-start(bf16[3,128,256]{2,1,0:T(8,128)(2,1)S(1)} %constant_dynamic-slice_fusion.refs_0_), channel_id=1, source_target_pairs={{0,1},{1,0},{2,3},{3,2},{4,5},{5,4},{6,7},{7,6},{8,9},{9,8},{10,11... | collective-permute-start | bytes 589832 | tf_op jit(solution)/shard_map/ppermute | solution.py:30
  12.2 7.8 %collective-permute-start.2 = (bf16[3,128,256]{2,1,0:T(8,128)(2,1)S(1)}, bf16[3,128,256]{2,1,0:T(8,128)(2,1)S(1)}, u32[]{:S(2)}, u32[]{:S(2)}) collective-permute-start(bf16[3,128,256]{2,1,0:T(8,128)(2,1)S(1)} %constant_dynamic-slice_fusion.refs_0_), channel_id=1, source_target_pairs={{0,2},{1,3},{2,0},{3,1},{4,6},{5,7},{6,4},{7,5},{8,10},{9,11},{10,... | collective-permute-start | bytes 589832 | tf_op jit(solution)/shard_map/ppermute | solution.py:30
  14.5 15.9 %collective-permute-start.3 = (bf16[3,128,256]{2,1,0:T(8,128)(2,1)S(1)}, bf16[3,128,256]{2,1,0:T(8,128)(2,1)S(1)}, u32[]{:S(2)}, u32[]{:S(2)}) collective-permute-start(bf16[3,128,256]{2,1,0:T(8,128)(2,1)S(1)} %constant_dynamic-slice_fusion.refs_0_), channel_id=1, source_target_pairs={{0,4},{1,5},{2,6},{3,7},{4,0},{5,1},{6,2},{7,3},{8,12},{9,13},{10,... | collective-permute-start | bytes 589832 | tf_op jit(solution)/shard_map/ppermute | solution.py:30
  17.8 19.0 %collective-permute-start.4 = (bf16[3,128,256]{2,1,0:T(8,128)(2,1)S(1)}, bf16[3,128,256]{2,1,0:T(8,128)(2,1)S(1)}, u32[]{:S(2)}, u32[]{:S(2)}) collective-permute-start(bf16[3,128,256]{2,1,0:T(8,128)(2,1)S(1)} %constant_dynamic-slice_fusion.refs_0_), channel_id=1, source_target_pairs={{0,6},{1,7},{2,4},{3,5},{4,2},{5,3},{6,0},{7,1},{8,14},{9,15},{10,... | collective-permute-start | bytes 589832 | tf_op jit(solution)/shard_map/ppermute | solution.py:30
  20.1 16.8 %collective-permute-start.5 = (bf16[3,128,256]{2,1,0:T(8,128)(2,1)S(1)}, bf16[3,128,256]{2,1,0:T(8,128)(2,1)S(1)}, u32[]{:S(2)}, u32[]{:S(2)}) collective-permute-start(bf16[3,128,256]{2,1,0:T(8,128)(2,1)S(1)} %collective-permute-done.2.refs_2_), channel_id=1, source_target_pairs={{0,1},{1,0},{2,3},{3,2},{4,5},{5,4},{6,7},{7,6},{8,9},{9,8},{10,11... | collective-permute-start | bytes 589832 | tf_op jit(solution)/shard_map/ppermute | solution.py:30
  36.9 35.4 %copy-start.4 = (bf16[1,320,1024]{2,1,0:T(8,128)(2,1)}, bf16[1,320,1024]{2,1,0:T(8,128)(2,1)S(1)}, u32[]{:S(2)}) copy-start(bf16[1,320,1024]{2,1,0:T(8,128)(2,1)S(1)} %collective-permute-done.6.refs_1_) | copy-start | bytes 1966084
  38.2 4.7 %collective-permute-start.7 = (bf16[2,256,1024]{2,1,0:T(8,128)(2,1)S(1)}, bf16[2,256,1024]{2,1,0:T(8,128)(2,1)S(1)}, u32[]{:S(2)}, u32[]{:S(2)}) collective-permute-start(bf16[2,256,1024]{2,1,0:T(8,128)(2,1)S(1)} %get-tuple-element.36.near_ref), channel_id=1, source_target_pairs={{0,8},{8,0},{16,24},{24,16},{1,9},{9,1},{17,25},{25,17},{2,10},{10... | collective-permute-start | bytes 3145736 | tf_op jit(solution)/shard_map/ppermute | solution.py:30
  38.3 25.8 %collective-permute-start.8 = (bf16[1,512,1024]{2,1,0:T(8,128)(2,1)}, bf16[1,512,1024]{2,1,0:T(8,128)(2,1)S(1)}, u32[]{:S(2)}, u32[]{:S(2)}) collective-permute-start(bf16[1,512,1024]{2,1,0:T(8,128)(2,1)} %slice.16), channel_id=1, source_target_pairs={{0,16},{8,24},{16,0},{24,8},{1,17},{9,25},{17,1},{25,9},{2,18},{10... | collective-permute-start | bytes 3145736 | tf_op jit(solution)/shard_map/ppermute | solution.py:30
  39.9 24.2 %collective-permute-start.9 = (bf16[3,128,256]{2,1,0:T(8,128)(2,1)S(1)}, bf16[3,128,256]{2,1,0:T(8,128)(2,1)S(1)}, u32[]{:S(2)}, u32[]{:S(2)}) collective-permute-start(bf16[3,128,256]{2,1,0:T(8,128)(2,1)S(1)} %collective-permute-done.3.refs_4_), channel_id=1, source_target_pairs={{0,1},{1,0},{2,3},{3,2},{4,5},{5,4},{6,7},{7,6},{8,9},{9,8},{10,11... | collective-permute-start | bytes 589832 | tf_op jit(solution)/shard_map/ppermute | solution.py:30
  41.0 23.1 %collective-permute-start.10 = (bf16[3,128,256]{2,1,0:T(8,128)(2,1)S(1)}, bf16[3,128,256]{2,1,0:T(8,128)(2,1)S(1)}, u32[]{:S(2)}, u32[]{:S(2)}) collective-permute-start(bf16[3,128,256]{2,1,0:T(8,128)(2,1)S(1)} %collective-permute-done.4.refs_6_), channel_id=1, source_target_pairs={{0,1},{1,0},{2,3},{3,2},{4,5},{5,4},{6,7},{7,6},{8,9},{9,8},{10,11... | collective-permute-start | bytes 589832 | tf_op jit(solution)/shard_map/ppermute | solution.py:30
  64.1 10.9 %collective-permute-start.11 = (bf16[1,192,1024]{2,1,0:T(8,128)(2,1)S(1)}, bf16[1,192,1024]{2,1,0:T(8,128)(2,1)S(1)}, u32[]{:S(2)}, u32[]{:S(2)}) collective-permute-start(bf16[1,192,1024]{2,1,0:T(8,128)(2,1)S(1)} %slice.17), channel_id=1, source_target_pairs={{0,16},{8,24},{16,0},{24,8},{1,17},{9,25},{17,1},{25,9},{2,18},{10... | collective-permute-start | bytes 1179656 | tf_op jit(solution)/shard_map/ppermute | solution.py:30
  75.7 11.2 %collective-permute-start.12 = (bf16[1024,512]{1,0:T(8,128)(2,1)}, bf16[1024,512]{1,0:T(8,128)(2,1)S(1)}, u32[]{:S(2)}, u32[]{:S(2)}) collective-permute-start(bf16[1024,512]{1,0:T(8,128)(2,1)} %all-gather.2.cloned.1.call-done.near_ref), channel_id=1, source_target_pairs={{0,8},{8,0},{16,24},{24,16},{1,9},{9,1},{17,25},{25,17},{2,10},{10... | collective-permute-start | bytes 3145736 | tf_op jit(solution)/shard_map/ppermute | solution.py:30
  75.7 3.7 %collective-permute-start.13 = (bf16[256,256]{1,0:T(8,128)(2,1)}, bf16[256,256]{1,0:T(8,128)(2,1)S(1)}, u32[]{:S(2)}, u32[]{:S(2)}) collective-permute-start(bf16[256,256]{1,0:T(8,128)(2,1)} %copy-done.26), channel_id=1, source_target_pairs={{0,8},{8,0},{16,24},{24,16},{1,9},{9,1},{17,25},{25,17},{2,10},{10... | collective-permute-start | bytes 393224 | tf_op jit(solution)/shard_map/ppermute | solution.py:30
  76.2 6.6 %collective-permute-start.14 = (bf16[256,256]{1,0:T(8,128)(2,1)}, bf16[256,256]{1,0:T(8,128)(2,1)S(1)}, u32[]{:S(2)}, u32[]{:S(2)}) collective-permute-start(bf16[256,256]{1,0:T(8,128)(2,1)} %copy-done.25), channel_id=1, source_target_pairs={{0,16},{8,24},{16,0},{24,8},{1,17},{9,25},{17,1},{25,9},{2,18},{10... | collective-permute-start | bytes 393224 | tf_op jit(solution)/shard_map/ppermute | solution.py:30
  77.6 6.0 %collective-permute-start.15 = (bf16[256,256]{1,0:T(8,128)(2,1)}, bf16[256,256]{1,0:T(8,128)(2,1)S(1)}, u32[]{:S(2)}, u32[]{:S(2)}) collective-permute-start(bf16[256,256]{1,0:T(8,128)(2,1)} %copy-done.24), channel_id=1, source_target_pairs={{0,24},{8,16},{16,8},{24,0},{1,25},{9,17},{17,9},{25,1},{2,26},{10... | collective-permute-start | bytes 393224 | tf_op jit(solution)/shard_map/ppermute | solution.py:30
  84.3 12.1 %collective-permute-start.16 = (bf16[1,192,1024]{2,1,0:T(8,128)(2,1)}, bf16[1,192,1024]{2,1,0:T(8,128)(2,1)}, u32[]{:S(2)}, u32[]{:S(2)}) collective-permute-start(bf16[1,192,1024]{2,1,0:T(8,128)(2,1)} %slice.18), channel_id=1, source_target_pairs={{0,16},{8,24},{16,0},{24,8},{1,17},{9,25},{17,1},{25,9},{2,18},{10... | collective-permute-start | bytes 1179656 | tf_op jit(solution)/shard_map/ppermute | solution.py:30
  96.5 34.1 %all-to-all-start = ((bf16[8,80,1024]{2,1,0:T(8,128)(2,1)}), bf16[8,80,1024]{2,1,0:T(8,128)(2,1)S(1)}, u32[]{:S(2)}, u32[]{:S(2)}) async-start(bf16[8,80,1024]{2,1,0:T(8,128)(2,1)} %bitcast.5), calls=%async_computation | async-start | bytes 2621440 | tf_op jit(solution)/shard_map/all_to_all | solution.py:336
  102.3 28.3 %copy-start.3 = (bf16[1,512,1024]{2,1,0:T(8,128)(2,1)S(1)}, bf16[1,512,1024]{2,1,0:T(8,128)(2,1)}, u32[]{:S(2)}) copy-start(bf16[1,512,1024]{2,1,0:T(8,128)(2,1)} %copy-done.2) | copy-start | bytes 3145732
  105.1 38.9 %collective-permute-start.21 = (bf16[1,832,1024]{2,1,0:T(8,128)(2,1)}, bf16[1,832,1024]{2,1,0:T(8,128)(2,1)}, u32[]{:S(2)}, u32[]{:S(2)}) collective-permute-start(bf16[1,832,1024]{2,1,0:T(8,128)(2,1)} %slice.19), channel_id=1, source_target_pairs={{0,16},{8,24},{16,0},{24,8},{1,17},{9,25},{17,1},{25,9},{2,18},{10... | collective-permute-start | bytes 5111816 | tf_op jit(solution)/shard_map/ppermute | solution.py:30
  106.5 44.2 %collective-permute-start.17 = (bf16[1,1024,1024]{2,1,0:T(8,128)(2,1)}, bf16[1,1024,1024]{2,1,0:T(8,128)(2,1)}, u32[]{:S(2)}, u32[]{:S(2)}) collective-permute-start(bf16[1,1024,1024]{2,1,0:T(8,128)(2,1)} %refs_0_.4), channel_id=1, source_target_pairs={{0,8},{8,0},{16,24},{24,16},{1,9},{9,1},{17,25},{25,17},{2,10},{10... | collective-permute-start | bytes 6291464 | tf_op jit(solution)/shard_map/ppermute | solution.py:30
  106.5 50.8 %collective-permute-start.22 = (bf16[1,1024,1024]{2,1,0:T(8,128)(2,1)}, bf16[1,1024,1024]{2,1,0:T(8,128)(2,1)}, u32[]{:S(2)}, u32[]{:S(2)}) collective-permute-start(bf16[1,1024,1024]{2,1,0:T(8,128)(2,1)} %refs_0_.5), channel_id=1, source_target_pairs={{0,8},{8,0},{16,24},{24,16},{1,9},{9,1},{17,25},{25,17},{2,10},{10... | collective-permute-start | bytes 6291464 | tf_op jit(solution)/shard_map/ppermute | solution.py:30
  144.0 13.3 %collective-permute-start.24 = (bf16[1,832,1024]{2,1,0:T(8,128)(2,1)}, bf16[1,832,1024]{2,1,0:T(8,128)(2,1)S(1)}, u32[]{:S(2)}, u32[]{:S(2)}) collective-permute-start(bf16[1,832,1024]{2,1,0:T(8,128)(2,1)} %collective-permute-done.21.refs_2_), channel_id=1, source_target_pairs={{0,8},{8,0},{16,24},{24,16},{1,9},{9,1},{17,25},{25,17},{2,10},{10... | collective-permute-start | bytes 5111816 | tf_op jit(solution)/shard_map/ppermute | solution.py:30
  144.0 3.8 %collective-permute-start.20 = (bf16[1,192,1024]{2,1,0:T(8,128)(2,1)S(1)}, bf16[1,192,1024]{2,1,0:T(8,128)(2,1)S(1)}, u32[]{:S(2)}, u32[]{:S(2)}) collective-permute-start(bf16[1,192,1024]{2,1,0:T(8,128)(2,1)S(1)} %copy-done.12), channel_id=1, source_target_pairs={{0,8},{8,0},{16,24},{24,16},{1,9},{9,1},{17,25},{25,17},{2,10},{10... | collective-permute-start | bytes 1179656 | tf_op jit(solution)/shard_map/ppermute | solution.py:30
  144.5 6.2 %collective-permute-start.19 = (bf16[1,512,1024]{2,1,0:T(8,128)(2,1)S(1)}, bf16[1,512,1024]{2,1,0:T(8,128)(2,1)S(1)}, u32[]{:S(2)}, u32[]{:S(2)}) collective-permute-start(bf16[1,512,1024]{2,1,0:T(8,128)(2,1)S(1)} %copy-done.3), channel_id=1, source_target_pairs={{0,8},{8,0},{16,24},{24,16},{1,9},{9,1},{17,25},{25,17},{2,10},{10... | collective-permute-start | bytes 3145736 | tf_op jit(solution)/shard_map/ppermute | solution.py:30
  147.8 2.8 %collective-permute-start.18 = (bf16[1,320,1024]{2,1,0:T(8,128)(2,1)S(1)}, bf16[1,320,1024]{2,1,0:T(8,128)(2,1)S(1)}, u32[]{:S(2)}, u32[]{:S(2)}) collective-permute-start(bf16[1,320,1024]{2,1,0:T(8,128)(2,1)S(1)} %copy-done.5), channel_id=1, source_target_pairs={{0,8},{8,0},{16,24},{24,16},{1,9},{9,1},{17,25},{25,17},{2,10},{10... | collective-permute-start | bytes 1966088 | tf_op jit(solution)/shard_map/ppermute | solution.py:30
  150.6 6.7 %collective-permute-start.23 = (bf16[1,192,1024]{2,1,0:T(8,128)(2,1)}, bf16[1,192,1024]{2,1,0:T(8,128)(2,1)S(1)}, u32[]{:S(2)}, u32[]{:S(2)}) collective-permute-start(bf16[1,192,1024]{2,1,0:T(8,128)(2,1)} %collective-permute-done.16.refs_1_), channel_id=1, source_target_pairs={{0,8},{8,0},{16,24},{24,16},{1,9},{9,1},{17,25},{25,17},{2,10},{10... | collective-permute-start | bytes 1179656 | tf_op jit(solution)/shard_map/ppermute | solution.py:30
  167.6 35.9 %copy-start.9 = (bf16[256,1024]{1,0:T(8,128)(2,1)S(1)}, bf16[256,1024]{1,0:T(8,128)(2,1)}, u32[]{:S(2)}) copy-start(bf16[256,1024]{1,0:T(8,128)(2,1)} %copy-done.8) | copy-start | bytes 1572868
  167.6 35.9 %copy-start.14 = (f32[256,128]{1,0:T(8,128)S(1)}, f32[256,128]{1,0:T(8,128)}, u32[]{:S(2)}) copy-start(f32[256,128]{1,0:T(8,128)} %copy-done.13) | copy-start | bytes 393220
  (25 other events, 126.1 us)
Sparse Core Ops, SparseCore 0:
  14.6 46.5 all-gather.1

commit v6 on v5

--- a/solution.py
+++ b/solution.py
@@ -52,7 +52,7 @@
 
 def attention_kernel(count, shards, me_ref, near_ref, far_ref, *refs):
     pieces, outs = refs[:shards], refs[shards : shards + count]
-    weights, sems = refs[shards + count :]
+    weights, held, sems, out_sems = refs[shards + count :]
     depth, cols = pieces[0].shape[1:]
     me = me_ref[0]
     copies = []
@@ -63,6 +63,7 @@
         copies.append(copy)
     for copy in copies:
         copy.wait()
+    sent = []
     frames = near_ref.shape[1]
     head = lax.broadcasted_iota(jnp.int32, (frames, cols), 1) // HEAD_DIM
     scale = HEAD_DIM**-0.5
@@ -85,24 +86,39 @@
             norm = 1.0 / jnp.sum(exps, axis=-1, keepdims=True)
             probs = (exps * norm).astype(BF16)
             total = jnp.where(mine, jnp.dot(probs, val, preferred_element_type=F32), total)
-        outs[k][...] = total.astype(BF16)
-
-
-def mix_kernel(
-    count, experts, capacity, me_ref, own_ref, near_ref, far_ref, gain_ref, router_ref, rows_ref, cols_ref, *refs
-):
-    blocks, (slots_ref, mixed_ref, gate_ref), (wide,) = refs[:count], refs[count : count + 3], refs[count + 3 :]
-    frames, depth = blocks[0].shape
+        held[k] = total.astype(BF16)
+        copy = pltpu.make_async_copy(held.at[k], outs[k], out_sems.at[k])
+        copy.start()
+        sent.append(copy)
+    for copy in sent:
+        copy.wait()
+
+
+def mix_kernel(count, experts, capacity, me_ref, gain_ref, router_ref, rows_ref, cols_ref, *refs):
+    sources, refs = refs[: count + 3], refs[count + 3 :]
+    slots_out, mixed_out, gate_ref, own_ref, near_ref, far_ref, blocks, wide, slots_ref, mixed_ref, sems = refs
+    places = [own_ref, near_ref, far_ref, *[blocks.at[k] for k in range(count)]]
+    copies = [
+        pltpu.make_async_copy(source, place, sems.at[k])
+        for k, (source, place) in enumerate(zip(sources, places))
+    ]
+    for copy in copies:
+        copy.start()
+    _, frames, depth = blocks.shape
     me = me_ref[0]
     part = near_ref.shape[1]
+    for copy in copies:
+        copy.wait()
     for held, side in ((near_ref, me & 1), (far_ref, 1 - (me & 1))):
         total = jnp.zeros((frames, part), F32)
         for k in range(count):
             rows = pl.ds(pl.multiple_of((me ^ k) * depth, depth), depth)
-            total += jnp.dot(blocks[k][...], held[rows, :], preferred_element_type=F32)
+            total += jnp.dot(blocks[k], held[rows, :], preferred_element_type=F32)
         wide[:, pl.ds(pl.multiple_of(side * part, part), part)] = total
     mixed = (own_ref[...].astype(F32) + wide[...]).astype(BF16)
     mixed_ref[...] = mixed
+    mixed_copy = pltpu.make_async_copy(mixed_ref, mixed_out, sems.at[0])
+    mixed_copy.start()
     normed = layer_norm(mixed.astype(F32), gain_ref[1:2, :]).astype(BF16)
     first, second = rows_ref[0:1, :], rows_ref[1:2, :]
     which = lax.broadcasted_iota(jnp.int32, (experts, frames), 0)
@@ -117,69 +133,86 @@
     place1 = jnp.sum(jnp.where(which == second, rank, 0.0), axis=0, keepdims=True)
     spread = ((slot == place0) | (slot == place1)).astype(F32).astype(BF16)
     slots_ref[...] = jnp.dot(spread, normed, preferred_element_type=F32).astype(BF16)
+    slots_copy = pltpu.make_async_copy(slots_ref, slots_out, sems.at[1])
+    slots_copy.start()
     high = router_ref[...].astype(BF16)
     rest = router_ref[...] - high.astype(F32)
     middle = rest.astype(BF16)
     low = (rest - middle.astype(F32)).astype(BF16)
-    logits = (
-        jnp.dot(normed, low, preferred_element_type=F32)
-        + jnp.dot(normed, middle, preferred_element_type=F32)
-    ) + jnp.dot(normed, high, preferred_element_type=F32)
+    logits = sum(
+        lax.dot_general(normed, term, (((1,), (1,)), ((), ())), preferred_element_type=F32)
+        for term in (low, middle, high)
+    )
     lane = lax.broadcasted_iota(jnp.int32, (frames, experts), 1)
     ahead = jnp.sum(jnp.where(lane == cols_ref[:, 0:1], logits, 0.0), axis=1, keepdims=True)
     behind = jnp.sum(jnp.where(lane == cols_ref[:, 1:2], logits, 0.0), axis=1, keepdims=True)
     gate_ref[...] = jnp.broadcast_to(jax.nn.sigmoid(ahead - behind), gate_ref.shape)
-
-
-def fetch(cuts, refs, buf, sems):
-    copies = [[] for _ in range(buf.shape[0])]
-    for k, (at, start, size) in enumerate(cuts):
-        copy = pltpu.make_async_copy(
-            refs[k].at[0], buf.at[at, pl.ds(start, size), :], sems.at[k]
-        )
+    mixed_copy.wait()
+    slots_copy.wait()
+
+
+def split_kernel(cuts, whole_ref, *refs):
+    outs, sems = refs[: len(cuts)], refs[len(cuts)]
+    copies = [
+        pltpu.make_async_copy(whole_ref.at[:, pl.ds(start, size), :], outs[k], sems.at[k])
+        for k, (start, size) in enumerate(cuts)
+    ]
+    for copy in copies:
         copy.start()
-        copies[at].append(copy)
+    for copy in copies:
+        copy.wait()
+
+
+def fetch(cuts, step, refs, buf, sems):
+    count, _, cols = buf.shape
+    copies = {(at, part): [] for at in range(count) for part in range(0, cols, step)}
+    for at, part in copies:
+        for k, (of, start, size) in enumerate(cuts):
+            if of == at:
+                where = pl.ds(part, step)
+                copy = pltpu.make_async_copy(
+                    refs[k].at[0, :, where],
+                    buf.at[at, pl.ds(start, size), where],
+                    sems.at[k, part // step],
+                )
+                copy.start()
+                copies[at, part].append(copy)
     return copies
 
 
-def hidden_kernel(cuts, slots_ref, *refs):
+def hidden_kernel(cuts, step, slots_ref, *refs):
     hidden_ref, buf, sems = refs[len(cuts) :]
-    count, _, inner = buf.shape
-    copies = fetch(cuts, refs, buf, sems)
-    step = min(512, inner)
-    for at in range(count):
-        for copy in copies[at]:
-            copy.wait()
-        for part in range(0, inner, step):
-            half = 0.5 * jnp.dot(
-                slots_ref[...], buf[at, :, part : part + step], preferred_element_type=F32
-            )
-            hidden_ref[at, :, part : part + step] = (half + half * jnp.tanh(half)).astype(BF16)
-
-
-def answer_kernel(cuts, near_ref, far_ref, *refs):
-    answer_ref, buf, total, sems = refs[len(cuts) :]
-    near = near_ref.shape[0]
-    count, _, width = buf.shape
-    copies = fetch(cuts, refs, buf, sems)
-    step = width // 2
-    for at in range(count):
-        for copy in copies[at]:
-            copy.wait()
-        hidden = near_ref[at] if at < near else far_ref[at - near]
-        for part in range(0, width, step):
-            where = slice(part, part + step)
-            down = jnp.dot(hidden, buf[at, :, where], preferred_element_type=F32)
-            if at == 0:
-                total[:, where] = down
-            elif at < count - 1:
-                total[:, where] += down
-            else:
-                answer_ref[:, where] = (total[:, where] + down).astype(BF16)
-
-
-def combine_kernel(experts, capacity, count, mixed_ref, gate_ref, cols_ref, *refs):
-    answers, out_ref = refs[:count], refs[count]
+    for (at, part), pieces in fetch(cuts, step, refs, buf, sems).items():
+        for piece in pieces:
+            piece.wait()
+        where = slice(part, part + step)
+        half = 0.5 * jnp.dot(slots_ref[...], buf[at, :, where], preferred_element_type=F32)
+        hidden_ref[at, :, where] = (half + half * jnp.tanh(half)).astype(BF16)
+
+
+def answer_kernel(slices, step, held, before, *refs):
+    hidden, weights, refs = refs[:held], refs[held : held + len(slices)], refs[held + len(slices) :]
+    total_ref = refs[0] if before else None
+    answer_ref, buf, sems = refs[1:] if before else refs
+    cuts = [(at, 0, buf.shape[1]) for at in range(len(slices))]
+    copies = fetch(cuts, step, weights, buf, sems)
+    for part in range(0, buf.shape[2], step):
+        where = slice(part, part + step)
+        total = total_ref[:, where] if before else 0.0
+        for at, (of, place) in enumerate(slices):
+            for piece in copies[at, part]:
+                piece.wait()
+            total += jnp.dot(hidden[of][place], buf[at, :, where], preferred_element_type=F32)
+        answer_ref[:, where] = total.astype(answer_ref.dtype)
+
+
+def combine_kernel(experts, capacity, gate_ref, cols_ref, mixed_in, answer_in, out_ref, mixed_ref, answer_ref, sems):
+    copies = [
+        pltpu.make_async_copy(answer_in, answer_ref, sems.at[0]),
+        pltpu.make_async_copy(mixed_in, mixed_ref, sems.at[1]),
+    ]
+    for copy in copies:
+        copy.start()
     frames = mixed_ref.shape[0]
     first, second = cols_ref[:, 0:1], cols_ref[:, 1:2]
     lane = lax.broadcasted_iota(jnp.int32, (frames, experts), 1)
@@ -195,10 +228,12 @@
         place = jnp.sum(jnp.where(lane == chosen, rank, 0.0), axis=1, keepdims=True)
         picks.append((slot == place).astype(F32).astype(BF16))
     gate = gate_ref[:, 0:1]
-    cols = mixed_ref.shape[1] // count
-    for c in range(count):
-        where = slice(c * cols, (c + 1) * cols)
-        back = [jnp.dot(pick, answers[c][...], preferred_element_type=F32) for pick in picks]
+    for copy in copies:
+        copy.wait()
+    step = mixed_ref.shape[1] // 2
+    for part in range(0, 2 * step, step):
+        where = slice(part, part + step)
+        back = [jnp.dot(pick, answer_ref[:, where], preferred_element_type=F32) for pick in picks]
         result = mixed_ref[:, where].astype(F32) + gate * back[0] + (1.0 - gate) * back[1]
         out_ref[0, :, where] = result.astype(BF16)
 
@@ -213,8 +248,8 @@
     return held
 
 
-def cut(size, sixteenths):
-    starts = [sum(sixteenths[:i]) * size // 16 for i in range(len(sixteenths) + 1)]
+def cut(size, shares):
+    starts = [sum(shares[:i]) * size // sum(shares) for i in range(len(shares) + 1)]
     return [(a, b - a) for a, b in zip(starts, starts[1:])]
 
 
@@ -253,10 +288,17 @@
         tiled=True,
     )
 
-    in_cuts = cut(width, (5, 8, 3))
-    out_cuts = cut(inner, (3, 13))
-    in_chunks = [lax.slice_in_dim(expert_in, a, a + n, axis=1) for a, n in in_cuts]
-    out_chunks = [lax.slice_in_dim(expert_out, a, a + n, axis=1) for a, n in out_cuts]
+    in_cuts = cut(width, (20, 23, 9, 12))
+    in_chunks = pl.pallas_call(
+        functools.partial(split_kernel, in_cuts),
+        out_shape=[jax.ShapeDtypeStruct((1, n, inner), BF16) for _, n in in_cuts],
+        in_specs=[HBM],
+        out_specs=[HBM] * len(in_cuts),
+        scratch_shapes=[pltpu.SemaphoreType.DMA((len(in_cuts),))],
+        compiler_params=params(32),
+        cost_estimate=cost(0, 4 << 20),
+        name="split",
+    )(expert_in)
     in_held = [spread_over(in_chunks[0], "dp", 2)]
 
     early = [qkv[1], *[qkv[k] for k in range(2, exp_count, 2)], qkv[3], in_held[0]]
@@ -288,10 +330,12 @@
         functools.partial(attention_kernel, dp_count, exp_count),
         out_shape=[jax.ShapeDtypeStruct((frames, share), BF16)] * dp_count,
         in_specs=[SMEM, VMEM, VMEM] + [ANY] * exp_count,
-        out_specs=[VMEM] * dp_count,
+        out_specs=[ANY] * dp_count,
         scratch_shapes=[
             pltpu.VMEM((3, width, share), BF16),
+            pltpu.VMEM((dp_count, frames, share), BF16),
             pltpu.SemaphoreType.DMA((exp_count,)),
+            pltpu.SemaphoreType.DMA((dp_count,)),
         ],
         compiler_params=params(32),
         cost_estimate=cost(
@@ -305,7 +349,7 @@
 
     proj_far = swap(after(proj_near, contexts), "dp", 1)
 
-    out_held = [spread_over(after(out_chunks[0], crossed), "dp", 2)]
+    in_held.append(spread_over(after(in_chunks[3], crossed), "dp", 2))
 
     cols = expert_ids[0]
     slots, mixed, gate = pl.pallas_call(
@@ -315,18 +359,27 @@
             jax.ShapeDtypeStruct((frames, width), BF16),
             jax.ShapeDtypeStruct((frames, 128), F32),
         ),
-        in_specs=[SMEM] + [VMEM] * (7 + dp_count),
-        out_specs=(VMEM, VMEM, VMEM),
-        scratch_shapes=[pltpu.VMEM((frames, width), F32)],
+        in_specs=[SMEM] + [VMEM] * 4 + [ANY] * (3 + dp_count),
+        out_specs=(ANY, ANY, VMEM),
+        scratch_shapes=[
+            pltpu.VMEM((frames, width), BF16),
+            pltpu.VMEM((width, rows), BF16),
+            pltpu.VMEM((width, rows), BF16),
+            pltpu.VMEM((dp_count, frames, share), BF16),
+            pltpu.VMEM((frames, width), F32),
+            pltpu.VMEM((slots_count, width), BF16),
+            pltpu.VMEM((frames, width), BF16),
+            pltpu.SemaphoreType.DMA((dp_count + 3,)),
+        ],
         compiler_params=params(32),
         cost_estimate=cost(2 * frames * width * (width + slots_count), 5 << 20),
         name="mix",
-    )(me[None], stream, proj_near, proj_far, norm_gains, router, cols.T, cols, contexts[0], *crossed)
-
-    slots = after(slots, out_held[0])
-    out_held.append(spread_over(after(out_chunks[1], (out_held[0], mixed)), "dp", 2))
+    )(me[None], norm_gains, router.T, cols.T, cols, stream, proj_near, proj_far, contexts[0], *crossed)
+
+    slots = after(slots, in_held[3])
+    out_held = spread_over(after(expert_out, (in_held[3], mixed)), "dp", 2)
     in_far, in_near, in_places = [swap(after(expert_in, mixed), "dp", 1)], [expert_in], [(0, 0, width)]
-    out_far, out_near, out_places = [swap(after(expert_out, mixed), "dp", 1)], [expert_out], [(0, 0, inner)]
+    out_own = swap(after(expert_out, mixed), "dp", 1)
     for k in range(2, dp_count, 2):
         for held, place in zip(in_held, in_cuts):
             in_near.append(held[k])
@@ -338,57 +391,71 @@
     ).reshape(slots_count, width)
 
 
+    arrived = after(arrived, (in_far, out_own))
+    step = min(256, inner)
+
     def hidden_units(slots_in, held, name):
         return pl.pallas_call(
-            functools.partial(hidden_kernel, in_places),
+            functools.partial(hidden_kernel, in_places, step),
             out_shape=jax.ShapeDtypeStruct((groups, slots_count, inner), BF16),
             in_specs=[VMEM] + [ANY] * len(in_places),
             out_specs=VMEM,
             scratch_shapes=[
                 pltpu.VMEM((groups, width, inner), BF16),
-                pltpu.SemaphoreType.DMA((len(in_places),)),
+                pltpu.SemaphoreType.DMA((len(in_places), inner // step)),
             ],
             compiler_params=params(48),
             cost_estimate=cost(2 * slots_count * width * inner * groups, 8 << 20),
             name=name,
         )(slots_in, *held)
 
-    hidden_near = hidden_units(arrived, in_near, "hidden_near")
-    hidden_far = hidden_units(after(arrived, hidden_near), in_far, "hidden_far")
-    for k in range(2, dp_count, 2):
-        for held, place in zip(out_held, out_cuts):
-            out_near.append(held[k])
-            out_far.append(swap(after(held[k], hidden_near), "dp", 1))
-            out_places.append((k // 2, *place))
-    out_places += [(groups + at, *place) for at, *place in out_places]
-
-    answer = pl.pallas_call(
-        functools.partial(answer_kernel, out_places),
-        out_shape=jax.ShapeDtypeStruct((slots_count, width), BF16),
-        in_specs=[VMEM, VMEM] + [ANY] * len(out_places),
-        out_specs=VMEM,
-        scratch_shapes=[
-            pltpu.VMEM((dp_count, inner, width), BF16),
-            pltpu.VMEM((slots_count, width), F32),
-            pltpu.SemaphoreType.DMA((len(out_places),)),
-        ],
-        compiler_params=params(48),
-        cost_estimate=cost(2 * slots_count * width * inner * dp_count, 10 << 20),
-        name="answer",
-    )(hidden_near, hidden_far, *out_near, *out_far)
+    hidden = [hidden_units(arrived, in_near, "hidden_near")]
+    hidden.append(hidden_units(after(arrived, hidden[0]), in_far, "hidden_far"))
+
+    def answers(slices, weights, before, name):
+        count = len(slices)
+        used = sorted({of for of, _ in slices})
+        slices = [(used.index(of), place) for of, place in slices]
+        inputs = [hidden[of] for of in used]
+        extra = [] if before is None else [before]
+        return pl.pallas_call(
+            functools.partial(answer_kernel, slices, 256, len(used), bool(extra)),
+            out_shape=jax.ShapeDtypeStruct((slots_count, width), BF16 if name == "answer_far" else F32),
+            in_specs=[VMEM] * len(used) + [ANY] * count + [VMEM] * len(extra),
+            out_specs=VMEM,
+            scratch_shapes=[
+                pltpu.VMEM((count, inner, width), BF16),
+                pltpu.SemaphoreType.DMA((count, width // 256)),
+            ],
+            compiler_params=params(40),
+            cost_estimate=cost(2 * slots_count * width * inner * count, 10 << 20),
+            name=name,
+        )(*inputs, *weights, *extra)
+
+    distant = range(1, groups)
+    answer = answers([(0, 0), (1, 0)], [expert_out, out_own], None, "answer_own")
+    out_near = [after(out_held[2 * k], hidden[1]) for k in distant]
+    out_far = [swap(block, "dp", 1) for block in out_near]
+    answer = answers([(0, k) for k in distant], out_near, answer, "answer_near")
+    answer = answers([(1, k) for k in distant], out_far, answer, "answer_far")
     returned = lax.all_to_all(
         answer.reshape(exp_count, capacity, width), "expert", split_axis=0, concat_axis=0, tiled=True
     ).reshape(slots_count, width)
 
     return pl.pallas_call(
-        functools.partial(combine_kernel, exp_count, capacity, 1),
+        functools.partial(combine_kernel, exp_count, capacity),
         out_shape=jax.ShapeDtypeStruct((1, frames, width), BF16),
-        in_specs=[VMEM] * 4,
+        in_specs=[VMEM, VMEM, ANY, ANY],
         out_specs=VMEM,
+        scratch_shapes=[
+            pltpu.VMEM((frames, width), BF16),
+            pltpu.VMEM((slots_count, width), BF16),
+            pltpu.SemaphoreType.DMA((2,)),
+        ],
         compiler_params=params(32),
         cost_estimate=cost(4 * frames * slots_count * width, 3 << 20),
         name="combine",
-    )(mixed, gate, cols, returned)
+    )(gate, cols, mixed, returned)
 
 
 def solution(mesh):

time: 216 us -> 217 us (level)
  waiting for transfers between devices: 75.6 us -> 61.5 us
  Pallas kernels: 36.3 us -> 50.2 us
    all_to_all x1, waiting for transfers between devices: 23.5 us -> 11.2 us  [body(): lax.all_to_all(slots.reshape(exp_count, capacity, width), 'expert', split...]
    pallas_call x4 -> x7, Pallas kernels: 25.4 us -> 37.1 us  [the longest x2 17.8 us: hidden_units(): pl.pallas_call(functools.partial(hidden_kernel, in_places, step), out_sha...]
    unnamed x62 -> x87, local copies, waits for them, and re-layouts: 14.7 us -> 25.8 us
    slice x5 -> x0, local copies, waits for them, and re-layouts: 10 us -> none  [the longest x3 5.37 us: body(): lax.slice_in_dim(expert_in, a, a + n, axis=1)]
  transfers between devices with their start and end apart: 27 -> 27, of which waited for: 11 -> 13; matrix products, arithmetic and copies ran while one was open for 5% -> 1% of each run, Pallas kernels for 11% -> 20%
where the time goes in v6:
time: 217 us; the launch traced here: 213 us
  waiting for transfers between devices  61.5 us (28%)
  Pallas kernels  50.2 us (23%)
  blocking collectives  36.7 us (17%)
  local copies, waits for them, and re-layouts  27.2 us (13%)
  starting transfers between devices  24 us (11%)
  between operations  13.7 us (6%)
    ppermute x25, waiting for transfers between devices, swap(): return lax.ppermute(block, axis, [(i, i ^ mask) for i in range(count)])  50.2 us
    all_to_all x1, blocking collectives, body(): lax.all_to_all(answer.reshape(exp_count, capacity, width), 'expert', spli...  36.7 us
    unnamed x87, local copies, waits for them, and re-layouts  25.8 us
    ppermute x25, starting transfers between devices, swap(): return lax.ppermute(block, axis, [(i, i ^ mask) for i in range(count)])  17.9 us
    pallas_call x2, Pallas kernels, hidden_units(): pl.pallas_call(functools.partial(hidden_kernel, in_places, step), out_sha...  17.8 us
    pallas_call x3, Pallas kernels, answers(): pl.pallas_call(functools.partial(answer_kernel, slices, 256, len(used), b...  16 us
    all_to_all x1, waiting for transfers between devices, body(): lax.all_to_all(slots.reshape(exp_count, capacity, width), 'expert', split...  11.2 us
    pallas_call x1, Pallas kernels, body(): pl.pallas_call(functools.partial(attention_kernel, dp_count, exp_count),...  7.67 us
  transfers between devices with their start and end apart: 27, of which 13 were waited for; matrix products, arithmetic and copies ran while one was open for 1% of the time, Pallas kernels for 20%

profile of v6, /device:TPU:16, one launch (start us, length us, event | category | flops | bytes accessed | tf_op | source)
XLA Modules:
  0.0 213.4 jit_solution(9718570206875682052)
XLA Ops:
  6.5 1.7 copy-done.4
  10.7 1.5 collective-permute-start.6
  15.3 2.3 %collective-permute-start.3 = (bf16[3,128,256]{2,1,0:T(8,128)(2,1)S(1)}, bf16[3,128,256]{2,1,0:T(8,128)(2,1)S(1)}, u32[]{:S(2)}, u32[]{:S(2)}) collective-permute-start(bf16[3,128,256]{2,1,0:T(8,128)(2,1)S(1)} %constant_dynamic-slice_fusion.refs_0_), channel_id=1, source_target_pairs={{0,4},{1,5},{2,6},{3,7},{4,0},{5,1},{6,2},{7,3},{8,12},{9,13},{10,... | collective-permute-start | bytes 589832 | tf_op jit(solution)/shard_map/ppermute | solution.py:30
  18.2 11.6 %collective-permute-done.4.refs_6_ = bf16[3,128,256]{2,1,0:T(8,128)(2,1)S(1)} collective-permute-done((bf16[3,128,256]{2,1,0:T(8,128)(2,1)S(1)}, bf16[3,128,256]{2,1,0:T(8,128)(2,1)S(1)}, u32[]{:S(2)}, u32[]{:S(2)}) %collective-permute-start.4) | collective-permute-done | bytes 196640 | tf_op jit(solution)/shard_map/ppermute | solution.py:30
  29.8 1.5 collective-permute-start.1
  31.9 2.7 %collective-permute-done.3.refs_4_ = bf16[3,128,256]{2,1,0:T(8,128)(2,1)S(1)} collective-permute-done((bf16[3,128,256]{2,1,0:T(8,128)(2,1)S(1)}, bf16[3,128,256]{2,1,0:T(8,128)(2,1)S(1)}, u32[]{:S(2)}, u32[]{:S(2)}) %collective-permute-start.3) | collective-permute-done | bytes 196640 | tf_op jit(solution)/shard_map/ppermute | solution.py:30
  35.5 2.1 collective-permute-done.5.refs_3_
  38.7 1.3 norm.1
  40.8 1.6 collective-permute-start.8
  42.4 1.5 collective-permute-start.10
  44.4 15.8 %collective-permute-done.8.refs_2_ = bf16[1,368,1024]{2,1,0:T(8,128)(2,1)S(1)} collective-permute-done((bf16[1,368,1024]{2,1,0:T(8,128)(2,1)}, bf16[1,368,1024]{2,1,0:T(8,128)(2,1)S(1)}, u32[]{:S(2)}, u32[]{:S(2)}) %collective-permute-start.8) | collective-permute-done | bytes 753696 | tf_op jit(solution)/shard_map/ppermute | solution.py:30
  60.2 1.6 collective-permute-start.11
  61.8 7.7 %attention.1 = (bf16[256,256]{1,0:T(8,128)(2,1)S(1)}, bf16[256,256]{1,0:T(8,128)(2,1)S(1)}, bf16[256,256]{1,0:T(8,128)(2,1)S(1)}, bf16[256,256]{1,0:T(8,128)(2,1)S(1)}) custom-call(s32[1]{0:T(128)} %bitcast.5.me_ref, bf16[2,256,1024]{2,1,0:T(8,128)(2,1)S(1)} %get-tuple-element.42.near_ref, bf16[2,256,1024]{2,1,0:T(8,128)(2,1)S(1)} %collective-permute-done.7.far_ref, ...), custom_call_target="tpu_custom_call" | custom-call | flops 10485760 | bytes 20480 | tf_op jit(solution)/shard_map/attention/pallas_call | solution.py:329
  74.5 4.0 %collective-permute-done.14.refs_5_ = bf16[256,256]{1,0:T(8,128)(2,1)S(1)} collective-permute-done((bf16[256,256]{1,0:T(8,128)(2,1)}, bf16[256,256]{1,0:T(8,128)(2,1)S(1)}, u32[]{:S(2)}, u32[]{:S(2)}) %collective-permute-start.14) | collective-permute-done | bytes 131104 | tf_op jit(solution)/shard_map/ppermute | solution.py:30
  80.3 1.2 copy-done.11
  85.3 4.2 %mix.1 = (bf16[640,1024]{1,0:T(8,128)(2,1)}, bf16[256,1024]{1,0:T(8,128)(2,1)S(1)}, f32[256,128]{1,0:T(8,128)S(1)}) custom-call(s32[1]{0:T(128)} %bitcast.me_ref, f32[2,1024]{1,0:T(2,128)S(1)} %copy-done.34, f32[8,1024]{1,0:T(8,128)S(1)} %bitcast.19, s32[2,256]{1,0:T(2,128)S(1)} %copy.13.rows_ref, s32[256,2]{1,0:T(8,128)S(1)} %bitcast.17, ...), custom_call_target="tpu_custom_call" | custom-call | flops 3407872 | bytes 20480 | tf_op jit(solution)/shard_map/mix/pallas_call | solution.py:355
  90.1 1.5 collective-permute-done.16.refs_4_
  91.6 6.1 %all-to-all-start = ((bf16[8,80,1024]{2,1,0:T(8,128)(2,1)}), bf16[8,80,1024]{2,1,0:T(8,128)(2,1)S(1)}, u32[]{:S(2)}, u32[]{:S(2)}) async-start(bf16[8,80,1024]{2,1,0:T(8,128)(2,1)} %bitcast.6), calls=%async_computation | async-start | bytes 2621440 | tf_op jit(solution)/shard_map/all_to_all | solution.py:389
  99.3 6.8 %collective-permute-done.20.refs_3_ = bf16[1,144,1024]{2,1,0:T(8,128)(2,1)S(1)} collective-permute-done((bf16[1,144,1024]{2,1,0:T(8,128)(2,1)}, bf16[1,144,1024]{2,1,0:T(8,128)(2,1)S(1)}, u32[]{:S(2)}, u32[]{:S(2)}) %collective-permute-start.20) | collective-permute-done | bytes 294944 | tf_op jit(solution)/shard_map/ppermute | solution.py:30
  108.1 2.1 collective-permute-done.18.refs_1_
  111.9 1.3 copy-done.9
  113.3 1.4 copy-done.7
  114.6 11.2 %all-to-all-done = bf16[8,80,1024]{2,1,0:T(8,128)(2,1)S(1)} async-done(((bf16[8,80,1024]{2,1,0:T(8,128)(2,1)}), bf16[8,80,1024]{2,1,0:T(8,128)(2,1)S(1)}, u32[]{:S(2)}, u32[]{:S(2)}) %all-to-all-start) | async-done | bytes 1310752 | tf_op jit(solution)/shard_map/all_to_all | solution.py:389
  125.9 1.6 copy-done.5
  128.6 8.8 %hidden_near.1.refs_0_ = bf16[2,640,1024]{2,1,0:T(8,128)(2,1)} custom-call(bf16[640,1024]{1,0:T(8,128)(2,1)S(1)} %bitcast.12, bf16[1,1024,1024]{2,1,0:T(8,128)(2,1)S(1)} %copy-done.5, bf16[1,320,1024]{2,1,0:T(8,128)(2,1)S(1)} %copy-done.15, bf16[1,368,1024]{2,1,0:T(8,128)(2,1)S(1)} %collective-permute-done.8.refs_2_, ...), custom_call_target="tpu_custom_call" | custom-call | flops 10485760 | bytes 32768 | tf_op jit(solution)/shard_map/hidden_near/pallas_call | solution.py:398
  140.5 8.9 %hidden_far.1.refs_1_.refs_0_ = bf16[2,640,1024]{2,1,0:T(8,128)(2,1)} custom-call(bf16[640,1024]{1,0:T(8,128)(2,1)S(1)} %bitcast.13, bf16[1,1024,1024]{2,1,0:T(8,128)(2,1)S(1)} %copy-done.10, bf16[1,320,1024]{2,1,0:T(8,128)(2,1)S(1)} %copy-done.17, bf16[1,368,1024]{2,1,0:T(8,128)(2,1)S(1)} %copy-done.13, bf16[1,144,1024]{2,1,0:T(8,128)(2,1)S(1)} %copy-done.24, ...), custom_call_target="tpu_custom_call" | custom-call | flops 10485760 | bytes 32768 | tf_op jit(solution)/shard_map/hidden_far/pallas_call | solution.py:398
  149.6 1.7 copy-done.1
  151.3 7.5 %answer_own.1.refs_2_ = f32[640,1024]{1,0:T(8,128)S(1)} custom-call(bf16[2,640,1024]{2,1,0:T(8,128)(2,1)S(1)} %copy-done.3, bf16[2,640,1024]{2,1,0:T(8,128)(2,1)S(1)} %copy-done.1, bf16[1,1024,1024]{2,1,0:T(8,128)(2,1)S(1)} %copy-done.6, bf16[1,1024,1024]{2,1,0:T(8,128)(2,1)S(1)} %copy-done.8), custom_call_target="tpu_custom_call" | custom-call | flops 10485760 | bytes 40960 | tf_op jit(solution)/shard_map/answer_own/pallas_call | solution.py:421
  158.9 4.7 %answer_near.1.refs_2_ = f32[640,1024]{1,0:T(8,128)S(1)} custom-call(bf16[2,640,1024]{2,1,0:T(8,128)(2,1)S(1)} %copy-done.3, bf16[1,1024,1024]{2,1,0:T(8,128)(2,1)} %collective-permute-done.23.refs_1_, f32[640,1024]{1,0:T(8,128)S(1)} %answer_own.1.refs_2_), custom_call_target="tpu_custom_call" | custom-call | flops 5242880 | bytes 40960 | tf_op jit(solution)/shard_map/answer_near/pallas_call | solution.py:421
  163.6 3.8 %answer_far.1 = bf16[640,1024]{1,0:T(8,128)(2,1)S(1)} custom-call(bf16[2,640,1024]{2,1,0:T(8,128)(2,1)S(1)} %copy-done.2, bf16[1,1024,1024]{2,1,0:T(8,128)(2,1)S(1)} %collective-permute-done.24.refs_1_, f32[640,1024]{1,0:T(8,128)S(1)} %answer_near.1.refs_2_), custom_call_target="tpu_custom_call" | custom-call | flops 5242880 | bytes 40960 | tf_op jit(solution)/shard_map/answer_far/pallas_call | solution.py:421
  167.4 36.7 %all_to_all.10 = bf16[8,80,1024]{2,1,0:T(8,128)(2,1)S(1)} all-to-all(bf16[8,80,1024]{2,1,0:T(8,128)(2,1)S(1)} %bitcast.15), channel_id=1, replica_groups=mesh['dp'=4,'expert'=8] {'expert'}, dimensions={0} | all-to-all | bytes 2621440 | tf_op jit(solution)/shard_map/all_to_all | solution.py:441
  204.1 2.4 %combine.1 = bf16[1,256,1024]{2,1,0:T(8,128)(2,1)} custom-call(f32[256,128]{1,0:T(8,128)S(1)} %copy-done.26, s32[256,2]{1,0:T(8,128)S(1)} %bitcast.18, bf16[256,1024]{1,0:T(8,128)(2,1)S(1)} %get-tuple-element.58.mixed_in, bf16[640,1024]{1,0:T(8,128)(2,1)S(1)} %bitcast.14), custom_call_target="tpu_custom_call" | custom-call | flops 2621440 | bytes 12288 | tf_op jit(solution)/shard_map/combine/pallas_call | solution.py:445
  (127 shorter events, 30.7 us)
Async XLA Ops:
  6.5 64.9 %all-gather.2.cloned.1.call-start = ((), (), s32[]{:S(2)}) async-start(), calls=%async_computation.2 | async-start | bytes 1179648 | tf_op jit(solution)/shard_map/all_gather | solution.py:284
  8.2 9.4 %copy-start.40 = (s32[16,2]{0,1:T(2,128)S(1)}, s32[16,2]{0,1:T(2,128)}, u32[]{:S(2)}) copy-start(s32[16,2]{0,1:T(2,128)} %param.10) | copy-start | bytes 388
  8.2 30.5 %copy-start.34 = (f32[2,1024]{1,0:T(2,128)S(1)}, f32[2,1024]{1,0:T(2,128)}, u32[]{:S(2)}) copy-start(f32[2,1024]{1,0:T(2,128)} %gain_ref.3) | copy-start | bytes 24580
  10.7 27.9 %collective-permute-start.6 = (bf16[1,320,1024]{2,1,0:T(8,128)(2,1)}, bf16[1,320,1024]{2,1,0:T(8,128)(2,1)S(1)}, u32[]{:S(2)}, u32[]{:S(2)}) collective-permute-start(bf16[1,320,1024]{2,1,0:T(8,128)(2,1)} %get-tuple-element.39), channel_id=1, source_target_pairs={{0,16},{8,24},{16,0},{24,8},{1,17},{9,25},{17,1},{25,9},{2,18},{10... | collective-permute-start | bytes 1966088 | tf_op jit(solution)/shard_map/ppermute | solution.py:30
  13.0 25.7 %collective-permute-start = (bf16[1,256,1024]{2,1,0:T(8,128)(2,1)S(1)}, bf16[1,256,1024]{2,1,0:T(8,128)(2,1)S(1)}, u32[]{:S(2)}, u32[]{:S(2)}) collective-permute-start(bf16[1,256,1024]{2,1,0:T(8,128)(2,1)S(1)} %copy-done.20), channel_id=1, source_target_pairs={{0,16},{8,24},{16,0},{24,8},{1,17},{9,25},{17,1},{25,9},{2,18},{10... | collective-permute-start | bytes 1572872 | tf_op jit(solution)/shard_map/ppermute | solution.py:30
  13.6 16.3 %collective-permute-start.4 = (bf16[3,128,256]{2,1,0:T(8,128)(2,1)S(1)}, bf16[3,128,256]{2,1,0:T(8,128)(2,1)S(1)}, u32[]{:S(2)}, u32[]{:S(2)}) collective-permute-start(bf16[3,128,256]{2,1,0:T(8,128)(2,1)S(1)} %constant_dynamic-slice_fusion.refs_0_), channel_id=1, source_target_pairs={{0,6},{1,7},{2,4},{3,5},{4,2},{5,3},{6,0},{7,1},{8,14},{9,15},{10,... | collective-permute-start | bytes 589832 | tf_op jit(solution)/shard_map/ppermute | solution.py:30
  14.1 17.3 %collective-permute-start.2 = (bf16[3,128,256]{2,1,0:T(8,128)(2,1)S(1)}, bf16[3,128,256]{2,1,0:T(8,128)(2,1)S(1)}, u32[]{:S(2)}, u32[]{:S(2)}) collective-permute-start(bf16[3,128,256]{2,1,0:T(8,128)(2,1)S(1)} %constant_dynamic-slice_fusion.refs_0_), channel_id=1, source_target_pairs={{0,2},{1,3},{2,0},{3,1},{4,6},{5,7},{6,4},{7,5},{8,10},{9,11},{10,... | collective-permute-start | bytes 589832 | tf_op jit(solution)/shard_map/ppermute | solution.py:30
  15.3 19.2 %collective-permute-start.3 = (bf16[3,128,256]{2,1,0:T(8,128)(2,1)S(1)}, bf16[3,128,256]{2,1,0:T(8,128)(2,1)S(1)}, u32[]{:S(2)}, u32[]{:S(2)}) collective-permute-start(bf16[3,128,256]{2,1,0:T(8,128)(2,1)S(1)} %constant_dynamic-slice_fusion.refs_0_), channel_id=1, source_target_pairs={{0,4},{1,5},{2,6},{3,7},{4,0},{5,1},{6,2},{7,3},{8,12},{9,13},{10,... | collective-permute-start | bytes 589832 | tf_op jit(solution)/shard_map/ppermute | solution.py:30
  29.8 5.7 %collective-permute-start.1 = (bf16[3,128,256]{2,1,0:T(8,128)(2,1)S(1)}, bf16[3,128,256]{2,1,0:T(8,128)(2,1)S(1)}, u32[]{:S(2)}, u32[]{:S(2)}) collective-permute-start(bf16[3,128,256]{2,1,0:T(8,128)(2,1)S(1)} %constant_dynamic-slice_fusion.refs_0_), channel_id=1, source_target_pairs={{0,1},{1,0},{2,3},{3,2},{4,5},{5,4},{6,7},{7,6},{8,9},{9,8},{10,11... | collective-permute-start | bytes 589832 | tf_op jit(solution)/shard_map/ppermute | solution.py:30
  31.3 6.3 %collective-permute-start.5 = (bf16[3,128,256]{2,1,0:T(8,128)(2,1)S(1)}, bf16[3,128,256]{2,1,0:T(8,128)(2,1)S(1)}, u32[]{:S(2)}, u32[]{:S(2)}) collective-permute-start(bf16[3,128,256]{2,1,0:T(8,128)(2,1)S(1)} %collective-permute-done.2.refs_2_), channel_id=1, source_target_pairs={{0,1},{1,0},{2,3},{3,2},{4,5},{5,4},{6,7},{7,6},{8,9},{9,8},{10,11... | collective-permute-start | bytes 589832 | tf_op jit(solution)/shard_map/ppermute | solution.py:30
  40.8 39.3 %copy-start.42 = (s32[1,256,2]{1,2,0:T(2,128)S(1)}, s32[1,256,2]{1,2,0:T(2,128)}, u32[]{:S(2)}) copy-start(s32[1,256,2]{1,2,0:T(2,128)} %param.11) | copy-start | bytes 6148
  40.8 39.5 %copy-start.33 = (f32[1024,8]{0,1:T(8,128)S(1)}, f32[1024,8]{0,1:T(8,128)}, u32[]{:S(2)}) copy-start(f32[1024,8]{0,1:T(8,128)} %param.15) | copy-start | bytes 98308
  40.8 19.5 %collective-permute-start.7 = (bf16[2,256,1024]{2,1,0:T(8,128)(2,1)S(1)}, bf16[2,256,1024]{2,1,0:T(8,128)(2,1)S(1)}, u32[]{:S(2)}, u32[]{:S(2)}) collective-permute-start(bf16[2,256,1024]{2,1,0:T(8,128)(2,1)S(1)} %get-tuple-element.42.near_ref), channel_id=1, source_target_pairs={{0,8},{8,0},{16,24},{24,16},{1,9},{9,1},{17,25},{25,17},{2,10},{10... | collective-permute-start | bytes 3145736 | tf_op jit(solution)/shard_map/ppermute | solution.py:30
  40.8 19.5 %collective-permute-start.8 = (bf16[1,368,1024]{2,1,0:T(8,128)(2,1)}, bf16[1,368,1024]{2,1,0:T(8,128)(2,1)S(1)}, u32[]{:S(2)}, u32[]{:S(2)}) collective-permute-start(bf16[1,368,1024]{2,1,0:T(8,128)(2,1)} %copy-done.35), channel_id=1, source_target_pairs={{0,16},{8,24},{16,0},{24,8},{1,17},{9,25},{17,1},{25,9},{2,18},{10... | collective-permute-start | bytes 2261000 | tf_op jit(solution)/shard_map/ppermute | solution.py:30
  42.4 17.9 %collective-permute-start.10 = (bf16[3,128,256]{2,1,0:T(8,128)(2,1)S(1)}, bf16[3,128,256]{2,1,0:T(8,128)(2,1)S(1)}, u32[]{:S(2)}, u32[]{:S(2)}) collective-permute-start(bf16[3,128,256]{2,1,0:T(8,128)(2,1)S(1)} %collective-permute-done.4.refs_6_), channel_id=1, source_target_pairs={{0,1},{1,0},{2,3},{3,2},{4,5},{5,4},{6,7},{7,6},{8,9},{9,8},{10,11... | collective-permute-start | bytes 589832 | tf_op jit(solution)/shard_map/ppermute | solution.py:30
  43.8 16.4 %collective-permute-start.9 = (bf16[3,128,256]{2,1,0:T(8,128)(2,1)S(1)}, bf16[3,128,256]{2,1,0:T(8,128)(2,1)S(1)}, u32[]{:S(2)}, u32[]{:S(2)}) collective-permute-start(bf16[3,128,256]{2,1,0:T(8,128)(2,1)S(1)} %collective-permute-done.3.refs_4_), channel_id=1, source_target_pairs={{0,1},{1,0},{2,3},{3,2},{4,5},{5,4},{6,7},{7,6},{8,9},{9,8},{10,11... | collective-permute-start | bytes 589832 | tf_op jit(solution)/shard_map/ppermute | solution.py:30
  60.2 11.2 %collective-permute-start.11 = (bf16[1,144,1024]{2,1,0:T(8,128)(2,1)}, bf16[1,144,1024]{2,1,0:T(8,128)(2,1)}, u32[]{:S(2)}, u32[]{:S(2)}) collective-permute-start(bf16[1,144,1024]{2,1,0:T(8,128)(2,1)} %copy-done.37), channel_id=1, source_target_pairs={{0,16},{8,24},{16,0},{24,8},{1,17},{9,25},{17,1},{25,9},{2,18},{10... | collective-permute-start | bytes 884744 | tf_op jit(solution)/shard_map/ppermute | solution.py:30
  71.4 8.8 %collective-permute-start.12 = (bf16[1024,512]{1,0:T(8,128)(2,1)}, bf16[1024,512]{1,0:T(8,128)(2,1)S(1)}, u32[]{:S(2)}, u32[]{:S(2)}) collective-permute-start(bf16[1024,512]{1,0:T(8,128)(2,1)} %all-gather.2.cloned.1.call-done.refs_1_), channel_id=1, source_target_pairs={{0,8},{8,0},{16,24},{24,16},{1,9},{9,1},{17,25},{25,17},{2,10},{10... | collective-permute-start | bytes 3145736 | tf_op jit(solution)/shard_map/ppermute | solution.py:30
  71.5 3.1 %collective-permute-start.13 = (bf16[256,256]{1,0:T(8,128)(2,1)}, bf16[256,256]{1,0:T(8,128)(2,1)S(1)}, u32[]{:S(2)}, u32[]{:S(2)}) collective-permute-start(bf16[256,256]{1,0:T(8,128)(2,1)} %copy-done.39), channel_id=1, source_target_pairs={{0,8},{8,0},{16,24},{24,16},{1,9},{9,1},{17,25},{25,17},{2,10},{10... | collective-permute-start | bytes 393224 | tf_op jit(solution)/shard_map/ppermute | solution.py:30
  72.0 6.6 %collective-permute-start.14 = (bf16[256,256]{1,0:T(8,128)(2,1)}, bf16[256,256]{1,0:T(8,128)(2,1)S(1)}, u32[]{:S(2)}, u32[]{:S(2)}) collective-permute-start(bf16[256,256]{1,0:T(8,128)(2,1)} %copy-done.38), channel_id=1, source_target_pairs={{0,16},{8,24},{16,0},{24,8},{1,17},{9,25},{17,1},{25,9},{2,18},{10... | collective-permute-start | bytes 393224 | tf_op jit(solution)/shard_map/ppermute | solution.py:30
  72.5 7.1 %collective-permute-start.15 = (bf16[256,256]{1,0:T(8,128)(2,1)S(1)}, bf16[256,256]{1,0:T(8,128)(2,1)S(1)}, u32[]{:S(2)}, u32[]{:S(2)}) collective-permute-start(bf16[256,256]{1,0:T(8,128)(2,1)S(1)} %get-tuple-element.55), channel_id=1, source_target_pairs={{0,24},{8,16},{16,8},{24,0},{1,25},{9,17},{17,9},{25,1},{2,26},{10... | collective-permute-start | bytes 393224 | tf_op jit(solution)/shard_map/ppermute | solution.py:30
  79.6 12.0 %collective-permute-start.16 = (bf16[1,192,1024]{2,1,0:T(8,128)(2,1)}, bf16[1,192,1024]{2,1,0:T(8,128)(2,1)}, u32[]{:S(2)}, u32[]{:S(2)}) collective-permute-start(bf16[1,192,1024]{2,1,0:T(8,128)(2,1)} %copy-done.36), channel_id=1, source_target_pairs={{0,16},{8,24},{16,0},{24,8},{1,17},{9,25},{17,1},{25,9},{2,18},{10... | collective-permute-start | bytes 1179656 | tf_op jit(solution)/shard_map/ppermute | solution.py:30
  91.6 34.3 %all-to-all-start = ((bf16[8,80,1024]{2,1,0:T(8,128)(2,1)}), bf16[8,80,1024]{2,1,0:T(8,128)(2,1)S(1)}, u32[]{:S(2)}, u32[]{:S(2)}) async-start(bf16[8,80,1024]{2,1,0:T(8,128)(2,1)} %bitcast.6), calls=%async_computation | async-start | bytes 2621440 | tf_op jit(solution)/shard_map/all_to_all | solution.py:389
  97.8 14.2 %collective-permute-start.17 = (bf16[1,1024,1024]{2,1,0:T(8,128)(2,1)}, bf16[1,1024,1024]{2,1,0:T(8,128)(2,1)S(1)}, u32[]{:S(2)}, u32[]{:S(2)}) collective-permute-start(bf16[1,1024,1024]{2,1,0:T(8,128)(2,1)} %refs_0_.3), channel_id=1, source_target_pairs={{0,8},{8,0},{16,24},{24,16},{1,9},{9,1},{17,25},{25,17},{2,10},{10... | collective-permute-start | bytes 6291464 | tf_op jit(solution)/shard_map/ppermute | solution.py:30
  97.8 15.5 %collective-permute-start.22 = (bf16[1,1024,1024]{2,1,0:T(8,128)(2,1)}, bf16[1,1024,1024]{2,1,0:T(8,128)(2,1)S(1)}, u32[]{:S(2)}, u32[]{:S(2)}) collective-permute-start(bf16[1,1024,1024]{2,1,0:T(8,128)(2,1)} %refs_2_.1), channel_id=1, source_target_pairs={{0,8},{8,0},{16,24},{24,16},{1,9},{9,1},{17,25},{25,17},{2,10},{10... | collective-permute-start | bytes 6291464 | tf_op jit(solution)/shard_map/ppermute | solution.py:30
  98.3 51.2 %collective-permute-start.23 = (bf16[1,1024,1024]{2,1,0:T(8,128)(2,1)}, bf16[1,1024,1024]{2,1,0:T(8,128)(2,1)}, u32[]{:S(2)}, u32[]{:S(2)}) collective-permute-start(bf16[1,1024,1024]{2,1,0:T(8,128)(2,1)} %refs_2_.1), channel_id=1, source_target_pairs={{0,16},{8,24},{16,0},{24,8},{1,17},{9,25},{17,1},{25,9},{2,18},{10... | collective-permute-start | bytes 6291464 | tf_op jit(solution)/shard_map/ppermute | solution.py:30
  98.8 8.2 %collective-permute-start.21 = (bf16[1,192,1024]{2,1,0:T(8,128)(2,1)}, bf16[1,192,1024]{2,1,0:T(8,128)(2,1)S(1)}, u32[]{:S(2)}, u32[]{:S(2)}) collective-permute-start(bf16[1,192,1024]{2,1,0:T(8,128)(2,1)} %collective-permute-done.16.refs_4_), channel_id=1, source_target_pairs={{0,8},{8,0},{16,24},{24,16},{1,9},{9,1},{17,25},{25,17},{2,10},{10... | collective-permute-start | bytes 1179656 | tf_op jit(solution)/shard_map/ppermute | solution.py:30
  98.8 7.3 %collective-permute-start.20 = (bf16[1,144,1024]{2,1,0:T(8,128)(2,1)}, bf16[1,144,1024]{2,1,0:T(8,128)(2,1)S(1)}, u32[]{:S(2)}, u32[]{:S(2)}) collective-permute-start(bf16[1,144,1024]{2,1,0:T(8,128)(2,1)} %collective-permute-done.11.refs_3_), channel_id=1, source_target_pairs={{0,8},{8,0},{16,24},{24,16},{1,9},{9,1},{17,25},{25,17},{2,10},{10... | collective-permute-start | bytes 884744 | tf_op jit(solution)/shard_map/ppermute | solution.py:30
  106.8 4.2 %collective-permute-start.19 = (bf16[1,368,1024]{2,1,0:T(8,128)(2,1)S(1)}, bf16[1,368,1024]{2,1,0:T(8,128)(2,1)S(1)}, u32[]{:S(2)}, u32[]{:S(2)}) collective-permute-start(bf16[1,368,1024]{2,1,0:T(8,128)(2,1)S(1)} %collective-permute-done.8.refs_2_), channel_id=1, source_target_pairs={{0,8},{8,0},{16,24},{24,16},{1,9},{9,1},{17,25},{25,17},{2,10},{10... | collective-permute-start | bytes 2261000 | tf_op jit(solution)/shard_map/ppermute | solution.py:30
  107.7 2.5 %collective-permute-start.18 = (bf16[1,320,1024]{2,1,0:T(8,128)(2,1)}, bf16[1,320,1024]{2,1,0:T(8,128)(2,1)S(1)}, u32[]{:S(2)}, u32[]{:S(2)}) collective-permute-start(bf16[1,320,1024]{2,1,0:T(8,128)(2,1)} %copy-done.14), channel_id=1, source_target_pairs={{0,8},{8,0},{16,24},{24,16},{1,9},{9,1},{17,25},{25,17},{2,10},{10... | collective-permute-start | bytes 1966088 | tf_op jit(solution)/shard_map/ppermute | solution.py:30
  149.4 14.1 %collective-permute-start.24 = (bf16[1,1024,1024]{2,1,0:T(8,128)(2,1)}, bf16[1,1024,1024]{2,1,0:T(8,128)(2,1)S(1)}, u32[]{:S(2)}, u32[]{:S(2)}) collective-permute-start(bf16[1,1024,1024]{2,1,0:T(8,128)(2,1)} %collective-permute-done.23.refs_1_), channel_id=1, source_target_pairs={{0,8},{8,0},{16,24},{24,16},{1,9},{9,1},{17,25},{25,17},{2,10},{10... | collective-permute-start | bytes 6291464 | tf_op jit(solution)/shard_map/ppermute | solution.py:30
  167.4 36.7 %copy-start.26 = (f32[256,128]{1,0:T(8,128)S(1)}, f32[256,128]{1,0:T(8,128)}, u32[]{:S(2)}) copy-start(f32[256,128]{1,0:T(8,128)} %copy-done.25) | copy-start | bytes 393220
  (38 other events, 96.1 us)
Sparse Core Ops, SparseCore 0:
  13.1 45.6 all-gather.1

commit v7 on v6

--- a/solution.py
+++ b/solution.py
@@ -52,17 +52,11 @@
 
 def attention_kernel(count, shards, me_ref, near_ref, far_ref, *refs):
     pieces, outs = refs[:shards], refs[shards : shards + count]
-    weights, held, sems, out_sems = refs[shards + count :]
+    weights, held, sems = refs[shards + count :]
     depth, cols = pieces[0].shape[1:]
     me = me_ref[0]
-    copies = []
     for k in range(shards):
-        rows = pl.ds(pl.multiple_of((me ^ k) * depth, depth), depth)
-        copy = pltpu.make_async_copy(pieces[k], weights.at[:, rows, :], sems.at[k])
-        copy.start()
-        copies.append(copy)
-    for copy in copies:
-        copy.wait()
+        weights[:, pl.ds(pl.multiple_of((me ^ k) * depth, depth), depth), :] = pieces[k][...]
     sent = []
     frames = near_ref.shape[1]
     head = lax.broadcasted_iota(jnp.int32, (frames, cols), 1) // HEAD_DIM
@@ -87,33 +81,25 @@
             probs = (exps * norm).astype(BF16)
             total = jnp.where(mine, jnp.dot(probs, val, preferred_element_type=F32), total)
         held[k] = total.astype(BF16)
-        copy = pltpu.make_async_copy(held.at[k], outs[k], out_sems.at[k])
+        copy = pltpu.make_async_copy(held.at[k], outs[k], sems.at[k])
         copy.start()
         sent.append(copy)
     for copy in sent:
         copy.wait()
 
 
-def mix_kernel(count, experts, capacity, me_ref, gain_ref, router_ref, rows_ref, cols_ref, *refs):
-    sources, refs = refs[: count + 3], refs[count + 3 :]
-    slots_out, mixed_out, gate_ref, own_ref, near_ref, far_ref, blocks, wide, slots_ref, mixed_ref, sems = refs
-    places = [own_ref, near_ref, far_ref, *[blocks.at[k] for k in range(count)]]
-    copies = [
-        pltpu.make_async_copy(source, place, sems.at[k])
-        for k, (source, place) in enumerate(zip(sources, places))
-    ]
-    for copy in copies:
-        copy.start()
-    _, frames, depth = blocks.shape
+def mix_kernel(
+    count, experts, capacity, me_ref, gain_ref, router_ref, rows_ref, cols_ref, own_ref, near_ref, far_ref, *refs
+):
+    blocks, (slots_out, mixed_out, gate_ref, wide, slots_ref, mixed_ref, sems) = refs[:count], refs[count:]
+    frames, depth = blocks[0].shape
     me = me_ref[0]
     part = near_ref.shape[1]
-    for copy in copies:
-        copy.wait()
     for held, side in ((near_ref, me & 1), (far_ref, 1 - (me & 1))):
         total = jnp.zeros((frames, part), F32)
         for k in range(count):
             rows = pl.ds(pl.multiple_of((me ^ k) * depth, depth), depth)
-            total += jnp.dot(blocks[k], held[rows, :], preferred_element_type=F32)
+            total += jnp.dot(blocks[k][...], held[rows, :], preferred_element_type=F32)
         wide[:, pl.ds(pl.multiple_of(side * part, part), part)] = total
     mixed = (own_ref[...].astype(F32) + wide[...]).astype(BF16)
     mixed_ref[...] = mixed
@@ -154,7 +140,7 @@
 def split_kernel(cuts, whole_ref, *refs):
     outs, sems = refs[: len(cuts)], refs[len(cuts)]
     copies = [
-        pltpu.make_async_copy(whole_ref.at[:, pl.ds(start, size), :], outs[k], sems.at[k])
+        pltpu.make_async_copy(whole_ref.at[:, :, pl.ds(start, size)], outs[k], sems.at[k])
         for k, (start, size) in enumerate(cuts)
     ]
     for copy in copies:
@@ -163,56 +149,29 @@
         copy.wait()
 
 
-def fetch(cuts, step, refs, buf, sems):
-    count, _, cols = buf.shape
-    copies = {(at, part): [] for at in range(count) for part in range(0, cols, step)}
-    for at, part in copies:
-        for k, (of, start, size) in enumerate(cuts):
-            if of == at:
-                where = pl.ds(part, step)
-                copy = pltpu.make_async_copy(
-                    refs[k].at[0, :, where],
-                    buf.at[at, pl.ds(start, size), where],
-                    sems.at[k, part // step],
-                )
-                copy.start()
-                copies[at, part].append(copy)
-    return copies
-
-
 def hidden_kernel(cuts, step, slots_ref, *refs):
-    hidden_ref, buf, sems = refs[len(cuts) :]
-    for (at, part), pieces in fetch(cuts, step, refs, buf, sems).items():
-        for piece in pieces:
-            piece.wait()
-        where = slice(part, part + step)
-        half = 0.5 * jnp.dot(slots_ref[...], buf[at, :, where], preferred_element_type=F32)
-        hidden_ref[at, :, where] = (half + half * jnp.tanh(half)).astype(BF16)
+    hidden_ref = refs[len(cuts)]
+    for weight, (at, start, size) in zip(refs, cuts):
+        for part in range(0, size, step):
+            end = min(part + step, size)
+            half = 0.5 * jnp.dot(slots_ref[...], weight[0, :, part:end], preferred_element_type=F32)
+            hidden_ref[at, :, start + part : start + end] = (half + half * jnp.tanh(half)).astype(BF16)
 
 
 def answer_kernel(slices, step, held, before, *refs):
     hidden, weights, refs = refs[:held], refs[held : held + len(slices)], refs[held + len(slices) :]
-    total_ref = refs[0] if before else None
-    answer_ref, buf, sems = refs[1:] if before else refs
-    cuts = [(at, 0, buf.shape[1]) for at in range(len(slices))]
-    copies = fetch(cuts, step, weights, buf, sems)
-    for part in range(0, buf.shape[2], step):
+    answer_ref = refs[-1]
+    for part in range(0, answer_ref.shape[1], step):
         where = slice(part, part + step)
-        total = total_ref[:, where] if before else 0.0
-        for at, (of, place) in enumerate(slices):
-            for piece in copies[at, part]:
-                piece.wait()
-            total += jnp.dot(hidden[of][place], buf[at, :, where], preferred_element_type=F32)
+        total = refs[0][:, where] if before else 0.0
+        for weight, (of, place) in zip(weights, slices):
+            total += jnp.dot(hidden[of][place], weight[0, :, where], preferred_element_type=F32)
         answer_ref[:, where] = total.astype(answer_ref.dtype)
 
 
-def combine_kernel(experts, capacity, gate_ref, cols_ref, mixed_in, answer_in, out_ref, mixed_ref, answer_ref, sems):
-    copies = [
-        pltpu.make_async_copy(answer_in, answer_ref, sems.at[0]),
-        pltpu.make_async_copy(mixed_in, mixed_ref, sems.at[1]),
-    ]
-    for copy in copies:
-        copy.start()
+def combine_kernel(experts, capacity, gate_ref, cols_ref, answer_ref, mixed_in, out_ref, mixed_ref, sems):
+    copy = pltpu.make_async_copy(mixed_in, mixed_ref, sems.at[0])
+    copy.start()
     frames = mixed_ref.shape[0]
     first, second = cols_ref[:, 0:1], cols_ref[:, 1:2]
     lane = lax.broadcasted_iota(jnp.int32, (frames, experts), 1)
@@ -228,8 +187,7 @@
         place = jnp.sum(jnp.where(lane == chosen, rank, 0.0), axis=1, keepdims=True)
         picks.append((slot == place).astype(F32).astype(BF16))
     gate = gate_ref[:, 0:1]
-    for copy in copies:
-        copy.wait()
+    copy.wait()
     step = mixed_ref.shape[1] // 2
     for part in range(0, 2 * step, step):
         where = slice(part, part + step)
@@ -249,7 +207,7 @@
 
 
 def cut(size, shares):
-    starts = [sum(shares[:i]) * size // sum(shares) for i in range(len(shares) + 1)]
+    starts = [round(sum(shares[:i]) * size / sum(shares) / 128) * 128 for i in range(len(shares) + 1)]
     return [(a, b - a) for a, b in zip(starts, starts[1:])]
 
 
@@ -288,14 +246,14 @@
         tiled=True,
     )
 
-    in_cuts = cut(width, (20, 23, 9, 12))
+    in_cuts = cut(inner, (2, 3, 1, 2))
     in_chunks = pl.pallas_call(
         functools.partial(split_kernel, in_cuts),
-        out_shape=[jax.ShapeDtypeStruct((1, n, inner), BF16) for _, n in in_cuts],
+        out_shape=[jax.ShapeDtypeStruct((1, width, n), BF16) for _, n in in_cuts],
         in_specs=[HBM],
         out_specs=[HBM] * len(in_cuts),
         scratch_shapes=[pltpu.SemaphoreType.DMA((len(in_cuts),))],
-        compiler_params=params(32),
+        compiler_params=params(20),
         cost_estimate=cost(0, 4 << 20),
         name="split",
     )(expert_in)
@@ -317,7 +275,7 @@
         ),
         in_specs=[SMEM, VMEM] + [VMEM] * groups,
         out_specs=(VMEM, VMEM),
-        compiler_params=params(32),
+        compiler_params=params(20),
         cost_estimate=cost(groups * frames * width * 8, groups * frames * width * 4),
         name="norm",
     )(place, norm_gains, *[raw[2 * k] for k in range(groups)])
@@ -329,15 +287,14 @@
     contexts = pl.pallas_call(
         functools.partial(attention_kernel, dp_count, exp_count),
         out_shape=[jax.ShapeDtypeStruct((frames, share), BF16)] * dp_count,
-        in_specs=[SMEM, VMEM, VMEM] + [ANY] * exp_count,
-        out_specs=[ANY] * dp_count,
+        in_specs=[SMEM, VMEM, VMEM] + [VMEM] * exp_count,
+        out_specs=[HBM] * dp_count,
         scratch_shapes=[
             pltpu.VMEM((3, width, share), BF16),
             pltpu.VMEM((dp_count, frames, share), BF16),
-            pltpu.SemaphoreType.DMA((exp_count,)),
             pltpu.SemaphoreType.DMA((dp_count,)),
         ],
-        compiler_params=params(32),
+        compiler_params=params(20),
         cost_estimate=cost(
             2 * frames * width * width * 3 + 16 * frames * frames * width, 5 << 20, frames * frames * 16
         ),
@@ -359,26 +316,22 @@
             jax.ShapeDtypeStruct((frames, width), BF16),
             jax.ShapeDtypeStruct((frames, 128), F32),
         ),
-        in_specs=[SMEM] + [VMEM] * 4 + [ANY] * (3 + dp_count),
-        out_specs=(ANY, ANY, VMEM),
+        in_specs=[SMEM] + [VMEM] * (7 + dp_count),
+        out_specs=(HBM, HBM, VMEM),
         scratch_shapes=[
-            pltpu.VMEM((frames, width), BF16),
-            pltpu.VMEM((width, rows), BF16),
-            pltpu.VMEM((width, rows), BF16),
-            pltpu.VMEM((dp_count, frames, share), BF16),
             pltpu.VMEM((frames, width), F32),
             pltpu.VMEM((slots_count, width), BF16),
             pltpu.VMEM((frames, width), BF16),
-            pltpu.SemaphoreType.DMA((dp_count + 3,)),
+            pltpu.SemaphoreType.DMA((2,)),
         ],
-        compiler_params=params(32),
+        compiler_params=params(20),
         cost_estimate=cost(2 * frames * width * (width + slots_count), 5 << 20),
         name="mix",
     )(me[None], norm_gains, router.T, cols.T, cols, stream, proj_near, proj_far, contexts[0], *crossed)
 
     slots = after(slots, in_held[3])
     out_held = spread_over(after(expert_out, (in_held[3], mixed)), "dp", 2)
-    in_far, in_near, in_places = [swap(after(expert_in, mixed), "dp", 1)], [expert_in], [(0, 0, width)]
+    in_far, in_near, in_places = [swap(after(expert_in, mixed), "dp", 1)], [expert_in], [(0, 0, inner)]
     out_own = swap(after(expert_out, mixed), "dp", 1)
     for k in range(2, dp_count, 2):
         for held, place in zip(in_held, in_cuts):
@@ -392,19 +345,15 @@
 
 
     arrived = after(arrived, (in_far, out_own))
-    step = min(256, inner)
+    step = min(512, inner)
 
     def hidden_units(slots_in, held, name):
         return pl.pallas_call(
             functools.partial(hidden_kernel, in_places, step),
             out_shape=jax.ShapeDtypeStruct((groups, slots_count, inner), BF16),
-            in_specs=[VMEM] + [ANY] * len(in_places),
+            in_specs=[VMEM] + [VMEM] * len(in_places),
             out_specs=VMEM,
-            scratch_shapes=[
-                pltpu.VMEM((groups, width, inner), BF16),
-                pltpu.SemaphoreType.DMA((len(in_places), inner // step)),
-            ],
-            compiler_params=params(48),
+            compiler_params=params(16),
             cost_estimate=cost(2 * slots_count * width * inner * groups, 8 << 20),
             name=name,
         )(slots_in, *held)
@@ -419,15 +368,11 @@
         inputs = [hidden[of] for of in used]
         extra = [] if before is None else [before]
         return pl.pallas_call(
-            functools.partial(answer_kernel, slices, 256, len(used), bool(extra)),
+            functools.partial(answer_kernel, slices, rows, len(used), bool(extra)),
             out_shape=jax.ShapeDtypeStruct((slots_count, width), BF16 if name == "answer_far" else F32),
-            in_specs=[VMEM] * len(used) + [ANY] * count + [VMEM] * len(extra),
+            in_specs=[VMEM] * (len(used) + count + len(extra)),
             out_specs=VMEM,
-            scratch_shapes=[
-                pltpu.VMEM((count, inner, width), BF16),
-                pltpu.SemaphoreType.DMA((count, width // 256)),
-            ],
-            compiler_params=params(40),
+            compiler_params=params(16),
             cost_estimate=cost(2 * slots_count * width * inner * count, 10 << 20),
             name=name,
         )(*inputs, *weights, *extra)
@@ -445,17 +390,13 @@
     return pl.pallas_call(
         functools.partial(combine_kernel, exp_count, capacity),
         out_shape=jax.ShapeDtypeStruct((1, frames, width), BF16),
-        in_specs=[VMEM, VMEM, ANY, ANY],
+        in_specs=[VMEM, VMEM, VMEM, HBM],
         out_specs=VMEM,
-        scratch_shapes=[
-            pltpu.VMEM((frames, width), BF16),
-            pltpu.VMEM((slots_count, width), BF16),
-            pltpu.SemaphoreType.DMA((2,)),
-        ],
-        compiler_params=params(32),
+        scratch_shapes=[pltpu.VMEM((frames, width), BF16), pltpu.SemaphoreType.DMA((1,))],
+        compiler_params=params(20),
         cost_estimate=cost(4 * frames * slots_count * width, 3 << 20),
         name="combine",
-    )(gate, cols, mixed, returned)
+    )(gate, cols, returned, mixed)
 
 
 def solution(mesh):

time: 217 us -> 211 us (0.972)
  Pallas kernels: 50.2 us -> 30.4 us
  waiting for transfers between devices: 61.5 us -> 74.4 us
  starting transfers between devices: 24 us -> 28.7 us
  local copies, waits for them, and re-layouts: 27.2 us -> 24.8 us
    ppermute x25, waiting for transfers between devices: 50.2 us -> 63.1 us  [swap(): return lax.ppermute(block, axis, [(i, i ^ mask) for i in range(count)])]
    pallas_call x2, Pallas kernels: 17.8 us -> 8.09 us  [hidden_units(): pl.pallas_call(functools.partial(hidden_kernel, in_places, step), out_sha...]
    pallas_call x3, Pallas kernels: 16 us -> 7.5 us  [answers(): pl.pallas_call(functools.partial(answer_kernel, slices, rows, len(used),...]
    unnamed x87 -> x81, local copies, waits for them, and re-layouts: 25.8 us -> 22.4 us
    all_to_all x1, starting transfers between devices: 6.14 us -> 9.27 us  [body(): lax.all_to_all(slots.reshape(exp_count, capacity, width), 'expert', split...]
  transfers between devices with their start and end apart: 27 -> 27, of which waited for: 13 -> 13; matrix products, arithmetic and copies ran while one was open for 1% -> 0% of each run, Pallas kernels for 20% -> 13%
where the time goes in v7:
time: 211 us; the launch traced here: 208 us
  waiting for transfers between devices  74.4 us (35%)
  blocking collectives  35.8 us (17%)
  Pallas kernels  30.4 us (14%)
  starting transfers between devices  28.7 us (14%)
  local copies, waits for them, and re-layouts  24.8 us (12%)
  between operations  13.7 us (6%)
    ppermute x25, waiting for transfers between devices, swap(): return lax.ppermute(block, axis, [(i, i ^ mask) for i in range(count)])  63.1 us
    all_to_all x1, blocking collectives, body(): lax.all_to_all(answer.reshape(exp_count, capacity, width), 'expert', spli...  35.8 us
    unnamed x81, local copies, waits for them, and re-layouts  22.4 us
    ppermute x25, starting transfers between devices, swap(): return lax.ppermute(block, axis, [(i, i ^ mask) for i in range(count)])  19.4 us
    all_to_all x1, waiting for transfers between devices, body(): lax.all_to_all(slots.reshape(exp_count, capacity, width), 'expert', split...  11.2 us
    all_to_all x1, starting transfers between devices, body(): lax.all_to_all(slots.reshape(exp_count, capacity, width), 'expert', split...  9.27 us
    pallas_call x2, Pallas kernels, hidden_units(): pl.pallas_call(functools.partial(hidden_kernel, in_places, step), out_sha...  8.09 us
    pallas_call x3, Pallas kernels, answers(): pl.pallas_call(functools.partial(answer_kernel, slices, rows, len(used),...  7.5 us
  transfers between devices with their start and end apart: 27, of which 13 were waited for; matrix products, arithmetic and copies ran while one was open for 0% of the time, Pallas kernels for 13%

profile of v7, /device:TPU:16, one launch (start us, length us, event | category | flops | bytes accessed | tf_op | source)
XLA Modules:
  0.0 207.7 jit_solution(8929376059054618494)
XLA Ops:
  6.6 1.6 constant_dynamic-slice_fusion.1
  8.2 1.6 collective-permute-start
  9.8 1.6 copy-done.1
  15.1 1.3 collective-permute-start.2
  16.4 2.1 %collective-permute-start.3 = (bf16[3,128,256]{2,1,0:T(8,128)(2,1)S(1)}, bf16[3,128,256]{2,1,0:T(8,128)(2,1)S(1)}, u32[]{:S(2)}, u32[]{:S(2)}) collective-permute-start(bf16[3,128,256]{2,1,0:T(8,128)(2,1)S(1)} %constant_dynamic-slice_fusion.refs_0_), channel_id=1, source_target_pairs={{0,4},{1,5},{2,6},{3,7},{4,0},{5,1},{6,2},{7,3},{8,12},{9,13},{10,... | collective-permute-start | bytes 589832 | tf_op jit(solution)/shard_map/ppermute | solution.py:30
  19.2 12.6 %collective-permute-done.4.refs_6_ = bf16[3,128,256]{2,1,0:T(8,128)(2,1)S(1)} collective-permute-done((bf16[3,128,256]{2,1,0:T(8,128)(2,1)S(1)}, bf16[3,128,256]{2,1,0:T(8,128)(2,1)S(1)}, u32[]{:S(2)}, u32[]{:S(2)}) %collective-permute-start.4) | collective-permute-done | bytes 196640 | tf_op jit(solution)/shard_map/ppermute | solution.py:30
  31.8 1.4 collective-permute-start.1
  33.8 2.0 collective-permute-done.3.refs_4_
  35.8 1.6 collective-permute-done.1.refs_1_
  37.5 2.1 %collective-permute-done.5.refs_3_ = bf16[3,128,256]{2,1,0:T(8,128)(2,1)S(1)} collective-permute-done((bf16[3,128,256]{2,1,0:T(8,128)(2,1)S(1)}, bf16[3,128,256]{2,1,0:T(8,128)(2,1)S(1)}, u32[]{:S(2)}, u32[]{:S(2)}) %collective-permute-start.5) | collective-permute-done | bytes 196640 | tf_op jit(solution)/shard_map/ppermute | solution.py:30
  41.7 2.1 %collective-permute-start.8 = (bf16[1,1024,384]{2,1,0:T(8,128)(2,1)}, bf16[1,1024,384]{2,1,0:T(8,128)(2,1)S(1)}, u32[]{:S(2)}, u32[]{:S(2)}) collective-permute-start(bf16[1,1024,384]{2,1,0:T(8,128)(2,1)} %copy-done.32), channel_id=1, source_target_pairs={{0,16},{8,24},{16,0},{24,8},{1,17},{9,25},{17,1},{25,9},{2,18},{10... | collective-permute-start | bytes 2359304 | tf_op jit(solution)/shard_map/ppermute | solution.py:30
  43.8 1.5 collective-permute-start.10
  45.8 16.3 %collective-permute-done.8.refs_2_ = bf16[1,1024,384]{2,1,0:T(8,128)(2,1)S(1)} collective-permute-done((bf16[1,1024,384]{2,1,0:T(8,128)(2,1)}, bf16[1,1024,384]{2,1,0:T(8,128)(2,1)S(1)}, u32[]{:S(2)}, u32[]{:S(2)}) %collective-permute-start.8) | collective-permute-done | bytes 786464 | tf_op jit(solution)/shard_map/ppermute | solution.py:30
  62.2 1.8 collective-permute-start.11
  64.9 7.0 %attention.1 = (bf16[256,256]{1,0:T(8,128)(2,1)S(1)}, bf16[256,256]{1,0:T(8,128)(2,1)S(1)}, bf16[256,256]{1,0:T(8,128)(2,1)S(1)}, bf16[256,256]{1,0:T(8,128)(2,1)S(1)}) custom-call(s32[1]{0:T(128)} %bitcast.5.me_ref, bf16[2,256,1024]{2,1,0:T(8,128)(2,1)S(1)} %get-tuple-element.42.near_ref, bf16[2,256,1024]{2,1,0:T(8,128)(2,1)S(1)} %collective-permute-done.7.far_ref, ...), custom_call_target="tpu_custom_call" | custom-call | flops 10485760 | bytes 20480 | tf_op jit(solution)/shard_map/attention/pallas_call | solution.py:287
  77.0 4.0 %collective-permute-done.14.refs_2_ = bf16[256,256]{1,0:T(8,128)(2,1)S(1)} collective-permute-done((bf16[256,256]{1,0:T(8,128)(2,1)}, bf16[256,256]{1,0:T(8,128)(2,1)S(1)}, u32[]{:S(2)}, u32[]{:S(2)}) %collective-permute-start.14) | collective-permute-done | bytes 131104 | tf_op jit(solution)/shard_map/ppermute | solution.py:30
  88.3 3.3 %mix.1 = (bf16[640,1024]{1,0:T(8,128)(2,1)}, bf16[256,1024]{1,0:T(8,128)(2,1)S(1)}, f32[256,128]{1,0:T(8,128)S(1)}) custom-call(s32[1]{0:T(128)} %bitcast.me_ref, f32[2,1024]{1,0:T(2,128)S(1)} %copy-done.31, f32[8,1024]{1,0:T(8,128)S(1)} %bitcast.19, s32[2,256]{1,0:T(2,128)S(1)} %copy.13.rows_ref, s32[256,2]{1,0:T(8,128)S(1)} %bitcast.17, ...), custom_call_target="tpu_custom_call" | custom-call | flops 3407872 | bytes 20480 | tf_op jit(solution)/shard_map/mix/pallas_call | solution.py:312
  93.1 4.4 %collective-permute-done.16.refs_4_ = bf16[1,1024,256]{2,1,0:T(8,128)(2,1)} collective-permute-done((bf16[1,1024,256]{2,1,0:T(8,128)(2,1)}, bf16[1,1024,256]{2,1,0:T(8,128)(2,1)}, u32[]{:S(2)}, u32[]{:S(2)}) %collective-permute-start.16) | collective-permute-done | bytes 524320 | tf_op jit(solution)/shard_map/ppermute | solution.py:30
  97.5 9.3 %all-to-all-start = ((bf16[8,80,1024]{2,1,0:T(8,128)(2,1)}), bf16[8,80,1024]{2,1,0:T(8,128)(2,1)S(1)}, u32[]{:S(2)}, u32[]{:S(2)}) async-start(bf16[8,80,1024]{2,1,0:T(8,128)(2,1)} %bitcast.6), calls=%async_computation | async-start | bytes 2621440 | tf_op jit(solution)/shard_map/all_to_all | solution.py:342
  107.3 1.4 collective-permute-start.23
  109.2 6.1 %collective-permute-done.20.refs_3_ = bf16[1,1024,128]{2,1,0:T(8,128)(2,1)S(1)} collective-permute-done((bf16[1,1024,128]{2,1,0:T(8,128)(2,1)}, bf16[1,1024,128]{2,1,0:T(8,128)(2,1)S(1)}, u32[]{:S(2)}, u32[]{:S(2)}) %collective-permute-start.20) | collective-permute-done | bytes 262176 | tf_op jit(solution)/shard_map/ppermute | solution.py:30
  117.3 1.9 collective-permute-done.21.refs_4_
  123.7 11.2 %all-to-all-done = bf16[8,80,1024]{2,1,0:T(8,128)(2,1)S(1)} async-done(((bf16[8,80,1024]{2,1,0:T(8,128)(2,1)}), bf16[8,80,1024]{2,1,0:T(8,128)(2,1)S(1)}, u32[]{:S(2)}, u32[]{:S(2)}) %all-to-all-start) | async-done | bytes 1310752 | tf_op jit(solution)/shard_map/all_to_all | solution.py:342
  134.9 1.6 copy-done.2
  136.5 4.7 %hidden_near.1.refs_0_ = bf16[2,640,1024]{2,1,0:T(8,128)(2,1)S(1)} custom-call(bf16[640,1024]{1,0:T(8,128)(2,1)S(1)} %bitcast.12, bf16[1,1024,1024]{2,1,0:T(8,128)(2,1)S(1)} %copy-done.2, bf16[1,1024,256]{2,1,0:T(8,128)(2,1)S(1)} %collective-permute-done.6.refs_1_, bf16[1,1024,384]{2,1,0:T(8,128)(2,1)S(1)} %collective-permute-done.8.refs_2_, ...), custom_call_target="tpu_custom_call" | custom-call | flops 10485760 | bytes 32768 | tf_op jit(solution)/shard_map/hidden_near/pallas_call | solution.py:351
  141.3 3.4 %hidden_far.1.refs_1_.refs_0_ = bf16[2,640,1024]{2,1,0:T(8,128)(2,1)S(1)} custom-call(bf16[640,1024]{1,0:T(8,128)(2,1)S(1)} %bitcast.13, bf16[1,1024,1024]{2,1,0:T(8,128)(2,1)S(1)} %copy-done.7, bf16[1,1024,256]{2,1,0:T(8,128)(2,1)S(1)} %copy-done.16, bf16[1,1024,384]{2,1,0:T(8,128)(2,1)S(1)} %copy-done.10, bf16[1,1024,128]{2,1,0:T(8,128)(2,1)S(1)} %copy-done.21, ...), custom_call_target="tpu_custom_call" | custom-call | flops 10485760 | bytes 32768 | tf_op jit(solution)/shard_map/hidden_far/pallas_call | solution.py:351
  144.7 10.4 %collective-permute-done.23.refs_1_ = bf16[1,1024,1024]{2,1,0:T(8,128)(2,1)} collective-permute-done((bf16[1,1024,1024]{2,1,0:T(8,128)(2,1)}, bf16[1,1024,1024]{2,1,0:T(8,128)(2,1)}, u32[]{:S(2)}, u32[]{:S(2)}) %collective-permute-start.23) | collective-permute-done | bytes 2097184 | tf_op jit(solution)/shard_map/ppermute | solution.py:30
  155.2 2.9 %answer_own.1.refs_2_ = f32[640,1024]{1,0:T(8,128)S(1)} custom-call(bf16[2,640,1024]{2,1,0:T(8,128)(2,1)S(1)} %hidden_near.1.refs_0_, bf16[2,640,1024]{2,1,0:T(8,128)(2,1)S(1)} %hidden_far.1.refs_1_.refs_0_, bf16[1,1024,1024]{2,1,0:T(8,128)(2,1)S(1)} %copy-done.3, bf16[1,1024,1024]{2,1,0:T(8,128)(2,1)S(1)} %copy-done.5), custom_call_target="tpu_custom_call" | custom-call | flops 10485760 | bytes 40960 | tf_op jit(solution)/shard_map/answer_own/pallas_call | solution.py:370
  158.0 3.1 %answer_near.1.refs_2_ = f32[640,1024]{1,0:T(8,128)S(1)} custom-call(bf16[2,640,1024]{2,1,0:T(8,128)(2,1)S(1)} %hidden_near.1.refs_0_, bf16[1,1024,1024]{2,1,0:T(8,128)(2,1)} %collective-permute-done.23.refs_1_, f32[640,1024]{1,0:T(8,128)S(1)} %answer_own.1.refs_2_), custom_call_target="tpu_custom_call" | custom-call | flops 5242880 | bytes 40960 | tf_op jit(solution)/shard_map/answer_near/pallas_call | solution.py:370
  161.2 1.5 answer_far.1
  162.7 35.8 %all_to_all.10 = bf16[8,80,1024]{2,1,0:T(8,128)(2,1)S(1)} all-to-all(bf16[8,80,1024]{2,1,0:T(8,128)(2,1)S(1)} %bitcast.15), channel_id=1, replica_groups=mesh['dp'=4,'expert'=8] {'expert'}, dimensions={0} | all-to-all | bytes 2621440 | tf_op jit(solution)/shard_map/all_to_all | solution.py:386
  198.6 2.3 %combine.1 = bf16[1,256,1024]{2,1,0:T(8,128)(2,1)} custom-call(f32[256,128]{1,0:T(8,128)S(1)} %copy-done.25, s32[256,2]{1,0:T(8,128)S(1)} %bitcast.18, bf16[640,1024]{1,0:T(8,128)(2,1)S(1)} %bitcast.14, bf16[256,1024]{1,0:T(8,128)(2,1)S(1)} %copy-done.12), custom_call_target="tpu_custom_call" | custom-call | flops 2621440 | bytes 12288 | tf_op jit(solution)/shard_map/combine/pallas_call | solution.py:390
  (121 shorter events, 29.8 us)
Async XLA Ops:
  6.5 33.0 %copy-start.31 = (f32[2,1024]{1,0:T(2,128)S(1)}, f32[2,1024]{1,0:T(2,128)}, u32[]{:S(2)}) copy-start(f32[2,1024]{1,0:T(2,128)} %gain_ref.3) | copy-start | bytes 24580
  6.5 67.4 %all-gather.2.cloned.1.call-start = ((), (), s32[]{:S(2)}) async-start(), calls=%async_computation.2 | async-start | bytes 1179648 | tf_op jit(solution)/shard_map/all_gather | solution.py:242
  8.2 31.3 %collective-permute-start = (bf16[1,256,1024]{2,1,0:T(8,128)(2,1)}, bf16[1,256,1024]{2,1,0:T(8,128)(2,1)S(1)}, u32[]{:S(2)}, u32[]{:S(2)}) collective-permute-start(bf16[1,256,1024]{2,1,0:T(8,128)(2,1)} %refs_0_.2), channel_id=1, source_target_pairs={{0,16},{8,24},{16,0},{24,8},{1,17},{9,25},{17,1},{25,9},{2,18},{10... | collective-permute-start | bytes 1572872 | tf_op jit(solution)/shard_map/ppermute | solution.py:30
  11.4 28.2 %copy-start.19 = (bf16[1,256,1024]{2,1,0:T(8,128)(2,1)S(1)}, bf16[1,256,1024]{2,1,0:T(8,128)(2,1)}, u32[]{:S(2)}) copy-start(bf16[1,256,1024]{2,1,0:T(8,128)(2,1)} %refs_0_.2) | copy-start | bytes 1572868
  13.9 25.6 %collective-permute-start.6 = (bf16[1,1024,256]{2,1,0:T(8,128)(2,1)}, bf16[1,1024,256]{2,1,0:T(8,128)(2,1)S(1)}, u32[]{:S(2)}, u32[]{:S(2)}) collective-permute-start(bf16[1,1024,256]{2,1,0:T(8,128)(2,1)} %get-tuple-element.39), channel_id=1, source_target_pairs={{0,16},{8,24},{16,0},{24,8},{1,17},{9,25},{17,1},{25,9},{2,18},{10... | collective-permute-start | bytes 1572872 | tf_op jit(solution)/shard_map/ppermute | solution.py:30
  14.6 17.2 %collective-permute-start.4 = (bf16[3,128,256]{2,1,0:T(8,128)(2,1)S(1)}, bf16[3,128,256]{2,1,0:T(8,128)(2,1)S(1)}, u32[]{:S(2)}, u32[]{:S(2)}) collective-permute-start(bf16[3,128,256]{2,1,0:T(8,128)(2,1)S(1)} %constant_dynamic-slice_fusion.refs_0_), channel_id=1, source_target_pairs={{0,6},{1,7},{2,4},{3,5},{4,2},{5,3},{6,0},{7,1},{8,14},{9,15},{10,... | collective-permute-start | bytes 589832 | tf_op jit(solution)/shard_map/ppermute | solution.py:30
  15.1 18.1 %collective-permute-start.2 = (bf16[3,128,256]{2,1,0:T(8,128)(2,1)S(1)}, bf16[3,128,256]{2,1,0:T(8,128)(2,1)S(1)}, u32[]{:S(2)}, u32[]{:S(2)}) collective-permute-start(bf16[3,128,256]{2,1,0:T(8,128)(2,1)S(1)} %constant_dynamic-slice_fusion.refs_0_), channel_id=1, source_target_pairs={{0,2},{1,3},{2,0},{3,1},{4,6},{5,7},{6,4},{7,5},{8,10},{9,11},{10,... | collective-permute-start | bytes 589832 | tf_op jit(solution)/shard_map/ppermute | solution.py:30
  16.4 19.4 %collective-permute-start.3 = (bf16[3,128,256]{2,1,0:T(8,128)(2,1)S(1)}, bf16[3,128,256]{2,1,0:T(8,128)(2,1)S(1)}, u32[]{:S(2)}, u32[]{:S(2)}) collective-permute-start(bf16[3,128,256]{2,1,0:T(8,128)(2,1)S(1)} %constant_dynamic-slice_fusion.refs_0_), channel_id=1, source_target_pairs={{0,4},{1,5},{2,6},{3,7},{4,0},{5,1},{6,2},{7,3},{8,12},{9,13},{10,... | collective-permute-start | bytes 589832 | tf_op jit(solution)/shard_map/ppermute | solution.py:30
  31.8 5.7 %collective-permute-start.1 = (bf16[3,128,256]{2,1,0:T(8,128)(2,1)S(1)}, bf16[3,128,256]{2,1,0:T(8,128)(2,1)S(1)}, u32[]{:S(2)}, u32[]{:S(2)}) collective-permute-start(bf16[3,128,256]{2,1,0:T(8,128)(2,1)S(1)} %constant_dynamic-slice_fusion.refs_0_), channel_id=1, source_target_pairs={{0,1},{1,0},{2,3},{3,2},{4,5},{5,4},{6,7},{7,6},{8,9},{9,8},{10,11... | collective-permute-start | bytes 589832 | tf_op jit(solution)/shard_map/ppermute | solution.py:30
  33.2 6.4 %collective-permute-start.5 = (bf16[3,128,256]{2,1,0:T(8,128)(2,1)S(1)}, bf16[3,128,256]{2,1,0:T(8,128)(2,1)S(1)}, u32[]{:S(2)}, u32[]{:S(2)}) collective-permute-start(bf16[3,128,256]{2,1,0:T(8,128)(2,1)S(1)} %collective-permute-done.2.refs_2_), channel_id=1, source_target_pairs={{0,1},{1,0},{2,3},{3,2},{4,5},{5,4},{6,7},{7,6},{8,9},{9,8},{10,11... | collective-permute-start | bytes 589832 | tf_op jit(solution)/shard_map/ppermute | solution.py:30
  41.7 41.5 %copy-start.39 = (s32[1,256,2]{1,2,0:T(2,128)S(1)}, s32[1,256,2]{1,2,0:T(2,128)}, u32[]{:S(2)}) copy-start(s32[1,256,2]{1,2,0:T(2,128)} %param.11) | copy-start | bytes 6148
  41.7 20.5 %collective-permute-start.7 = (bf16[2,256,1024]{2,1,0:T(8,128)(2,1)S(1)}, bf16[2,256,1024]{2,1,0:T(8,128)(2,1)S(1)}, u32[]{:S(2)}, u32[]{:S(2)}) collective-permute-start(bf16[2,256,1024]{2,1,0:T(8,128)(2,1)S(1)} %get-tuple-element.42.near_ref), channel_id=1, source_target_pairs={{0,8},{8,0},{16,24},{24,16},{1,9},{9,1},{17,25},{25,17},{2,10},{10... | collective-permute-start | bytes 3145736 | tf_op jit(solution)/shard_map/ppermute | solution.py:30
  41.7 20.5 %collective-permute-start.8 = (bf16[1,1024,384]{2,1,0:T(8,128)(2,1)}, bf16[1,1024,384]{2,1,0:T(8,128)(2,1)S(1)}, u32[]{:S(2)}, u32[]{:S(2)}) collective-permute-start(bf16[1,1024,384]{2,1,0:T(8,128)(2,1)} %copy-done.32), channel_id=1, source_target_pairs={{0,16},{8,24},{16,0},{24,8},{1,17},{9,25},{17,1},{25,9},{2,18},{10... | collective-permute-start | bytes 2359304 | tf_op jit(solution)/shard_map/ppermute | solution.py:30
  43.8 18.4 %collective-permute-start.10 = (bf16[3,128,256]{2,1,0:T(8,128)(2,1)S(1)}, bf16[3,128,256]{2,1,0:T(8,128)(2,1)S(1)}, u32[]{:S(2)}, u32[]{:S(2)}) collective-permute-start(bf16[3,128,256]{2,1,0:T(8,128)(2,1)S(1)} %collective-permute-done.4.refs_6_), channel_id=1, source_target_pairs={{0,1},{1,0},{2,3},{3,2},{4,5},{5,4},{6,7},{7,6},{8,9},{9,8},{10,11... | collective-permute-start | bytes 589832 | tf_op jit(solution)/shard_map/ppermute | solution.py:30
  45.3 16.9 %collective-permute-start.9 = (bf16[3,128,256]{2,1,0:T(8,128)(2,1)S(1)}, bf16[3,128,256]{2,1,0:T(8,128)(2,1)S(1)}, u32[]{:S(2)}, u32[]{:S(2)}) collective-permute-start(bf16[3,128,256]{2,1,0:T(8,128)(2,1)S(1)} %collective-permute-done.3.refs_4_), channel_id=1, source_target_pairs={{0,1},{1,0},{2,3},{3,2},{4,5},{5,4},{6,7},{7,6},{8,9},{9,8},{10,11... | collective-permute-start | bytes 589832 | tf_op jit(solution)/shard_map/ppermute | solution.py:30
  62.2 11.7 %collective-permute-start.11 = (bf16[1,1024,128]{2,1,0:T(8,128)(2,1)}, bf16[1,1024,128]{2,1,0:T(8,128)(2,1)}, u32[]{:S(2)}, u32[]{:S(2)}) collective-permute-start(bf16[1,1024,128]{2,1,0:T(8,128)(2,1)} %copy-done.34), channel_id=1, source_target_pairs={{0,16},{8,24},{16,0},{24,8},{1,17},{9,25},{17,1},{25,9},{2,18},{10... | collective-permute-start | bytes 786440 | tf_op jit(solution)/shard_map/ppermute | solution.py:30
  73.9 9.5 %collective-permute-start.12 = (bf16[1024,512]{1,0:T(8,128)(2,1)}, bf16[1024,512]{1,0:T(8,128)(2,1)S(1)}, u32[]{:S(2)}, u32[]{:S(2)}) collective-permute-start(bf16[1024,512]{1,0:T(8,128)(2,1)} %all-gather.2.cloned.1.call-done.near_ref), channel_id=1, source_target_pairs={{0,8},{8,0},{16,24},{24,16},{1,9},{9,1},{17,25},{25,17},{2,10},{10... | collective-permute-start | bytes 3145736 | tf_op jit(solution)/shard_map/ppermute | solution.py:30
  73.9 3.1 %collective-permute-start.13 = (bf16[256,256]{1,0:T(8,128)(2,1)}, bf16[256,256]{1,0:T(8,128)(2,1)S(1)}, u32[]{:S(2)}, u32[]{:S(2)}) collective-permute-start(bf16[256,256]{1,0:T(8,128)(2,1)} %copy-done.37), channel_id=1, source_target_pairs={{0,8},{8,0},{16,24},{24,16},{1,9},{9,1},{17,25},{25,17},{2,10},{10... | collective-permute-start | bytes 393224 | tf_op jit(solution)/shard_map/ppermute | solution.py:30
  74.4 6.6 %collective-permute-start.14 = (bf16[256,256]{1,0:T(8,128)(2,1)}, bf16[256,256]{1,0:T(8,128)(2,1)S(1)}, u32[]{:S(2)}, u32[]{:S(2)}) collective-permute-start(bf16[256,256]{1,0:T(8,128)(2,1)} %copy-done.36), channel_id=1, source_target_pairs={{0,16},{8,24},{16,0},{24,8},{1,17},{9,25},{17,1},{25,9},{2,18},{10... | collective-permute-start | bytes 393224 | tf_op jit(solution)/shard_map/ppermute | solution.py:30
  74.7 7.3 %collective-permute-start.15 = (bf16[256,256]{1,0:T(8,128)(2,1)}, bf16[256,256]{1,0:T(8,128)(2,1)S(1)}, u32[]{:S(2)}, u32[]{:S(2)}) collective-permute-start(bf16[256,256]{1,0:T(8,128)(2,1)} %copy-done.35), channel_id=1, source_target_pairs={{0,24},{8,16},{16,8},{24,0},{1,25},{9,17},{17,9},{25,1},{2,26},{10... | collective-permute-start | bytes 393224 | tf_op jit(solution)/shard_map/ppermute | solution.py:30
  82.7 14.9 %collective-permute-start.16 = (bf16[1,1024,256]{2,1,0:T(8,128)(2,1)}, bf16[1,1024,256]{2,1,0:T(8,128)(2,1)}, u32[]{:S(2)}, u32[]{:S(2)}) collective-permute-start(bf16[1,1024,256]{2,1,0:T(8,128)(2,1)} %copy-done.33), channel_id=1, source_target_pairs={{0,16},{8,24},{16,0},{24,8},{1,17},{9,25},{17,1},{25,9},{2,18},{10... | collective-permute-start | bytes 1572872 | tf_op jit(solution)/shard_map/ppermute | solution.py:30
  97.5 37.4 %all-to-all-start = ((bf16[8,80,1024]{2,1,0:T(8,128)(2,1)}), bf16[8,80,1024]{2,1,0:T(8,128)(2,1)S(1)}, u32[]{:S(2)}, u32[]{:S(2)}) async-start(bf16[8,80,1024]{2,1,0:T(8,128)(2,1)} %bitcast.6), calls=%async_computation | async-start | bytes 2621440 | tf_op jit(solution)/shard_map/all_to_all | solution.py:342
  106.8 14.2 %collective-permute-start.17 = (bf16[1,1024,1024]{2,1,0:T(8,128)(2,1)}, bf16[1,1024,1024]{2,1,0:T(8,128)(2,1)S(1)}, u32[]{:S(2)}, u32[]{:S(2)}) collective-permute-start(bf16[1,1024,1024]{2,1,0:T(8,128)(2,1)} %refs_0_.3), channel_id=1, source_target_pairs={{0,8},{8,0},{16,24},{24,16},{1,9},{9,1},{17,25},{25,17},{2,10},{10... | collective-permute-start | bytes 6291464 | tf_op jit(solution)/shard_map/ppermute | solution.py:30
  106.8 15.6 %collective-permute-start.22 = (bf16[1,1024,1024]{2,1,0:T(8,128)(2,1)}, bf16[1,1024,1024]{2,1,0:T(8,128)(2,1)S(1)}, u32[]{:S(2)}, u32[]{:S(2)}) collective-permute-start(bf16[1,1024,1024]{2,1,0:T(8,128)(2,1)} %refs_2_.1), channel_id=1, source_target_pairs={{0,8},{8,0},{16,24},{24,16},{1,9},{9,1},{17,25},{25,17},{2,10},{10... | collective-permute-start | bytes 6291464 | tf_op jit(solution)/shard_map/ppermute | solution.py:30
  107.3 47.9 %collective-permute-start.23 = (bf16[1,1024,1024]{2,1,0:T(8,128)(2,1)}, bf16[1,1024,1024]{2,1,0:T(8,128)(2,1)}, u32[]{:S(2)}, u32[]{:S(2)}) collective-permute-start(bf16[1,1024,1024]{2,1,0:T(8,128)(2,1)} %refs_2_.1), channel_id=1, source_target_pairs={{0,16},{8,24},{16,0},{24,8},{1,17},{9,25},{17,1},{25,9},{2,18},{10... | collective-permute-start | bytes 6291464 | tf_op jit(solution)/shard_map/ppermute | solution.py:30
  108.7 7.5 %collective-permute-start.18 = (bf16[1,1024,256]{2,1,0:T(8,128)(2,1)S(1)}, bf16[1,1024,256]{2,1,0:T(8,128)(2,1)S(1)}, u32[]{:S(2)}, u32[]{:S(2)}) collective-permute-start(bf16[1,1024,256]{2,1,0:T(8,128)(2,1)S(1)} %collective-permute-done.6.refs_1_), channel_id=1, source_target_pairs={{0,8},{8,0},{16,24},{24,16},{1,9},{9,1},{17,25},{25,17},{2,10},{10... | collective-permute-start | bytes 1572872 | tf_op jit(solution)/shard_map/ppermute | solution.py:30
  108.7 6.6 %collective-permute-start.20 = (bf16[1,1024,128]{2,1,0:T(8,128)(2,1)}, bf16[1,1024,128]{2,1,0:T(8,128)(2,1)S(1)}, u32[]{:S(2)}, u32[]{:S(2)}) collective-permute-start(bf16[1,1024,128]{2,1,0:T(8,128)(2,1)} %collective-permute-done.11.refs_3_), channel_id=1, source_target_pairs={{0,8},{8,0},{16,24},{24,16},{1,9},{9,1},{17,25},{25,17},{2,10},{10... | collective-permute-start | bytes 786440 | tf_op jit(solution)/shard_map/ppermute | solution.py:30
  116.0 4.1 %collective-permute-start.19 = (bf16[1,1024,384]{2,1,0:T(8,128)(2,1)S(1)}, bf16[1,1024,384]{2,1,0:T(8,128)(2,1)S(1)}, u32[]{:S(2)}, u32[]{:S(2)}) collective-permute-start(bf16[1,1024,384]{2,1,0:T(8,128)(2,1)S(1)} %collective-permute-done.8.refs_2_), channel_id=1, source_target_pairs={{0,8},{8,0},{16,24},{24,16},{1,9},{9,1},{17,25},{25,17},{2,10},{10... | collective-permute-start | bytes 2359304 | tf_op jit(solution)/shard_map/ppermute | solution.py:30
  116.9 2.3 %collective-permute-start.21 = (bf16[1,1024,256]{2,1,0:T(8,128)(2,1)}, bf16[1,1024,256]{2,1,0:T(8,128)(2,1)S(1)}, u32[]{:S(2)}, u32[]{:S(2)}) collective-permute-start(bf16[1,1024,256]{2,1,0:T(8,128)(2,1)} %collective-permute-done.16.refs_4_), channel_id=1, source_target_pairs={{0,8},{8,0},{16,24},{24,16},{1,9},{9,1},{17,25},{25,17},{2,10},{10... | collective-permute-start | bytes 1572872 | tf_op jit(solution)/shard_map/ppermute | solution.py:30
  155.2 6.0 %collective-permute-start.24 = (bf16[1,1024,1024]{2,1,0:T(8,128)(2,1)}, bf16[1,1024,1024]{2,1,0:T(8,128)(2,1)S(1)}, u32[]{:S(2)}, u32[]{:S(2)}) collective-permute-start(bf16[1,1024,1024]{2,1,0:T(8,128)(2,1)} %collective-permute-done.23.refs_1_), channel_id=1, source_target_pairs={{0,8},{8,0},{16,24},{24,16},{1,9},{9,1},{17,25},{25,17},{2,10},{10... | collective-permute-start | bytes 6291464 | tf_op jit(solution)/shard_map/ppermute | solution.py:30
  162.7 35.9 %copy-start.12 = (bf16[256,1024]{1,0:T(8,128)(2,1)S(1)}, bf16[256,1024]{1,0:T(8,128)(2,1)}, u32[]{:S(2)}) copy-start(bf16[256,1024]{1,0:T(8,128)(2,1)} %copy-done.11) | copy-start | bytes 1572868
  162.7 35.9 %copy-start.25 = (f32[256,128]{1,0:T(8,128)S(1)}, f32[256,128]{1,0:T(8,128)}, u32[]{:S(2)}) copy-start(f32[256,128]{1,0:T(8,128)} %copy-done.24) | copy-start | bytes 393220
  (35 other events, 102.6 us)
Sparse Core Ops, SparseCore 0:
  9.5 45.6 all-gather.1

commit v8 on v7

--- a/solution.py
+++ b/solution.py
@@ -169,9 +169,21 @@
         answer_ref[:, where] = total.astype(answer_ref.dtype)
 
 
-def combine_kernel(experts, capacity, gate_ref, cols_ref, answer_ref, mixed_in, out_ref, mixed_ref, sems):
+def last_answer_kernel(slices, step, held, blocks, *refs):
+    me_ref, refs = refs[0], refs[1:]
+    inputs, outs, total_ref = refs[: -blocks - 1], refs[-blocks - 1 : -1], refs[-1]
+    answer_kernel(slices, step, held, True, *inputs, total_ref)
+    size = outs[0].shape[0]
+    for k, out in enumerate(outs):
+        out[...] = total_ref[pl.ds(pl.multiple_of((me_ref[0] ^ k) * size, size), size), :]
+
+
+def combine_kernel(experts, capacity, me_ref, gate_ref, cols_ref, mixed_in, *refs):
+    blocks, (out_ref, mixed_ref, answer_ref, sems) = refs[:experts], refs[experts:]
     copy = pltpu.make_async_copy(mixed_in, mixed_ref, sems.at[0])
     copy.start()
+    for k, block in enumerate(blocks):
+        answer_ref[k * capacity : (k + 1) * capacity, :] = block[...]
     frames = mixed_ref.shape[0]
     first, second = cols_ref[:, 0:1], cols_ref[:, 1:2]
     lane = lax.broadcasted_iota(jnp.int32, (frames, experts), 1)
@@ -180,7 +192,7 @@
         lax.broadcasted_iota(jnp.int32, (frames, frames), 1)
         < lax.broadcasted_iota(jnp.int32, (frames, frames), 0)
     ).astype(F32)
-    rank = jnp.dot(before, named, preferred_element_type=F32) + (lane * capacity).astype(F32)
+    rank = jnp.dot(before, named, preferred_element_type=F32) + ((lane ^ me_ref[0]) * capacity).astype(F32)
     slot = lax.broadcasted_iota(jnp.int32, (frames, experts * capacity), 1).astype(F32)
     picks = []
     for chosen in (first, second):
@@ -207,8 +219,11 @@
 
 
 def cut(size, shares):
-    starts = [round(sum(shares[:i]) * size / sum(shares) / 128) * 128 for i in range(len(shares) + 1)]
-    return [(a, b - a) for a, b in zip(starts, starts[1:])]
+    starts, tiles, count = [0], size // 128, len(shares)
+    for i in range(1, count + 1):
+        wanted = round(sum(shares[:i]) * tiles / sum(shares))
+        starts.append(min(max(wanted, starts[-1] + 1), tiles - (count - i)))
+    return [(a * 128, (b - a) * 128) for a, b in zip(starts, starts[1:])]
 
 
 def after(values, earlier):
@@ -224,7 +239,7 @@
     exp_index = lax.axis_index("expert").astype(jnp.int32)
     frames, width = frames_in.shape[1:]
     top = expert_ids.shape[2]
-    capacity = frames * top * 5 // (4 * exp_count)
+    capacity = -(-frames * top * 5 // (4 * exp_count * 16)) * 16
     slots_count = exp_count * capacity
     half = dp_count // 2
     share = width // dp_count
@@ -246,7 +261,7 @@
         tiled=True,
     )
 
-    in_cuts = cut(inner, (2, 3, 1, 2))
+    in_cuts = cut(inner, (3, 1, 2, 2))
     in_chunks = pl.pallas_call(
         functools.partial(split_kernel, in_cuts),
         out_shape=[jax.ShapeDtypeStruct((1, width, n), BF16) for _, n in in_cuts],
@@ -257,10 +272,9 @@
         cost_estimate=cost(0, 4 << 20),
         name="split",
     )(expert_in)
-    in_held = [spread_over(in_chunks[0], "dp", 2)]
-
-    early = [qkv[1], *[qkv[k] for k in range(2, exp_count, 2)], qkv[3], in_held[0]]
-    raw[half] = after(raw[half], early)
+    in_held = [spread_over(after(in_chunks[0], qkv[1]), "dp", 2)]
+    in_held.append(spread_over(after(in_chunks[1], (in_held[0], qkv[exp_count - 2])), "dp", 2))
+    raw[half] = after(raw[half], (qkv, in_held[1]))
 
     groups = len(raw)
     member = jnp.arange(groups, dtype=jnp.int32) * 2
@@ -280,9 +294,7 @@
         name="norm",
     )(place, norm_gains, *[raw[2 * k] for k in range(groups)])
     far = swap(near, "dp", 1)
-    in_held.append(spread_over(after(in_chunks[1], near), "dp", 2))
-    far = after(far, in_held[1])
-    in_held.append(spread_over(after(in_chunks[2], (in_held[1], far, qkv)), "dp", 2))
+    in_held.append(spread_over(after(in_chunks[2], near), "dp", 2))
 
     contexts = pl.pallas_call(
         functools.partial(attention_kernel, dp_count, exp_count),
@@ -367,9 +379,20 @@
         slices = [(used.index(of), place) for of, place in slices]
         inputs = [hidden[of] for of in used]
         extra = [] if before is None else [before]
+        if name == "answer_far":
+            return pl.pallas_call(
+                functools.partial(last_answer_kernel, slices, rows, len(used), exp_count),
+                out_shape=[jax.ShapeDtypeStruct((capacity, width), BF16)] * exp_count,
+                in_specs=[SMEM] + [VMEM] * (len(used) + count + len(extra)),
+                out_specs=[VMEM] * exp_count,
+                scratch_shapes=[pltpu.VMEM((slots_count, width), BF16)],
+                compiler_params=params(16),
+                cost_estimate=cost(2 * slots_count * width * inner * count, 10 << 20),
+                name=name,
+            )(exp_index[None], *inputs, *weights, *extra)
         return pl.pallas_call(
             functools.partial(answer_kernel, slices, rows, len(used), bool(extra)),
-            out_shape=jax.ShapeDtypeStruct((slots_count, width), BF16 if name == "answer_far" else F32),
+            out_shape=jax.ShapeDtypeStruct((slots_count, width), F32),
             in_specs=[VMEM] * (len(used) + count + len(extra)),
             out_specs=VMEM,
             compiler_params=params(16),
@@ -383,20 +406,23 @@
     out_far = [swap(block, "dp", 1) for block in out_near]
     answer = answers([(0, k) for k in distant], out_near, answer, "answer_near")
     answer = answers([(1, k) for k in distant], out_far, answer, "answer_far")
-    returned = lax.all_to_all(
-        answer.reshape(exp_count, capacity, width), "expert", split_axis=0, concat_axis=0, tiled=True
-    ).reshape(slots_count, width)
+    returned = {k: swap(answer[k], "expert", k) for k in reversed(range(1, exp_count))}
+    returned[0] = answer[0]
 
     return pl.pallas_call(
         functools.partial(combine_kernel, exp_count, capacity),
         out_shape=jax.ShapeDtypeStruct((1, frames, width), BF16),
-        in_specs=[VMEM, VMEM, VMEM, HBM],
+        in_specs=[SMEM, VMEM, VMEM, HBM] + [VMEM] * exp_count,
         out_specs=VMEM,
-        scratch_shapes=[pltpu.VMEM((frames, width), BF16), pltpu.SemaphoreType.DMA((1,))],
+        scratch_shapes=[
+            pltpu.VMEM((frames, width), BF16),
+            pltpu.VMEM((slots_count, width), BF16),
+            pltpu.SemaphoreType.DMA((1,)),
+        ],
         compiler_params=params(20),
         cost_estimate=cost(4 * frames * slots_count * width, 3 << 20),
         name="combine",
-    )(gate, cols, returned, mixed)
+    )(exp_index[None], gate, cols, mixed, *[returned[k] for k in range(exp_count)])
 
 
 def solution(mesh):

time: 211 us -> 204 us (0.967); the launches traced: 208 us -> 203 us
  blocking collectives: 35.8 us -> 0 us
  waiting for transfers between devices: 74.4 us -> 101 us
  starting transfers between devices: 28.7 us -> 31 us
    all_to_all x1 -> x0, blocking collectives: 35.8 us -> none  [body(): lax.all_to_all(answer.reshape(exp_count, capacity, width), 'expert', spli...]
    ppermute x25 -> x32, waiting for transfers between devices: 63.1 us -> 89.9 us  [swap(): return lax.ppermute(block, axis, [(i, i ^ mask) for i in range(count)])]
    ppermute x25 -> x32, starting transfers between devices: 19.4 us -> 23.8 us  [swap(): return lax.ppermute(block, axis, [(i, i ^ mask) for i in range(count)])]
    unnamed x81 -> x87, local copies, waits for them, and re-layouts: 22.4 us -> 24.2 us
    pallas_call x3 -> x2, Pallas kernels: 7.5 us -> 5.99 us  [answers(): pl.pallas_call(functools.partial(answer_kernel, slices, rows, len(used),...]
  transfers between devices with their start and end apart: 27 -> 34, of which waited for: 13 -> 21; matrix products, arithmetic and copies ran while one was open for 0% -> 1% of each run, Pallas kernels for 13% -> 14%
where the time goes in v8:
time: 204 us; the launch traced here: 203 us
  waiting for transfers between devices  101 us (50%)
  Pallas kernels  31.6 us (15%)
  starting transfers between devices  31 us (15%)
  local copies, waits for them, and re-layouts  25.6 us (13%)
  between operations  13.7 us (7%)
    ppermute x32, waiting for transfers between devices, swap(): return lax.ppermute(block, axis, [(i, i ^ mask) for i in range(count)])  89.9 us
    unnamed x87, local copies, waits for them, and re-layouts  24.2 us
    ppermute x32, starting transfers between devices, swap(): return lax.ppermute(block, axis, [(i, i ^ mask) for i in range(count)])  23.8 us
    all_to_all x1, waiting for transfers between devices, body(): lax.all_to_all(slots.reshape(exp_count, capacity, width), 'expert', split...  11.3 us
    pallas_call x1, Pallas kernels, body(): pl.pallas_call(functools.partial(attention_kernel, dp_count, exp_count),...  8.06 us
    pallas_call x2, Pallas kernels, hidden_units(): pl.pallas_call(functools.partial(hidden_kernel, in_places, step), out_sha...  8.04 us
    all_to_all x1, starting transfers between devices, body(): lax.all_to_all(slots.reshape(exp_count, capacity, width), 'expert', split...  7.23 us
    pallas_call x2, Pallas kernels, answers(): pl.pallas_call(functools.partial(answer_kernel, slices, rows, len(used),...  5.99 us
  transfers between devices with their start and end apart: 34, of which 21 were waited for; matrix products, arithmetic and copies ran while one was open for 1% of the time, Pallas kernels for 14%

profile of v8, /device:TPU:16, one launch (start us, length us, event | category | flops | bytes accessed | tf_op | source)
XLA Modules:
  0.0 203.3 jit_solution(11485983934608879217)
XLA Ops:
  7.7 1.6 collective-permute-start.1
  9.3 1.6 copy-done.1
  14.4 1.5 collective-permute-start.8
  17.7 3.5 %collective-permute-start.4 = (bf16[3,128,256]{2,1,0:T(8,128)(2,1)S(1)}, bf16[3,128,256]{2,1,0:T(8,128)(2,1)}, u32[]{:S(2)}, u32[]{:S(2)}) collective-permute-start(bf16[3,128,256]{2,1,0:T(8,128)(2,1)S(1)} %constant_dynamic-slice_fusion.refs_0_), channel_id=1, source_target_pairs={{0,4},{1,5},{2,6},{3,7},{4,0},{5,1},{6,2},{7,3},{8,12},{9,13},{10,... | collective-permute-start | bytes 589832 | tf_op jit(solution)/shard_map/ppermute | solution.py:30
  21.1 15.5 %collective-permute-done.6.refs_6_ = bf16[3,128,256]{2,1,0:T(8,128)(2,1)S(1)} collective-permute-done((bf16[3,128,256]{2,1,0:T(8,128)(2,1)S(1)}, bf16[3,128,256]{2,1,0:T(8,128)(2,1)S(1)}, u32[]{:S(2)}, u32[]{:S(2)}) %collective-permute-start.6) | collective-permute-done | bytes 196640 | tf_op jit(solution)/shard_map/ppermute | solution.py:30
  41.1 4.3 %collective-permute-done.7.refs_7_ = bf16[3,128,256]{2,1,0:T(8,128)(2,1)S(1)} collective-permute-done((bf16[3,128,256]{2,1,0:T(8,128)(2,1)S(1)}, bf16[3,128,256]{2,1,0:T(8,128)(2,1)S(1)}, u32[]{:S(2)}, u32[]{:S(2)}) %collective-permute-start.7) | collective-permute-done | bytes 196640 | tf_op jit(solution)/shard_map/ppermute | solution.py:30
  45.4 6.4 %collective-permute-done.5.refs_5_ = bf16[3,128,256]{2,1,0:T(8,128)(2,1)S(1)} collective-permute-done((bf16[3,128,256]{2,1,0:T(8,128)(2,1)}, bf16[3,128,256]{2,1,0:T(8,128)(2,1)S(1)}, u32[]{:S(2)}, u32[]{:S(2)}) %collective-permute-start.5) | collective-permute-done | bytes 196640 | tf_op jit(solution)/shard_map/ppermute | solution.py:30
  51.8 3.0 %collective-permute-done.3.refs_3_ = bf16[3,128,256]{2,1,0:T(8,128)(2,1)S(1)} collective-permute-done((bf16[3,128,256]{2,1,0:T(8,128)(2,1)}, bf16[3,128,256]{2,1,0:T(8,128)(2,1)S(1)}, u32[]{:S(2)}, u32[]{:S(2)}) %collective-permute-start.3) | collective-permute-done | bytes 196640 | tf_op jit(solution)/shard_map/ppermute | solution.py:30
  57.1 2.5 %collective-permute-done.10.far_ref = bf16[2,256,1024]{2,1,0:T(8,128)(2,1)S(1)} collective-permute-done((bf16[2,256,1024]{2,1,0:T(8,128)(2,1)S(1)}, bf16[2,256,1024]{2,1,0:T(8,128)(2,1)S(1)}, u32[]{:S(2)}, u32[]{:S(2)}) %collective-permute-start.10) | collective-permute-done | bytes 1048608 | tf_op jit(solution)/shard_map/ppermute | solution.py:30
  60.5 8.1 %attention.1 = (bf16[256,256]{1,0:T(8,128)(2,1)S(1)}, bf16[256,256]{1,0:T(8,128)(2,1)S(1)}, bf16[256,256]{1,0:T(8,128)(2,1)S(1)}, bf16[256,256]{1,0:T(8,128)(2,1)S(1)}) custom-call(s32[1]{0:T(128)} %bitcast.me_ref.refs_0_, bf16[2,256,1024]{2,1,0:T(8,128)(2,1)S(1)} %get-tuple-element.53.near_ref, bf16[2,256,1024]{2,1,0:T(8,128)(2,1)S(1)} %collective-permute-done.10.far_ref, ...), custom_call_target="tpu_custom_call" | custom-call | flops 10485760 | bytes 20480 | tf_op jit(solution)/shard_map/attention/pallas_call | solution.py:299
  74.6 4.0 %collective-permute-done.14.refs_2_ = bf16[256,256]{1,0:T(8,128)(2,1)S(1)} collective-permute-done((bf16[256,256]{1,0:T(8,128)(2,1)}, bf16[256,256]{1,0:T(8,128)(2,1)S(1)}, u32[]{:S(2)}, u32[]{:S(2)}) %collective-permute-start.14) | collective-permute-done | bytes 131104 | tf_op jit(solution)/shard_map/ppermute | solution.py:30
  85.8 3.4 %mix.1 = (bf16[640,1024]{1,0:T(8,128)(2,1)}, bf16[256,1024]{1,0:T(8,128)(2,1)S(1)}, f32[256,128]{1,0:T(8,128)S(1)}) custom-call(s32[1]{0:T(128)} %bitcast.1.me_ref, f32[2,1024]{1,0:T(2,128)S(1)} %copy-done.33, f32[8,1024]{1,0:T(8,128)S(1)} %bitcast.15, s32[2,256]{1,0:T(2,128)S(1)} %copy.13.rows_ref, s32[256,2]{1,0:T(8,128)S(1)} %bitcast.13, ...), custom_call_target="tpu_custom_call" | custom-call | flops 3407872 | bytes 20480 | tf_op jit(solution)/shard_map/mix/pallas_call | solution.py:324
  90.6 4.4 %collective-permute-done.16.refs_4_ = bf16[1,1024,256]{2,1,0:T(8,128)(2,1)} collective-permute-done((bf16[1,1024,256]{2,1,0:T(8,128)(2,1)}, bf16[1,1024,256]{2,1,0:T(8,128)(2,1)}, u32[]{:S(2)}, u32[]{:S(2)}) %collective-permute-start.16) | collective-permute-done | bytes 524320 | tf_op jit(solution)/shard_map/ppermute | solution.py:30
  95.1 7.2 %all-to-all-start = ((bf16[8,80,1024]{2,1,0:T(8,128)(2,1)}), bf16[8,80,1024]{2,1,0:T(8,128)(2,1)S(1)}, u32[]{:S(2)}, u32[]{:S(2)}) async-start(bf16[8,80,1024]{2,1,0:T(8,128)(2,1)} %bitcast.6), calls=%async_computation | async-start | bytes 2621440 | tf_op jit(solution)/shard_map/all_to_all | solution.py:354
  103.6 7.2 %collective-permute-done.19.refs_2_ = bf16[1,1024,128]{2,1,0:T(8,128)(2,1)S(1)} collective-permute-done((bf16[1,1024,128]{2,1,0:T(8,128)(2,1)}, bf16[1,1024,128]{2,1,0:T(8,128)(2,1)S(1)}, u32[]{:S(2)}, u32[]{:S(2)}) %collective-permute-start.19) | collective-permute-done | bytes 262176 | tf_op jit(solution)/shard_map/ppermute | solution.py:30
  112.8 1.9 collective-permute-done.21.refs_4_
  119.2 11.3 %all-to-all-done = bf16[8,80,1024]{2,1,0:T(8,128)(2,1)S(1)} async-done(((bf16[8,80,1024]{2,1,0:T(8,128)(2,1)}), bf16[8,80,1024]{2,1,0:T(8,128)(2,1)S(1)}, u32[]{:S(2)}, u32[]{:S(2)}) %all-to-all-start) | async-done | bytes 1310752 | tf_op jit(solution)/shard_map/all_to_all | solution.py:354
  130.5 1.6 copy-done.2
  133.1 4.6 %hidden_near.1.refs_0_ = bf16[2,640,1024]{2,1,0:T(8,128)(2,1)S(1)} custom-call(bf16[640,1024]{1,0:T(8,128)(2,1)S(1)} %bitcast.10, bf16[1,1024,1024]{2,1,0:T(8,128)(2,1)S(1)} %copy-done.2, bf16[1,1024,384]{2,1,0:T(8,128)(2,1)S(1)} %collective-permute-done.8.refs_1_, bf16[1,1024,128]{2,1,0:T(8,128)(2,1)S(1)} %copy-done.21, ...), custom_call_target="tpu_custom_call" | custom-call | flops 10485760 | bytes 32768 | tf_op jit(solution)/shard_map/hidden_near/pallas_call | solution.py:363
  137.8 3.4 %hidden_far.1.refs_1_ = bf16[2,640,1024]{2,1,0:T(8,128)(2,1)S(1)} custom-call(bf16[640,1024]{1,0:T(8,128)(2,1)S(1)} %bitcast.11, bf16[1,1024,1024]{2,1,0:T(8,128)(2,1)S(1)} %copy-done.7, bf16[1,1024,384]{2,1,0:T(8,128)(2,1)S(1)} %copy-done.10, bf16[1,1024,128]{2,1,0:T(8,128)(2,1)S(1)} %copy-done.23, bf16[1,1024,256]{2,1,0:T(8,128)(2,1)S(1)} %copy-done.14, ...), custom_call_target="tpu_custom_call" | custom-call | flops 10485760 | bytes 32768 | tf_op jit(solution)/shard_map/hidden_far/pallas_call | solution.py:363
  141.2 9.5 %collective-permute-done.23.refs_1_ = bf16[1,1024,1024]{2,1,0:T(8,128)(2,1)} collective-permute-done((bf16[1,1024,1024]{2,1,0:T(8,128)(2,1)}, bf16[1,1024,1024]{2,1,0:T(8,128)(2,1)}, u32[]{:S(2)}, u32[]{:S(2)}) %collective-permute-start.23) | collective-permute-done | bytes 2097184 | tf_op jit(solution)/shard_map/ppermute | solution.py:30
  150.7 2.9 %answer_own.1.refs_2_ = f32[640,1024]{1,0:T(8,128)S(1)} custom-call(bf16[2,640,1024]{2,1,0:T(8,128)(2,1)S(1)} %hidden_near.1.refs_0_, bf16[2,640,1024]{2,1,0:T(8,128)(2,1)S(1)} %hidden_far.1.refs_1_, bf16[1,1024,1024]{2,1,0:T(8,128)(2,1)S(1)} %copy-done.3, bf16[1,1024,1024]{2,1,0:T(8,128)(2,1)S(1)} %copy-done.5), custom_call_target="tpu_custom_call" | custom-call | flops 10485760 | bytes 40960 | tf_op jit(solution)/shard_map/answer_own/pallas_call | solution.py:393
  153.6 3.1 %answer_near.1.refs_3_ = f32[640,1024]{1,0:T(8,128)S(1)} custom-call(bf16[2,640,1024]{2,1,0:T(8,128)(2,1)S(1)} %hidden_near.1.refs_0_, bf16[1,1024,1024]{2,1,0:T(8,128)(2,1)} %collective-permute-done.23.refs_1_, f32[640,1024]{1,0:T(8,128)S(1)} %answer_own.1.refs_2_), custom_call_target="tpu_custom_call" | custom-call | flops 5242880 | bytes 40960 | tf_op jit(solution)/shard_map/answer_near/pallas_call | solution.py:393
  156.7 1.6 answer_far.1
  158.3 1.5 collective-permute-start.25
  161.9 3.7 %collective-permute-start.29 = (bf16[80,1024]{1,0:T(8,128)(2,1)S(1)}, bf16[80,1024]{1,0:T(8,128)(2,1)S(1)}, u32[]{:S(2)}, u32[]{:S(2)}) collective-permute-start(bf16[80,1024]{1,0:T(8,128)(2,1)S(1)} %get-tuple-element.86), channel_id=1, source_target_pairs={{0,5},{1,4},{2,7},{3,6},{4,1},{5,0},{6,3},{7,2},{8,13},{9,12},{10,... | collective-permute-start | bytes 491528 | tf_op jit(solution)/shard_map/ppermute | solution.py:30
  166.3 4.3 %collective-permute-done.26.refs_2_ = bf16[80,1024]{1,0:T(8,128)(2,1)S(1)} collective-permute-done((bf16[80,1024]{1,0:T(8,128)(2,1)S(1)}, bf16[80,1024]{1,0:T(8,128)(2,1)S(1)}, u32[]{:S(2)}, u32[]{:S(2)}) %collective-permute-start.26) | collective-permute-done | bytes 163872 | tf_op jit(solution)/shard_map/ppermute | solution.py:30
  170.6 2.8 %collective-permute-done.27.refs_3_ = bf16[80,1024]{1,0:T(8,128)(2,1)S(1)} collective-permute-done((bf16[80,1024]{1,0:T(8,128)(2,1)S(1)}, bf16[80,1024]{1,0:T(8,128)(2,1)S(1)}, u32[]{:S(2)}, u32[]{:S(2)}) %collective-permute-start.27) | collective-permute-done | bytes 163872 | tf_op jit(solution)/shard_map/ppermute | solution.py:30
  174.0 10.4 %collective-permute-done.29.refs_5_ = bf16[80,1024]{1,0:T(8,128)(2,1)S(1)} collective-permute-done((bf16[80,1024]{1,0:T(8,128)(2,1)S(1)}, bf16[80,1024]{1,0:T(8,128)(2,1)S(1)}, u32[]{:S(2)}, u32[]{:S(2)}) %collective-permute-start.29) | collective-permute-done | bytes 163872 | tf_op jit(solution)/shard_map/ppermute | solution.py:30
  184.4 6.5 %collective-permute-done.30.refs_6_ = bf16[80,1024]{1,0:T(8,128)(2,1)S(1)} collective-permute-done((bf16[80,1024]{1,0:T(8,128)(2,1)S(1)}, bf16[80,1024]{1,0:T(8,128)(2,1)S(1)}, u32[]{:S(2)}, u32[]{:S(2)}) %collective-permute-start.30) | collective-permute-done | bytes 163872 | tf_op jit(solution)/shard_map/ppermute | solution.py:30
  190.9 3.1 %collective-permute-done.31.refs_7_ = bf16[80,1024]{1,0:T(8,128)(2,1)S(1)} collective-permute-done((bf16[80,1024]{1,0:T(8,128)(2,1)S(1)}, bf16[80,1024]{1,0:T(8,128)(2,1)S(1)}, u32[]{:S(2)}, u32[]{:S(2)}) %collective-permute-start.31) | collective-permute-done | bytes 163872 | tf_op jit(solution)/shard_map/ppermute | solution.py:30
  194.1 2.3 %combine.1 = bf16[1,256,1024]{2,1,0:T(8,128)(2,1)} custom-call(s32[1]{0:T(128)} %bitcast.me_ref.refs_0_, f32[256,128]{1,0:T(8,128)S(1)} %copy-done.27, s32[256,2]{1,0:T(8,128)S(1)} %bitcast.14, bf16[256,1024]{1,0:T(8,128)(2,1)S(1)} %copy-done.19, bf16[80,1024]{1,0:T(8,128)(2,1)S(1)} %get-tuple-element.81.refs_0_, ...), custom_call_target="tpu_custom_call" | custom-call | flops 2621440 | bytes 12288 | tf_op jit(solution)/shard_map/combine/pallas_call | solution.py:412
  (140 shorter events, 40.7 us)
Async XLA Ops:
  6.5 65.0 %all-gather.2.cloned.1.call-start = ((), (), s32[]{:S(2)}) async-start(), calls=%async_computation.1 | async-start | bytes 1179648 | tf_op jit(solution)/shard_map/all_gather | solution.py:257
  7.7 6.7 %collective-permute-start.1 = (bf16[3,128,256]{2,1,0:T(8,128)(2,1)S(1)}, bf16[3,128,256]{2,1,0:T(8,128)(2,1)S(1)}, u32[]{:S(2)}, u32[]{:S(2)}) collective-permute-start(bf16[3,128,256]{2,1,0:T(8,128)(2,1)S(1)} %constant_dynamic-slice_fusion.refs_0_), channel_id=1, source_target_pairs={{0,1},{1,0},{2,3},{3,2},{4,5},{5,4},{6,7},{7,6},{8,9},{9,8},{10,11... | collective-permute-start | bytes 589832 | tf_op jit(solution)/shard_map/ppermute | solution.py:30
  14.4 22.2 %collective-permute-start.8 = (bf16[1,1024,384]{2,1,0:T(8,128)(2,1)}, bf16[1,1024,384]{2,1,0:T(8,128)(2,1)S(1)}, u32[]{:S(2)}, u32[]{:S(2)}) collective-permute-start(bf16[1,1024,384]{2,1,0:T(8,128)(2,1)} %get-tuple-element.49), channel_id=1, source_target_pairs={{0,16},{8,24},{16,0},{24,8},{1,17},{9,25},{17,1},{25,9},{2,18},{10... | collective-permute-start | bytes 2359304 | tf_op jit(solution)/shard_map/ppermute | solution.py:30
  16.6 20.0 %collective-permute-start.6 = (bf16[3,128,256]{2,1,0:T(8,128)(2,1)S(1)}, bf16[3,128,256]{2,1,0:T(8,128)(2,1)S(1)}, u32[]{:S(2)}, u32[]{:S(2)}) collective-permute-start(bf16[3,128,256]{2,1,0:T(8,128)(2,1)S(1)} %constant_dynamic-slice_fusion.refs_0_), channel_id=1, source_target_pairs={{0,6},{1,7},{2,4},{3,5},{4,2},{5,3},{6,0},{7,1},{8,14},{9,15},{10,... | collective-permute-start | bytes 589832 | tf_op jit(solution)/shard_map/ppermute | solution.py:30
  17.1 37.7 %collective-permute-start = (bf16[1,256,1024]{2,1,0:T(8,128)(2,1)S(1)}, bf16[1,256,1024]{2,1,0:T(8,128)(2,1)S(1)}, u32[]{:S(2)}, u32[]{:S(2)}) collective-permute-start(bf16[1,256,1024]{2,1,0:T(8,128)(2,1)S(1)} %copy-done.17), channel_id=1, source_target_pairs={{0,16},{8,24},{16,0},{24,8},{1,17},{9,25},{17,1},{25,9},{2,18},{10... | collective-permute-start | bytes 1572872 | tf_op jit(solution)/shard_map/ppermute | solution.py:30
  17.7 21.4 %collective-permute-start.4 = (bf16[3,128,256]{2,1,0:T(8,128)(2,1)S(1)}, bf16[3,128,256]{2,1,0:T(8,128)(2,1)}, u32[]{:S(2)}, u32[]{:S(2)}) collective-permute-start(bf16[3,128,256]{2,1,0:T(8,128)(2,1)S(1)} %constant_dynamic-slice_fusion.refs_0_), channel_id=1, source_target_pairs={{0,4},{1,5},{2,6},{3,7},{4,0},{5,1},{6,2},{7,3},{8,12},{9,13},{10,... | collective-permute-start | bytes 589832 | tf_op jit(solution)/shard_map/ppermute | solution.py:30
  21.1 18.4 %collective-permute-start.2 = (bf16[3,128,256]{2,1,0:T(8,128)(2,1)S(1)}, bf16[3,128,256]{2,1,0:T(8,128)(2,1)}, u32[]{:S(2)}, u32[]{:S(2)}) collective-permute-start(bf16[3,128,256]{2,1,0:T(8,128)(2,1)S(1)} %constant_dynamic-slice_fusion.refs_0_), channel_id=1, source_target_pairs={{0,2},{1,3},{2,0},{3,1},{4,6},{5,7},{6,4},{7,5},{8,10},{9,11},{10,... | collective-permute-start | bytes 589832 | tf_op jit(solution)/shard_map/ppermute | solution.py:30
  36.7 18.2 %collective-permute-start.9 = (bf16[1,1024,128]{2,1,0:T(8,128)(2,1)}, bf16[1,1024,128]{2,1,0:T(8,128)(2,1)S(1)}, u32[]{:S(2)}, u32[]{:S(2)}) collective-permute-start(bf16[1,1024,128]{2,1,0:T(8,128)(2,1)} %copy-done.36), channel_id=1, source_target_pairs={{0,16},{8,24},{16,0},{24,8},{1,17},{9,25},{17,1},{25,9},{2,18},{10... | collective-permute-start | bytes 786440 | tf_op jit(solution)/shard_map/ppermute | solution.py:30
  37.6 7.8 %collective-permute-start.7 = (bf16[3,128,256]{2,1,0:T(8,128)(2,1)S(1)}, bf16[3,128,256]{2,1,0:T(8,128)(2,1)S(1)}, u32[]{:S(2)}, u32[]{:S(2)}) collective-permute-start(bf16[3,128,256]{2,1,0:T(8,128)(2,1)S(1)} %collective-permute-done.6.refs_6_), channel_id=1, source_target_pairs={{0,1},{1,0},{2,3},{3,2},{4,5},{5,4},{6,7},{7,6},{8,9},{9,8},{10,11... | collective-permute-start | bytes 589832 | tf_op jit(solution)/shard_map/ppermute | solution.py:30
  39.1 12.7 %collective-permute-start.5 = (bf16[3,128,256]{2,1,0:T(8,128)(2,1)}, bf16[3,128,256]{2,1,0:T(8,128)(2,1)S(1)}, u32[]{:S(2)}, u32[]{:S(2)}) collective-permute-start(bf16[3,128,256]{2,1,0:T(8,128)(2,1)} %collective-permute-done.4.refs_4_), channel_id=1, source_target_pairs={{0,1},{1,0},{2,3},{3,2},{4,5},{5,4},{6,7},{7,6},{8,9},{9,8},{10,11... | collective-permute-start | bytes 589832 | tf_op jit(solution)/shard_map/ppermute | solution.py:30
  39.6 15.2 %collective-permute-start.3 = (bf16[3,128,256]{2,1,0:T(8,128)(2,1)}, bf16[3,128,256]{2,1,0:T(8,128)(2,1)S(1)}, u32[]{:S(2)}, u32[]{:S(2)}) collective-permute-start(bf16[3,128,256]{2,1,0:T(8,128)(2,1)} %collective-permute-done.2.refs_2_), channel_id=1, source_target_pairs={{0,1},{1,0},{2,3},{3,2},{4,5},{5,4},{6,7},{7,6},{8,9},{9,8},{10,11... | collective-permute-start | bytes 589832 | tf_op jit(solution)/shard_map/ppermute | solution.py:30
  57.0 14.5 %collective-permute-start.11 = (bf16[1,1024,256]{2,1,0:T(8,128)(2,1)}, bf16[1,1024,256]{2,1,0:T(8,128)(2,1)S(1)}, u32[]{:S(2)}, u32[]{:S(2)}) collective-permute-start(bf16[1,1024,256]{2,1,0:T(8,128)(2,1)} %copy-done.35), channel_id=1, source_target_pairs={{0,16},{8,24},{16,0},{24,8},{1,17},{9,25},{17,1},{25,9},{2,18},{10... | collective-permute-start | bytes 1572872 | tf_op jit(solution)/shard_map/ppermute | solution.py:30
  71.5 9.5 %collective-permute-start.12 = (bf16[1024,512]{1,0:T(8,128)(2,1)}, bf16[1024,512]{1,0:T(8,128)(2,1)S(1)}, u32[]{:S(2)}, u32[]{:S(2)}) collective-permute-start(bf16[1024,512]{1,0:T(8,128)(2,1)} %all-gather.2.cloned.1.call-done.near_ref), channel_id=1, source_target_pairs={{0,8},{8,0},{16,24},{24,16},{1,9},{9,1},{17,25},{25,17},{2,10},{10... | collective-permute-start | bytes 3145736 | tf_op jit(solution)/shard_map/ppermute | solution.py:30
  71.5 3.1 %collective-permute-start.13 = (bf16[256,256]{1,0:T(8,128)(2,1)}, bf16[256,256]{1,0:T(8,128)(2,1)S(1)}, u32[]{:S(2)}, u32[]{:S(2)}) collective-permute-start(bf16[256,256]{1,0:T(8,128)(2,1)} %copy-done.39), channel_id=1, source_target_pairs={{0,8},{8,0},{16,24},{24,16},{1,9},{9,1},{17,25},{25,17},{2,10},{10... | collective-permute-start | bytes 393224 | tf_op jit(solution)/shard_map/ppermute | solution.py:30
  72.0 6.6 %collective-permute-start.14 = (bf16[256,256]{1,0:T(8,128)(2,1)}, bf16[256,256]{1,0:T(8,128)(2,1)S(1)}, u32[]{:S(2)}, u32[]{:S(2)}) collective-permute-start(bf16[256,256]{1,0:T(8,128)(2,1)} %copy-done.38), channel_id=1, source_target_pairs={{0,16},{8,24},{16,0},{24,8},{1,17},{9,25},{17,1},{25,9},{2,18},{10... | collective-permute-start | bytes 393224 | tf_op jit(solution)/shard_map/ppermute | solution.py:30
  72.3 7.2 %collective-permute-start.15 = (bf16[256,256]{1,0:T(8,128)(2,1)}, bf16[256,256]{1,0:T(8,128)(2,1)S(1)}, u32[]{:S(2)}, u32[]{:S(2)}) collective-permute-start(bf16[256,256]{1,0:T(8,128)(2,1)} %copy-done.37), channel_id=1, source_target_pairs={{0,24},{8,16},{16,8},{24,0},{1,25},{9,17},{17,9},{25,1},{2,26},{10... | collective-permute-start | bytes 393224 | tf_op jit(solution)/shard_map/ppermute | solution.py:30
  80.1 14.9 %collective-permute-start.16 = (bf16[1,1024,256]{2,1,0:T(8,128)(2,1)}, bf16[1,1024,256]{2,1,0:T(8,128)(2,1)}, u32[]{:S(2)}, u32[]{:S(2)}) collective-permute-start(bf16[1,1024,256]{2,1,0:T(8,128)(2,1)} %copy-done.34), channel_id=1, source_target_pairs={{0,16},{8,24},{16,0},{24,8},{1,17},{9,25},{17,1},{25,9},{2,18},{10... | collective-permute-start | bytes 1572872 | tf_op jit(solution)/shard_map/ppermute | solution.py:30
  95.1 35.4 %all-to-all-start = ((bf16[8,80,1024]{2,1,0:T(8,128)(2,1)}), bf16[8,80,1024]{2,1,0:T(8,128)(2,1)S(1)}, u32[]{:S(2)}, u32[]{:S(2)}) async-start(bf16[8,80,1024]{2,1,0:T(8,128)(2,1)} %bitcast.6), calls=%async_computation | async-start | bytes 2621440 | tf_op jit(solution)/shard_map/all_to_all | solution.py:354
  102.3 14.2 %collective-permute-start.17 = (bf16[1,1024,1024]{2,1,0:T(8,128)(2,1)}, bf16[1,1024,1024]{2,1,0:T(8,128)(2,1)S(1)}, u32[]{:S(2)}, u32[]{:S(2)}) collective-permute-start(bf16[1,1024,1024]{2,1,0:T(8,128)(2,1)} %refs_0_.3), channel_id=1, source_target_pairs={{0,8},{8,0},{16,24},{24,16},{1,9},{9,1},{17,25},{25,17},{2,10},{10... | collective-permute-start | bytes 6291464 | tf_op jit(solution)/shard_map/ppermute | solution.py:30
  102.3 15.5 %collective-permute-start.22 = (bf16[1,1024,1024]{2,1,0:T(8,128)(2,1)}, bf16[1,1024,1024]{2,1,0:T(8,128)(2,1)S(1)}, u32[]{:S(2)}, u32[]{:S(2)}) collective-permute-start(bf16[1,1024,1024]{2,1,0:T(8,128)(2,1)} %refs_2_.1), channel_id=1, source_target_pairs={{0,8},{8,0},{16,24},{24,16},{1,9},{9,1},{17,25},{25,17},{2,10},{10... | collective-permute-start | bytes 6291464 | tf_op jit(solution)/shard_map/ppermute | solution.py:30
  102.8 47.9 %collective-permute-start.23 = (bf16[1,1024,1024]{2,1,0:T(8,128)(2,1)}, bf16[1,1024,1024]{2,1,0:T(8,128)(2,1)}, u32[]{:S(2)}, u32[]{:S(2)}) collective-permute-start(bf16[1,1024,1024]{2,1,0:T(8,128)(2,1)} %refs_2_.1), channel_id=1, source_target_pairs={{0,16},{8,24},{16,0},{24,8},{1,17},{9,25},{17,1},{25,9},{2,18},{10... | collective-permute-start | bytes 6291464 | tf_op jit(solution)/shard_map/ppermute | solution.py:30
  103.1 8.5 %collective-permute-start.20 = (bf16[1,1024,256]{2,1,0:T(8,128)(2,1)S(1)}, bf16[1,1024,256]{2,1,0:T(8,128)(2,1)S(1)}, u32[]{:S(2)}, u32[]{:S(2)}) collective-permute-start(bf16[1,1024,256]{2,1,0:T(8,128)(2,1)S(1)} %collective-permute-done.11.refs_3_), channel_id=1, source_target_pairs={{0,8},{8,0},{16,24},{24,16},{1,9},{9,1},{17,25},{25,17},{2,10},{10... | collective-permute-start | bytes 1572872 | tf_op jit(solution)/shard_map/ppermute | solution.py:30
  103.1 7.7 %collective-permute-start.19 = (bf16[1,1024,128]{2,1,0:T(8,128)(2,1)}, bf16[1,1024,128]{2,1,0:T(8,128)(2,1)S(1)}, u32[]{:S(2)}, u32[]{:S(2)}) collective-permute-start(bf16[1,1024,128]{2,1,0:T(8,128)(2,1)} %copy-done.20), channel_id=1, source_target_pairs={{0,8},{8,0},{16,24},{24,16},{1,9},{9,1},{17,25},{25,17},{2,10},{10... | collective-permute-start | bytes 786440 | tf_op jit(solution)/shard_map/ppermute | solution.py:30
  111.5 4.0 %collective-permute-start.18 = (bf16[1,1024,384]{2,1,0:T(8,128)(2,1)S(1)}, bf16[1,1024,384]{2,1,0:T(8,128)(2,1)S(1)}, u32[]{:S(2)}, u32[]{:S(2)}) collective-permute-start(bf16[1,1024,384]{2,1,0:T(8,128)(2,1)S(1)} %collective-permute-done.8.refs_1_), channel_id=1, source_target_pairs={{0,8},{8,0},{16,24},{24,16},{1,9},{9,1},{17,25},{25,17},{2,10},{10... | collective-permute-start | bytes 2359304 | tf_op jit(solution)/shard_map/ppermute | solution.py:30
  150.7 6.0 %collective-permute-start.24 = (bf16[1,1024,1024]{2,1,0:T(8,128)(2,1)}, bf16[1,1024,1024]{2,1,0:T(8,128)(2,1)S(1)}, u32[]{:S(2)}, u32[]{:S(2)}) collective-permute-start(bf16[1,1024,1024]{2,1,0:T(8,128)(2,1)} %collective-permute-done.23.refs_1_), channel_id=1, source_target_pairs={{0,8},{8,0},{16,24},{24,16},{1,9},{9,1},{17,25},{25,17},{2,10},{10... | collective-permute-start | bytes 6291464 | tf_op jit(solution)/shard_map/ppermute | solution.py:30
  158.3 7.4 %collective-permute-start.25 = (bf16[80,1024]{1,0:T(8,128)(2,1)S(1)}, bf16[80,1024]{1,0:T(8,128)(2,1)S(1)}, u32[]{:S(2)}, u32[]{:S(2)}) collective-permute-start(bf16[80,1024]{1,0:T(8,128)(2,1)S(1)} %get-tuple-element.82), channel_id=1, source_target_pairs={{0,1},{1,0},{2,3},{3,2},{4,5},{5,4},{6,7},{7,6},{8,9},{9,8},{10,11... | collective-permute-start | bytes 491528 | tf_op jit(solution)/shard_map/ppermute | solution.py:30
  159.8 10.7 %collective-permute-start.26 = (bf16[80,1024]{1,0:T(8,128)(2,1)S(1)}, bf16[80,1024]{1,0:T(8,128)(2,1)S(1)}, u32[]{:S(2)}, u32[]{:S(2)}) collective-permute-start(bf16[80,1024]{1,0:T(8,128)(2,1)S(1)} %get-tuple-element.83), channel_id=1, source_target_pairs={{0,2},{1,3},{2,0},{3,1},{4,6},{5,7},{6,4},{7,5},{8,10},{9,11},{10,... | collective-permute-start | bytes 491528 | tf_op jit(solution)/shard_map/ppermute | solution.py:30
  161.3 12.1 %collective-permute-start.27 = (bf16[80,1024]{1,0:T(8,128)(2,1)S(1)}, bf16[80,1024]{1,0:T(8,128)(2,1)S(1)}, u32[]{:S(2)}, u32[]{:S(2)}) collective-permute-start(bf16[80,1024]{1,0:T(8,128)(2,1)S(1)} %get-tuple-element.84), channel_id=1, source_target_pairs={{0,3},{1,2},{2,1},{3,0},{4,7},{5,6},{6,5},{7,4},{8,11},{9,10},{10,... | collective-permute-start | bytes 491528 | tf_op jit(solution)/shard_map/ppermute | solution.py:30
  161.9 12.1 %collective-permute-start.28 = (bf16[80,1024]{1,0:T(8,128)(2,1)S(1)}, bf16[80,1024]{1,0:T(8,128)(2,1)S(1)}, u32[]{:S(2)}, u32[]{:S(2)}) collective-permute-start(bf16[80,1024]{1,0:T(8,128)(2,1)S(1)} %get-tuple-element.85), channel_id=1, source_target_pairs={{0,4},{1,5},{2,6},{3,7},{4,0},{5,1},{6,2},{7,3},{8,12},{9,13},{10,... | collective-permute-start | bytes 491528 | tf_op jit(solution)/shard_map/ppermute | solution.py:30
  161.9 22.5 %collective-permute-start.29 = (bf16[80,1024]{1,0:T(8,128)(2,1)S(1)}, bf16[80,1024]{1,0:T(8,128)(2,1)S(1)}, u32[]{:S(2)}, u32[]{:S(2)}) collective-permute-start(bf16[80,1024]{1,0:T(8,128)(2,1)S(1)} %get-tuple-element.86), channel_id=1, source_target_pairs={{0,5},{1,4},{2,7},{3,6},{4,1},{5,0},{6,3},{7,2},{8,13},{9,12},{10,... | collective-permute-start | bytes 491528 | tf_op jit(solution)/shard_map/ppermute | solution.py:30
  165.7 25.2 %collective-permute-start.30 = (bf16[80,1024]{1,0:T(8,128)(2,1)S(1)}, bf16[80,1024]{1,0:T(8,128)(2,1)S(1)}, u32[]{:S(2)}, u32[]{:S(2)}) collective-permute-start(bf16[80,1024]{1,0:T(8,128)(2,1)S(1)} %get-tuple-element.87), channel_id=1, source_target_pairs={{0,6},{1,7},{2,4},{3,5},{4,2},{5,3},{6,0},{7,1},{8,14},{9,15},{10,... | collective-permute-start | bytes 491528 | tf_op jit(solution)/shard_map/ppermute | solution.py:30
  170.6 23.5 %collective-permute-start.31 = (bf16[80,1024]{1,0:T(8,128)(2,1)S(1)}, bf16[80,1024]{1,0:T(8,128)(2,1)S(1)}, u32[]{:S(2)}, u32[]{:S(2)}) collective-permute-start(bf16[80,1024]{1,0:T(8,128)(2,1)S(1)} %get-tuple-element.88), channel_id=1, source_target_pairs={{0,7},{1,6},{2,5},{3,4},{4,3},{5,2},{6,1},{7,0},{8,15},{9,14},{10,... | collective-permute-start | bytes 491528 | tf_op jit(solution)/shard_map/ppermute | solution.py:30
  (45 other events, 296.8 us)
Sparse Core Ops, SparseCore 0:
  16.7 44.1 all-gather.1

commit v9 on v8

--- a/solution.py
+++ b/solution.py
@@ -140,7 +140,7 @@
 def split_kernel(cuts, whole_ref, *refs):
     outs, sems = refs[: len(cuts)], refs[len(cuts)]
     copies = [
-        pltpu.make_async_copy(whole_ref.at[:, :, pl.ds(start, size)], outs[k], sems.at[k])
+        pltpu.make_async_copy(whole_ref.at[:, pl.ds(start, size), :], outs[k], sems.at[k])
         for k, (start, size) in enumerate(cuts)
     ]
     for copy in copies:
@@ -149,13 +149,13 @@
         copy.wait()
 
 
-def hidden_kernel(cuts, step, slots_ref, *refs):
-    hidden_ref = refs[len(cuts)]
-    for weight, (at, start, size) in zip(refs, cuts):
-        for part in range(0, size, step):
-            end = min(part + step, size)
-            half = 0.5 * jnp.dot(slots_ref[...], weight[0, :, part:end], preferred_element_type=F32)
-            hidden_ref[at, :, start + part : start + end] = (half + half * jnp.tanh(half)).astype(BF16)
+def hidden_kernel(step, slots_ref, *refs):
+    hidden_ref = refs[-1]
+    for at, weight in enumerate(refs[:-1]):
+        for part in range(0, weight.shape[2], step):
+            where = slice(part, part + step)
+            half = 0.5 * jnp.dot(slots_ref[...], weight[0, :, where], preferred_element_type=F32)
+            hidden_ref[at, :, where] = (half + half * jnp.tanh(half)).astype(BF16)
 
 
 def answer_kernel(slices, step, held, before, *refs):
@@ -164,8 +164,9 @@
     for part in range(0, answer_ref.shape[1], step):
         where = slice(part, part + step)
         total = refs[0][:, where] if before else 0.0
-        for weight, (of, place) in zip(weights, slices):
-            total += jnp.dot(hidden[of][place], weight[0, :, where], preferred_element_type=F32)
+        for weight, (of, place, start) in zip(weights, slices):
+            units = hidden[of][place, :, start : start + weight.shape[1]]
+            total += jnp.dot(units, weight[0, :, where], preferred_element_type=F32)
         answer_ref[:, where] = total.astype(answer_ref.dtype)
 
 
@@ -261,20 +262,9 @@
         tiled=True,
     )
 
-    in_cuts = cut(inner, (3, 1, 2, 2))
-    in_chunks = pl.pallas_call(
-        functools.partial(split_kernel, in_cuts),
-        out_shape=[jax.ShapeDtypeStruct((1, width, n), BF16) for _, n in in_cuts],
-        in_specs=[HBM],
-        out_specs=[HBM] * len(in_cuts),
-        scratch_shapes=[pltpu.SemaphoreType.DMA((len(in_cuts),))],
-        compiler_params=params(20),
-        cost_estimate=cost(0, 4 << 20),
-        name="split",
-    )(expert_in)
-    in_held = [spread_over(after(in_chunks[0], qkv[1]), "dp", 2)]
-    in_held.append(spread_over(after(in_chunks[1], (in_held[0], qkv[exp_count - 2])), "dp", 2))
-    raw[half] = after(raw[half], (qkv, in_held[1]))
+    in_near = spread_over(after(expert_in, (raw[half], qkv[1], qkv[2], qkv[4])), "dp", 2)
+
+    raw[half] = after(raw[half], qkv)
 
     groups = len(raw)
     member = jnp.arange(groups, dtype=jnp.int32) * 2
@@ -294,7 +284,6 @@
         name="norm",
     )(place, norm_gains, *[raw[2 * k] for k in range(groups)])
     far = swap(near, "dp", 1)
-    in_held.append(spread_over(after(in_chunks[2], near), "dp", 2))
 
     contexts = pl.pallas_call(
         functools.partial(attention_kernel, dp_count, exp_count),
@@ -313,12 +302,23 @@
         name="attention",
     )(exp_index[None], near, far, *[qkv[k] for k in range(exp_count)])
 
-    contexts = after(contexts, in_held[2])
+    contexts = [*contexts[:-1], after(contexts[-1], in_near)]
     crossed = [swap(contexts[k], "dp", k) for k in range(1, dp_count)]
 
     proj_far = swap(after(proj_near, contexts), "dp", 1)
 
-    in_held.append(spread_over(after(in_chunks[3], crossed), "dp", 2))
+    out_cuts = cut(inner, (1, 3))
+    out_chunks = pl.pallas_call(
+        functools.partial(split_kernel, out_cuts),
+        out_shape=[jax.ShapeDtypeStruct((1, n, width), BF16) for _, n in out_cuts],
+        in_specs=[HBM],
+        out_specs=[HBM] * len(out_cuts),
+        scratch_shapes=[pltpu.SemaphoreType.DMA((len(out_cuts),))],
+        compiler_params=params(20),
+        cost_estimate=cost(0, 4 << 20),
+        name="split",
+    )(after(expert_out, qkv))
+    out_held = [spread_over(after(out_chunks[0], crossed), "dp", 2)]
 
     cols = expert_ids[0]
     slots, mixed, gate = pl.pallas_call(
@@ -341,42 +341,38 @@
         name="mix",
     )(me[None], norm_gains, router.T, cols.T, cols, stream, proj_near, proj_far, contexts[0], *crossed)
 
-    slots = after(slots, in_held[3])
-    out_held = spread_over(after(expert_out, (in_held[3], mixed)), "dp", 2)
-    in_far, in_near, in_places = [swap(after(expert_in, mixed), "dp", 1)], [expert_in], [(0, 0, inner)]
-    out_own = swap(after(expert_out, mixed), "dp", 1)
-    for k in range(2, dp_count, 2):
-        for held, place in zip(in_held, in_cuts):
-            in_near.append(held[k])
-            in_far.append(swap(after(held[k], mixed), "dp", 1))
-            in_places.append((k // 2, *place))
+    slots = after(slots, out_held[0])
+    out_held.append(spread_over(after(out_chunks[1], (out_held[0], gate)), "dp", 2))
+    in_far = {k: swap(after(block, gate), "dp", 1) for k, block in in_near.items()}
+    out_own = swap(after(expert_out, gate), "dp", 1)
 
     arrived = lax.all_to_all(
         slots.reshape(exp_count, capacity, width), "expert", split_axis=0, concat_axis=0, tiled=True
     ).reshape(slots_count, width)
 
 
-    arrived = after(arrived, (in_far, out_own))
+    out_first = {k: swap(after(block, gate), "dp", 1) for k, block in out_held[0].items() if k}
+    arrived = after(arrived, (in_far, out_own, out_first))
     step = min(512, inner)
 
     def hidden_units(slots_in, held, name):
         return pl.pallas_call(
-            functools.partial(hidden_kernel, in_places, step),
+            functools.partial(hidden_kernel, step),
             out_shape=jax.ShapeDtypeStruct((groups, slots_count, inner), BF16),
-            in_specs=[VMEM] + [VMEM] * len(in_places),
+            in_specs=[VMEM] * (1 + groups),
             out_specs=VMEM,
             compiler_params=params(16),
             cost_estimate=cost(2 * slots_count * width * inner * groups, 8 << 20),
             name=name,
-        )(slots_in, *held)
+        )(slots_in, *[held[k] for k in sorted(held)])
 
     hidden = [hidden_units(arrived, in_near, "hidden_near")]
     hidden.append(hidden_units(after(arrived, hidden[0]), in_far, "hidden_far"))
 
     def answers(slices, weights, before, name):
         count = len(slices)
-        used = sorted({of for of, _ in slices})
-        slices = [(used.index(of), place) for of, place in slices]
+        used = sorted({of for of, _, _ in slices})
+        slices = [(used.index(of), place, start) for of, place, start in slices]
         inputs = [hidden[of] for of in used]
         extra = [] if before is None else [before]
         if name == "answer_far":
@@ -401,11 +397,17 @@
         )(*inputs, *weights, *extra)
 
     distant = range(1, groups)
-    answer = answers([(0, 0), (1, 0)], [expert_out, out_own], None, "answer_own")
-    out_near = [after(out_held[2 * k], hidden[1]) for k in distant]
+    (_, _), (rest, _) = out_cuts
+    answer = answers(
+        [(0, 0, 0), (1, 0, 0)] + [(of, k, 0) for of in (0, 1) for k in distant],
+        [expert_out, out_own] + [held[2 * k] for held in (out_held[0], out_first) for k in distant],
+        None,
+        "answer_first",
+    )
+    out_near = [after(out_held[1][2 * k], hidden[0]) for k in distant]
     out_far = [swap(block, "dp", 1) for block in out_near]
-    answer = answers([(0, k) for k in distant], out_near, answer, "answer_near")
-    answer = answers([(1, k) for k in distant], out_far, answer, "answer_far")
+    answer = answers([(0, k, rest) for k in distant], out_near, answer, "answer_near")
+    answer = answers([(1, k, rest) for k in distant], out_far, answer, "answer_far")
     returned = {k: swap(answer[k], "expert", k) for k in reversed(range(1, exp_count))}
     returned[0] = answer[0]
 

time: 204 us -> 191 us (0.936)
  waiting for transfers between devices: 101 us -> 89.7 us
    ppermute x32 -> x28, waiting for transfers between devices: 89.9 us -> 74 us  [swap(): return lax.ppermute(block, axis, [(i, i ^ mask) for i in range(count)])]
    all_to_all x1, waiting for transfers between devices: 11.3 us -> 15.7 us  [body(): lax.all_to_all(slots.reshape(exp_count, capacity, width), 'expert', split...]
    unnamed x87 -> x73, local copies, waits for them, and re-layouts: 24.2 us -> 21.9 us
    ppermute x32 -> x28, starting transfers between devices: 23.8 us -> 24.1 us  [swap(): return lax.ppermute(block, axis, [(i, i ^ mask) for i in range(count)])]
  transfers between devices with their start and end apart: 34 -> 30, of which waited for: 21 -> 21; matrix products, arithmetic and copies ran while one was open for 1% -> 2% of each run, Pallas kernels for 14% -> 15%
where the time goes in v9:
time: 191 us; the launch traced here: 190 us
  waiting for transfers between devices  89.7 us (47%)
  Pallas kernels  31.6 us (17%)
  starting transfers between devices  30.5 us (16%)
  local copies, waits for them, and re-layouts  24.9 us (13%)
  between operations  13.7 us (7%)
    ppermute x28, waiting for transfers between devices, swap(): return lax.ppermute(block, axis, [(i, i ^ mask) for i in range(count)])  74 us
    ppermute x28, starting transfers between devices, swap(): return lax.ppermute(block, axis, [(i, i ^ mask) for i in range(count)])  24.1 us
    unnamed x73, local copies, waits for them, and re-layouts  21.9 us
    all_to_all x1, waiting for transfers between devices, body(): lax.all_to_all(slots.reshape(exp_count, capacity, width), 'expert', split...  15.7 us
    pallas_call x2, Pallas kernels, hidden_units(): pl.pallas_call(functools.partial(hidden_kernel, step), out_shape=jax.Shap...  8.15 us
    pallas_call x1, Pallas kernels, body(): pl.pallas_call(functools.partial(attention_kernel, dp_count, exp_count),...  7.04 us
    all_to_all x1, starting transfers between devices, body(): lax.all_to_all(slots.reshape(exp_count, capacity, width), 'expert', split...  6.38 us
    pallas_call x2, Pallas kernels, answers(): pl.pallas_call(functools.partial(answer_kernel, slices, rows, len(used),...  6.14 us
  transfers between devices with their start and end apart: 30, of which 21 were waited for; matrix products, arithmetic and copies ran while one was open for 2% of the time, Pallas kernels for 15%

profile of v9, /device:TPU:16, one launch (start us, length us, event | category | flops | bytes accessed | tf_op | source)
XLA Modules:
  0.0 190.4 jit_solution(4456576577807931499)
XLA Ops:
  6.5 1.5 collective-permute-start
  8.5 1.6 collective-permute-start.2
  11.6 5.4 %collective-permute-done.4.refs_4_ = bf16[3,128,256]{2,1,0:T(8,128)(2,1)S(1)} collective-permute-done((bf16[3,128,256]{2,1,0:T(8,128)(2,1)S(1)}, bf16[3,128,256]{2,1,0:T(8,128)(2,1)S(1)}, u32[]{:S(2)}, u32[]{:S(2)}) %collective-permute-start.4) | collective-permute-done | bytes 196640 | tf_op jit(solution)/shard_map/ppermute | solution.py:30
  16.9 1.7 collective-permute-done.2.refs_2_
  18.7 1.7 collective-permute-done.refs_1_
  21.9 1.6 constant_dynamic-slice_fusion.1
  27.4 5.9 %collective-permute-done.6.refs_6_ = bf16[3,128,256]{2,1,0:T(8,128)(2,1)S(1)} collective-permute-done((bf16[3,128,256]{2,1,0:T(8,128)(2,1)S(1)}, bf16[3,128,256]{2,1,0:T(8,128)(2,1)S(1)}, u32[]{:S(2)}, u32[]{:S(2)}) %collective-permute-start.6) | collective-permute-done | bytes 196640 | tf_op jit(solution)/shard_map/ppermute | solution.py:30
  35.5 4.9 %collective-permute-done.7.refs_7_ = bf16[3,128,256]{2,1,0:T(8,128)(2,1)S(1)} collective-permute-done((bf16[3,128,256]{2,1,0:T(8,128)(2,1)S(1)}, bf16[3,128,256]{2,1,0:T(8,128)(2,1)S(1)}, u32[]{:S(2)}, u32[]{:S(2)}) %collective-permute-start.7) | collective-permute-done | bytes 196640 | tf_op jit(solution)/shard_map/ppermute | solution.py:30
  44.3 2.7 %collective-permute-done.8.far_ref = bf16[2,256,1024]{2,1,0:T(8,128)(2,1)S(1)} collective-permute-done((bf16[2,256,1024]{2,1,0:T(8,128)(2,1)S(1)}, bf16[2,256,1024]{2,1,0:T(8,128)(2,1)S(1)}, u32[]{:S(2)}, u32[]{:S(2)}) %collective-permute-start.8) | collective-permute-done | bytes 1048608 | tf_op jit(solution)/shard_map/ppermute | solution.py:30
  48.8 7.0 %attention.1 = (bf16[256,256]{1,0:T(8,128)(2,1)S(1)}, bf16[256,256]{1,0:T(8,128)(2,1)S(1)}, bf16[256,256]{1,0:T(8,128)(2,1)S(1)}, bf16[256,256]{1,0:T(8,128)(2,1)S(1)}) custom-call(s32[1]{0:T(128)} %bitcast.me_ref.refs_0_, bf16[2,256,1024]{2,1,0:T(8,128)(2,1)S(1)} %get-tuple-element.41.near_ref, bf16[2,256,1024]{2,1,0:T(8,128)(2,1)S(1)} %collective-permute-done.8.far_ref, ...), custom_call_target="tpu_custom_call" | custom-call | flops 10485760 | bytes 20480 | tf_op jit(solution)/shard_map/attention/pallas_call | solution.py:288
  58.4 8.8 %collective-permute-done.9.refs_1_ = bf16[1,1024,1024]{2,1,0:T(8,128)(2,1)} collective-permute-done((bf16[1,1024,1024]{2,1,0:T(8,128)(2,1)}, bf16[1,1024,1024]{2,1,0:T(8,128)(2,1)}, u32[]{:S(2)}, u32[]{:S(2)}) %collective-permute-start.9) | collective-permute-done | bytes 2097184 | tf_op jit(solution)/shard_map/ppermute | solution.py:30
  70.8 3.4 %collective-permute-done.12.refs_2_ = bf16[256,256]{1,0:T(8,128)(2,1)S(1)} collective-permute-done((bf16[256,256]{1,0:T(8,128)(2,1)}, bf16[256,256]{1,0:T(8,128)(2,1)S(1)}, u32[]{:S(2)}, u32[]{:S(2)}) %collective-permute-start.12) | collective-permute-done | bytes 131104 | tf_op jit(solution)/shard_map/ppermute | solution.py:30
  83.2 4.5 %mix.1 = (bf16[640,1024]{1,0:T(8,128)(2,1)}, bf16[256,1024]{1,0:T(8,128)(2,1)S(1)}, f32[256,128]{1,0:T(8,128)S(1)}) custom-call(s32[1]{0:T(128)} %bitcast.1.me_ref, f32[2,1024]{1,0:T(2,128)S(1)} %copy-done.30, f32[8,1024]{1,0:T(8,128)S(1)} %bitcast.15, s32[2,256]{1,0:T(2,128)S(1)} %copy.13.rows_ref, s32[256,2]{1,0:T(8,128)S(1)} %bitcast.13, ...), custom_call_target="tpu_custom_call" | custom-call | flops 3407872 | bytes 20480 | tf_op jit(solution)/shard_map/mix/pallas_call | solution.py:324
  88.6 2.1 %collective-permute-done.14.refs_4_ = bf16[1,256,1024]{2,1,0:T(8,128)(2,1)S(1)} collective-permute-done((bf16[1,256,1024]{2,1,0:T(8,128)(2,1)}, bf16[1,256,1024]{2,1,0:T(8,128)(2,1)S(1)}, u32[]{:S(2)}, u32[]{:S(2)}) %collective-permute-start.14) | collective-permute-done | bytes 524320 | tf_op jit(solution)/shard_map/ppermute | solution.py:30
  90.7 6.4 %all-to-all-start = ((bf16[8,80,1024]{2,1,0:T(8,128)(2,1)}), bf16[8,80,1024]{2,1,0:T(8,128)(2,1)S(1)}, u32[]{:S(2)}, u32[]{:S(2)}) async-start(bf16[8,80,1024]{2,1,0:T(8,128)(2,1)} %bitcast.6), calls=%async_computation | async-start | bytes 2621440 | tf_op jit(solution)/shard_map/all_to_all | solution.py:349
  99.2 3.5 %collective-permute-done.18.refs_5_ = bf16[1,256,1024]{2,1,0:T(8,128)(2,1)S(1)} collective-permute-done((bf16[1,256,1024]{2,1,0:T(8,128)(2,1)S(1)}, bf16[1,256,1024]{2,1,0:T(8,128)(2,1)S(1)}, u32[]{:S(2)}, u32[]{:S(2)}) %collective-permute-start.18) | collective-permute-done | bytes 524320 | tf_op jit(solution)/shard_map/ppermute | solution.py:30
  106.5 1.7 collective-permute-done.17.refs_3_
  109.6 15.7 %all-to-all-done = bf16[8,80,1024]{2,1,0:T(8,128)(2,1)S(1)} async-done(((bf16[8,80,1024]{2,1,0:T(8,128)(2,1)}), bf16[8,80,1024]{2,1,0:T(8,128)(2,1)S(1)}, u32[]{:S(2)}, u32[]{:S(2)}) %all-to-all-start) | async-done | bytes 1310752 | tf_op jit(solution)/shard_map/all_to_all | solution.py:349
  125.3 1.6 copy-done.5
  126.9 4.9 %hidden_near.1.refs_0_ = bf16[2,640,1024]{2,1,0:T(8,128)(2,1)S(1)} custom-call(bf16[640,1024]{1,0:T(8,128)(2,1)S(1)} %bitcast.10, bf16[1,1024,1024]{2,1,0:T(8,128)(2,1)S(1)} %copy-done.5, bf16[1,1024,1024]{2,1,0:T(8,128)(2,1)} %collective-permute-done.9.refs_1_), custom_call_target="tpu_custom_call" | custom-call | flops 10485760 | bytes 32768 | tf_op jit(solution)/shard_map/hidden_near/pallas_call | solution.py:359
  131.8 2.9 %collective-permute-done.19.refs_1_ = bf16[1,768,1024]{2,1,0:T(8,128)(2,1)} collective-permute-done((bf16[1,768,1024]{2,1,0:T(8,128)(2,1)}, bf16[1,768,1024]{2,1,0:T(8,128)(2,1)}, u32[]{:S(2)}, u32[]{:S(2)}) %collective-permute-start.19) | collective-permute-done | bytes 1572896 | tf_op jit(solution)/shard_map/ppermute | solution.py:30
  134.7 3.2 %hidden_far.1.refs_1_ = bf16[2,640,1024]{2,1,0:T(8,128)(2,1)S(1)} custom-call(bf16[640,1024]{1,0:T(8,128)(2,1)S(1)} %bitcast.11, bf16[1,1024,1024]{2,1,0:T(8,128)(2,1)S(1)} %copy-done.7, bf16[1,1024,1024]{2,1,0:T(8,128)(2,1)S(1)} %copy-done.9), custom_call_target="tpu_custom_call" | custom-call | flops 10485760 | bytes 32768 | tf_op jit(solution)/shard_map/hidden_far/pallas_call | solution.py:359
  137.9 3.5 %answer_first.1.refs_2_ = f32[640,1024]{1,0:T(8,128)S(1)} custom-call(bf16[2,640,1024]{2,1,0:T(8,128)(2,1)S(1)} %hidden_near.1.refs_0_, bf16[2,640,1024]{2,1,0:T(8,128)(2,1)S(1)} %hidden_far.1.refs_1_, bf16[1,1024,1024]{2,1,0:T(8,128)(2,1)S(1)} %copy-done.2, bf16[1,1024,1024]{2,1,0:T(8,128)(2,1)S(1)} %copy-done.4, ...), custom_call_target="tpu_custom_call" | custom-call | flops 20971520 | bytes 40960 | tf_op jit(solution)/shard_map/answer_first/pallas_call | solution.py:389
  141.5 2.6 %answer_near.1.refs_3_ = f32[640,1024]{1,0:T(8,128)S(1)} custom-call(bf16[2,640,1024]{2,1,0:T(8,128)(2,1)S(1)} %hidden_near.1.refs_0_, bf16[1,768,1024]{2,1,0:T(8,128)(2,1)} %collective-permute-done.19.refs_1_, f32[640,1024]{1,0:T(8,128)S(1)} %answer_first.1.refs_2_), custom_call_target="tpu_custom_call" | custom-call | flops 5242880 | bytes 40960 | tf_op jit(solution)/shard_map/answer_near/pallas_call | solution.py:389
  145.4 1.5 collective-permute-start.21
  149.5 3.3 %collective-permute-start.25 = (bf16[80,1024]{1,0:T(8,128)(2,1)S(1)}, bf16[80,1024]{1,0:T(8,128)(2,1)S(1)}, u32[]{:S(2)}, u32[]{:S(2)}) collective-permute-start(bf16[80,1024]{1,0:T(8,128)(2,1)S(1)} %get-tuple-element.70), channel_id=1, source_target_pairs={{0,5},{1,4},{2,7},{3,6},{4,1},{5,0},{6,3},{7,2},{8,13},{9,12},{10,... | collective-permute-start | bytes 491528 | tf_op jit(solution)/shard_map/ppermute | solution.py:30
  153.3 4.3 %collective-permute-done.22.refs_2_ = bf16[80,1024]{1,0:T(8,128)(2,1)S(1)} collective-permute-done((bf16[80,1024]{1,0:T(8,128)(2,1)S(1)}, bf16[80,1024]{1,0:T(8,128)(2,1)S(1)}, u32[]{:S(2)}, u32[]{:S(2)}) %collective-permute-start.22) | collective-permute-done | bytes 163872 | tf_op jit(solution)/shard_map/ppermute | solution.py:30
  157.7 2.7 %collective-permute-done.23.refs_3_ = bf16[80,1024]{1,0:T(8,128)(2,1)S(1)} collective-permute-done((bf16[80,1024]{1,0:T(8,128)(2,1)S(1)}, bf16[80,1024]{1,0:T(8,128)(2,1)S(1)}, u32[]{:S(2)}, u32[]{:S(2)}) %collective-permute-start.23) | collective-permute-done | bytes 163872 | tf_op jit(solution)/shard_map/ppermute | solution.py:30
  161.1 10.4 %collective-permute-done.25.refs_5_ = bf16[80,1024]{1,0:T(8,128)(2,1)S(1)} collective-permute-done((bf16[80,1024]{1,0:T(8,128)(2,1)S(1)}, bf16[80,1024]{1,0:T(8,128)(2,1)S(1)}, u32[]{:S(2)}, u32[]{:S(2)}) %collective-permute-start.25) | collective-permute-done | bytes 163872 | tf_op jit(solution)/shard_map/ppermute | solution.py:30
  171.5 6.5 %collective-permute-done.26.refs_6_ = bf16[80,1024]{1,0:T(8,128)(2,1)S(1)} collective-permute-done((bf16[80,1024]{1,0:T(8,128)(2,1)S(1)}, bf16[80,1024]{1,0:T(8,128)(2,1)S(1)}, u32[]{:S(2)}, u32[]{:S(2)}) %collective-permute-start.26) | collective-permute-done | bytes 163872 | tf_op jit(solution)/shard_map/ppermute | solution.py:30
  178.0 3.1 %collective-permute-done.27.refs_7_ = bf16[80,1024]{1,0:T(8,128)(2,1)S(1)} collective-permute-done((bf16[80,1024]{1,0:T(8,128)(2,1)S(1)}, bf16[80,1024]{1,0:T(8,128)(2,1)S(1)}, u32[]{:S(2)}, u32[]{:S(2)}) %collective-permute-start.27) | collective-permute-done | bytes 163872 | tf_op jit(solution)/shard_map/ppermute | solution.py:30
  181.1 2.3 %combine.1 = bf16[1,256,1024]{2,1,0:T(8,128)(2,1)} custom-call(s32[1]{0:T(128)} %bitcast.me_ref.refs_0_, f32[256,128]{1,0:T(8,128)S(1)} %get-tuple-element.49.gate_ref, s32[256,2]{1,0:T(8,128)S(1)} %bitcast.14, bf16[256,1024]{1,0:T(8,128)(2,1)S(1)} %copy-done.15, bf16[80,1024]{1,0:T(8,128)(2,1)S(1)} %get-tuple-element.65.refs_0_, ...), custom_call_target="tpu_custom_call" | custom-call | flops 2621440 | bytes 12288 | tf_op jit(solution)/shard_map/combine/pallas_call | solution.py:414
  (118 shorter events, 43.5 us)
Async XLA Ops:
  6.5 60.7 %all-gather.2.cloned.1.call-start = ((), (), s32[]{:S(2)}) async-start(), calls=%async_computation.1 | async-start | bytes 1179648 | tf_op jit(solution)/shard_map/all_gather | solution.py:258
  6.5 13.9 %collective-permute-start = (bf16[1,256,1024]{2,1,0:T(8,128)(2,1)}, bf16[1,256,1024]{2,1,0:T(8,128)(2,1)S(1)}, u32[]{:S(2)}, u32[]{:S(2)}) collective-permute-start(bf16[1,256,1024]{2,1,0:T(8,128)(2,1)} %refs_0_.1), channel_id=1, source_target_pairs={{0,16},{8,24},{16,0},{24,8},{1,17},{9,25},{17,1},{25,9},{2,18},{10... | collective-permute-start | bytes 1572872 | tf_op jit(solution)/shard_map/ppermute | solution.py:30
  8.1 8.8 %collective-permute-start.4 = (bf16[3,128,256]{2,1,0:T(8,128)(2,1)S(1)}, bf16[3,128,256]{2,1,0:T(8,128)(2,1)S(1)}, u32[]{:S(2)}, u32[]{:S(2)}) collective-permute-start(bf16[3,128,256]{2,1,0:T(8,128)(2,1)S(1)} %constant_dynamic-slice_fusion.refs_0_), channel_id=1, source_target_pairs={{0,4},{1,5},{2,6},{3,7},{4,0},{5,1},{6,2},{7,3},{8,12},{9,13},{10,... | collective-permute-start | bytes 589832 | tf_op jit(solution)/shard_map/ppermute | solution.py:30
  8.5 10.2 %collective-permute-start.2 = (bf16[3,128,256]{2,1,0:T(8,128)(2,1)S(1)}, bf16[3,128,256]{2,1,0:T(8,128)(2,1)S(1)}, u32[]{:S(2)}, u32[]{:S(2)}) collective-permute-start(bf16[3,128,256]{2,1,0:T(8,128)(2,1)S(1)} %constant_dynamic-slice_fusion.refs_0_), channel_id=1, source_target_pairs={{0,2},{1,3},{2,0},{3,1},{4,6},{5,7},{6,4},{7,5},{8,10},{9,11},{10,... | collective-permute-start | bytes 589832 | tf_op jit(solution)/shard_map/ppermute | solution.py:30
  10.1 8.6 %collective-permute-start.1 = (bf16[3,128,256]{2,1,0:T(8,128)(2,1)S(1)}, bf16[3,128,256]{2,1,0:T(8,128)(2,1)S(1)}, u32[]{:S(2)}, u32[]{:S(2)}) collective-permute-start(bf16[3,128,256]{2,1,0:T(8,128)(2,1)S(1)} %constant_dynamic-slice_fusion.refs_0_), channel_id=1, source_target_pairs={{0,1},{1,0},{2,3},{3,2},{4,5},{5,4},{6,7},{7,6},{8,9},{9,8},{10,11... | collective-permute-start | bytes 589832 | tf_op jit(solution)/shard_map/ppermute | solution.py:30
  20.4 46.8 %collective-permute-start.9 = (bf16[1,1024,1024]{2,1,0:T(8,128)(2,1)}, bf16[1,1024,1024]{2,1,0:T(8,128)(2,1)}, u32[]{:S(2)}, u32[]{:S(2)}) collective-permute-start(bf16[1,1024,1024]{2,1,0:T(8,128)(2,1)} %refs_0_.2), channel_id=1, source_target_pairs={{0,16},{8,24},{16,0},{24,8},{1,17},{9,25},{17,1},{25,9},{2,18},{10... | collective-permute-start | bytes 6291464 | tf_op jit(solution)/shard_map/ppermute | solution.py:30
  23.5 9.8 %collective-permute-start.6 = (bf16[3,128,256]{2,1,0:T(8,128)(2,1)S(1)}, bf16[3,128,256]{2,1,0:T(8,128)(2,1)S(1)}, u32[]{:S(2)}, u32[]{:S(2)}) collective-permute-start(bf16[3,128,256]{2,1,0:T(8,128)(2,1)S(1)} %constant_dynamic-slice_fusion.refs_0_), channel_id=1, source_target_pairs={{0,6},{1,7},{2,4},{3,5},{4,2},{5,3},{6,0},{7,1},{8,14},{9,15},{10,... | collective-permute-start | bytes 589832 | tf_op jit(solution)/shard_map/ppermute | solution.py:30
  25.4 15.0 %collective-permute-start.5 = (bf16[3,128,256]{2,1,0:T(8,128)(2,1)S(1)}, bf16[3,128,256]{2,1,0:T(8,128)(2,1)S(1)}, u32[]{:S(2)}, u32[]{:S(2)}) collective-permute-start(bf16[3,128,256]{2,1,0:T(8,128)(2,1)S(1)} %collective-permute-done.4.refs_4_), channel_id=1, source_target_pairs={{0,1},{1,0},{2,3},{3,2},{4,5},{5,4},{6,7},{7,6},{8,9},{9,8},{10,11... | collective-permute-start | bytes 589832 | tf_op jit(solution)/shard_map/ppermute | solution.py:30
  26.9 13.6 %collective-permute-start.3 = (bf16[3,128,256]{2,1,0:T(8,128)(2,1)S(1)}, bf16[3,128,256]{2,1,0:T(8,128)(2,1)S(1)}, u32[]{:S(2)}, u32[]{:S(2)}) collective-permute-start(bf16[3,128,256]{2,1,0:T(8,128)(2,1)S(1)} %collective-permute-done.2.refs_2_), channel_id=1, source_target_pairs={{0,1},{1,0},{2,3},{3,2},{4,5},{5,4},{6,7},{7,6},{8,9},{9,8},{10,11... | collective-permute-start | bytes 589832 | tf_op jit(solution)/shard_map/ppermute | solution.py:30
  33.3 7.1 %collective-permute-start.7 = (bf16[3,128,256]{2,1,0:T(8,128)(2,1)S(1)}, bf16[3,128,256]{2,1,0:T(8,128)(2,1)S(1)}, u32[]{:S(2)}, u32[]{:S(2)}) collective-permute-start(bf16[3,128,256]{2,1,0:T(8,128)(2,1)S(1)} %collective-permute-done.6.refs_6_), channel_id=1, source_target_pairs={{0,1},{1,0},{2,3},{3,2},{4,5},{5,4},{6,7},{7,6},{8,9},{9,8},{10,11... | collective-permute-start | bytes 589832 | tf_op jit(solution)/shard_map/ppermute | solution.py:30
  44.3 2.7 %collective-permute-start.8 = (bf16[2,256,1024]{2,1,0:T(8,128)(2,1)S(1)}, bf16[2,256,1024]{2,1,0:T(8,128)(2,1)S(1)}, u32[]{:S(2)}, u32[]{:S(2)}) collective-permute-start(bf16[2,256,1024]{2,1,0:T(8,128)(2,1)S(1)} %get-tuple-element.41.near_ref), channel_id=1, source_target_pairs={{0,8},{8,0},{16,24},{24,16},{1,9},{9,1},{17,25},{25,17},{2,10},{10... | collective-permute-start | bytes 3145736 | tf_op jit(solution)/shard_map/ppermute | solution.py:30
  48.8 28.6 %copy-start.35 = (s32[1,256,2]{1,2,0:T(2,128)S(1)}, s32[1,256,2]{1,2,0:T(2,128)}, u32[]{:S(2)}) copy-start(s32[1,256,2]{1,2,0:T(2,128)} %param.11) | copy-start | bytes 6148
  67.2 10.4 %collective-permute-start.10 = (bf16[1024,512]{1,0:T(8,128)(2,1)}, bf16[1024,512]{1,0:T(8,128)(2,1)}, u32[]{:S(2)}, u32[]{:S(2)}) collective-permute-start(bf16[1024,512]{1,0:T(8,128)(2,1)} %all-gather.2.cloned.1.call-done.near_ref), channel_id=1, source_target_pairs={{0,8},{8,0},{16,24},{24,16},{1,9},{9,1},{17,25},{25,17},{2,10},{10... | collective-permute-start | bytes 3145736 | tf_op jit(solution)/shard_map/ppermute | solution.py:30
  67.2 2.9 %collective-permute-start.11 = (bf16[256,256]{1,0:T(8,128)(2,1)}, bf16[256,256]{1,0:T(8,128)(2,1)S(1)}, u32[]{:S(2)}, u32[]{:S(2)}) collective-permute-start(bf16[256,256]{1,0:T(8,128)(2,1)} %copy-done.34), channel_id=1, source_target_pairs={{0,8},{8,0},{16,24},{24,16},{1,9},{9,1},{17,25},{25,17},{2,10},{10... | collective-permute-start | bytes 393224 | tf_op jit(solution)/shard_map/ppermute | solution.py:30
  67.7 6.5 %collective-permute-start.12 = (bf16[256,256]{1,0:T(8,128)(2,1)}, bf16[256,256]{1,0:T(8,128)(2,1)S(1)}, u32[]{:S(2)}, u32[]{:S(2)}) collective-permute-start(bf16[256,256]{1,0:T(8,128)(2,1)} %copy-done.33), channel_id=1, source_target_pairs={{0,16},{8,24},{16,0},{24,8},{1,17},{9,25},{17,1},{25,9},{2,18},{10... | collective-permute-start | bytes 393224 | tf_op jit(solution)/shard_map/ppermute | solution.py:30
  69.3 6.0 %collective-permute-start.13 = (bf16[256,256]{1,0:T(8,128)(2,1)}, bf16[256,256]{1,0:T(8,128)(2,1)S(1)}, u32[]{:S(2)}, u32[]{:S(2)}) collective-permute-start(bf16[256,256]{1,0:T(8,128)(2,1)} %copy-done.32), channel_id=1, source_target_pairs={{0,24},{8,16},{16,8},{24,0},{1,25},{9,17},{17,9},{25,1},{2,26},{10... | collective-permute-start | bytes 393224 | tf_op jit(solution)/shard_map/ppermute | solution.py:30
  76.0 14.7 %collective-permute-start.14 = (bf16[1,256,1024]{2,1,0:T(8,128)(2,1)}, bf16[1,256,1024]{2,1,0:T(8,128)(2,1)S(1)}, u32[]{:S(2)}, u32[]{:S(2)}) collective-permute-start(bf16[1,256,1024]{2,1,0:T(8,128)(2,1)} %get-tuple-element.54), channel_id=1, source_target_pairs={{0,16},{8,24},{16,0},{24,8},{1,17},{9,25},{17,1},{25,9},{2,18},{10... | collective-permute-start | bytes 1572872 | tf_op jit(solution)/shard_map/ppermute | solution.py:30
  90.7 34.6 %all-to-all-start = ((bf16[8,80,1024]{2,1,0:T(8,128)(2,1)}), bf16[8,80,1024]{2,1,0:T(8,128)(2,1)S(1)}, u32[]{:S(2)}, u32[]{:S(2)}) async-start(bf16[8,80,1024]{2,1,0:T(8,128)(2,1)} %bitcast.6), calls=%async_computation | async-start | bytes 2621440 | tf_op jit(solution)/shard_map/all_to_all | solution.py:349
  97.1 5.7 %collective-permute-start.15 = (bf16[1,1024,1024]{2,1,0:T(8,128)(2,1)}, bf16[1,1024,1024]{2,1,0:T(8,128)(2,1)S(1)}, u32[]{:S(2)}, u32[]{:S(2)}) collective-permute-start(bf16[1,1024,1024]{2,1,0:T(8,128)(2,1)} %refs_0_.2), channel_id=1, source_target_pairs={{0,8},{8,0},{16,24},{24,16},{1,9},{9,1},{17,25},{25,17},{2,10},{10... | collective-permute-start | bytes 6291464 | tf_op jit(solution)/shard_map/ppermute | solution.py:30
  97.1 8.1 %collective-permute-start.16 = (bf16[1,1024,1024]{2,1,0:T(8,128)(2,1)}, bf16[1,1024,1024]{2,1,0:T(8,128)(2,1)S(1)}, u32[]{:S(2)}, u32[]{:S(2)}) collective-permute-start(bf16[1,1024,1024]{2,1,0:T(8,128)(2,1)} %collective-permute-done.9.refs_1_), channel_id=1, source_target_pairs={{0,8},{8,0},{16,24},{24,16},{1,9},{9,1},{17,25},{25,17},{2,10},{10... | collective-permute-start | bytes 6291464 | tf_op jit(solution)/shard_map/ppermute | solution.py:30
  97.6 10.6 %collective-permute-start.17 = (bf16[1,1024,1024]{2,1,0:T(8,128)(2,1)}, bf16[1,1024,1024]{2,1,0:T(8,128)(2,1)S(1)}, u32[]{:S(2)}, u32[]{:S(2)}) collective-permute-start(bf16[1,1024,1024]{2,1,0:T(8,128)(2,1)} %refs_2_.1), channel_id=1, source_target_pairs={{0,8},{8,0},{16,24},{24,16},{1,9},{9,1},{17,25},{25,17},{2,10},{10... | collective-permute-start | bytes 6291464 | tf_op jit(solution)/shard_map/ppermute | solution.py:30
  97.6 37.1 %collective-permute-start.19 = (bf16[1,768,1024]{2,1,0:T(8,128)(2,1)}, bf16[1,768,1024]{2,1,0:T(8,128)(2,1)}, u32[]{:S(2)}, u32[]{:S(2)}) collective-permute-start(bf16[1,768,1024]{2,1,0:T(8,128)(2,1)} %copy-done.31), channel_id=1, source_target_pairs={{0,16},{8,24},{16,0},{24,8},{1,17},{9,25},{17,1},{25,9},{2,18},{10... | collective-permute-start | bytes 4718600 | tf_op jit(solution)/shard_map/ppermute | solution.py:30
  99.0 3.7 %collective-permute-start.18 = (bf16[1,256,1024]{2,1,0:T(8,128)(2,1)S(1)}, bf16[1,256,1024]{2,1,0:T(8,128)(2,1)S(1)}, u32[]{:S(2)}, u32[]{:S(2)}) collective-permute-start(bf16[1,256,1024]{2,1,0:T(8,128)(2,1)S(1)} %collective-permute-done.14.refs_4_), channel_id=1, source_target_pairs={{0,8},{8,0},{16,24},{24,16},{1,9},{9,1},{17,25},{25,17},{2,10},{10... | collective-permute-start | bytes 1572872 | tf_op jit(solution)/shard_map/ppermute | solution.py:30
  134.7 9.4 %collective-permute-start.20 = (bf16[1,768,1024]{2,1,0:T(8,128)(2,1)}, bf16[1,768,1024]{2,1,0:T(8,128)(2,1)S(1)}, u32[]{:S(2)}, u32[]{:S(2)}) collective-permute-start(bf16[1,768,1024]{2,1,0:T(8,128)(2,1)} %collective-permute-done.19.refs_1_), channel_id=1, source_target_pairs={{0,8},{8,0},{16,24},{24,16},{1,9},{9,1},{17,25},{25,17},{2,10},{10... | collective-permute-start | bytes 4718600 | tf_op jit(solution)/shard_map/ppermute | solution.py:30
  144.1 37.1 %copy-start.15 = (bf16[256,1024]{1,0:T(8,128)(2,1)S(1)}, bf16[256,1024]{1,0:T(8,128)(2,1)}, u32[]{:S(2)}) copy-start(bf16[256,1024]{1,0:T(8,128)(2,1)} %copy-done.14) | copy-start | bytes 1572868
  145.4 7.4 %collective-permute-start.21 = (bf16[80,1024]{1,0:T(8,128)(2,1)S(1)}, bf16[80,1024]{1,0:T(8,128)(2,1)S(1)}, u32[]{:S(2)}, u32[]{:S(2)}) collective-permute-start(bf16[80,1024]{1,0:T(8,128)(2,1)S(1)} %get-tuple-element.66), channel_id=1, source_target_pairs={{0,1},{1,0},{2,3},{3,2},{4,5},{5,4},{6,7},{7,6},{8,9},{9,8},{10,11... | collective-permute-start | bytes 491528 | tf_op jit(solution)/shard_map/ppermute | solution.py:30
  146.9 10.7 %collective-permute-start.22 = (bf16[80,1024]{1,0:T(8,128)(2,1)S(1)}, bf16[80,1024]{1,0:T(8,128)(2,1)S(1)}, u32[]{:S(2)}, u32[]{:S(2)}) collective-permute-start(bf16[80,1024]{1,0:T(8,128)(2,1)S(1)} %get-tuple-element.67), channel_id=1, source_target_pairs={{0,2},{1,3},{2,0},{3,1},{4,6},{5,7},{6,4},{7,5},{8,10},{9,11},{10,... | collective-permute-start | bytes 491528 | tf_op jit(solution)/shard_map/ppermute | solution.py:30
  148.4 12.1 %collective-permute-start.23 = (bf16[80,1024]{1,0:T(8,128)(2,1)S(1)}, bf16[80,1024]{1,0:T(8,128)(2,1)S(1)}, u32[]{:S(2)}, u32[]{:S(2)}) collective-permute-start(bf16[80,1024]{1,0:T(8,128)(2,1)S(1)} %get-tuple-element.68), channel_id=1, source_target_pairs={{0,3},{1,2},{2,1},{3,0},{4,7},{5,6},{6,5},{7,4},{8,11},{9,10},{10,... | collective-permute-start | bytes 491528 | tf_op jit(solution)/shard_map/ppermute | solution.py:30
  149.0 12.1 %collective-permute-start.24 = (bf16[80,1024]{1,0:T(8,128)(2,1)S(1)}, bf16[80,1024]{1,0:T(8,128)(2,1)S(1)}, u32[]{:S(2)}, u32[]{:S(2)}) collective-permute-start(bf16[80,1024]{1,0:T(8,128)(2,1)S(1)} %get-tuple-element.69), channel_id=1, source_target_pairs={{0,4},{1,5},{2,6},{3,7},{4,0},{5,1},{6,2},{7,3},{8,12},{9,13},{10,... | collective-permute-start | bytes 491528 | tf_op jit(solution)/shard_map/ppermute | solution.py:30
  149.5 22.0 %collective-permute-start.25 = (bf16[80,1024]{1,0:T(8,128)(2,1)S(1)}, bf16[80,1024]{1,0:T(8,128)(2,1)S(1)}, u32[]{:S(2)}, u32[]{:S(2)}) collective-permute-start(bf16[80,1024]{1,0:T(8,128)(2,1)S(1)} %get-tuple-element.70), channel_id=1, source_target_pairs={{0,5},{1,4},{2,7},{3,6},{4,1},{5,0},{6,3},{7,2},{8,13},{9,12},{10,... | collective-permute-start | bytes 491528 | tf_op jit(solution)/shard_map/ppermute | solution.py:30
  152.8 25.2 %collective-permute-start.26 = (bf16[80,1024]{1,0:T(8,128)(2,1)S(1)}, bf16[80,1024]{1,0:T(8,128)(2,1)S(1)}, u32[]{:S(2)}, u32[]{:S(2)}) collective-permute-start(bf16[80,1024]{1,0:T(8,128)(2,1)S(1)} %get-tuple-element.71), channel_id=1, source_target_pairs={{0,6},{1,7},{2,4},{3,5},{4,2},{5,3},{6,0},{7,1},{8,14},{9,15},{10,... | collective-permute-start | bytes 491528 | tf_op jit(solution)/shard_map/ppermute | solution.py:30
  157.6 23.5 %collective-permute-start.27 = (bf16[80,1024]{1,0:T(8,128)(2,1)S(1)}, bf16[80,1024]{1,0:T(8,128)(2,1)S(1)}, u32[]{:S(2)}, u32[]{:S(2)}) collective-permute-start(bf16[80,1024]{1,0:T(8,128)(2,1)S(1)} %get-tuple-element.72), channel_id=1, source_target_pairs={{0,7},{1,6},{2,5},{3,4},{4,3},{5,2},{6,1},{7,0},{8,15},{9,14},{10,... | collective-permute-start | bytes 491528 | tf_op jit(solution)/shard_map/ppermute | solution.py:30
  (34 other events, 142.2 us)
Sparse Core Ops, SparseCore 0:
  23.6 39.8 all-gather.1

commit v10 on v8

--- a/solution.py
+++ b/solution.py
@@ -91,7 +91,8 @@
 def mix_kernel(
     count, experts, capacity, me_ref, gain_ref, router_ref, rows_ref, cols_ref, own_ref, near_ref, far_ref, *refs
 ):
-    blocks, (slots_out, mixed_out, gate_ref, wide, slots_ref, mixed_ref, sems) = refs[:count], refs[count:]
+    blocks, refs = refs[:count], refs[count:]
+    slots_out, (mixed_out, gate_ref, wide, slots_ref, mixed_ref, sems) = refs[:experts], refs[experts:]
     frames, depth = blocks[0].shape
     me = me_ref[0]
     part = near_ref.shape[1]
@@ -119,8 +120,8 @@
     place1 = jnp.sum(jnp.where(which == second, rank, 0.0), axis=0, keepdims=True)
     spread = ((slot == place0) | (slot == place1)).astype(F32).astype(BF16)
     slots_ref[...] = jnp.dot(spread, normed, preferred_element_type=F32).astype(BF16)
-    slots_copy = pltpu.make_async_copy(slots_ref, slots_out, sems.at[1])
-    slots_copy.start()
+    for k, out in enumerate(slots_out):
+        out[...] = slots_ref[pl.ds(pl.multiple_of((me_ref[1] ^ k) * capacity, capacity), capacity), :]
     high = router_ref[...].astype(BF16)
     rest = router_ref[...] - high.astype(F32)
     middle = rest.astype(BF16)
@@ -134,7 +135,6 @@
     behind = jnp.sum(jnp.where(lane == cols_ref[:, 1:2], logits, 0.0), axis=1, keepdims=True)
     gate_ref[...] = jnp.broadcast_to(jax.nn.sigmoid(ahead - behind), gate_ref.shape)
     mixed_copy.wait()
-    slots_copy.wait()
 
 
 def split_kernel(cuts, whole_ref, *refs):
@@ -149,9 +149,13 @@
         copy.wait()
 
 
-def hidden_kernel(cuts, step, slots_ref, *refs):
-    hidden_ref = refs[len(cuts)]
-    for weight, (at, start, size) in zip(refs, cuts):
+def hidden_kernel(places, blocks, step, _, *refs):
+    hidden_ref, slots_ref = refs[-2:]
+    size = refs[0].shape[0]
+    for k in range(blocks):
+        slots_ref[k * size : (k + 1) * size, :] = refs[k][...]
+    for weight, (at, start) in zip(refs[blocks:], places):
+        size = weight.shape[2]
         for part in range(0, size, step):
             end = min(part + step, size)
             half = 0.5 * jnp.dot(slots_ref[...], weight[0, :, part:end], preferred_element_type=F32)
@@ -164,18 +168,18 @@
     for part in range(0, answer_ref.shape[1], step):
         where = slice(part, part + step)
         total = refs[0][:, where] if before else 0.0
-        for weight, (of, place) in zip(weights, slices):
-            total += jnp.dot(hidden[of][place], weight[0, :, where], preferred_element_type=F32)
+        for weight, (of, place, start) in zip(weights, slices):
+            units = hidden[of][place, :, start : start + weight.shape[1]]
+            total += jnp.dot(units, weight[0, :, where], preferred_element_type=F32)
         answer_ref[:, where] = total.astype(answer_ref.dtype)
 
 
 def last_answer_kernel(slices, step, held, blocks, *refs):
-    me_ref, refs = refs[0], refs[1:]
     inputs, outs, total_ref = refs[: -blocks - 1], refs[-blocks - 1 : -1], refs[-1]
     answer_kernel(slices, step, held, True, *inputs, total_ref)
     size = outs[0].shape[0]
     for k, out in enumerate(outs):
-        out[...] = total_ref[pl.ds(pl.multiple_of((me_ref[0] ^ k) * size, size), size), :]
+        out[...] = total_ref[k * size : (k + 1) * size, :]
 
 
 def combine_kernel(experts, capacity, me_ref, gate_ref, cols_ref, mixed_in, *refs):
@@ -261,20 +265,21 @@
         tiled=True,
     )
 
-    in_cuts = cut(inner, (3, 1, 2, 2))
+    in_cuts = cut(inner, (4, 2, 2))
     in_chunks = pl.pallas_call(
         functools.partial(split_kernel, in_cuts),
         out_shape=[jax.ShapeDtypeStruct((1, width, n), BF16) for _, n in in_cuts],
         in_specs=[HBM],
         out_specs=[HBM] * len(in_cuts),
         scratch_shapes=[pltpu.SemaphoreType.DMA((len(in_cuts),))],
-        compiler_params=params(20),
+        compiler_params=params(1),
         cost_estimate=cost(0, 4 << 20),
         name="split",
     )(expert_in)
-    in_held = [spread_over(after(in_chunks[0], qkv[1]), "dp", 2)]
-    in_held.append(spread_over(after(in_chunks[1], (in_held[0], qkv[exp_count - 2])), "dp", 2))
-    raw[half] = after(raw[half], (qkv, in_held[1]))
+    first = after(in_chunks[0], (raw[half], qkv[1], qkv[2], qkv[4]))
+    in_held = [spread_over(first, "dp", 2)]
+
+    raw[half] = after(raw[half], (qkv, in_held[0]))
 
     groups = len(raw)
     member = jnp.arange(groups, dtype=jnp.int32) * 2
@@ -294,7 +299,8 @@
         name="norm",
     )(place, norm_gains, *[raw[2 * k] for k in range(groups)])
     far = swap(near, "dp", 1)
-    in_held.append(spread_over(after(in_chunks[2], near), "dp", 2))
+    in_held.append(spread_over(after(in_chunks[1], near), "dp", 2))
+    in_core, out_own = [swap(block, "dp", 1) for block in after((expert_in, expert_out), (far, qkv))]
 
     contexts = pl.pallas_call(
         functools.partial(attention_kernel, dp_count, exp_count),
@@ -313,83 +319,86 @@
         name="attention",
     )(exp_index[None], near, far, *[qkv[k] for k in range(exp_count)])
 
-    contexts = after(contexts, in_held[2])
+    contexts = [*contexts[:-1], after(contexts[-1], (in_held[1], in_core, out_own, proj_near))]
     crossed = [swap(contexts[k], "dp", k) for k in range(1, dp_count)]
 
     proj_far = swap(after(proj_near, contexts), "dp", 1)
 
-    in_held.append(spread_over(after(in_chunks[3], crossed), "dp", 2))
+    in_held.append(spread_over(after(in_chunks[2], crossed), "dp", 2))
+    in_hop = [
+        {k: swap(after(block, crossed), "dp", 1) for k, block in held.items() if k} for held in in_held[:2]
+    ]
 
     cols = expert_ids[0]
-    slots, mixed, gate = pl.pallas_call(
+    *slots, mixed, gate = pl.pallas_call(
         functools.partial(mix_kernel, dp_count, exp_count, capacity),
-        out_shape=(
-            jax.ShapeDtypeStruct((slots_count, width), BF16),
+        out_shape=[jax.ShapeDtypeStruct((capacity, width), BF16)] * exp_count
+        + [
             jax.ShapeDtypeStruct((frames, width), BF16),
             jax.ShapeDtypeStruct((frames, 128), F32),
-        ),
+        ],
         in_specs=[SMEM] + [VMEM] * (7 + dp_count),
-        out_specs=(HBM, HBM, VMEM),
+        out_specs=[VMEM] * exp_count + [HBM, VMEM],
         scratch_shapes=[
             pltpu.VMEM((frames, width), F32),
             pltpu.VMEM((slots_count, width), BF16),
             pltpu.VMEM((frames, width), BF16),
-            pltpu.SemaphoreType.DMA((2,)),
+            pltpu.SemaphoreType.DMA((1,)),
         ],
         compiler_params=params(20),
         cost_estimate=cost(2 * frames * width * (width + slots_count), 5 << 20),
         name="mix",
-    )(me[None], norm_gains, router.T, cols.T, cols, stream, proj_near, proj_far, contexts[0], *crossed)
-
-    slots = after(slots, in_held[3])
-    out_held = spread_over(after(expert_out, (in_held[3], mixed)), "dp", 2)
-    in_far, in_near, in_places = [swap(after(expert_in, mixed), "dp", 1)], [expert_in], [(0, 0, inner)]
-    out_own = swap(after(expert_out, mixed), "dp", 1)
+    )(after(jnp.stack([me, exp_index]), (in_held[2], in_hop)), norm_gains, router.T, cols.T, cols, stream, proj_near, proj_far, contexts[0], *crossed)
+
+    out_near = spread_over(after(expert_out, in_held[2]), "dp", 2)
+    long = range(exp_count // 2, exp_count)
+    arrived = {k: swap(slots[k], "expert", k) for k in long}
+    for k in range(1, long[0]):
+        arrived[k] = swap(after(slots[k], arrived[long[0]]), "expert", k)
+    arrived[0] = slots[0]
+    turn = [arrived[k] for k in long]
+    in_hop.append({k: swap(after(block, turn), "dp", 1) for k, block in in_held[2].items() if k})
+    in_near, in_far, places = [expert_in], [in_core], [(0, 0)]
     for k in range(2, dp_count, 2):
-        for held, place in zip(in_held, in_cuts):
+        for held, hop, (start, _) in zip(in_held, in_hop, in_cuts):
             in_near.append(held[k])
-            in_far.append(swap(after(held[k], mixed), "dp", 1))
-            in_places.append((k // 2, *place))
-
-    arrived = lax.all_to_all(
-        slots.reshape(exp_count, capacity, width), "expert", split_axis=0, concat_axis=0, tiled=True
-    ).reshape(slots_count, width)
-
-
-    arrived = after(arrived, (in_far, out_own))
+            in_far.append(hop[k])
+            places.append((k // 2, start))
+
     step = min(512, inner)
 
-    def hidden_units(slots_in, held, name):
+    def hidden_units(order, held, name):
         return pl.pallas_call(
-            functools.partial(hidden_kernel, in_places, step),
+            functools.partial(hidden_kernel, places, exp_count, step),
             out_shape=jax.ShapeDtypeStruct((groups, slots_count, inner), BF16),
-            in_specs=[VMEM] + [VMEM] * len(in_places),
+            in_specs=[SMEM] + [VMEM] * (exp_count + len(held)),
             out_specs=VMEM,
+            scratch_shapes=[pltpu.VMEM((slots_count, width), BF16)],
             compiler_params=params(16),
             cost_estimate=cost(2 * slots_count * width * inner * groups, 8 << 20),
             name=name,
-        )(slots_in, *held)
-
-    hidden = [hidden_units(arrived, in_near, "hidden_near")]
-    hidden.append(hidden_units(after(arrived, hidden[0]), in_far, "hidden_far"))
+        )(order, *[arrived[k] for k in range(exp_count)], *held)
+
+    hidden = [hidden_units(me[None], in_near, "hidden_near")]
+    hidden.append(hidden_units(after(me[None], hidden[0]), in_far, "hidden_far"))
 
     def answers(slices, weights, before, name):
         count = len(slices)
-        used = sorted({of for of, _ in slices})
-        slices = [(used.index(of), place) for of, place in slices]
+        used = sorted({of for of, _, _ in slices})
+        slices = [(used.index(of), place, start) for of, place, start in slices]
         inputs = [hidden[of] for of in used]
         extra = [] if before is None else [before]
         if name == "answer_far":
             return pl.pallas_call(
                 functools.partial(last_answer_kernel, slices, rows, len(used), exp_count),
                 out_shape=[jax.ShapeDtypeStruct((capacity, width), BF16)] * exp_count,
-                in_specs=[SMEM] + [VMEM] * (len(used) + count + len(extra)),
+                in_specs=[VMEM] * (len(used) + count + len(extra)),
                 out_specs=[VMEM] * exp_count,
                 scratch_shapes=[pltpu.VMEM((slots_count, width), BF16)],
                 compiler_params=params(16),
                 cost_estimate=cost(2 * slots_count * width * inner * count, 10 << 20),
                 name=name,
-            )(exp_index[None], *inputs, *weights, *extra)
+            )(*inputs, *weights, *extra)
         return pl.pallas_call(
             functools.partial(answer_kernel, slices, rows, len(used), bool(extra)),
             out_shape=jax.ShapeDtypeStruct((slots_count, width), F32),
@@ -401,11 +410,11 @@
         )(*inputs, *weights, *extra)
 
     distant = range(1, groups)
-    answer = answers([(0, 0), (1, 0)], [expert_out, out_own], None, "answer_own")
-    out_near = [after(out_held[2 * k], hidden[1]) for k in distant]
-    out_far = [swap(block, "dp", 1) for block in out_near]
-    answer = answers([(0, k) for k in distant], out_near, answer, "answer_near")
-    answer = answers([(1, k) for k in distant], out_far, answer, "answer_far")
+    answer = answers([(0, 0, 0), (1, 0, 0)], [expert_out, out_own], None, "answer_own")
+    near_weights = [after(out_near[2 * k], hidden[0]) for k in distant]
+    far_weights = [swap(block, "dp", 1) for block in near_weights]
+    answer = answers([(0, k, 0) for k in distant], near_weights, answer, "answer_near")
+    answer = answers([(1, k, 0) for k in distant], far_weights, answer, "answer_far")
     returned = {k: swap(answer[k], "expert", k) for k in reversed(range(1, exp_count))}
     returned[0] = answer[0]
 

time: 204 us -> 236 us (1.16)
  waiting for transfers between devices: 101 us -> 120 us
  starting transfers between devices: 31 us -> 37.1 us
  Pallas kernels: 31.6 us -> 35.2 us
  local copies, waits for them, and re-layouts: 25.6 us -> 28.2 us
    all_gather x1, waiting for transfers between devices: 0.01 us -> 23.3 us  [body(): lax.all_gather(lax.dynamic_slice_in_dim(attn_out, me % 2 * rows, rows, ax...]
    ppermute x32 -> x37, starting transfers between devices: 23.8 us -> 37.1 us  [swap(): return lax.ppermute(block, axis, [(i, i ^ mask) for i in range(count)])]
    all_to_all x1 -> x0, waiting for transfers between devices: 11.3 us -> none  [body(): lax.all_to_all(slots.reshape(exp_count, capacity, width), 'expert', split...]
    all_to_all x1 -> x0, starting transfers between devices: 7.23 us -> none  [body(): lax.all_to_all(slots.reshape(exp_count, capacity, width), 'expert', split...]
    ppermute x32 -> x37, waiting for transfers between devices: 89.9 us -> 97.1 us  [swap(): return lax.ppermute(block, axis, [(i, i ^ mask) for i in range(count)])]
    unnamed x87 -> x71, local copies, waits for them, and re-layouts: 24.2 us -> 25.9 us
  transfers between devices with their start and end apart: 34 -> 38, of which waited for: 21 -> 23; matrix products, arithmetic and copies ran while one was open for 1% -> 1% of each run, Pallas kernels for 14% -> 13%
where the time goes in v10:
time: 236 us; the launch traced here: 235 us
  waiting for transfers between devices  120 us (51%)
  starting transfers between devices  37.1 us (16%)
  Pallas kernels  35.2 us (15%)
  local copies, waits for them, and re-layouts  28.2 us (12%)
  between operations  13.6 us (6%)
    ppermute x37, waiting for transfers between devices, swap(): return lax.ppermute(block, axis, [(i, i ^ mask) for i in range(count)])  97.1 us
    ppermute x37, starting transfers between devices, swap(): return lax.ppermute(block, axis, [(i, i ^ mask) for i in range(count)])  37.1 us
    unnamed x71, local copies, waits for them, and re-layouts  25.9 us
    all_gather x1, waiting for transfers between devices, body(): lax.all_gather(lax.dynamic_slice_in_dim(attn_out, me % 2 * rows, rows, ax...  23.3 us
    pallas_call x2, Pallas kernels, hidden_units(): pl.pallas_call(functools.partial(hidden_kernel, places, exp_count, step),...  9.73 us
    pallas_call x2, Pallas kernels, answers(): pl.pallas_call(functools.partial(answer_kernel, slices, rows, len(used),...  7.61 us
    pallas_call x1, Pallas kernels, body(): pl.pallas_call(functools.partial(attention_kernel, dp_count, exp_count),...  7.4 us
  transfers between devices with their start and end apart: 38, of which 23 were waited for; matrix products, arithmetic and copies ran while one was open for 1% of the time, Pallas kernels for 13%

profile of v10, /device:TPU:16, one launch (start us, length us, event | category | flops | bytes accessed | tf_op | source)
XLA Modules:
  0.0 234.7 jit_solution(4179415792417482947)
XLA Ops:
  17.0 1.7 collective-permute-done.2.refs_2_
  25.3 6.8 %collective-permute-done.6.refs_6_ = bf16[3,128,256]{2,1,0:T(8,128)(2,1)} collective-permute-done((bf16[3,128,256]{2,1,0:T(8,128)(2,1)S(1)}, bf16[3,128,256]{2,1,0:T(8,128)(2,1)}, u32[]{:S(2)}, u32[]{:S(2)}) %collective-permute-start.6) | collective-permute-done | bytes 196640 | tf_op jit(solution)/shard_map/ppermute | solution.py:30
  33.6 4.4 %collective-permute-done.7.refs_7_ = bf16[3,128,256]{2,1,0:T(8,128)(2,1)S(1)} collective-permute-done((bf16[3,128,256]{2,1,0:T(8,128)(2,1)}, bf16[3,128,256]{2,1,0:T(8,128)(2,1)S(1)}, u32[]{:S(2)}, u32[]{:S(2)}) %collective-permute-start.7) | collective-permute-done | bytes 196640 | tf_op jit(solution)/shard_map/ppermute | solution.py:30
  40.0 4.9 %collective-permute-done.8.refs_9_ = bf16[1,1024,512]{2,1,0:T(8,128)(2,1)} collective-permute-done((bf16[1,1024,512]{2,1,0:T(8,128)(2,1)}, bf16[1,1024,512]{2,1,0:T(8,128)(2,1)}, u32[]{:S(2)}, u32[]{:S(2)}) %collective-permute-start.8) | collective-permute-done | bytes 1048608 | tf_op jit(solution)/shard_map/ppermute | solution.py:30
  46.0 1.8 norm.1
  62.1 7.4 %attention.1 = (bf16[256,256]{1,0:T(8,128)(2,1)S(1)}, bf16[256,256]{1,0:T(8,128)(2,1)}, bf16[256,256]{1,0:T(8,128)(2,1)}, bf16[256,256]{1,0:T(8,128)(2,1)S(1)}) custom-call(s32[1]{0:T(128)} %bitcast.me_ref, bf16[2,256,1024]{2,1,0:T(8,128)(2,1)S(1)} %copy-done.6, bf16[2,256,1024]{2,1,0:T(8,128)(2,1)S(1)} %copy-done.8, ...), custom_call_target="tpu_custom_call" | custom-call | flops 10485760 | bytes 20480 | tf_op jit(solution)/shard_map/attention/pallas_call | solution.py:305
  71.3 23.3 %all-gather.2.cloned.1.call-done.near_ref = bf16[1024,512]{1,0:T(8,128)(2,1)} async-done(((bf16[128,512]{1,0:T(8,128)(2,1)}), bf16[1024,512]{1,0:T(8,128)(2,1)}) %all-gather.2.cloned.1.call-update) | async-done | bytes 1048592 | tf_op jit(solution)/shard_map/all_gather | solution.py:261
  96.5 4.2 %collective-permute-done.15.refs_3_ = bf16[256,256]{1,0:T(8,128)(2,1)S(1)} collective-permute-done((bf16[256,256]{1,0:T(8,128)(2,1)}, bf16[256,256]{1,0:T(8,128)(2,1)S(1)}, u32[]{:S(2)}, u32[]{:S(2)}) %collective-permute-start.15) | collective-permute-done | bytes 131104 | tf_op jit(solution)/shard_map/ppermute | solution.py:30
  102.4 13.0 %collective-permute-done.16.refs_11_ = bf16[1,1024,256]{2,1,0:T(8,128)(2,1)S(1)} collective-permute-done((bf16[1,1024,256]{2,1,0:T(8,128)(2,1)}, bf16[1,1024,256]{2,1,0:T(8,128)(2,1)S(1)}, u32[]{:S(2)}, u32[]{:S(2)}) %collective-permute-start.16) | collective-permute-done | bytes 524320 | tf_op jit(solution)/shard_map/ppermute | solution.py:30
  117.1 4.4 %collective-permute-done.18.refs_10_ = bf16[1,1024,256]{2,1,0:T(8,128)(2,1)} collective-permute-done((bf16[1,1024,256]{2,1,0:T(8,128)(2,1)}, bf16[1,1024,256]{2,1,0:T(8,128)(2,1)}, u32[]{:S(2)}, u32[]{:S(2)}) %collective-permute-start.18) | collective-permute-done | bytes 524320 | tf_op jit(solution)/shard_map/ppermute | solution.py:30
  128.2 3.8 %mix.1 = (bf16[80,1024]{1,0:T(8,128)(2,1)S(1)}, bf16[80,1024]{1,0:T(8,128)(2,1)S(1)}, bf16[80,1024]{1,0:T(8,128)(2,1)S(1)}, bf16[80,1024]{1,0:T(8,128)(2,1)S(1)}...) custom-call(s32[2]{0:T(128)S(1)} %pad_add_fusion.me_ref, ...), custom_call_target="tpu_custom_call" | custom-call | flops 3407872 | bytes 20480 | tf_op jit(solution)/shard_map/mix/pallas_call | solution.py:333
  131.9 1.8 collective-permute-start.20
  135.7 2.1 collective-permute-start.26
  137.8 13.7 %collective-permute-done.20.refs_4_ = bf16[80,1024]{1,0:T(8,128)(2,1)S(1)} collective-permute-done((bf16[80,1024]{1,0:T(8,128)(2,1)S(1)}, bf16[80,1024]{1,0:T(8,128)(2,1)S(1)}, u32[]{:S(2)}, u32[]{:S(2)}) %collective-permute-start.20) | collective-permute-done | bytes 163872 | tf_op jit(solution)/shard_map/ppermute | solution.py:30
  152.1 2.9 %collective-permute-done.24.refs_5_ = bf16[80,1024]{1,0:T(8,128)(2,1)S(1)} collective-permute-done((bf16[80,1024]{1,0:T(8,128)(2,1)S(1)}, bf16[80,1024]{1,0:T(8,128)(2,1)S(1)}, u32[]{:S(2)}, u32[]{:S(2)}) %collective-permute-start.24) | collective-permute-done | bytes 163872 | tf_op jit(solution)/shard_map/ppermute | solution.py:30
  155.1 3.2 %collective-permute-start.22 = (bf16[80,1024]{1,0:T(8,128)(2,1)S(1)}, bf16[80,1024]{1,0:T(8,128)(2,1)S(1)}, u32[]{:S(2)}, u32[]{:S(2)}) collective-permute-start(bf16[80,1024]{1,0:T(8,128)(2,1)S(1)} %get-tuple-element.77), channel_id=1, source_target_pairs={{0,2},{1,3},{2,0},{3,1},{4,6},{5,7},{6,4},{7,5},{8,10},{9,11},{10,... | collective-permute-start | bytes 491528 | tf_op jit(solution)/shard_map/ppermute | solution.py:30
  158.2 2.1 collective-permute-done.25.refs_6_
  160.3 3.4 %collective-permute-done.26.refs_7_ = bf16[80,1024]{1,0:T(8,128)(2,1)S(1)} collective-permute-done((bf16[80,1024]{1,0:T(8,128)(2,1)S(1)}, bf16[80,1024]{1,0:T(8,128)(2,1)S(1)}, u32[]{:S(2)}, u32[]{:S(2)}) %collective-permute-start.26) | collective-permute-done | bytes 163872 | tf_op jit(solution)/shard_map/ppermute | solution.py:30
  163.7 3.6 %collective-permute-done.23.refs_3_ = bf16[80,1024]{1,0:T(8,128)(2,1)S(1)} collective-permute-done((bf16[80,1024]{1,0:T(8,128)(2,1)S(1)}, bf16[80,1024]{1,0:T(8,128)(2,1)S(1)}, u32[]{:S(2)}, u32[]{:S(2)}) %collective-permute-start.23) | collective-permute-done | bytes 163872 | tf_op jit(solution)/shard_map/ppermute | solution.py:30
  167.3 4.5 %hidden_near.1.refs_0_ = bf16[2,640,1024]{2,1,0:T(8,128)(2,1)S(1)} custom-call(s32[1]{0:T(128)} %bitcast.1._, bf16[80,1024]{1,0:T(8,128)(2,1)S(1)} %get-tuple-element.72.refs_0_, bf16[80,1024]{1,0:T(8,128)(2,1)S(1)} %collective-permute-done.21.refs_1_, bf16[80,1024]{1,0:T(8,128)(2,1)S(1)} %collective-permute-done.22.refs_2_, ...), custom_call_target="tpu_custom_call" | custom-call | flops 10485760 | bytes 32768 | tf_op jit(solution)/shard_map/hidden_near/pallas_call | solution.py:371
  172.4 4.0 %collective-permute-done.27.refs_11_ = bf16[1,1024,256]{2,1,0:T(8,128)(2,1)S(1)} collective-permute-done((bf16[1,1024,256]{2,1,0:T(8,128)(2,1)S(1)}, bf16[1,1024,256]{2,1,0:T(8,128)(2,1)S(1)}, u32[]{:S(2)}, u32[]{:S(2)}) %collective-permute-start.27) | collective-permute-done | bytes 524320 | tf_op jit(solution)/shard_map/ppermute | solution.py:30
  176.5 5.2 %hidden_far.1.refs_1_.refs_0_ = bf16[2,640,1024]{2,1,0:T(8,128)(2,1)S(1)} custom-call(s32[1]{0:T(128)} %bitcast.1._, bf16[80,1024]{1,0:T(8,128)(2,1)S(1)} %get-tuple-element.72.refs_0_, bf16[80,1024]{1,0:T(8,128)(2,1)S(1)} %collective-permute-done.21.refs_1_, bf16[80,1024]{1,0:T(8,128)(2,1)S(1)} %collective-permute-done.22.refs_2_, ...), custom_call_target="tpu_custom_call" | custom-call | flops 10485760 | bytes 32768 | tf_op jit(solution)/shard_map/hidden_far/pallas_call | solution.py:371
  181.7 4.5 %answer_own.1.refs_2_ = f32[640,1024]{1,0:T(8,128)S(1)} custom-call(bf16[2,640,1024]{2,1,0:T(8,128)(2,1)S(1)} %hidden_near.1.refs_0_, bf16[2,640,1024]{2,1,0:T(8,128)(2,1)S(1)} %hidden_far.1.refs_1_.refs_0_, bf16[1,1024,1024]{2,1,0:T(8,128)(2,1)S(1)} %copy-done.3, bf16[1,1024,1024]{2,1,0:T(8,128)(2,1)} %collective-permute-done.14.refs_3_), custom_call_target="tpu_custom_call" | custom-call | flops 10485760 | bytes 40960 | tf_op jit(solution)/shard_map/answer_own/pallas_call | solution.py:402
  186.2 3.1 %answer_near.1.refs_2_ = f32[640,1024]{1,0:T(8,128)S(1)} custom-call(bf16[2,640,1024]{2,1,0:T(8,128)(2,1)S(1)} %hidden_near.1.refs_0_, bf16[1,1024,1024]{2,1,0:T(8,128)(2,1)} %collective-permute-done.28.refs_1_, f32[640,1024]{1,0:T(8,128)S(1)} %answer_own.1.refs_2_), custom_call_target="tpu_custom_call" | custom-call | flops 5242880 | bytes 40960 | tf_op jit(solution)/shard_map/answer_near/pallas_call | solution.py:402
  196.1 2.1 collective-permute-start.34
  199.0 3.0 %collective-permute-done.31.refs_2_ = bf16[80,1024]{1,0:T(8,128)(2,1)S(1)} collective-permute-done((bf16[80,1024]{1,0:T(8,128)(2,1)S(1)}, bf16[80,1024]{1,0:T(8,128)(2,1)S(1)}, u32[]{:S(2)}, u32[]{:S(2)}) %collective-permute-start.31) | collective-permute-done | bytes 163872 | tf_op jit(solution)/shard_map/ppermute | solution.py:30
  202.0 2.6 %collective-permute-start.36 = (bf16[80,1024]{1,0:T(8,128)(2,1)S(1)}, bf16[80,1024]{1,0:T(8,128)(2,1)S(1)}, u32[]{:S(2)}, u32[]{:S(2)}) collective-permute-start(bf16[80,1024]{1,0:T(8,128)(2,1)S(1)} %get-tuple-element.94), channel_id=1, source_target_pairs={{0,7},{1,6},{2,5},{3,4},{4,3},{5,2},{6,1},{7,0},{8,15},{9,14},{10,... | collective-permute-start | bytes 491528 | tf_op jit(solution)/shard_map/ppermute | solution.py:30
  205.0 1.7 collective-permute-done.33.refs_4_
  206.7 11.5 %collective-permute-done.34.refs_5_ = bf16[80,1024]{1,0:T(8,128)(2,1)S(1)} collective-permute-done((bf16[80,1024]{1,0:T(8,128)(2,1)S(1)}, bf16[80,1024]{1,0:T(8,128)(2,1)S(1)}, u32[]{:S(2)}, u32[]{:S(2)}) %collective-permute-start.34) | collective-permute-done | bytes 163872 | tf_op jit(solution)/shard_map/ppermute | solution.py:30
  218.3 5.1 %collective-permute-done.35.refs_6_ = bf16[80,1024]{1,0:T(8,128)(2,1)S(1)} collective-permute-done((bf16[80,1024]{1,0:T(8,128)(2,1)S(1)}, bf16[80,1024]{1,0:T(8,128)(2,1)S(1)}, u32[]{:S(2)}, u32[]{:S(2)}) %collective-permute-start.35) | collective-permute-done | bytes 163872 | tf_op jit(solution)/shard_map/ppermute | solution.py:30
  223.4 2.0 collective-permute-done.36.refs_7_
  225.4 2.3 combine.1
  (133 shorter events, 60.6 us)
Async XLA Ops:
  6.5 88.0 %all-gather.2.cloned.1.call-start = ((), (), s32[]{:S(2)}) async-start(), calls=%async_computation | async-start | bytes 1179648 | tf_op jit(solution)/shard_map/all_gather | solution.py:261
  6.5 14.0 %collective-permute-start = (bf16[1,256,1024]{2,1,0:T(8,128)(2,1)}, bf16[1,256,1024]{2,1,0:T(8,128)(2,1)}, u32[]{:S(2)}, u32[]{:S(2)}) collective-permute-start(bf16[1,256,1024]{2,1,0:T(8,128)(2,1)} %refs_0_.1), channel_id=1, source_target_pairs={{0,16},{8,24},{16,0},{24,8},{1,17},{9,25},{17,1},{25,9},{2,18},{10... | collective-permute-start | bytes 1572872 | tf_op jit(solution)/shard_map/ppermute | solution.py:30
  8.2 8.8 %collective-permute-start.4 = (bf16[3,128,256]{2,1,0:T(8,128)(2,1)S(1)}, bf16[3,128,256]{2,1,0:T(8,128)(2,1)S(1)}, u32[]{:S(2)}, u32[]{:S(2)}) collective-permute-start(bf16[3,128,256]{2,1,0:T(8,128)(2,1)S(1)} %constant_dynamic-slice_fusion.refs_0_), channel_id=1, source_target_pairs={{0,4},{1,5},{2,6},{3,7},{4,0},{5,1},{6,2},{7,3},{8,12},{9,13},{10,... | collective-permute-start | bytes 589832 | tf_op jit(solution)/shard_map/ppermute | solution.py:30
  8.6 10.2 %collective-permute-start.2 = (bf16[3,128,256]{2,1,0:T(8,128)(2,1)S(1)}, bf16[3,128,256]{2,1,0:T(8,128)(2,1)S(1)}, u32[]{:S(2)}, u32[]{:S(2)}) collective-permute-start(bf16[3,128,256]{2,1,0:T(8,128)(2,1)S(1)} %constant_dynamic-slice_fusion.refs_0_), channel_id=1, source_target_pairs={{0,2},{1,3},{2,0},{3,1},{4,6},{5,7},{6,4},{7,5},{8,10},{9,11},{10,... | collective-permute-start | bytes 589832 | tf_op jit(solution)/shard_map/ppermute | solution.py:30
  10.1 8.6 %collective-permute-start.1 = (bf16[3,128,256]{2,1,0:T(8,128)(2,1)S(1)}, bf16[3,128,256]{2,1,0:T(8,128)(2,1)S(1)}, u32[]{:S(2)}, u32[]{:S(2)}) collective-permute-start(bf16[3,128,256]{2,1,0:T(8,128)(2,1)S(1)} %constant_dynamic-slice_fusion.refs_0_), channel_id=1, source_target_pairs={{0,1},{1,0},{2,3},{3,2},{4,5},{5,4},{6,7},{7,6},{8,9},{9,8},{10,11... | collective-permute-start | bytes 589832 | tf_op jit(solution)/shard_map/ppermute | solution.py:30
  20.6 24.3 %collective-permute-start.8 = (bf16[1,1024,512]{2,1,0:T(8,128)(2,1)}, bf16[1,1024,512]{2,1,0:T(8,128)(2,1)}, u32[]{:S(2)}, u32[]{:S(2)}) collective-permute-start(bf16[1,1024,512]{2,1,0:T(8,128)(2,1)} %get-tuple-element.52), channel_id=1, source_target_pairs={{0,16},{8,24},{16,0},{24,8},{1,17},{9,25},{17,1},{25,9},{2,18},{10... | collective-permute-start | bytes 3145736 | tf_op jit(solution)/shard_map/ppermute | solution.py:30
  22.1 10.0 %collective-permute-start.6 = (bf16[3,128,256]{2,1,0:T(8,128)(2,1)S(1)}, bf16[3,128,256]{2,1,0:T(8,128)(2,1)}, u32[]{:S(2)}, u32[]{:S(2)}) collective-permute-start(bf16[3,128,256]{2,1,0:T(8,128)(2,1)S(1)} %constant_dynamic-slice_fusion.refs_0_), channel_id=1, source_target_pairs={{0,6},{1,7},{2,4},{3,5},{4,2},{5,3},{6,0},{7,1},{8,14},{9,15},{10,... | collective-permute-start | bytes 589832 | tf_op jit(solution)/shard_map/ppermute | solution.py:30
  23.2 15.4 %collective-permute-start.5 = (bf16[3,128,256]{2,1,0:T(8,128)(2,1)S(1)}, bf16[3,128,256]{2,1,0:T(8,128)(2,1)S(1)}, u32[]{:S(2)}, u32[]{:S(2)}) collective-permute-start(bf16[3,128,256]{2,1,0:T(8,128)(2,1)S(1)} %collective-permute-done.4.refs_4_), channel_id=1, source_target_pairs={{0,1},{1,0},{2,3},{3,2},{4,5},{5,4},{6,7},{7,6},{8,9},{9,8},{10,11... | collective-permute-start | bytes 589832 | tf_op jit(solution)/shard_map/ppermute | solution.py:30
  24.7 14.6 %collective-permute-start.3 = (bf16[3,128,256]{2,1,0:T(8,128)(2,1)S(1)}, bf16[3,128,256]{2,1,0:T(8,128)(2,1)S(1)}, u32[]{:S(2)}, u32[]{:S(2)}) collective-permute-start(bf16[3,128,256]{2,1,0:T(8,128)(2,1)S(1)} %collective-permute-done.2.refs_2_), channel_id=1, source_target_pairs={{0,1},{1,0},{2,3},{3,2},{4,5},{5,4},{6,7},{7,6},{8,9},{9,8},{10,11... | collective-permute-start | bytes 589832 | tf_op jit(solution)/shard_map/ppermute | solution.py:30
  52.2 42.3 %collective-permute-start.13 = (bf16[1,1024,1024]{2,1,0:T(8,128)(2,1)S(1)}, bf16[1,1024,1024]{2,1,0:T(8,128)(2,1)}, u32[]{:S(2)}, u32[]{:S(2)}) collective-permute-start(bf16[1,1024,1024]{2,1,0:T(8,128)(2,1)S(1)} %copy-done.2), channel_id=1, source_target_pairs={{0,8},{8,0},{16,24},{24,16},{1,9},{9,1},{17,25},{25,17},{2,10},{10... | collective-permute-start | bytes 6291464 | tf_op jit(solution)/shard_map/ppermute | solution.py:30
  52.4 42.2 %collective-permute-start.14 = (bf16[1,1024,1024]{2,1,0:T(8,128)(2,1)}, bf16[1,1024,1024]{2,1,0:T(8,128)(2,1)}, u32[]{:S(2)}, u32[]{:S(2)}) collective-permute-start(bf16[1,1024,1024]{2,1,0:T(8,128)(2,1)} %refs_2_.1), channel_id=1, source_target_pairs={{0,8},{8,0},{16,24},{24,16},{1,9},{9,1},{17,25},{25,17},{2,10},{10... | collective-permute-start | bytes 6291464 | tf_op jit(solution)/shard_map/ppermute | solution.py:30
  54.3 40.2 %collective-permute-start.12 = (bf16[1,1024,256]{2,1,0:T(8,128)(2,1)}, bf16[1,1024,256]{2,1,0:T(8,128)(2,1)}, u32[]{:S(2)}, u32[]{:S(2)}) collective-permute-start(bf16[1,1024,256]{2,1,0:T(8,128)(2,1)} %copy-done.31), channel_id=1, source_target_pairs={{0,16},{8,24},{16,0},{24,8},{1,17},{9,25},{17,1},{25,9},{2,18},{10... | collective-permute-start | bytes 1572872 | tf_op jit(solution)/shard_map/ppermute | solution.py:30
  70.8 24.4 %collective-permute-start.10 = (bf16[256,256]{1,0:T(8,128)(2,1)}, bf16[256,256]{1,0:T(8,128)(2,1)S(1)}, u32[]{:S(2)}, u32[]{:S(2)}) collective-permute-start(bf16[256,256]{1,0:T(8,128)(2,1)} %get-tuple-element.55), channel_id=1, source_target_pairs={{0,8},{8,0},{16,24},{24,16},{1,9},{9,1},{17,25},{25,17},{2,10},{10... | collective-permute-start | bytes 393224 | tf_op jit(solution)/shard_map/ppermute | solution.py:30
  70.8 25.0 %collective-permute-start.11 = (bf16[256,256]{1,0:T(8,128)(2,1)}, bf16[256,256]{1,0:T(8,128)(2,1)S(1)}, u32[]{:S(2)}, u32[]{:S(2)}) collective-permute-start(bf16[256,256]{1,0:T(8,128)(2,1)} %get-tuple-element.56), channel_id=1, source_target_pairs={{0,16},{8,24},{16,0},{24,8},{1,17},{9,25},{17,1},{25,9},{2,18},{10... | collective-permute-start | bytes 393224 | tf_op jit(solution)/shard_map/ppermute | solution.py:30
  94.6 6.0 %collective-permute-start.15 = (bf16[256,256]{1,0:T(8,128)(2,1)}, bf16[256,256]{1,0:T(8,128)(2,1)S(1)}, u32[]{:S(2)}, u32[]{:S(2)}) collective-permute-start(bf16[256,256]{1,0:T(8,128)(2,1)} %copy-done.32), channel_id=1, source_target_pairs={{0,24},{8,16},{16,8},{24,0},{1,25},{9,17},{17,9},{25,1},{2,26},{10... | collective-permute-start | bytes 393224 | tf_op jit(solution)/shard_map/ppermute | solution.py:30
  101.3 14.2 %collective-permute-start.16 = (bf16[1,1024,256]{2,1,0:T(8,128)(2,1)}, bf16[1,1024,256]{2,1,0:T(8,128)(2,1)S(1)}, u32[]{:S(2)}, u32[]{:S(2)}) collective-permute-start(bf16[1,1024,256]{2,1,0:T(8,128)(2,1)} %copy-done.30), channel_id=1, source_target_pairs={{0,16},{8,24},{16,0},{24,8},{1,17},{9,25},{17,1},{25,9},{2,18},{10... | collective-permute-start | bytes 1572872 | tf_op jit(solution)/shard_map/ppermute | solution.py:30
  115.4 56.4 %collective-permute-start.28 = (bf16[1,1024,1024]{2,1,0:T(8,128)(2,1)}, bf16[1,1024,1024]{2,1,0:T(8,128)(2,1)}, u32[]{:S(2)}, u32[]{:S(2)}) collective-permute-start(bf16[1,1024,1024]{2,1,0:T(8,128)(2,1)} %refs_2_.1), channel_id=1, source_target_pairs={{0,16},{8,24},{16,0},{24,8},{1,17},{9,25},{17,1},{25,9},{2,18},{10... | collective-permute-start | bytes 6291464 | tf_op jit(solution)/shard_map/ppermute | solution.py:30
  131.9 19.6 %collective-permute-start.20 = (bf16[80,1024]{1,0:T(8,128)(2,1)S(1)}, bf16[80,1024]{1,0:T(8,128)(2,1)S(1)}, u32[]{:S(2)}, u32[]{:S(2)}) collective-permute-start(bf16[80,1024]{1,0:T(8,128)(2,1)S(1)} %get-tuple-element.74), channel_id=1, source_target_pairs={{0,4},{1,5},{2,6},{3,7},{4,0},{5,1},{6,2},{7,3},{8,12},{9,13},{10,... | collective-permute-start | bytes 491528 | tf_op jit(solution)/shard_map/ppermute | solution.py:30
  133.7 21.4 %collective-permute-start.24 = (bf16[80,1024]{1,0:T(8,128)(2,1)S(1)}, bf16[80,1024]{1,0:T(8,128)(2,1)S(1)}, u32[]{:S(2)}, u32[]{:S(2)}) collective-permute-start(bf16[80,1024]{1,0:T(8,128)(2,1)S(1)} %get-tuple-element.80), channel_id=1, source_target_pairs={{0,5},{1,4},{2,7},{3,6},{4,1},{5,0},{6,3},{7,2},{8,13},{9,12},{10,... | collective-permute-start | bytes 491528 | tf_op jit(solution)/shard_map/ppermute | solution.py:30
  134.9 25.4 %collective-permute-start.25 = (bf16[80,1024]{1,0:T(8,128)(2,1)S(1)}, bf16[80,1024]{1,0:T(8,128)(2,1)S(1)}, u32[]{:S(2)}, u32[]{:S(2)}) collective-permute-start(bf16[80,1024]{1,0:T(8,128)(2,1)S(1)} %get-tuple-element.81), channel_id=1, source_target_pairs={{0,6},{1,7},{2,4},{3,5},{4,2},{5,3},{6,0},{7,1},{8,14},{9,15},{10,... | collective-permute-start | bytes 491528 | tf_op jit(solution)/shard_map/ppermute | solution.py:30
  135.7 28.0 %collective-permute-start.26 = (bf16[80,1024]{1,0:T(8,128)(2,1)S(1)}, bf16[80,1024]{1,0:T(8,128)(2,1)S(1)}, u32[]{:S(2)}, u32[]{:S(2)}) collective-permute-start(bf16[80,1024]{1,0:T(8,128)(2,1)S(1)} %get-tuple-element.82), channel_id=1, source_target_pairs={{0,7},{1,6},{2,5},{3,4},{4,3},{5,2},{6,1},{7,0},{8,15},{9,14},{10,... | collective-permute-start | bytes 491528 | tf_op jit(solution)/shard_map/ppermute | solution.py:30
  151.6 12.1 %collective-permute-start.21 = (bf16[80,1024]{1,0:T(8,128)(2,1)S(1)}, bf16[80,1024]{1,0:T(8,128)(2,1)S(1)}, u32[]{:S(2)}, u32[]{:S(2)}) collective-permute-start(bf16[80,1024]{1,0:T(8,128)(2,1)S(1)} %get-tuple-element.75), channel_id=1, source_target_pairs={{0,1},{1,0},{2,3},{3,2},{4,5},{5,4},{6,7},{7,6},{8,9},{9,8},{10,11... | collective-permute-start | bytes 491528 | tf_op jit(solution)/shard_map/ppermute | solution.py:30
  155.1 8.6 %collective-permute-start.22 = (bf16[80,1024]{1,0:T(8,128)(2,1)S(1)}, bf16[80,1024]{1,0:T(8,128)(2,1)S(1)}, u32[]{:S(2)}, u32[]{:S(2)}) collective-permute-start(bf16[80,1024]{1,0:T(8,128)(2,1)S(1)} %get-tuple-element.77), channel_id=1, source_target_pairs={{0,2},{1,3},{2,0},{3,1},{4,6},{5,7},{6,4},{7,5},{8,10},{9,11},{10,... | collective-permute-start | bytes 491528 | tf_op jit(solution)/shard_map/ppermute | solution.py:30
  160.3 7.0 %collective-permute-start.23 = (bf16[80,1024]{1,0:T(8,128)(2,1)S(1)}, bf16[80,1024]{1,0:T(8,128)(2,1)S(1)}, u32[]{:S(2)}, u32[]{:S(2)}) collective-permute-start(bf16[80,1024]{1,0:T(8,128)(2,1)S(1)} %get-tuple-element.79), channel_id=1, source_target_pairs={{0,3},{1,2},{2,1},{3,0},{4,7},{5,6},{6,5},{7,4},{8,11},{9,10},{10,... | collective-permute-start | bytes 491528 | tf_op jit(solution)/shard_map/ppermute | solution.py:30
  171.9 17.4 %collective-permute-start.29 = (bf16[1,1024,1024]{2,1,0:T(8,128)(2,1)}, bf16[1,1024,1024]{2,1,0:T(8,128)(2,1)S(1)}, u32[]{:S(2)}, u32[]{:S(2)}) collective-permute-start(bf16[1,1024,1024]{2,1,0:T(8,128)(2,1)} %collective-permute-done.28.refs_1_), channel_id=1, source_target_pairs={{0,8},{8,0},{16,24},{24,16},{1,9},{9,1},{17,25},{25,17},{2,10},{10... | collective-permute-start | bytes 6291464 | tf_op jit(solution)/shard_map/ppermute | solution.py:30
  190.9 7.3 %collective-permute-start.30 = (bf16[80,1024]{1,0:T(8,128)(2,1)S(1)}, bf16[80,1024]{1,0:T(8,128)(2,1)S(1)}, u32[]{:S(2)}, u32[]{:S(2)}) collective-permute-start(bf16[80,1024]{1,0:T(8,128)(2,1)S(1)} %get-tuple-element.88), channel_id=1, source_target_pairs={{0,1},{1,0},{2,3},{3,2},{4,5},{5,4},{6,7},{7,6},{8,9},{9,8},{10,11... | collective-permute-start | bytes 491528 | tf_op jit(solution)/shard_map/ppermute | solution.py:30
  192.3 9.7 %collective-permute-start.31 = (bf16[80,1024]{1,0:T(8,128)(2,1)S(1)}, bf16[80,1024]{1,0:T(8,128)(2,1)S(1)}, u32[]{:S(2)}, u32[]{:S(2)}) collective-permute-start(bf16[80,1024]{1,0:T(8,128)(2,1)S(1)} %get-tuple-element.89), channel_id=1, source_target_pairs={{0,2},{1,3},{2,0},{3,1},{4,6},{5,7},{6,4},{7,5},{8,10},{9,11},{10,... | collective-permute-start | bytes 491528 | tf_op jit(solution)/shard_map/ppermute | solution.py:30
  192.8 12.2 %collective-permute-start.32 = (bf16[80,1024]{1,0:T(8,128)(2,1)S(1)}, bf16[80,1024]{1,0:T(8,128)(2,1)S(1)}, u32[]{:S(2)}, u32[]{:S(2)}) collective-permute-start(bf16[80,1024]{1,0:T(8,128)(2,1)S(1)} %get-tuple-element.90), channel_id=1, source_target_pairs={{0,3},{1,2},{2,1},{3,0},{4,7},{5,6},{6,5},{7,4},{8,11},{9,10},{10,... | collective-permute-start | bytes 491528 | tf_op jit(solution)/shard_map/ppermute | solution.py:30
  194.4 12.3 %collective-permute-start.33 = (bf16[80,1024]{1,0:T(8,128)(2,1)S(1)}, bf16[80,1024]{1,0:T(8,128)(2,1)S(1)}, u32[]{:S(2)}, u32[]{:S(2)}) collective-permute-start(bf16[80,1024]{1,0:T(8,128)(2,1)S(1)} %get-tuple-element.91), channel_id=1, source_target_pairs={{0,4},{1,5},{2,6},{3,7},{4,0},{5,1},{6,2},{7,3},{8,12},{9,13},{10,... | collective-permute-start | bytes 491528 | tf_op jit(solution)/shard_map/ppermute | solution.py:30
  196.1 22.2 %collective-permute-start.34 = (bf16[80,1024]{1,0:T(8,128)(2,1)S(1)}, bf16[80,1024]{1,0:T(8,128)(2,1)S(1)}, u32[]{:S(2)}, u32[]{:S(2)}) collective-permute-start(bf16[80,1024]{1,0:T(8,128)(2,1)S(1)} %get-tuple-element.92), channel_id=1, source_target_pairs={{0,5},{1,4},{2,7},{3,6},{4,1},{5,0},{6,3},{7,2},{8,13},{9,12},{10,... | collective-permute-start | bytes 491528 | tf_op jit(solution)/shard_map/ppermute | solution.py:30
  198.2 25.2 %collective-permute-start.35 = (bf16[80,1024]{1,0:T(8,128)(2,1)S(1)}, bf16[80,1024]{1,0:T(8,128)(2,1)S(1)}, u32[]{:S(2)}, u32[]{:S(2)}) collective-permute-start(bf16[80,1024]{1,0:T(8,128)(2,1)S(1)} %get-tuple-element.93), channel_id=1, source_target_pairs={{0,6},{1,7},{2,4},{3,5},{4,2},{5,3},{6,0},{7,1},{8,14},{9,15},{10,... | collective-permute-start | bytes 491528 | tf_op jit(solution)/shard_map/ppermute | solution.py:30
  202.0 23.5 %collective-permute-start.36 = (bf16[80,1024]{1,0:T(8,128)(2,1)S(1)}, bf16[80,1024]{1,0:T(8,128)(2,1)S(1)}, u32[]{:S(2)}, u32[]{:S(2)}) collective-permute-start(bf16[80,1024]{1,0:T(8,128)(2,1)S(1)} %get-tuple-element.94), channel_id=1, source_target_pairs={{0,7},{1,6},{2,5},{3,4},{4,3},{5,2},{6,1},{7,0},{8,15},{9,14},{10,... | collective-permute-start | bytes 491528 | tf_op jit(solution)/shard_map/ppermute | solution.py:30
  (41 other events, 227.2 us)
Sparse Core Ops, SparseCore 0:
  54.5 40.0 all-gather.1

commit v11 on v9

--- a/solution.py
+++ b/solution.py
@@ -137,10 +137,10 @@
     slots_copy.wait()
 
 
-def split_kernel(cuts, whole_ref, *refs):
+def split_kernel(cuts, axis, whole_ref, *refs):
     outs, sems = refs[: len(cuts)], refs[len(cuts)]
     copies = [
-        pltpu.make_async_copy(whole_ref.at[:, pl.ds(start, size), :], outs[k], sems.at[k])
+        pltpu.make_async_copy(whole_ref.at[(slice(None),) * axis + (pl.ds(start, size),)], outs[k], sems.at[k])
         for k, (start, size) in enumerate(cuts)
     ]
     for copy in copies:
@@ -149,13 +149,14 @@
         copy.wait()
 
 
-def hidden_kernel(step, slots_ref, *refs):
+def hidden_kernel(places, step, slots_ref, *refs):
     hidden_ref = refs[-1]
-    for at, weight in enumerate(refs[:-1]):
-        for part in range(0, weight.shape[2], step):
-            where = slice(part, part + step)
-            half = 0.5 * jnp.dot(slots_ref[...], weight[0, :, where], preferred_element_type=F32)
-            hidden_ref[at, :, where] = (half + half * jnp.tanh(half)).astype(BF16)
+    for weight, (at, start) in zip(refs, places):
+        size = weight.shape[2]
+        for part in range(0, size, step):
+            end = min(part + step, size)
+            half = 0.5 * jnp.dot(slots_ref[...], weight[0, :, part:end], preferred_element_type=F32)
+            hidden_ref[at, :, start + part : start + end] = (half + half * jnp.tanh(half)).astype(BF16)
 
 
 def answer_kernel(slices, step, held, before, *refs):
@@ -262,7 +263,19 @@
         tiled=True,
     )
 
-    in_near = spread_over(after(expert_in, (raw[half], qkv[1], qkv[2], qkv[4])), "dp", 2)
+    in_cuts = cut(inner, (7, 1))
+    in_chunks = pl.pallas_call(
+        functools.partial(split_kernel, in_cuts, 2),
+        out_shape=[jax.ShapeDtypeStruct((1, width, n), BF16) for _, n in in_cuts],
+        in_specs=[HBM],
+        out_specs=[HBM] * len(in_cuts),
+        scratch_shapes=[pltpu.SemaphoreType.DMA((len(in_cuts),))],
+        compiler_params=params(1),
+        cost_estimate=cost(0, 4 << 20),
+        name="split_in",
+    )(expert_in)
+    first = after(in_chunks[0], (raw[half], qkv[1], qkv[2], qkv[4]))
+    in_held = [spread_over(first, "dp", 2)]
 
     raw[half] = after(raw[half], qkv)
 
@@ -302,23 +315,25 @@
         name="attention",
     )(exp_index[None], near, far, *[qkv[k] for k in range(exp_count)])
 
-    contexts = [*contexts[:-1], after(contexts[-1], in_near)]
+    contexts = [*contexts[:-1], after(contexts[-1], in_held[0])]
     crossed = [swap(contexts[k], "dp", k) for k in range(1, dp_count)]
 
     proj_far = swap(after(proj_near, contexts), "dp", 1)
+
+    in_held.append(spread_over(after(in_chunks[1], crossed), "dp", 2))
 
     out_cuts = cut(inner, (1, 3))
     out_chunks = pl.pallas_call(
-        functools.partial(split_kernel, out_cuts),
+        functools.partial(split_kernel, out_cuts, 1),
         out_shape=[jax.ShapeDtypeStruct((1, n, width), BF16) for _, n in out_cuts],
         in_specs=[HBM],
         out_specs=[HBM] * len(out_cuts),
         scratch_shapes=[pltpu.SemaphoreType.DMA((len(out_cuts),))],
-        compiler_params=params(20),
+        compiler_params=params(1),
         cost_estimate=cost(0, 4 << 20),
-        name="split",
+        name="split_out",
     )(after(expert_out, qkv))
-    out_held = [spread_over(after(out_chunks[0], crossed), "dp", 2)]
+    out_held = [spread_over(after(out_chunks[0], in_held[1]), "dp", 2)]
 
     cols = expert_ids[0]
     slots, mixed, gate = pl.pallas_call(
@@ -339,11 +354,16 @@
         compiler_params=params(20),
         cost_estimate=cost(2 * frames * width * (width + slots_count), 5 << 20),
         name="mix",
-    )(me[None], norm_gains, router.T, cols.T, cols, stream, proj_near, proj_far, contexts[0], *crossed)
+    )(after(me[None], in_held[1]), norm_gains, router.T, cols.T, cols, stream, proj_near, proj_far, contexts[0], *crossed)
 
     slots = after(slots, out_held[0])
     out_held.append(spread_over(after(out_chunks[1], (out_held[0], gate)), "dp", 2))
-    in_far = {k: swap(after(block, gate), "dp", 1) for k, block in in_near.items()}
+    in_near, in_far, places = [expert_in], [swap(after(expert_in, gate), "dp", 1)], [(0, 0)]
+    for k in range(2, dp_count, 2):
+        for held, (start, _) in zip(in_held, in_cuts):
+            in_near.append(held[k])
+            in_far.append(swap(after(held[k], gate), "dp", 1))
+            places.append((k // 2, start))
     out_own = swap(after(expert_out, gate), "dp", 1)
 
     arrived = lax.all_to_all(
@@ -357,14 +377,14 @@
 
     def hidden_units(slots_in, held, name):
         return pl.pallas_call(
-            functools.partial(hidden_kernel, step),
+            functools.partial(hidden_kernel, places, step),
             out_shape=jax.ShapeDtypeStruct((groups, slots_count, inner), BF16),
-            in_specs=[VMEM] * (1 + groups),
+            in_specs=[VMEM] * (1 + len(places)),
             out_specs=VMEM,
             compiler_params=params(16),
             cost_estimate=cost(2 * slots_count * width * inner * groups, 8 << 20),
             name=name,
-        )(slots_in, *[held[k] for k in sorted(held)])
+        )(slots_in, *held)
 
     hidden = [hidden_units(arrived, in_near, "hidden_near")]
     hidden.append(hidden_units(after(arrived, hidden[0]), in_far, "hidden_far"))

time: 191 us -> 195 us (1.021)
    unnamed x73 -> x93, local copies, waits for them, and re-layouts: 21.9 us -> 25.2 us
    all_to_all x1, waiting for transfers between devices: 15.7 us -> 12.5 us  [body(): lax.all_to_all(slots.reshape(exp_count, capacity, width), 'expert', split...]
    ppermute x28 -> x30, waiting for transfers between devices: 74 us -> 76.8 us  [swap(): return lax.ppermute(block, axis, [(i, i ^ mask) for i in range(count)])]
    ppermute x28 -> x30, starting transfers between devices: 24.1 us -> 25.8 us  [swap(): return lax.ppermute(block, axis, [(i, i ^ mask) for i in range(count)])]
    pallas_call x3 -> x4, Pallas kernels: 8.97 us -> 9.78 us  [the longest x2 8.63 us: hidden_units(): pl.pallas_call(functools.partial(hidden_kernel, places, step), out_shape=...]
  transfers between devices with their start and end apart: 30 -> 32, of which waited for: 21 -> 24; matrix products, arithmetic and copies ran while one was open for 2% -> 1% of each run, Pallas kernels for 15% -> 15%
where the time goes in v11:
time: 195 us
  waiting for transfers between devices  90.3 us (46%)
  Pallas kernels  32.4 us (17%)
  starting transfers between devices  31.5 us (16%)
  local copies, waits for them, and re-layouts  26.6 us (14%)
  between operations  13.7 us (7%)
    ppermute x30, waiting for transfers between devices, swap(): return lax.ppermute(block, axis, [(i, i ^ mask) for i in range(count)])  76.8 us
    ppermute x30, starting transfers between devices, swap(): return lax.ppermute(block, axis, [(i, i ^ mask) for i in range(count)])  25.8 us
    unnamed x93, local copies, waits for them, and re-layouts  25.2 us
    all_to_all x1, waiting for transfers between devices, body(): lax.all_to_all(slots.reshape(exp_count, capacity, width), 'expert', split...  12.5 us
    pallas_call x2, Pallas kernels, hidden_units(): pl.pallas_call(functools.partial(hidden_kernel, places, step), out_shape=...  8.63 us
    pallas_call x1, Pallas kernels, body(): pl.pallas_call(functools.partial(attention_kernel, dp_count, exp_count),...  7.04 us
    pallas_call x2, Pallas kernels, answers(): pl.pallas_call(functools.partial(answer_kernel, slices, rows, len(used),...  6.13 us
    all_to_all x1, starting transfers between devices, body(): lax.all_to_all(slots.reshape(exp_count, capacity, width), 'expert', split...  5.68 us
  transfers between devices with their start and end apart: 32, of which 24 were waited for; matrix products, arithmetic and copies ran while one was open for 1% of the time, Pallas kernels for 15%

profile of v11, /device:TPU:16, one launch (start us, length us, event | category | flops | bytes accessed | tf_op | source)
XLA Modules:
  0.0 194.6 jit_solution(6138269862399552135)
XLA Ops:
  6.6 1.6 collective-permute-start
  8.6 1.6 collective-permute-start.2
  11.7 1.6 copy-done.3
  14.8 2.2 %collective-permute-done.4.refs_4_ = bf16[3,128,256]{2,1,0:T(8,128)(2,1)S(1)} collective-permute-done((bf16[3,128,256]{2,1,0:T(8,128)(2,1)S(1)}, bf16[3,128,256]{2,1,0:T(8,128)(2,1)S(1)}, u32[]{:S(2)}, u32[]{:S(2)}) %collective-permute-start.4) | collective-permute-done | bytes 196640 | tf_op jit(solution)/shard_map/ppermute | solution.py:30
  17.0 1.7 collective-permute-done.2.refs_2_
  18.8 1.7 collective-permute-done.refs_1_
  25.9 6.6 %collective-permute-done.6.refs_6_ = bf16[3,128,256]{2,1,0:T(8,128)(2,1)S(1)} collective-permute-done((bf16[3,128,256]{2,1,0:T(8,128)(2,1)S(1)}, bf16[3,128,256]{2,1,0:T(8,128)(2,1)S(1)}, u32[]{:S(2)}, u32[]{:S(2)}) %collective-permute-start.6) | collective-permute-done | bytes 196640 | tf_op jit(solution)/shard_map/ppermute | solution.py:30
  34.7 4.3 %collective-permute-done.7.refs_7_ = bf16[3,128,256]{2,1,0:T(8,128)(2,1)S(1)} collective-permute-done((bf16[3,128,256]{2,1,0:T(8,128)(2,1)S(1)}, bf16[3,128,256]{2,1,0:T(8,128)(2,1)S(1)}, u32[]{:S(2)}, u32[]{:S(2)}) %collective-permute-start.7) | collective-permute-done | bytes 196640 | tf_op jit(solution)/shard_map/ppermute | solution.py:30
  41.1 2.7 %collective-permute-done.8.far_ref = bf16[2,256,1024]{2,1,0:T(8,128)(2,1)S(1)} collective-permute-done((bf16[2,256,1024]{2,1,0:T(8,128)(2,1)S(1)}, bf16[2,256,1024]{2,1,0:T(8,128)(2,1)S(1)}, u32[]{:S(2)}, u32[]{:S(2)}) %collective-permute-start.8) | collective-permute-done | bytes 1048608 | tf_op jit(solution)/shard_map/ppermute | solution.py:30
  45.6 7.0 %attention.1 = (bf16[256,256]{1,0:T(8,128)(2,1)S(1)}, bf16[256,256]{1,0:T(8,128)(2,1)S(1)}, bf16[256,256]{1,0:T(8,128)(2,1)S(1)}, bf16[256,256]{1,0:T(8,128)(2,1)S(1)}) custom-call(s32[1]{0:T(128)} %bitcast.me_ref.refs_0_, bf16[2,256,1024]{2,1,0:T(8,128)(2,1)S(1)} %get-tuple-element.46.near_ref, bf16[2,256,1024]{2,1,0:T(8,128)(2,1)S(1)} %collective-permute-done.8.far_ref, ...), custom_call_target="tpu_custom_call" | custom-call | flops 10485760 | bytes 20480 | tf_op jit(solution)/shard_map/attention/pallas_call | solution.py:301
  55.2 6.5 %collective-permute-done.11.refs_1_ = bf16[1,1024,896]{2,1,0:T(8,128)(2,1)} collective-permute-done((bf16[1,1024,896]{2,1,0:T(8,128)(2,1)}, bf16[1,1024,896]{2,1,0:T(8,128)(2,1)}, u32[]{:S(2)}, u32[]{:S(2)}) %collective-permute-start.11) | collective-permute-done | bytes 1835040 | tf_op jit(solution)/shard_map/ppermute | solution.py:30
  66.1 3.7 %collective-permute-done.10.refs_2_ = bf16[256,256]{1,0:T(8,128)(2,1)S(1)} collective-permute-done((bf16[256,256]{1,0:T(8,128)(2,1)}, bf16[256,256]{1,0:T(8,128)(2,1)S(1)}, u32[]{:S(2)}, u32[]{:S(2)}) %collective-permute-start.10) | collective-permute-done | bytes 131104 | tf_op jit(solution)/shard_map/ppermute | solution.py:30
  74.8 5.8 %collective-permute-done.13.refs_2_ = bf16[1,1024,128]{2,1,0:T(8,128)(2,1)S(1)} collective-permute-done((bf16[1,1024,128]{2,1,0:T(8,128)(2,1)}, bf16[1,1024,128]{2,1,0:T(8,128)(2,1)S(1)}, u32[]{:S(2)}, u32[]{:S(2)}) %collective-permute-start.13) | collective-permute-done | bytes 262176 | tf_op jit(solution)/shard_map/ppermute | solution.py:30
  87.7 4.6 %mix.1 = (bf16[640,1024]{1,0:T(8,128)(2,1)}, bf16[256,1024]{1,0:T(8,128)(2,1)S(1)}, f32[256,128]{1,0:T(8,128)S(1)}) custom-call(s32[1]{0:T(128)} %bitcast.1.me_ref, f32[2,1024]{1,0:T(2,128)S(1)} %copy-done.36, f32[8,1024]{1,0:T(8,128)S(1)} %bitcast.15, s32[2,256]{1,0:T(2,128)S(1)} %copy.13.rows_ref, s32[256,2]{1,0:T(8,128)S(1)} %bitcast.13, ...), custom_call_target="tpu_custom_call" | custom-call | flops 3407872 | bytes 20480 | tf_op jit(solution)/shard_map/mix/pallas_call | solution.py:339
  95.3 5.7 %all-to-all-start = ((bf16[8,80,1024]{2,1,0:T(8,128)(2,1)}), bf16[8,80,1024]{2,1,0:T(8,128)(2,1)S(1)}, u32[]{:S(2)}, u32[]{:S(2)}) async-start(bf16[8,80,1024]{2,1,0:T(8,128)(2,1)} %bitcast.6), calls=%async_computation | async-start | bytes 2621440 | tf_op jit(solution)/shard_map/all_to_all | solution.py:369
  103.3 2.6 %collective-permute-done.18.refs_2_ = bf16[1,1024,128]{2,1,0:T(8,128)(2,1)S(1)} collective-permute-done((bf16[1,1024,128]{2,1,0:T(8,128)(2,1)S(1)}, bf16[1,1024,128]{2,1,0:T(8,128)(2,1)S(1)}, u32[]{:S(2)}, u32[]{:S(2)}) %collective-permute-start.18) | collective-permute-done | bytes 262176 | tf_op jit(solution)/shard_map/ppermute | solution.py:30
  106.7 3.3 %collective-permute-done.20.refs_5_ = bf16[1,256,1024]{2,1,0:T(8,128)(2,1)S(1)} collective-permute-done((bf16[1,256,1024]{2,1,0:T(8,128)(2,1)S(1)}, bf16[1,256,1024]{2,1,0:T(8,128)(2,1)S(1)}, u32[]{:S(2)}, u32[]{:S(2)}) %collective-permute-start.20) | collective-permute-done | bytes 524320 | tf_op jit(solution)/shard_map/ppermute | solution.py:30
  110.0 2.1 %collective-permute-done.17.refs_1_ = bf16[1,1024,896]{2,1,0:T(8,128)(2,1)S(1)} collective-permute-done((bf16[1,1024,896]{2,1,0:T(8,128)(2,1)}, bf16[1,1024,896]{2,1,0:T(8,128)(2,1)S(1)}, u32[]{:S(2)}, u32[]{:S(2)}) %collective-permute-start.17) | collective-permute-done | bytes 1835040 | tf_op jit(solution)/shard_map/ppermute | solution.py:30
  116.1 12.5 %all-to-all-done = bf16[8,80,1024]{2,1,0:T(8,128)(2,1)S(1)} async-done(((bf16[8,80,1024]{2,1,0:T(8,128)(2,1)}), bf16[8,80,1024]{2,1,0:T(8,128)(2,1)S(1)}, u32[]{:S(2)}, u32[]{:S(2)}) %all-to-all-start) | async-done | bytes 1310752 | tf_op jit(solution)/shard_map/all_to_all | solution.py:369
  128.5 1.6 copy-done.4
  130.1 5.1 %hidden_near.1.refs_0_ = bf16[2,640,1024]{2,1,0:T(8,128)(2,1)S(1)} custom-call(bf16[640,1024]{1,0:T(8,128)(2,1)S(1)} %bitcast.10, bf16[1,1024,1024]{2,1,0:T(8,128)(2,1)S(1)} %copy-done.4, bf16[1,1024,896]{2,1,0:T(8,128)(2,1)} %collective-permute-done.11.refs_1_, bf16[1,1024,128]{2,1,0:T(8,128)(2,1)S(1)} %copy-done.18), custom_call_target="tpu_custom_call" | custom-call | flops 10485760 | bytes 32768 | tf_op jit(solution)/shard_map/hidden_near/pallas_call | solution.py:379
  135.3 3.3 %collective-permute-done.21.refs_1_ = bf16[1,768,1024]{2,1,0:T(8,128)(2,1)} collective-permute-done((bf16[1,768,1024]{2,1,0:T(8,128)(2,1)}, bf16[1,768,1024]{2,1,0:T(8,128)(2,1)}, u32[]{:S(2)}, u32[]{:S(2)}) %collective-permute-start.21) | collective-permute-done | bytes 1572896 | tf_op jit(solution)/shard_map/ppermute | solution.py:30
  138.6 3.5 %hidden_far.1.refs_1_ = bf16[2,640,1024]{2,1,0:T(8,128)(2,1)S(1)} custom-call(bf16[640,1024]{1,0:T(8,128)(2,1)S(1)} %bitcast.11, bf16[1,1024,1024]{2,1,0:T(8,128)(2,1)S(1)} %copy-done.8, bf16[1,1024,896]{2,1,0:T(8,128)(2,1)S(1)} %copy-done.10, bf16[1,1024,128]{2,1,0:T(8,128)(2,1)S(1)} %copy-done.20), custom_call_target="tpu_custom_call" | custom-call | flops 10485760 | bytes 32768 | tf_op jit(solution)/shard_map/hidden_far/pallas_call | solution.py:379
  142.1 3.5 %answer_first.1.refs_2_ = f32[640,1024]{1,0:T(8,128)S(1)} custom-call(bf16[2,640,1024]{2,1,0:T(8,128)(2,1)S(1)} %hidden_near.1.refs_0_, bf16[2,640,1024]{2,1,0:T(8,128)(2,1)S(1)} %hidden_far.1.refs_1_, bf16[1,1024,1024]{2,1,0:T(8,128)(2,1)S(1)} %copy-done.2, bf16[1,1024,1024]{2,1,0:T(8,128)(2,1)S(1)} %copy-done.6, ...), custom_call_target="tpu_custom_call" | custom-call | flops 20971520 | bytes 40960 | tf_op jit(solution)/shard_map/answer_first/pallas_call | solution.py:409
  145.7 2.6 %answer_near.1.refs_3_ = f32[640,1024]{1,0:T(8,128)S(1)} custom-call(bf16[2,640,1024]{2,1,0:T(8,128)(2,1)S(1)} %hidden_near.1.refs_0_, bf16[1,768,1024]{2,1,0:T(8,128)(2,1)} %collective-permute-done.21.refs_1_, f32[640,1024]{1,0:T(8,128)S(1)} %answer_first.1.refs_2_), custom_call_target="tpu_custom_call" | custom-call | flops 5242880 | bytes 40960 | tf_op jit(solution)/shard_map/answer_near/pallas_call | solution.py:409
  153.5 3.5 %collective-permute-start.27 = (bf16[80,1024]{1,0:T(8,128)(2,1)S(1)}, bf16[80,1024]{1,0:T(8,128)(2,1)S(1)}, u32[]{:S(2)}, u32[]{:S(2)}) collective-permute-start(bf16[80,1024]{1,0:T(8,128)(2,1)S(1)} %get-tuple-element.80), channel_id=1, source_target_pairs={{0,5},{1,4},{2,7},{3,6},{4,1},{5,0},{6,3},{7,2},{8,13},{9,12},{10,... | collective-permute-start | bytes 491528 | tf_op jit(solution)/shard_map/ppermute | solution.py:30
  157.6 4.3 %collective-permute-done.24.refs_2_ = bf16[80,1024]{1,0:T(8,128)(2,1)S(1)} collective-permute-done((bf16[80,1024]{1,0:T(8,128)(2,1)S(1)}, bf16[80,1024]{1,0:T(8,128)(2,1)S(1)}, u32[]{:S(2)}, u32[]{:S(2)}) %collective-permute-start.24) | collective-permute-done | bytes 163872 | tf_op jit(solution)/shard_map/ppermute | solution.py:30
  161.9 2.8 %collective-permute-done.25.refs_3_ = bf16[80,1024]{1,0:T(8,128)(2,1)S(1)} collective-permute-done((bf16[80,1024]{1,0:T(8,128)(2,1)S(1)}, bf16[80,1024]{1,0:T(8,128)(2,1)S(1)}, u32[]{:S(2)}, u32[]{:S(2)}) %collective-permute-start.25) | collective-permute-done | bytes 163872 | tf_op jit(solution)/shard_map/ppermute | solution.py:30
  165.3 10.4 %collective-permute-done.27.refs_5_ = bf16[80,1024]{1,0:T(8,128)(2,1)S(1)} collective-permute-done((bf16[80,1024]{1,0:T(8,128)(2,1)S(1)}, bf16[80,1024]{1,0:T(8,128)(2,1)S(1)}, u32[]{:S(2)}, u32[]{:S(2)}) %collective-permute-start.27) | collective-permute-done | bytes 163872 | tf_op jit(solution)/shard_map/ppermute | solution.py:30
  175.7 6.5 %collective-permute-done.28.refs_6_ = bf16[80,1024]{1,0:T(8,128)(2,1)S(1)} collective-permute-done((bf16[80,1024]{1,0:T(8,128)(2,1)S(1)}, bf16[80,1024]{1,0:T(8,128)(2,1)S(1)}, u32[]{:S(2)}, u32[]{:S(2)}) %collective-permute-start.28) | collective-permute-done | bytes 163872 | tf_op jit(solution)/shard_map/ppermute | solution.py:30
  182.2 3.1 %collective-permute-done.29.refs_7_ = bf16[80,1024]{1,0:T(8,128)(2,1)S(1)} collective-permute-done((bf16[80,1024]{1,0:T(8,128)(2,1)S(1)}, bf16[80,1024]{1,0:T(8,128)(2,1)S(1)}, u32[]{:S(2)}, u32[]{:S(2)}) %collective-permute-start.29) | collective-permute-done | bytes 163872 | tf_op jit(solution)/shard_map/ppermute | solution.py:30
  185.4 2.3 %combine.1 = bf16[1,256,1024]{2,1,0:T(8,128)(2,1)} custom-call(s32[1]{0:T(128)} %bitcast.me_ref.refs_0_, f32[256,128]{1,0:T(8,128)S(1)} %copy-done.26, s32[256,2]{1,0:T(8,128)S(1)} %bitcast.14, bf16[256,1024]{1,0:T(8,128)(2,1)S(1)} %copy-done.16, bf16[80,1024]{1,0:T(8,128)(2,1)S(1)} %get-tuple-element.75.refs_0_, ...), custom_call_target="tpu_custom_call" | custom-call | flops 2621440 | bytes 12288 | tf_op jit(solution)/shard_map/combine/pallas_call | solution.py:434
  (143 shorter events, 50.6 us)
Async XLA Ops:
  6.5 56.2 %all-gather.2.cloned.1.call-start = ((), (), s32[]{:S(2)}) async-start(), calls=%async_computation.1 | async-start | bytes 1179648 | tf_op jit(solution)/shard_map/all_gather | solution.py:259
  6.6 13.9 %collective-permute-start = (bf16[1,256,1024]{2,1,0:T(8,128)(2,1)}, bf16[1,256,1024]{2,1,0:T(8,128)(2,1)S(1)}, u32[]{:S(2)}, u32[]{:S(2)}) collective-permute-start(bf16[1,256,1024]{2,1,0:T(8,128)(2,1)} %refs_0_.2), channel_id=1, source_target_pairs={{0,16},{8,24},{16,0},{24,8},{1,17},{9,25},{17,1},{25,9},{2,18},{10... | collective-permute-start | bytes 1572872 | tf_op jit(solution)/shard_map/ppermute | solution.py:30
  8.2 8.8 %collective-permute-start.4 = (bf16[3,128,256]{2,1,0:T(8,128)(2,1)S(1)}, bf16[3,128,256]{2,1,0:T(8,128)(2,1)S(1)}, u32[]{:S(2)}, u32[]{:S(2)}) collective-permute-start(bf16[3,128,256]{2,1,0:T(8,128)(2,1)S(1)} %constant_dynamic-slice_fusion.refs_0_), channel_id=1, source_target_pairs={{0,4},{1,5},{2,6},{3,7},{4,0},{5,1},{6,2},{7,3},{8,12},{9,13},{10,... | collective-permute-start | bytes 589832 | tf_op jit(solution)/shard_map/ppermute | solution.py:30
  8.6 10.2 %collective-permute-start.2 = (bf16[3,128,256]{2,1,0:T(8,128)(2,1)S(1)}, bf16[3,128,256]{2,1,0:T(8,128)(2,1)S(1)}, u32[]{:S(2)}, u32[]{:S(2)}) collective-permute-start(bf16[3,128,256]{2,1,0:T(8,128)(2,1)S(1)} %constant_dynamic-slice_fusion.refs_0_), channel_id=1, source_target_pairs={{0,2},{1,3},{2,0},{3,1},{4,6},{5,7},{6,4},{7,5},{8,10},{9,11},{10,... | collective-permute-start | bytes 589832 | tf_op jit(solution)/shard_map/ppermute | solution.py:30
  10.2 8.6 %collective-permute-start.1 = (bf16[3,128,256]{2,1,0:T(8,128)(2,1)S(1)}, bf16[3,128,256]{2,1,0:T(8,128)(2,1)S(1)}, u32[]{:S(2)}, u32[]{:S(2)}) collective-permute-start(bf16[3,128,256]{2,1,0:T(8,128)(2,1)S(1)} %constant_dynamic-slice_fusion.refs_0_), channel_id=1, source_target_pairs={{0,1},{1,0},{2,3},{3,2},{4,5},{5,4},{6,7},{7,6},{8,9},{9,8},{10,11... | collective-permute-start | bytes 589832 | tf_op jit(solution)/shard_map/ppermute | solution.py:30
  20.5 41.2 %collective-permute-start.11 = (bf16[1,1024,896]{2,1,0:T(8,128)(2,1)}, bf16[1,1024,896]{2,1,0:T(8,128)(2,1)}, u32[]{:S(2)}, u32[]{:S(2)}) collective-permute-start(bf16[1,1024,896]{2,1,0:T(8,128)(2,1)} %copy-done.37), channel_id=1, source_target_pairs={{0,16},{8,24},{16,0},{24,8},{1,17},{9,25},{17,1},{25,9},{2,18},{10... | collective-permute-start | bytes 5505032 | tf_op jit(solution)/shard_map/ppermute | solution.py:30
  22.7 9.8 %collective-permute-start.6 = (bf16[3,128,256]{2,1,0:T(8,128)(2,1)S(1)}, bf16[3,128,256]{2,1,0:T(8,128)(2,1)S(1)}, u32[]{:S(2)}, u32[]{:S(2)}) collective-permute-start(bf16[3,128,256]{2,1,0:T(8,128)(2,1)S(1)} %constant_dynamic-slice_fusion.refs_0_), channel_id=1, source_target_pairs={{0,6},{1,7},{2,4},{3,5},{4,2},{5,3},{6,0},{7,1},{8,14},{9,15},{10,... | collective-permute-start | bytes 589832 | tf_op jit(solution)/shard_map/ppermute | solution.py:30
  23.9 15.0 %collective-permute-start.5 = (bf16[3,128,256]{2,1,0:T(8,128)(2,1)S(1)}, bf16[3,128,256]{2,1,0:T(8,128)(2,1)S(1)}, u32[]{:S(2)}, u32[]{:S(2)}) collective-permute-start(bf16[3,128,256]{2,1,0:T(8,128)(2,1)S(1)} %collective-permute-done.4.refs_4_), channel_id=1, source_target_pairs={{0,1},{1,0},{2,3},{3,2},{4,5},{5,4},{6,7},{7,6},{8,9},{9,8},{10,11... | collective-permute-start | bytes 589832 | tf_op jit(solution)/shard_map/ppermute | solution.py:30
  25.4 13.6 %collective-permute-start.3 = (bf16[3,128,256]{2,1,0:T(8,128)(2,1)S(1)}, bf16[3,128,256]{2,1,0:T(8,128)(2,1)S(1)}, u32[]{:S(2)}, u32[]{:S(2)}) collective-permute-start(bf16[3,128,256]{2,1,0:T(8,128)(2,1)S(1)} %collective-permute-done.2.refs_2_), channel_id=1, source_target_pairs={{0,1},{1,0},{2,3},{3,2},{4,5},{5,4},{6,7},{7,6},{8,9},{9,8},{10,11... | collective-permute-start | bytes 589832 | tf_op jit(solution)/shard_map/ppermute | solution.py:30
  32.5 6.4 %collective-permute-start.7 = (bf16[3,128,256]{2,1,0:T(8,128)(2,1)S(1)}, bf16[3,128,256]{2,1,0:T(8,128)(2,1)S(1)}, u32[]{:S(2)}, u32[]{:S(2)}) collective-permute-start(bf16[3,128,256]{2,1,0:T(8,128)(2,1)S(1)} %collective-permute-done.6.refs_6_), channel_id=1, source_target_pairs={{0,1},{1,0},{2,3},{3,2},{4,5},{5,4},{6,7},{7,6},{8,9},{9,8},{10,11... | collective-permute-start | bytes 589832 | tf_op jit(solution)/shard_map/ppermute | solution.py:30
  41.1 2.7 %collective-permute-start.8 = (bf16[2,256,1024]{2,1,0:T(8,128)(2,1)S(1)}, bf16[2,256,1024]{2,1,0:T(8,128)(2,1)S(1)}, u32[]{:S(2)}, u32[]{:S(2)}) collective-permute-start(bf16[2,256,1024]{2,1,0:T(8,128)(2,1)S(1)} %get-tuple-element.46.near_ref), channel_id=1, source_target_pairs={{0,8},{8,0},{16,24},{24,16},{1,9},{9,1},{17,25},{25,17},{2,10},{10... | collective-permute-start | bytes 3145736 | tf_op jit(solution)/shard_map/ppermute | solution.py:30
  62.8 20.2 %collective-permute-start.14 = (bf16[1024,512]{1,0:T(8,128)(2,1)}, bf16[1024,512]{1,0:T(8,128)(2,1)}, u32[]{:S(2)}, u32[]{:S(2)}) collective-permute-start(bf16[1024,512]{1,0:T(8,128)(2,1)} %all-gather.2.cloned.1.call-done.near_ref), channel_id=1, source_target_pairs={{0,8},{8,0},{16,24},{24,16},{1,9},{9,1},{17,25},{25,17},{2,10},{10... | collective-permute-start | bytes 3145736 | tf_op jit(solution)/shard_map/ppermute | solution.py:30
  62.8 2.7 %collective-permute-start.9 = (bf16[256,256]{1,0:T(8,128)(2,1)}, bf16[256,256]{1,0:T(8,128)(2,1)S(1)}, u32[]{:S(2)}, u32[]{:S(2)}) collective-permute-start(bf16[256,256]{1,0:T(8,128)(2,1)} %copy-done.42), channel_id=1, source_target_pairs={{0,8},{8,0},{16,24},{24,16},{1,9},{9,1},{17,25},{25,17},{2,10},{10... | collective-permute-start | bytes 393224 | tf_op jit(solution)/shard_map/ppermute | solution.py:30
  63.3 6.6 %collective-permute-start.10 = (bf16[256,256]{1,0:T(8,128)(2,1)}, bf16[256,256]{1,0:T(8,128)(2,1)S(1)}, u32[]{:S(2)}, u32[]{:S(2)}) collective-permute-start(bf16[256,256]{1,0:T(8,128)(2,1)} %copy-done.41), channel_id=1, source_target_pairs={{0,16},{8,24},{16,0},{24,8},{1,17},{9,25},{17,1},{25,9},{2,18},{10... | collective-permute-start | bytes 393224 | tf_op jit(solution)/shard_map/ppermute | solution.py:30
  64.7 6.0 %collective-permute-start.12 = (bf16[256,256]{1,0:T(8,128)(2,1)}, bf16[256,256]{1,0:T(8,128)(2,1)S(1)}, u32[]{:S(2)}, u32[]{:S(2)}) collective-permute-start(bf16[256,256]{1,0:T(8,128)(2,1)} %copy-done.40), channel_id=1, source_target_pairs={{0,24},{8,16},{16,8},{24,0},{1,25},{9,17},{17,9},{25,1},{2,26},{10... | collective-permute-start | bytes 393224 | tf_op jit(solution)/shard_map/ppermute | solution.py:30
  71.4 9.2 %collective-permute-start.13 = (bf16[1,1024,128]{2,1,0:T(8,128)(2,1)}, bf16[1,1024,128]{2,1,0:T(8,128)(2,1)S(1)}, u32[]{:S(2)}, u32[]{:S(2)}) collective-permute-start(bf16[1,1024,128]{2,1,0:T(8,128)(2,1)} %copy-done.39), channel_id=1, source_target_pairs={{0,16},{8,24},{16,0},{24,8},{1,17},{9,25},{17,1},{25,9},{2,18},{10... | collective-permute-start | bytes 786440 | tf_op jit(solution)/shard_map/ppermute | solution.py:30
  81.3 13.9 %collective-permute-start.15 = (bf16[1,256,1024]{2,1,0:T(8,128)(2,1)}, bf16[1,256,1024]{2,1,0:T(8,128)(2,1)S(1)}, u32[]{:S(2)}, u32[]{:S(2)}) collective-permute-start(bf16[1,256,1024]{2,1,0:T(8,128)(2,1)} %get-tuple-element.63), channel_id=1, source_target_pairs={{0,16},{8,24},{16,0},{24,8},{1,17},{9,25},{17,1},{25,9},{2,18},{10... | collective-permute-start | bytes 1572872 | tf_op jit(solution)/shard_map/ppermute | solution.py:30
  95.3 33.2 %all-to-all-start = ((bf16[8,80,1024]{2,1,0:T(8,128)(2,1)}), bf16[8,80,1024]{2,1,0:T(8,128)(2,1)S(1)}, u32[]{:S(2)}, u32[]{:S(2)}) async-start(bf16[8,80,1024]{2,1,0:T(8,128)(2,1)} %bitcast.6), calls=%async_computation | async-start | bytes 2621440 | tf_op jit(solution)/shard_map/all_to_all | solution.py:369
  101.0 12.4 %collective-permute-start.16 = (bf16[1,1024,1024]{2,1,0:T(8,128)(2,1)}, bf16[1,1024,1024]{2,1,0:T(8,128)(2,1)S(1)}, u32[]{:S(2)}, u32[]{:S(2)}) collective-permute-start(bf16[1,1024,1024]{2,1,0:T(8,128)(2,1)} %refs_0_.3), channel_id=1, source_target_pairs={{0,8},{8,0},{16,24},{24,16},{1,9},{9,1},{17,25},{25,17},{2,10},{10... | collective-permute-start | bytes 6291464 | tf_op jit(solution)/shard_map/ppermute | solution.py:30
  101.0 13.8 %collective-permute-start.19 = (bf16[1,1024,1024]{2,1,0:T(8,128)(2,1)}, bf16[1,1024,1024]{2,1,0:T(8,128)(2,1)S(1)}, u32[]{:S(2)}, u32[]{:S(2)}) collective-permute-start(bf16[1,1024,1024]{2,1,0:T(8,128)(2,1)} %refs_2_.1), channel_id=1, source_target_pairs={{0,8},{8,0},{16,24},{24,16},{1,9},{9,1},{17,25},{25,17},{2,10},{10... | collective-permute-start | bytes 6291464 | tf_op jit(solution)/shard_map/ppermute | solution.py:30
  101.5 10.6 %collective-permute-start.17 = (bf16[1,1024,896]{2,1,0:T(8,128)(2,1)}, bf16[1,1024,896]{2,1,0:T(8,128)(2,1)S(1)}, u32[]{:S(2)}, u32[]{:S(2)}) collective-permute-start(bf16[1,1024,896]{2,1,0:T(8,128)(2,1)} %collective-permute-done.11.refs_1_), channel_id=1, source_target_pairs={{0,8},{8,0},{16,24},{24,16},{1,9},{9,1},{17,25},{25,17},{2,10},{10... | collective-permute-start | bytes 5505032 | tf_op jit(solution)/shard_map/ppermute | solution.py:30
  101.5 37.1 %collective-permute-start.21 = (bf16[1,768,1024]{2,1,0:T(8,128)(2,1)}, bf16[1,768,1024]{2,1,0:T(8,128)(2,1)}, u32[]{:S(2)}, u32[]{:S(2)}) collective-permute-start(bf16[1,768,1024]{2,1,0:T(8,128)(2,1)} %copy-done.38), channel_id=1, source_target_pairs={{0,16},{8,24},{16,0},{24,8},{1,17},{9,25},{17,1},{25,9},{2,18},{10... | collective-permute-start | bytes 4718600 | tf_op jit(solution)/shard_map/ppermute | solution.py:30
  103.0 2.8 %collective-permute-start.18 = (bf16[1,1024,128]{2,1,0:T(8,128)(2,1)S(1)}, bf16[1,1024,128]{2,1,0:T(8,128)(2,1)S(1)}, u32[]{:S(2)}, u32[]{:S(2)}) collective-permute-start(bf16[1,1024,128]{2,1,0:T(8,128)(2,1)S(1)} %copy-done.18), channel_id=1, source_target_pairs={{0,8},{8,0},{16,24},{24,16},{1,9},{9,1},{17,25},{25,17},{2,10},{10... | collective-permute-start | bytes 786440 | tf_op jit(solution)/shard_map/ppermute | solution.py:30
  106.6 3.4 %collective-permute-start.20 = (bf16[1,256,1024]{2,1,0:T(8,128)(2,1)S(1)}, bf16[1,256,1024]{2,1,0:T(8,128)(2,1)S(1)}, u32[]{:S(2)}, u32[]{:S(2)}) collective-permute-start(bf16[1,256,1024]{2,1,0:T(8,128)(2,1)S(1)} %collective-permute-done.15.refs_4_), channel_id=1, source_target_pairs={{0,8},{8,0},{16,24},{24,16},{1,9},{9,1},{17,25},{25,17},{2,10},{10... | collective-permute-start | bytes 1572872 | tf_op jit(solution)/shard_map/ppermute | solution.py:30
  138.6 9.7 %collective-permute-start.22 = (bf16[1,768,1024]{2,1,0:T(8,128)(2,1)}, bf16[1,768,1024]{2,1,0:T(8,128)(2,1)S(1)}, u32[]{:S(2)}, u32[]{:S(2)}) collective-permute-start(bf16[1,768,1024]{2,1,0:T(8,128)(2,1)} %collective-permute-done.21.refs_1_), channel_id=1, source_target_pairs={{0,8},{8,0},{16,24},{24,16},{1,9},{9,1},{17,25},{25,17},{2,10},{10... | collective-permute-start | bytes 4718600 | tf_op jit(solution)/shard_map/ppermute | solution.py:30
  149.6 7.4 %collective-permute-start.23 = (bf16[80,1024]{1,0:T(8,128)(2,1)S(1)}, bf16[80,1024]{1,0:T(8,128)(2,1)S(1)}, u32[]{:S(2)}, u32[]{:S(2)}) collective-permute-start(bf16[80,1024]{1,0:T(8,128)(2,1)S(1)} %get-tuple-element.76), channel_id=1, source_target_pairs={{0,1},{1,0},{2,3},{3,2},{4,5},{5,4},{6,7},{7,6},{8,9},{9,8},{10,11... | collective-permute-start | bytes 491528 | tf_op jit(solution)/shard_map/ppermute | solution.py:30
  151.1 10.7 %collective-permute-start.24 = (bf16[80,1024]{1,0:T(8,128)(2,1)S(1)}, bf16[80,1024]{1,0:T(8,128)(2,1)S(1)}, u32[]{:S(2)}, u32[]{:S(2)}) collective-permute-start(bf16[80,1024]{1,0:T(8,128)(2,1)S(1)} %get-tuple-element.77), channel_id=1, source_target_pairs={{0,2},{1,3},{2,0},{3,1},{4,6},{5,7},{6,4},{7,5},{8,10},{9,11},{10,... | collective-permute-start | bytes 491528 | tf_op jit(solution)/shard_map/ppermute | solution.py:30
  152.6 12.0 %collective-permute-start.25 = (bf16[80,1024]{1,0:T(8,128)(2,1)S(1)}, bf16[80,1024]{1,0:T(8,128)(2,1)S(1)}, u32[]{:S(2)}, u32[]{:S(2)}) collective-permute-start(bf16[80,1024]{1,0:T(8,128)(2,1)S(1)} %get-tuple-element.78), channel_id=1, source_target_pairs={{0,3},{1,2},{2,1},{3,0},{4,7},{5,6},{6,5},{7,4},{8,11},{9,10},{10,... | collective-permute-start | bytes 491528 | tf_op jit(solution)/shard_map/ppermute | solution.py:30
  153.1 12.2 %collective-permute-start.26 = (bf16[80,1024]{1,0:T(8,128)(2,1)S(1)}, bf16[80,1024]{1,0:T(8,128)(2,1)S(1)}, u32[]{:S(2)}, u32[]{:S(2)}) collective-permute-start(bf16[80,1024]{1,0:T(8,128)(2,1)S(1)} %get-tuple-element.79), channel_id=1, source_target_pairs={{0,4},{1,5},{2,6},{3,7},{4,0},{5,1},{6,2},{7,3},{8,12},{9,13},{10,... | collective-permute-start | bytes 491528 | tf_op jit(solution)/shard_map/ppermute | solution.py:30
  153.5 22.2 %collective-permute-start.27 = (bf16[80,1024]{1,0:T(8,128)(2,1)S(1)}, bf16[80,1024]{1,0:T(8,128)(2,1)S(1)}, u32[]{:S(2)}, u32[]{:S(2)}) collective-permute-start(bf16[80,1024]{1,0:T(8,128)(2,1)S(1)} %get-tuple-element.80), channel_id=1, source_target_pairs={{0,5},{1,4},{2,7},{3,6},{4,1},{5,0},{6,3},{7,2},{8,13},{9,12},{10,... | collective-permute-start | bytes 491528 | tf_op jit(solution)/shard_map/ppermute | solution.py:30
  157.0 25.2 %collective-permute-start.28 = (bf16[80,1024]{1,0:T(8,128)(2,1)S(1)}, bf16[80,1024]{1,0:T(8,128)(2,1)S(1)}, u32[]{:S(2)}, u32[]{:S(2)}) collective-permute-start(bf16[80,1024]{1,0:T(8,128)(2,1)S(1)} %get-tuple-element.81), channel_id=1, source_target_pairs={{0,6},{1,7},{2,4},{3,5},{4,2},{5,3},{6,0},{7,1},{8,14},{9,15},{10,... | collective-permute-start | bytes 491528 | tf_op jit(solution)/shard_map/ppermute | solution.py:30
  161.9 23.5 %collective-permute-start.29 = (bf16[80,1024]{1,0:T(8,128)(2,1)S(1)}, bf16[80,1024]{1,0:T(8,128)(2,1)S(1)}, u32[]{:S(2)}, u32[]{:S(2)}) collective-permute-start(bf16[80,1024]{1,0:T(8,128)(2,1)S(1)} %get-tuple-element.82), channel_id=1, source_target_pairs={{0,7},{1,6},{2,5},{3,4},{4,3},{5,2},{6,1},{7,0},{8,15},{9,14},{10,... | collective-permute-start | bytes 491528 | tf_op jit(solution)/shard_map/ppermute | solution.py:30
  (46 other events, 385.8 us)
Sparse Core Ops, SparseCore 0:
  22.8 39.8 all-gather.1
